TPU v7x, 32 devices: a whole 2x2x4 slice. The times are simulated.
32 devices in a mesh: slab: 8 (over z, x), grp: 4 (over y, core).
Axes of the slice: x: 2, y: 2, z: 4, core: 2. Of those that a mesh axis runs over, the one named last changes fastest.
Arguments:
- fine_input: bfloat16 [16, 128, 128, 128], P('slab', 'grp'), may hold values from -6 to 6
- out_grad: bfloat16 [16, 128, 128, 128], P('slab', 'grp')
- pre_norm: bfloat16 [256, 8, 4096], P('slab', None, 'grp')
- act_out: bfloat16 [256, 8, 4096], P('slab', None, 'grp'), as said below
- norm_gain: float32 [256], P('slab'), may hold values from 0.5 to 2
- w_down: bfloat16 [27, 128, 256], replicated, may hold values from -0.109375 to 0.109375
- w_up: bfloat16 [8, 256, 128], replicated, may hold values from -0.375 to 0.375
Outputs:
- grad_input: bfloat16 [16, 128, 128, 128], P('slab', 'grp')
- grad_down: float32 [256, 27, 128], P(('slab', 'grp'))
- grad_gain: float32 [256], P('slab')
- grad_shift: float32 [256], P('slab')
Inputs may be any that keep to these rules, and one draw needn't show every extreme that they name: `act_out`: the ReLU's output saved by the forward pass, zero where a unit was off.
All inputs are finite; a program needn't handle non-finite values.
Results may differ from a plain program's by a relative error of at most 0.0095.
Values may be sent and summed in bfloat16 or wider, within the bound.
No kernel may reach another device: no remote copies, remote signals or barrier semaphores. Data moves between devices by JAX's collectives and lax.ppermute only.
A program may use at most 64 MiB of HBM per device.

v0:
```python
import math

import jax
import jax.numpy as jnp
from jax import lax
from jax.sharding import PartitionSpec as P

tap_places = ((1, 1), (0, 0), (1, 0))


def from_behind(shard, axis, by):
    devices = lax.axis_size(axis)
    pairs = [(i, i + by) for i in range(devices) if 0 <= i + by < devices]
    return lax.ppermute(shard, axis, pairs)


def norm_backward(
    values, grad_vals, saved_act, gain_vals, cell_total, reduce_moments, reduce_terms
):
    moment_one, moment_two = reduce_moments(
        jnp.sum(values, axis=(1, 2)), jnp.sum(values * values, axis=(1, 2))
    )
    channel_mean = moment_one / cell_total
    variance = moment_two / cell_total - channel_mean * channel_mean
    inv_std = lax.rsqrt(variance + 1e-05)
    normed = (values - channel_mean[:, None, None]) * inv_std[:, None, None]
    masked = jnp.where(saved_act > 0, grad_vals, jnp.zeros_like(grad_vals))
    total_one, total_two = reduce_terms(
        jnp.sum(masked, axis=(1, 2)), jnp.sum(masked * normed, axis=(1, 2))
    )
    shift_grad = total_one / cell_total
    gain_grad = total_two / cell_total
    grad_act = (
        (gain_vals * inv_std)[:, None, None]
        * (masked - shift_grad[:, None, None] - normed * gain_grad[:, None, None])
    ).astype(jnp.bfloat16)
    return (grad_act, gain_grad, shift_grad)


def local(fine_input, out_grad, pre_norm, act_out, norm_gain, w_down, w_up):
    fine_planes, fine_rows, fine_depth, width_in = fine_input.shape
    plane_count = fine_planes // 2
    row_count = fine_rows // 2
    depth = fine_depth // 2
    width_deep = w_up.shape[1]
    cell_count = plane_count * row_count * depth
    cell_total = pre_norm.shape[1] * pre_norm.shape[2] * lax.axis_size("grp")
    parity_grad = (
        out_grad.reshape(plane_count, 2, row_count, 2, depth, 2, width_in)
        .transpose(1, 3, 5, 0, 2, 4, 6)
        .reshape(8, cell_count, width_in)
    )
    deep_grad = jnp.einsum("poj,pnj->on", w_up, parity_grad, preferred_element_type=jnp.float32)
    deep_shape = (width_deep, plane_count, row_count * depth)
    deep_bf = deep_grad.astype(jnp.bfloat16).reshape(deep_shape)
    channel_grad = lax.all_to_all(deep_bf, "slab", split_axis=0, concat_axis=1, tiled=True)
    grad_channels, grad_gain, grad_shift = norm_backward(
        pre_norm.astype(jnp.float32),
        channel_grad.astype(jnp.float32),
        act_out,
        norm_gain,
        cell_total,
        lambda first_sum, second_sum: lax.psum((first_sum, second_sum), "grp"),
        lambda first_sum, second_sum: lax.psum((first_sum, second_sum), "grp"),
    )
    back_first = lax.all_to_all(grad_channels, "slab", split_axis=1, concat_axis=0, tiled=True)
    upper = from_behind(back_first, "slab", -1)
    with_plane = jnp.concatenate([back_first, upper], axis=1)
    row_data = from_behind(with_plane[:, :, :depth], "grp", -1)
    extended = jnp.concatenate([with_plane, row_data], axis=2)
    positions = lax.broadcasted_iota(jnp.int32, (1, 1, extended.shape[2]), 2) % depth
    tail_zero = jnp.zeros((width_deep, plane_count + 1, 1), jnp.bfloat16)
    shifted = jnp.where(
        positions != depth - 1,
        jnp.concatenate([extended[:, :, 1:], tail_zero], axis=2),
        jnp.zeros_like(extended),
    )
    fine_split = fine_input.reshape(plane_count, 2, row_count, 2, depth, 2, width_in)

    def window(sources, offsets):
        off_x, off_y, off_z = offsets
        source = sources[1] if off_z else sources[0]
        start_yz = off_y * depth
        return source[
            :, off_x : off_x + plane_count, start_yz : start_yz + row_count * depth
        ].reshape(source.shape[0], cell_count)

    tap_list = []
    for tap_index in range(27):
        par_x, off_x = tap_places[tap_index // 9]
        par_y, off_y = tap_places[tap_index // 3 % 3]
        par_z, off_z = tap_places[tap_index % 3]
        tap_list.append((tap_index, (par_x, par_y, par_z), (off_x, off_y, off_z)))
    fine_blocks = {}
    for par_x in range(2):
        for par_y in range(2):
            for par_z in range(2):
                fine_blocks[par_x, par_y, par_z] = fine_split[
                    :, par_x, :, par_y, :, par_z, :
                ].reshape(cell_count, width_in)
    blocks = {}
    for tap_index, parity, offsets in tap_list:
        term = jnp.einsum(
            "on,jo->nj",
            window((extended, shifted), offsets),
            w_down[tap_index],
            preferred_element_type=jnp.float32,
        )
        if parity in blocks:
            blocks[parity] = blocks[parity] + term
        else:
            blocks[parity] = term
    ordered = [
        blocks[par_x, par_y, par_z]
        for par_x in range(2)
        for par_y in range(2)
        for par_z in range(2)
    ]
    stacked = jnp.stack(ordered, 0).reshape(2, 2, 2, plane_count, row_count, depth, width_in)
    grad_input = (
        stacked.transpose(3, 0, 4, 1, 5, 2, 6)
        .reshape(fine_planes, fine_rows, fine_depth, width_in)
        .astype(jnp.bfloat16)
    )
    grad_scale = 1.0 / math.sqrt(cell_total)
    pieces = (extended, shifted)
    rows_out = [
        jnp.dot(window(pieces, offsets), fine_blocks[parity], preferred_element_type=jnp.float32)
        for tap_index, parity, offsets in tap_list
    ]
    slab_rows = lax.psum_scatter(
        jnp.stack(rows_out, 1) * grad_scale, "slab", scatter_dimension=0, tiled=True
    )
    grad_down = lax.psum_scatter(
        slab_rows.astype(jnp.bfloat16), "grp", scatter_dimension=0, tiled=True
    ).astype(jnp.float32)
    return (grad_input, grad_down, grad_gain, grad_shift)


def solution(mesh):
    return jax.shard_map(
        local,
        mesh=mesh,
        in_specs=(
            P("slab", "grp", None, None),
            P("slab", "grp", None, None),
            P("slab", None, "grp"),
            P("slab", None, "grp"),
            P("slab"),
            P(),
            P(),
        ),
        out_specs=(
            P("slab", "grp", None, None),
            P(("slab", "grp"), None, None),
            P("slab"),
            P("slab"),
        ),
        check_vma=False,
    )
```

profile of v0, /device:TPU:0, one launch (start us, length us, event | category | flops | bytes accessed | tf_op | source)
XLA Modules:
  0.0 213.3 jit_solution(13646476012696015012)
XLA Ops:
  7.2 2.2 %copy.24 = bf16[2,2,2,1,16,64,128]{6,5,4,2,1,0,3:T(8,128)(2,1)S(1)} copy(bf16[2,2,2,1,16,64,128]{6,2,5,1,4,0,3:T(2,128)(2,1)} %bitcast.405) | data formatting | bytes 4194304 | tf_op jit(solution)/shard_map/transpose | solution.py:50
  9.4 0.7 fusion.1
  10.7 1.0 reduce
  11.7 1.2 reshape.139
  12.9 7.3 %all-to-all-start = ((bf16[8,2,16384]{2,1,0:T(2,128)(2,1)}), bf16[8,2,16384]{2,1,0:T(2,128)(2,1)S(1)}, u32[]{:S(2)}, u32[]{:S(2)}) async-start(bf16[8,2,16384]{2,1,0:T(2,128)(2,1)} %reshape.139), calls=%async_computation | async-start | bytes 1048576 | tf_op jit(solution)/shard_map/all_to_all | solution.py:56
  20.6 6.6 %all-reduce.3 = (f32[32]{0:T(128)S(1)}, f32[32]{0:T(128)S(1)}) all-reduce(f32[32]{0:T(128)S(1)} %get-tuple-element.7, f32[32]{0:T(128)S(1)} %get-tuple-element.6), channel_id=1, replica_groups=mesh['slab'=8,'grp'=4] {'grp'}, use_global_device_ids=true, to_apply=%region_1.0 | all-reduce | flops 64 | bytes 512 | tf_op jit(solution)/shard_map/psum | solution.py:63
  27.2 7.4 %all-to-all-done = bf16[8,2,16384]{2,1,0:T(2,128)(2,1)S(1)} async-done(((bf16[8,2,16384]{2,1,0:T(2,128)(2,1)}), bf16[8,2,16384]{2,1,0:T(2,128)(2,1)S(1)}, u32[]{:S(2)}, u32[]{:S(2)}) %all-to-all-start) | async-done | bytes 524320 | tf_op jit(solution)/shard_map/all_to_all | solution.py:56
  35.4 1.9 fusion.74
  37.3 5.7 %all-reduce.2 = (f32[32]{0:T(128)S(1)}, f32[32]{0:T(128)S(1)}) all-reduce(f32[32]{0:T(128)S(1)} %get-tuple-element.5, f32[32]{0:T(128)S(1)} %get-tuple-element.4), channel_id=1, replica_groups=mesh['slab'=8,'grp'=4] {'grp'}, use_global_device_ids=true, to_apply=%region_7.8 | all-reduce | flops 64 | bytes 512 | tf_op jit(solution)/shard_map/psum | solution.py:64
  43.7 17.9 %all_to_all.27 = bf16[32,8,1024]{2,0,1:T(8,128)(2,1)S(1)} all-to-all(bf16[32,8,1024]{2,0,1:T(8,128)(2,1)S(1)} %fusion.60), channel_id=1, replica_groups=mesh['slab'=8,'grp'=4] {'slab'}, dimensions={1} | all-to-all | bytes 1048576 | tf_op jit(solution)/shard_map/all_to_all | solution.py:66
  61.7 1.3 collective-permute-start
  63.0 6.2 %fusion.137 = (bf16[1,1,16,1,64,1,128]{6,5,4,3,2,1,0:T(2,128)(2,1)S(1)}, bf16[1,1,16,1,64,1,128]{6,5,4,3,2,1,0:T(2,128)(2,1)S(1)}, bf16[1,1,16,1,64,1,128]{6,5,4...) fusion(bf16[1,2,16,2,64,2,128]{6,5,4,3,2,1,0:T(2,128)(2,1)S(1)}, ...), kind=kLoop, calls=%fused_computation.205 | loop fusion | bytes 4194304 | tf_op jit(solution)/shard_map/slice | solution.py:98
  69.6 6.3 %collective-permute-done = bf16[256,1,1024]{2,0,1:T(8,128)(2,1)S(1)} collective-permute-done((bf16[256,1,1024]{2,0,1:T(8,128)(2,1)S(1)}, bf16[256,1,1024]{2,0,1:T(8,128)(2,1)S(1)}, u32[]{:S(2)}, u32[]{:S(2)}) %collective-permute-start) | collective-permute-done | bytes 524320 | tf_op jit(solution)/shard_map/ppermute | solution.py:14
  75.9 1.5 collective-permute-start.1
  77.4 1.7 collective-permute-done.1
  88.7 2.1 broadcast_multiply_fusion
  92.7 1.3 fusion.25
  94.0 1.2 fusion.99
  106.2 65.3 %reduce-scatter.3.cloned.1.call-done = f32[32,27,128]{2,0,1:T(8,128)} async-done(((f32[256,27,128]{2,0,1:T(8,128)}), f32[32,27,128]{2,0,1:T(8,128)}) %reduce-scatter.3.cloned.1.call-update) | async-done | bytes 442384 | tf_op jit(solution)/shard_map/reduce_scatter | solution.py:131
  171.4 1.7 convert_element_type.47
  173.2 1.9 fusion.11
  175.1 5.1 %copy.26 = bf16[1,2,16,2,64,2,128]{6,5,4,3,2,1,0:T(2,128)(2,1)} copy(bf16[1,2,16,2,64,2,128]{6,4,2,5,3,1,0:T(8,128)(2,1)} %bitcast.407) | data formatting | bytes 4194304 | tf_op jit(solution)/shard_map/convert_element_type | solution.py:123
  180.2 24.8 %all-reduce.6.cloned.1.call-done = bf16[32,27,128]{2,0,1:T(8,128)(2,1)} async-done(((bf16[32,27,128]{2,0,1:T(8,128)(2,1)}), bf16[32,27,128]{2,0,1:T(8,128)(2,1)}) %all-reduce.6.cloned.1.call-update) | async-done | bytes 221200
  205.0 1.5 dynamic-slice_convert_fusion
  (100 shorter events, 24.2 us)
Async XLA Ops:
  7.2 2.2 %copy-start = (bf16[8,256,128]{2,1,0:T(8,128)(2,1)S(1)}, bf16[8,256,128]{2,1,0:T(8,128)(2,1)}, u32[]{:S(2)}) copy-start(bf16[8,256,128]{2,1,0:T(8,128)(2,1)} %param.13) | copy-start | bytes 1572868
  10.1 10.0 %copy-start.4 = (bf16[32,8,1024]{2,1,0:T(8,128)(2,1)S(1)}, bf16[32,8,1024]{2,1,0:T(8,128)(2,1)}, u32[]{:S(2)}) copy-start(bf16[32,8,1024]{2,1,0:T(8,128)(2,1)} %param.9) | copy-start | bytes 1572868
  10.7 16.5 %copy-start.10 = (f32[32]{0:T(128)S(1)}, f32[32]{0:T(128)}, u32[]{:S(2)}) copy-start(f32[32]{0:T(128)} %param.11) | copy-start | bytes 388
  12.9 21.7 %all-to-all-start = ((bf16[8,2,16384]{2,1,0:T(2,128)(2,1)}), bf16[8,2,16384]{2,1,0:T(2,128)(2,1)S(1)}, u32[]{:S(2)}, u32[]{:S(2)}) async-start(bf16[8,2,16384]{2,1,0:T(2,128)(2,1)} %reshape.139), calls=%async_computation | async-start | bytes 1048576 | tf_op jit(solution)/shard_map/all_to_all | solution.py:56
  20.1 151.3 %reduce-scatter.3.cloned.1.call-start = ((), (), s32[]{:S(2)}) async-start(), calls=%async_computation.3 | async-start | bytes 3981312 | tf_op jit(solution)/shard_map/reduce_scatter | solution.py:131
  35.4 7.6 %copy-start.5 = (bf16[32,8,1024]{2,1,0:T(8,128)(2,1)S(1)}, bf16[32,8,1024]{2,1,0:T(8,128)(2,1)}, u32[]{:S(2)}) copy-start(bf16[32,8,1024]{2,1,0:T(8,128)(2,1)} %param.10) | copy-start | bytes 1572868
  43.0 18.7 %copy-start.8 = (f32[32]{0:T(128)}, f32[32]{0:T(128)S(1)}, u32[]{:S(2)}) copy-start(f32[32]{0:T(128)S(1)} %get-tuple-element.23) | copy-start | bytes 388
  43.0 18.7 %copy-start.9 = (f32[32]{0:T(128)}, f32[32]{0:T(128)S(1)}, u32[]{:S(2)}) copy-start(f32[32]{0:T(128)S(1)} %get-tuple-element.24) | copy-start | bytes 388
  43.0 20.0 %copy-start.3 = (bf16[2,32,128,128]{3,2,1,0:T(8,128)(2,1)S(1)}, bf16[2,32,128,128]{3,2,1,0:T(8,128)(2,1)}, u32[]{:S(2)}) copy-start(bf16[2,32,128,128]{3,2,1,0:T(8,128)(2,1)} %param.7) | copy-start | bytes 6291460
  61.7 14.2 %collective-permute-start = (bf16[256,1,1024]{2,0,1:T(8,128)(2,1)S(1)}, bf16[256,1,1024]{2,0,1:T(8,128)(2,1)S(1)}, u32[]{:S(2)}, u32[]{:S(2)}) collective-permute-start(bf16[256,1,1024]{2,0,1:T(8,128)(2,1)S(1)} %bitcast.365), channel_id=1, source_target_pairs={{4,0},{8,4},{12,8},{16,12},{20,16},{24,20},{28,24},{5,1},{9,5},{13... | collective-permute-start | bytes 1572872 | tf_op jit(solution)/shard_map/ppermute | solution.py:14
  75.9 3.2 %collective-permute-start.1 = (bf16[256,2,64]{2,0,1:T(8,128)(2,1)S(1)}, bf16[256,2,64]{2,0,1:T(8,128)(2,1)S(1)}, u32[]{:S(2)}, u32[]{:S(2)}) collective-permute-start(bf16[256,2,64]{2,0,1:T(8,128)(2,1)S(1)} %pad_maximum_fusion.1), channel_id=1, source_target_pairs={{1,0},{2,1},{3,2},{5,4},{6,5},{7,6},{9,8},{10,9},{11,10},{13,12},{... | collective-permute-start | bytes 196616 | tf_op jit(solution)/shard_map/ppermute | solution.py:14
  79.2 7.4 %copy-start.1 = (bf16[256,2,1088]{2,0,1:T(8,128)(2,1)}, bf16[256,2,1088]{2,0,1:T(8,128)(2,1)S(1)}, u32[]{:S(2)}) copy-start(bf16[256,2,1088]{2,0,1:T(8,128)(2,1)S(1)} %pad_maximum_fusion) | copy-start | bytes 3342340
  90.8 0.7 copy-start.11
  90.8 114.2 %all-reduce.6.cloned.1.call-start = ((), (), s32[]{:S(2)}) async-start(), calls=%async_computation.4 | async-start | bytes 442368
  92.7 2.5 %copy-start.7 = (bf16[27,128,256]{2,1,0:T(8,128)(2,1)S(1)}, bf16[27,128,256]{2,1,0:T(8,128)(2,1)}, u32[]{:S(2)}) copy-start(bf16[27,128,256]{2,1,0:T(8,128)(2,1)} %param.12) | copy-start | bytes 5308420
  97.4 1.4 copy-start.2
  103.9 1.9 copy-start.6
Sparse Core Ops, SparseCore 0:
  90.9 80.4 reduce-scatter.2
  173.8 31.1 all-reduce.5
where the time goes:
time: 214 us; the launch traced here: 213 us
  waiting for transfers between devices  106 us (50%)
  blocking collectives  30.2 us (14%)
  matrix products  24.3 us (11%)
  local copies, waits for them, and re-layouts  17.9 us (8%)
  between operations  15.3 us (7%)
  starting transfers between devices  10.3 us (5%)
  other arithmetic  9.67 us (5%)
    reduce_scatter x1, waiting for transfers between devices, local(): lax.psum_scatter(jnp.stack(rows_out, 1) * grad_scale, 'slab', scatter_dim...  65.3 us
    unnamed x3, waiting for transfers between devices  24.9 us
    all_to_all x1, blocking collectives, local(): lax.all_to_all(grad_channels, 'slab', split_axis=1, concat_axis=0, tiled=...  17.9 us
    dot_general x27, matrix products, local(): jnp.einsum('on,jo->nj', window((extended, shifted), offsets), w_down[tap_...  15.2 us
    psum x2, blocking collectives, local(): lax.psum((first_sum, second_sum), 'grp')  12.3 us
    dot_general x27, matrix products, local(): jnp.dot(window(pieces, offsets), fine_blocks[parity], preferred_element_t...  8.41 us
    ppermute x2, waiting for transfers between devices, from_behind(): return lax.ppermute(shard, axis, pairs)  8.02 us
    all_to_all x1, waiting for transfers between devices, local(): lax.all_to_all(deep_bf, 'slab', split_axis=0, concat_axis=1, tiled=True)  7.41 us
  transfers between devices with their start and end apart: 5, of which 5 were waited for; matrix products, arithmetic and copies ran while one was open for 13% of the time, Pallas kernels for 0%

commit v1 on v0

--- a/solution.py
+++ b/solution.py
@@ -12,6 +12,67 @@
     devices = lax.axis_size(axis)
     pairs = [(i, i + by) for i in range(devices) if 0 <= i + by < devices]
     return lax.ppermute(shard, axis, pairs)
+
+
+def bit_pairs(slabs, groups, slab_bits, grp_bits):
+    return [
+        (s * groups + g, (s ^ slab_bits) * groups + (g ^ grp_bits))
+        for s in range(slabs)
+        for g in range(groups)
+    ]
+
+
+def sum_over_grp(values):
+    groups = lax.axis_size("grp")
+    parts = {0: values}
+    for step in range(1, groups):
+        parts[step] = lax.ppermute(values, "grp", [(i, i ^ step) for i in range(groups)])
+    width = 1
+    while width < groups:
+        for step in range(0, groups, 2 * width):
+            parts[step] = parts[step] + parts[step + width]
+        width *= 2
+    return parts[0]
+
+
+def sum_to_owner(partial):
+    slabs = lax.axis_size("slab")
+    groups = lax.axis_size("grp")
+    slab = lax.axis_index("slab")
+    grp = lax.axis_index("grp")
+    slab_bits = slabs.bit_length() - 1
+    grp_bits = groups.bit_length() - 1
+    bits = slab_bits + grp_bits
+    place = slab * groups + grp
+    columns = partial.shape[1]
+    rows = partial.shape[0] // (slabs * groups)
+    held = partial.astype(jnp.bfloat16).reshape((2,) * bits + (rows, columns))
+    stages = [[0]]
+    left = list(range(1, bits))
+    while left:
+        stages.append(left[:2])
+        left = left[2:]
+
+    def pick(array, dims, flips):
+        for dim, flip in zip(dims, flips):
+            bit = (place >> (bits - 1 - dim)) & 1
+            array = lax.dynamic_slice_in_dim(array, bit ^ flip, 1, dim)
+        return array
+
+    for stage in stages:
+        dims = [bits - 1 - b for b in stage]
+        total = pick(held, dims, [0] * len(dims)).astype(jnp.float32)
+        for code in range((1 << len(stage)) - 1, 0, -1):
+            flips = [code >> n & 1 for n in range(len(stage))]
+            mask = sum(f << b for f, b in zip(flips, stage))
+            arrived = lax.ppermute(
+                pick(held, dims, flips),
+                ("slab", "grp"),
+                bit_pairs(slabs, groups, mask >> grp_bits, mask & (groups - 1)),
+            )
+            total = total + arrived.astype(jnp.float32)
+        held = total if stage is stages[-1] else total.astype(jnp.bfloat16)
+    return held.reshape(rows, columns)
 
 
 def norm_backward(
@@ -60,8 +121,8 @@
         act_out,
         norm_gain,
         cell_total,
-        lambda first_sum, second_sum: lax.psum((first_sum, second_sum), "grp"),
-        lambda first_sum, second_sum: lax.psum((first_sum, second_sum), "grp"),
+        lambda first_sum, second_sum: sum_over_grp(jnp.stack((first_sum, second_sum))),
+        lambda first_sum, second_sum: sum_over_grp(jnp.stack((first_sum, second_sum))),
     )
     back_first = lax.all_to_all(grad_channels, "slab", split_axis=1, concat_axis=0, tiled=True)
     upper = from_behind(back_first, "slab", -1)
@@ -128,12 +189,8 @@
         jnp.dot(window(pieces, offsets), fine_blocks[parity], preferred_element_type=jnp.float32)
         for tap_index, parity, offsets in tap_list
     ]
-    slab_rows = lax.psum_scatter(
-        jnp.stack(rows_out, 1) * grad_scale, "slab", scatter_dimension=0, tiled=True
-    )
-    grad_down = lax.psum_scatter(
-        slab_rows.astype(jnp.bfloat16), "grp", scatter_dimension=0, tiled=True
-    ).astype(jnp.float32)
+    stacked_rows = jnp.stack(rows_out, 1) * grad_scale
+    grad_down = sum_to_owner(stacked_rows.reshape(width_deep, -1)).reshape(-1, 27, width_in)
     return (grad_input, grad_down, grad_gain, grad_shift)
 
 

time: 214 us -> 139 us (0.65)
  waiting for transfers between devices: 106 us -> 38.5 us
  blocking collectives: 30.2 us -> 0 us
  starting transfers between devices: 10.3 us -> 28 us
  between operations: 15.3 us -> 1.36 us
  matrix products: 24.3 us -> 37.2 us
  local copies, waits for them, and re-layouts: 17.9 us -> 27.4 us
  other arithmetic: 9.67 us -> 5.74 us
    reduce_scatter x1 -> x0, waiting for transfers between devices: 65.3 us -> none  [local(): lax.psum_scatter(jnp.stack(rows_out, 1) * grad_scale, 'slab', scatter_dim...]
    unnamed x3 -> x0, waiting for transfers between devices: 24.9 us -> none
    all_to_all x1 -> x0, blocking collectives: 17.9 us -> none  [local(): lax.all_to_all(grad_channels, 'slab', split_axis=1, concat_axis=0, tiled=...]
    ppermute x0 -> x13, waiting for transfers between devices: none -> 15.6 us  [the longest x7 10.2 us: sum_to_owner(): lax.ppermute(pick(held, dims, flips), ('slab', 'grp'), bit_pairs(slabs, g...]
    ppermute x0 -> x13, starting transfers between devices: none -> 14.3 us  [the longest x7 10.5 us: sum_to_owner(): lax.ppermute(pick(held, dims, flips), ('slab', 'grp'), bit_pairs(slabs, g...]
    dot_general x27, matrix products: 15.2 us -> 28.1 us  [local(): jnp.einsum('on,jo->nj', window((extended, shifted), offsets), w_down[tap_...]
    psum x2 -> x0, blocking collectives: 12.3 us -> none  [local(): lax.psum((first_sum, second_sum), 'grp')]
    convert_element_type x0 -> x2, local copies, waits for them, and re-layouts: none -> 6.54 us  [sum_to_owner(): held = partial.astype(jnp.bfloat16).reshape((2,) * bits + (rows, columns))]
  transfers between devices with their start and end apart: 5 -> 17, of which waited for: 5 -> 9; matrix products, arithmetic and copies ran while one was open for 13% -> 22% of each run, Pallas kernels for 0% -> 0%
where the time goes in v1:
time: 139 us; the launch traced here: 138 us
  waiting for transfers between devices  38.5 us (28%)
  matrix products  37.2 us (27%)
  starting transfers between devices  28 us (20%)
  local copies, waits for them, and re-layouts  27.4 us (20%)
  other arithmetic  5.74 us (4%)
    dot_general x27, matrix products, local(): jnp.einsum('on,jo->nj', window((extended, shifted), offsets), w_down[tap_...  28.1 us
    ppermute x7, starting transfers between devices, sum_to_owner(): lax.ppermute(pick(held, dims, flips), ('slab', 'grp'), bit_pairs(slabs, g...  10.5 us
    ppermute x7, waiting for transfers between devices, sum_to_owner(): lax.ppermute(pick(held, dims, flips), ('slab', 'grp'), bit_pairs(slabs, g...  10.2 us
    all_to_all x1, waiting for transfers between devices, local(): lax.all_to_all(deep_bf, 'slab', split_axis=0, concat_axis=1, tiled=True)  9.36 us
    dot_general x27, matrix products, local(): jnp.dot(window(pieces, offsets), fine_blocks[parity], preferred_element_t...  8.35 us
    unnamed x63, local copies, waits for them, and re-layouts  7.62 us
    ppermute x2, waiting for transfers between devices, from_behind(): return lax.ppermute(shard, axis, pairs)  7.39 us
    all_to_all x1, starting transfers between devices, local(): lax.all_to_all(deep_bf, 'slab', split_axis=0, concat_axis=1, tiled=True)  7.26 us
  transfers between devices with their start and end apart: 17, of which 9 were waited for; matrix products, arithmetic and copies ran while one was open for 22% of the time, Pallas kernels for 0%

profile of v1, /device:TPU:0, one launch (start us, length us, event | category | flops | bytes accessed | tf_op | source)
XLA Modules:
  0.0 138.2 jit_solution(16191942080870550607)
XLA Ops:
  0.6 2.2 %copy.26 = bf16[2,2,2,1,16,64,128]{6,5,4,2,1,0,3:T(8,128)(2,1)S(1)} copy(bf16[2,2,2,1,16,64,128]{6,2,5,1,4,0,3:T(2,128)(2,1)} %bitcast.424) | data formatting | bytes 4194304 | tf_op jit(solution)/shard_map/transpose | solution.py:111
  6.3 7.3 %all-to-all-start = ((bf16[8,2,16384]{2,1,0:T(2,128)(2,1)}), bf16[8,2,16384]{2,1,0:T(2,128)(2,1)S(1)}, u32[]{:S(2)}, u32[]{:S(2)}) async-start(bf16[8,2,16384]{2,1,0:T(2,128)(2,1)} %reshape.174), calls=%async_computation | async-start | bytes 1048576 | tf_op jit(solution)/shard_map/all_to_all | solution.py:117
  15.9 1.8 %collective-permute-done.1 = f32[2,32]{1,0:T(2,128)S(1)} collective-permute-done((f32[2,32]{1,0:T(2,128)S(1)}, f32[2,32]{1,0:T(2,128)S(1)}, u32[]{:S(2)}, u32[]{:S(2)}) %collective-permute-start.1) | collective-permute-done | bytes 288 | tf_op jit(solution)/shard_map/ppermute | solution.py:29
  18.7 9.4 %all-to-all-done = bf16[8,2,16384]{2,1,0:T(2,128)(2,1)S(1)} async-done(((bf16[8,2,16384]{2,1,0:T(2,128)(2,1)}), bf16[8,2,16384]{2,1,0:T(2,128)(2,1)S(1)}, u32[]{:S(2)}, u32[]{:S(2)}) %all-to-all-start) | async-done | bytes 524320 | tf_op jit(solution)/shard_map/all_to_all | solution.py:117
  36.0 3.6 %all-to-all-start.1 = ((bf16[32,8,1024]{2,0,1:T(8,128)(2,1)}), bf16[32,8,1024]{2,0,1:T(8,128)(2,1)S(1)}, u32[]{:S(2)}, u32[]{:S(2)}) async-start(bf16[32,8,1024]{2,0,1:T(8,128)(2,1)} %fusion.60), calls=%async_computation.1 | async-start | bytes 1048576 | tf_op jit(solution)/shard_map/all_to_all | solution.py:127
  39.6 4.9 %fusion.140 = (bf16[1,1,16,1,64,1,128]{6,5,4,3,2,1,0:T(2,128)(2,1)S(1)}, bf16[1,1,16,1,64,1,128]{6,5,4,3,2,1,0:T(2,128)(2,1)S(1)}, bf16[1,1,16,1,64,1,128]{6,5,4...) fusion(bf16[1,2,16,2,64,2,128]{6,5,4,3,2,1,0:T(2,128)(2,1)S(1)}, ...), kind=kLoop, calls=%fused_computation.220 | loop fusion | bytes 4194304 | tf_op jit(solution)/shard_map/slice | solution.py:159
  48.4 6.1 %all-to-all-done.1 = bf16[32,8,1024]{2,0,1:T(8,128)(2,1)S(1)} async-done(((bf16[32,8,1024]{2,0,1:T(8,128)(2,1)}), bf16[32,8,1024]{2,0,1:T(8,128)(2,1)S(1)}, u32[]{:S(2)}, u32[]{:S(2)}) %all-to-all-start.1) | async-done | bytes 524320 | tf_op jit(solution)/shard_map/all_to_all | solution.py:127
  55.8 1.9 %fusion.25 = bf16[8,1024,128]{2,1,0:T(8,128)(2,1)} fusion(bf16[256,1024]{1,0:T(8,128)(2,1)S(1)} %bitcast.385, bf16[27,128,256]{2,1,0:T(8,128)(2,1)} %param.12), kind=kOutput, calls=%fused_computation.52 | convolution fusion | flops 67239936 | bytes 851968 | tf_op jit(solution)/shard_map/on,jo->nj/dot_general | solution.py:164
  57.7 2.0 %fusion.99 = f32[1024,128]{1,0:T(8,128)} fusion(bf16[256,1024]{1,0:T(8,128)(2,1)S(1)} %bitcast.386, bf16[27,128,256]{2,1,0:T(8,128)(2,1)} %param.12), kind=kOutput, calls=%fused_computation.163 | convolution fusion | flops 67108864 | bytes 1114112 | tf_op jit(solution)/shard_map/on,jo->nj/dot_general | solution.py:164
  59.7 2.0 %fusion.92 = f32[1024,128]{1,0:T(8,128)} fusion(bf16[256,1024]{1,0:T(8,128)(2,1)S(1)} %bitcast.387, bf16[27,128,256]{2,1,0:T(8,128)(2,1)} %param.12), kind=kOutput, calls=%fused_computation.156 | convolution fusion | flops 67108864 | bytes 1114112 | tf_op jit(solution)/shard_map/on,jo->nj/dot_general | solution.py:164
  61.7 7.4 %collective-permute-done.6 = bf16[256,1,1024]{2,0,1:T(8,128)(2,1)S(1)} collective-permute-done((bf16[256,1,1024]{2,0,1:T(8,128)(2,1)S(1)}, bf16[256,1,1024]{2,0,1:T(8,128)(2,1)S(1)}, u32[]{:S(2)}, u32[]{:S(2)}) %collective-permute-start.6) | collective-permute-done | bytes 524320 | tf_op jit(solution)/shard_map/ppermute | solution.py:14
  70.6 2.0 %fusion.66 = f32[1024,128]{1,0:T(8,128)} fusion(bf16[256,1,1024]{2,0,1:T(8,128)(2,1)S(1)} %collective-permute-done.6, bf16[27,128,256]{2,1,0:T(8,128)(2,1)} %param.12), kind=kOutput, calls=%fused_computation.127 | convolution fusion | flops 67108864 | bytes 1114112 | tf_op jit(solution)/shard_map/on,jo->nj/dot_general | solution.py:164
  73.6 2.2 %fusion.70 = f32[1024,128]{1,0:T(8,128)} fusion(bf16[256,2,1088]{2,0,1:T(8,128)(2,1)S(1)} %pad_select_fusion, bf16[27,128,256]{2,1,0:T(8,128)(2,1)} %param.12), kind=kOutput, calls=%fused_computation.131 | convolution fusion | flops 67108864 | bytes 1114112 | tf_op jit(solution)/shard_map/on,jo->nj/dot_general | solution.py:164
  75.8 2.3 %fusion.71 = f32[1024,128]{1,0:T(8,128)} fusion(bf16[256,2,1088]{2,0,1:T(8,128)(2,1)S(1)} %pad_select_fusion, bf16[27,128,256]{2,1,0:T(8,128)(2,1)} %param.12), kind=kOutput, calls=%fused_computation.133 | convolution fusion | flops 67108864 | bytes 1114112 | tf_op jit(solution)/shard_map/on,jo->nj/dot_general | solution.py:164
  78.1 2.0 %fusion.73 = f32[1024,128]{1,0:T(8,128)} fusion(bf16[256,2,1088]{2,0,1:T(8,128)(2,1)S(1)} %pad_select_fusion, bf16[27,128,256]{2,1,0:T(8,128)(2,1)} %param.12), kind=kOutput, calls=%fused_computation.135 | convolution fusion | flops 67108864 | bytes 1114112 | tf_op jit(solution)/shard_map/on,jo->nj/dot_general | solution.py:164
  80.1 2.2 %fusion.72 = f32[1024,128]{1,0:T(8,128)} fusion(bf16[256,2,1088]{2,0,1:T(8,128)(2,1)S(1)} %pad_select_fusion, bf16[27,128,256]{2,1,0:T(8,128)(2,1)} %param.12), kind=kOutput, calls=%fused_computation.134 | convolution fusion | flops 67108864 | bytes 1114112 | tf_op jit(solution)/shard_map/on,jo->nj/dot_general | solution.py:164
  82.3 2.0 %fusion.75 = f32[1024,128]{1,0:T(8,128)} fusion(bf16[256,2,1088]{2,0,1:T(8,128)(2,1)S(1)} %pad_select_fusion, bf16[27,128,256]{2,1,0:T(8,128)(2,1)} %param.12), kind=kOutput, calls=%fused_computation.139 | convolution fusion | flops 67108864 | bytes 1114112 | tf_op jit(solution)/shard_map/on,jo->nj/dot_general | solution.py:164
  93.4 2.5 %copy.29 = bf16[256,27,128]{2,1,0:T(8,128)(2,1)} copy(bf16[256,27,128]{2,0,1:T(8,128)(2,1)S(1)} %multiply_convert_fusion) | data formatting | bytes 3538944 | tf_op jit(solution)/shard_map/convert_element_type | solution.py:49
  96.0 4.0 %convert_element_type.85 = bf16[2,2,2,2,2,8,3456]{6,5,4,3,2,1,0:T(8,128)(2,1)} reshape(bf16[256,27,128]{2,1,0:T(8,128)(2,1)} %copy.29) | data formatting | bytes 3538944 | tf_op jit(solution)/shard_map/convert_element_type | solution.py:49
  114.1 2.7 %collective-permute-start.10 = (bf16[2,2,1,1,1,8,3456]{6,5,4,3,2,1,0:T(8,128)(2,1)S(1)}, bf16[2,2,1,1,1,8,3456]{6,5,4,3,2,1,0:T(8,128)(2,1)S(1)}, u32[]{:S(2)}, u32[]{:S(2)}) collective-permute-start(bf16[2,2,1,1,1,8,3456]{6,5,4,3,2,1,0:T(8,128)(2,1)S(1)} %get-tuple-element.20), channel_id=1, source_target_pairs={{0,4},{1,5},{2,6},{3,7},{4,0},{5,1},{6,2},{7,3},{8,12},{9,13},{10,... | collective-permute-start | bytes 663560 | tf_op jit(solution)/shard_map/ppermute | solution.py:68
  118.8 4.3 %collective-permute-done.10 = bf16[2,2,1,1,1,8,3456]{6,5,4,3,2,1,0:T(8,128)(2,1)S(1)} collective-permute-done((bf16[2,2,1,1,1,8,3456]{6,5,4,3,2,1,0:T(8,128)(2,1)S(1)}, bf16[2,2,1,1,1,8,3456]{6,5,4,3,2,1,0:T(8,128)(2,1)S(1)}, u32[]{:S(2)}, u32[]{:S(2)}) %collective-permute-start.10) | collective-permute-done | bytes 221216 | tf_op jit(solution)/shard_map/ppermute | solution.py:68
  123.1 5.9 %collective-permute-done.11 = bf16[2,2,1,1,1,8,3456]{6,5,4,3,2,1,0:T(8,128)(2,1)S(1)} collective-permute-done((bf16[2,2,1,1,1,8,3456]{6,5,4,3,2,1,0:T(8,128)(2,1)S(1)}, bf16[2,2,1,1,1,8,3456]{6,5,4,3,2,1,0:T(8,128)(2,1)S(1)}, u32[]{:S(2)}, u32[]{:S(2)}) %collective-permute-start.11) | collective-permute-done | bytes 221216 | tf_op jit(solution)/shard_map/ppermute | solution.py:68
  130.6 3.1 %collective-permute-start.14 = (bf16[1,1,1,1,1,8,3456]{6,5,4,3,2,1,0:T(8,128)(2,1)S(1)}, bf16[1,1,1,1,1,8,3456]{6,5,4,3,2,1,0:T(8,128)(2,1)S(1)}, u32[]{:S(2)}, u32[]{:S(2)}) collective-permute-start(bf16[1,1,1,1,1,8,3456]{6,5,4,3,2,1,0:T(8,128)(2,1)S(1)} %get-tuple-element.22), channel_id=1, source_target_pairs={{0,8},{1,9},{2,10},{3,11},{4,12},{5,13},{6,14},{7,15},{8,0},{9,1},... | collective-permute-start | bytes 165896 | tf_op jit(solution)/shard_map/ppermute | solution.py:68
  134.0 3.5 %copy.28 = bf16[1,2,16,2,64,2,128]{6,5,4,3,2,1,0:T(2,128)(2,1)} copy(bf16[1,2,16,2,64,2,128]{6,4,2,5,3,1,0:T(8,128)(2,1)S(1)} %bitcast.425) | data formatting | bytes 4194304 | tf_op jit(solution)/shard_map/convert_element_type | solution.py:184
  (157 shorter events, 49.7 us)
Async XLA Ops:
  3.6 10.0 %copy-start.5 = (bf16[32,8,1024]{2,1,0:T(8,128)(2,1)S(1)}, bf16[32,8,1024]{2,1,0:T(8,128)(2,1)}, u32[]{:S(2)}) copy-start(bf16[32,8,1024]{2,1,0:T(8,128)(2,1)} %param.9) | copy-start | bytes 1572868
  4.1 14.6 %copy-start.25 = (f32[32]{0:T(128)S(1)}, f32[32]{0:T(128)}, u32[]{:S(2)}) copy-start(f32[32]{0:T(128)} %param.11) | copy-start | bytes 388
  6.3 21.7 %all-to-all-start = ((bf16[8,2,16384]{2,1,0:T(2,128)(2,1)}), bf16[8,2,16384]{2,1,0:T(2,128)(2,1)S(1)}, u32[]{:S(2)}, u32[]{:S(2)}) async-start(bf16[8,2,16384]{2,1,0:T(2,128)(2,1)} %reshape.174), calls=%async_computation | async-start | bytes 1048576 | tf_op jit(solution)/shard_map/all_to_all | solution.py:117
  14.0 1.9 %collective-permute-start = (f32[2,32]{1,0:T(2,128)S(1)}, f32[2,32]{1,0:T(2,128)S(1)}, u32[]{:S(2)}, u32[]{:S(2)}) collective-permute-start(f32[2,32]{1,0:T(2,128)S(1)} %pad_maximum_fusion.2), channel_id=1, source_target_pairs={{0,1},{1,0},{2,3},{3,2},{4,5},{5,4},{6,7},{7,6},{8,9},{9,8},{10,11... | collective-permute-start | bytes 776 | tf_op jit(solution)/shard_map/ppermute | solution.py:29
  14.1 3.6 %collective-permute-start.1 = (f32[2,32]{1,0:T(2,128)S(1)}, f32[2,32]{1,0:T(2,128)S(1)}, u32[]{:S(2)}, u32[]{:S(2)}) collective-permute-start(f32[2,32]{1,0:T(2,128)S(1)} %pad_maximum_fusion.2), channel_id=1, source_target_pairs={{0,2},{1,3},{2,0},{3,1},{4,6},{5,7},{6,4},{7,5},{8,10},{9,11},{10,... | collective-permute-start | bytes 776 | tf_op jit(solution)/shard_map/ppermute | solution.py:29
  15.7 3.0 %collective-permute-start.2 = (f32[2,32]{1,0:T(2,128)S(1)}, f32[2,32]{1,0:T(2,128)S(1)}, u32[]{:S(2)}, u32[]{:S(2)}) collective-permute-start(f32[2,32]{1,0:T(2,128)S(1)} %pad_maximum_fusion.2), channel_id=1, source_target_pairs={{0,3},{1,2},{2,1},{3,0},{4,7},{5,6},{6,5},{7,4},{8,11},{9,10},{10,... | collective-permute-start | bytes 776 | tf_op jit(solution)/shard_map/ppermute | solution.py:29
  18.7 10.1 %copy-start.7 = (bf16[32,8,1024]{2,1,0:T(8,128)(2,1)S(1)}, bf16[32,8,1024]{2,1,0:T(8,128)(2,1)}, u32[]{:S(2)}) copy-start(bf16[32,8,1024]{2,1,0:T(8,128)(2,1)} %param.10) | copy-start | bytes 1572868
  28.6 5.8 %copy-start.8 = (bf16[32,8,1024]{2,1,0:T(8,128)(2,1)S(1)}, bf16[32,8,1024]{2,1,0:T(8,128)(2,1)}, u32[]{:S(2)}) copy-start(bf16[32,8,1024]{2,1,0:T(8,128)(2,1)} %param.10) | copy-start | bytes 1572868
  29.7 1.9 %collective-permute-start.3 = (f32[2,32]{1,0:T(2,128)S(1)}, f32[2,32]{1,0:T(2,128)S(1)}, u32[]{:S(2)}, u32[]{:S(2)}) collective-permute-start(f32[2,32]{1,0:T(2,128)S(1)} %pad_maximum_fusion.3), channel_id=1, source_target_pairs={{0,1},{1,0},{2,3},{3,2},{4,5},{5,4},{6,7},{7,6},{8,9},{9,8},{10,11... | collective-permute-start | bytes 776 | tf_op jit(solution)/shard_map/ppermute | solution.py:29
  29.8 3.6 %collective-permute-start.4 = (f32[2,32]{1,0:T(2,128)S(1)}, f32[2,32]{1,0:T(2,128)S(1)}, u32[]{:S(2)}, u32[]{:S(2)}) collective-permute-start(f32[2,32]{1,0:T(2,128)S(1)} %pad_maximum_fusion.3), channel_id=1, source_target_pairs={{0,2},{1,3},{2,0},{3,1},{4,6},{5,7},{6,4},{7,5},{8,10},{9,11},{10,... | collective-permute-start | bytes 776 | tf_op jit(solution)/shard_map/ppermute | solution.py:29
  31.4 3.0 %collective-permute-start.5 = (f32[2,32]{1,0:T(2,128)S(1)}, f32[2,32]{1,0:T(2,128)S(1)}, u32[]{:S(2)}, u32[]{:S(2)}) collective-permute-start(f32[2,32]{1,0:T(2,128)S(1)} %pad_maximum_fusion.3), channel_id=1, source_target_pairs={{0,3},{1,2},{2,1},{3,0},{4,7},{5,6},{6,5},{7,4},{8,11},{9,10},{10,... | collective-permute-start | bytes 776 | tf_op jit(solution)/shard_map/ppermute | solution.py:29
  34.4 5.2 %copy-start.3 = (bf16[2,32,128,128]{3,2,1,0:T(8,128)(2,1)S(1)}, bf16[2,32,128,128]{3,2,1,0:T(8,128)(2,1)}, u32[]{:S(2)}) copy-start(bf16[2,32,128,128]{3,2,1,0:T(8,128)(2,1)} %param.7) | copy-start | bytes 6291460
  36.0 18.5 %all-to-all-start.1 = ((bf16[32,8,1024]{2,0,1:T(8,128)(2,1)}), bf16[32,8,1024]{2,0,1:T(8,128)(2,1)S(1)}, u32[]{:S(2)}, u32[]{:S(2)}) async-start(bf16[32,8,1024]{2,0,1:T(8,128)(2,1)} %fusion.60), calls=%async_computation.1 | async-start | bytes 1048576 | tf_op jit(solution)/shard_map/all_to_all | solution.py:127
  54.5 14.6 %collective-permute-start.6 = (bf16[256,1,1024]{2,0,1:T(8,128)(2,1)S(1)}, bf16[256,1,1024]{2,0,1:T(8,128)(2,1)S(1)}, u32[]{:S(2)}, u32[]{:S(2)}) collective-permute-start(bf16[256,1,1024]{2,0,1:T(8,128)(2,1)S(1)} %bitcast.384), channel_id=1, source_target_pairs={{4,0},{8,4},{12,8},{16,12},{20,16},{24,20},{28,24},{5,1},{9,5},{13... | collective-permute-start | bytes 1572872 | tf_op jit(solution)/shard_map/ppermute | solution.py:14
  69.1 3.5 %collective-permute-start.7 = (bf16[256,2,64]{2,0,1:T(8,128)(2,1)S(1)}, bf16[256,2,64]{2,0,1:T(8,128)(2,1)S(1)}, u32[]{:S(2)}, u32[]{:S(2)}) collective-permute-start(bf16[256,2,64]{2,0,1:T(8,128)(2,1)S(1)} %pad_maximum_fusion.1), channel_id=1, source_target_pairs={{1,0},{2,1},{3,2},{5,4},{6,5},{7,6},{9,8},{10,9},{11,10},{13,12},{... | collective-permute-start | bytes 196616 | tf_op jit(solution)/shard_map/ppermute | solution.py:14
  72.7 18.1 %copy-start.1 = (bf16[256,2,1088]{2,0,1:T(8,128)(2,1)}, bf16[256,2,1088]{2,0,1:T(8,128)(2,1)S(1)}, u32[]{:S(2)}) copy-start(bf16[256,2,1088]{2,0,1:T(8,128)(2,1)S(1)} %pad_maximum_fusion) | copy-start | bytes 3342340
  101.3 4.4 %copy-start.17 = (f32[1024,128]{1,0:T(8,128)S(1)}, f32[1024,128]{1,0:T(8,128)}, u32[]{:S(2)}) copy-start(f32[1024,128]{1,0:T(8,128)} %fusion.71) | copy-start | bytes 1572868
  101.3 12.1 %collective-permute-start.8 = (bf16[2,2,2,2,1,8,3456]{6,5,4,3,2,1,0:T(8,128)(2,1)S(1)}, bf16[2,2,2,2,1,8,3456]{6,5,4,3,2,1,0:T(8,128)(2,1)S(1)}, u32[]{:S(2)}, u32[]{:S(2)}) collective-permute-start(bf16[2,2,2,2,1,8,3456]{6,5,4,3,2,1,0:T(8,128)(2,1)S(1)} %constant_dynamic-slice_fusion.6), channel_id=1, source_target_pairs={{0,1},{1,0},{2,3},{3,2},{4,5},{5,4},{6,7},{7,6},{8,9},{9,8},{10,11... | collective-permute-start | bytes 2654216 | tf_op jit(solution)/shard_map/ppermute | solution.py:68
  114.1 9.0 %collective-permute-start.10 = (bf16[2,2,1,1,1,8,3456]{6,5,4,3,2,1,0:T(8,128)(2,1)S(1)}, bf16[2,2,1,1,1,8,3456]{6,5,4,3,2,1,0:T(8,128)(2,1)S(1)}, u32[]{:S(2)}, u32[]{:S(2)}) collective-permute-start(bf16[2,2,1,1,1,8,3456]{6,5,4,3,2,1,0:T(8,128)(2,1)S(1)} %get-tuple-element.20), channel_id=1, source_target_pairs={{0,4},{1,5},{2,6},{3,7},{4,0},{5,1},{6,2},{7,3},{8,12},{9,13},{10,... | collective-permute-start | bytes 663560 | tf_op jit(solution)/shard_map/ppermute | solution.py:68
  116.9 12.2 %collective-permute-start.11 = (bf16[2,2,1,1,1,8,3456]{6,5,4,3,2,1,0:T(8,128)(2,1)S(1)}, bf16[2,2,1,1,1,8,3456]{6,5,4,3,2,1,0:T(8,128)(2,1)S(1)}, u32[]{:S(2)}, u32[]{:S(2)}) collective-permute-start(bf16[2,2,1,1,1,8,3456]{6,5,4,3,2,1,0:T(8,128)(2,1)S(1)} %get-tuple-element.19), channel_id=1, source_target_pairs={{0,2},{1,3},{2,0},{3,1},{4,6},{5,7},{6,4},{7,5},{8,10},{9,11},{10,... | collective-permute-start | bytes 663560 | tf_op jit(solution)/shard_map/ppermute | solution.py:68
  117.0 12.0 %collective-permute-start.9 = (bf16[2,2,1,1,1,8,3456]{6,5,4,3,2,1,0:T(8,128)(2,1)S(1)}, bf16[2,2,1,1,1,8,3456]{6,5,4,3,2,1,0:T(8,128)(2,1)S(1)}, u32[]{:S(2)}, u32[]{:S(2)}) collective-permute-start(bf16[2,2,1,1,1,8,3456]{6,5,4,3,2,1,0:T(8,128)(2,1)S(1)} %get-tuple-element.18), channel_id=1, source_target_pairs={{0,6},{1,7},{2,4},{3,5},{4,2},{5,3},{6,0},{7,1},{8,14},{9,15},{10,... | collective-permute-start | bytes 663560 | tf_op jit(solution)/shard_map/ppermute | solution.py:68
  129.2 8.4 %collective-permute-start.12 = (bf16[1,1,1,1,1,8,3456]{6,5,4,3,2,1,0:T(8,128)(2,1)S(1)}, bf16[1,1,1,1,1,8,3456]{6,5,4,3,2,1,0:T(8,128)(2,1)S(1)}, u32[]{:S(2)}, u32[]{:S(2)}) collective-permute-start(bf16[1,1,1,1,1,8,3456]{6,5,4,3,2,1,0:T(8,128)(2,1)S(1)} %get-tuple-element.21), channel_id=1, source_target_pairs={{0,24},{1,25},{2,26},{3,27},{4,28},{5,29},{6,30},{7,31},{8,16},{9,... | collective-permute-start | bytes 165896 | tf_op jit(solution)/shard_map/ppermute | solution.py:68
  129.3 8.3 %collective-permute-start.13 = (bf16[1,1,1,1,1,8,3456]{6,5,4,3,2,1,0:T(8,128)(2,1)S(1)}, bf16[1,1,1,1,1,8,3456]{6,5,4,3,2,1,0:T(8,128)(2,1)S(1)}, u32[]{:S(2)}, u32[]{:S(2)}) collective-permute-start(bf16[1,1,1,1,1,8,3456]{6,5,4,3,2,1,0:T(8,128)(2,1)S(1)} %get-tuple-element.23), channel_id=1, source_target_pairs={{0,16},{1,17},{2,18},{3,19},{4,20},{5,21},{6,22},{7,23},{8,24},{9,... | collective-permute-start | bytes 165896 | tf_op jit(solution)/shard_map/ppermute | solution.py:68
  130.6 7.0 %collective-permute-start.14 = (bf16[1,1,1,1,1,8,3456]{6,5,4,3,2,1,0:T(8,128)(2,1)S(1)}, bf16[1,1,1,1,1,8,3456]{6,5,4,3,2,1,0:T(8,128)(2,1)S(1)}, u32[]{:S(2)}, u32[]{:S(2)}) collective-permute-start(bf16[1,1,1,1,1,8,3456]{6,5,4,3,2,1,0:T(8,128)(2,1)S(1)} %get-tuple-element.22), channel_id=1, source_target_pairs={{0,8},{1,9},{2,10},{3,11},{4,12},{5,13},{6,14},{7,15},{8,0},{9,1},... | collective-permute-start | bytes 165896 | tf_op jit(solution)/shard_map/ppermute | solution.py:68
  (19 other events, 33.5 us)

commit v2 on v1

v2 whole, which is shorter than its diff:
```python
import functools
import math

import jax
import jax.numpy as jnp
from jax import lax
from jax.experimental import pallas as pl
from jax.experimental.pallas import tpu as pltpu
from jax.sharding import PartitionSpec as P

LANES = 128


def bit_pairs(slabs, groups, slab_bits, grp_bits):
    return [
        (s * groups + g, (s ^ slab_bits) * groups + (g ^ grp_bits))
        for s in range(slabs)
        for g in range(groups)
    ]


def from_next(shard, axis):
    devices = lax.axis_size(axis)
    return lax.ppermute(shard, axis, [(i, i - 1) for i in range(1, devices)])


def sum_over_grp(values):
    groups = lax.axis_size("grp")
    parts = {0: values}
    for step in range(1, groups):
        parts[step] = lax.ppermute(values, "grp", [(i, i ^ step) for i in range(groups)])
    width = 1
    while width < groups:
        for step in range(0, groups, 2 * width):
            parts[step] = parts[step] + parts[step + width]
        width *= 2
    return parts[0]


def sum_to_owner(partial):
    slabs = lax.axis_size("slab")
    groups = lax.axis_size("grp")
    slab = lax.axis_index("slab")
    grp = lax.axis_index("grp")
    slab_bits = slabs.bit_length() - 1
    grp_bits = groups.bit_length() - 1
    bits = slab_bits + grp_bits
    place = slab * groups + grp
    columns = partial.shape[1]
    rows = partial.shape[0] // (slabs * groups)
    held = partial.reshape((2,) * bits + (rows, columns))
    stages = [[0]]
    left = list(range(1, bits))
    while left:
        stages.append(left[:2])
        left = left[2:]

    def pick(array, dims, flips):
        for dim, flip in zip(dims, flips):
            bit = (place >> (bits - 1 - dim)) & 1
            array = lax.dynamic_slice_in_dim(array, bit ^ flip, 1, dim)
        return array

    for stage in stages:
        dims = [bits - 1 - b for b in stage]
        total = pick(held, dims, [0] * len(dims)).astype(jnp.float32)
        for code in range((1 << len(stage)) - 1, 0, -1):
            flips = [code >> n & 1 for n in range(len(stage))]
            mask = sum(f << b for f, b in zip(flips, stage))
            arrived = lax.ppermute(
                pick(held, dims, flips),
                ("slab", "grp"),
                bit_pairs(slabs, groups, mask >> grp_bits, mask & (groups - 1)),
            )
            total = total + arrived.astype(jnp.float32)
        held = total if stage is stages[-1] else total.astype(jnp.bfloat16)
    return held.reshape(rows, columns)


def deep_kernel(rows_ref, taps_ref, out_ref, wide):
    depth = rows_ref.shape[2] // 2
    blocks = []
    for pair in range(rows_ref.shape[1] // 2):
        pieces = []
        for px in range(2):
            for py in range(2):
                wide[...] = rows_ref[px, 2 * pair + py].astype(jnp.float32)
                for pz in range(2):
                    pieces.append(wide[pl.ds(pz, depth, stride=2), :].astype(jnp.bfloat16))
        blocks.append(jnp.concatenate(pieces, axis=1))
    cells = jnp.concatenate(blocks, axis=0)
    taps = jnp.concatenate([taps_ref[p] for p in range(8)], axis=1)
    out_ref[...] = lax.dot_general(
        taps, cells, (((1,), (1,)), ((), ())), preferred_element_type=jnp.float32
    ).astype(jnp.bfloat16)


def deep_gradient(out_grad, w_up):
    _, rows, fine_depth, width_in = out_grad.shape
    width_deep = w_up.shape[1]
    cells = rows * fine_depth // 4
    step = 4
    return pl.pallas_call(
        deep_kernel,
        grid=(rows // (2 * step),),
        in_specs=[
            pl.BlockSpec((2, 2 * step, fine_depth, width_in), lambda i: (0, i, 0, 0)),
            pl.BlockSpec((8, width_deep, width_in), lambda i: (0, 0, 0)),
        ],
        out_specs=pl.BlockSpec((width_deep, step * fine_depth // 2), lambda i: (0, i)),
        out_shape=jax.ShapeDtypeStruct((width_deep, cells), jnp.bfloat16),
        scratch_shapes=[pltpu.VMEM((fine_depth, width_in), jnp.float32)],
        compiler_params=pltpu.CompilerParams(vmem_limit_bytes=32 << 20),
        cost_estimate=pl.CostEstimate(
            flops=2 * 8 * cells * width_deep * width_in,
            bytes_accessed=2 * (out_grad.size + w_up.size + width_deep * cells),
            transcendentals=0,
        ),
        name="deep_gradient",
    )(out_grad, w_up)


def shifted_kernel(fine_ref, out_ref, wide):
    fine_rows, fine_depth, width = fine_ref.shape[1:]
    depth = fine_depth // 2
    cells = fine_rows // 2 * depth
    wide[0:8, :] = jnp.zeros((8, width), jnp.float32)
    out_ref[0, 0:depth, 0 : 3 * width] = jnp.zeros((depth, 3 * width), jnp.bfloat16)
    tail = out_ref.shape[1] - cells
    out_ref[0, cells:, 3 * width :] = jnp.zeros((tail, 6 * width), jnp.bfloat16)
    out_ref[0, cells + depth :, 0 : 3 * width] = jnp.zeros((tail - depth, 3 * width), jnp.bfloat16)

    def row(y, carry):
        start = pl.multiple_of(y * depth, depth)
        for py in range(2):
            wide[8:, :] = fine_ref[0, 2 * y + py].astype(jnp.float32)
            for kz in range(3):
                piece = wide[pl.ds(7 + kz, depth, stride=2), :].astype(jnp.bfloat16)
                if py:
                    out_ref[0, pl.ds(start, depth), (6 + kz) * width : (7 + kz) * width] = piece
                    out_ref[0, pl.ds(start + depth, depth), kz * width : (kz + 1) * width] = piece
                else:
                    out_ref[0, pl.ds(start, depth), (3 + kz) * width : (4 + kz) * width] = piece
        return carry

    lax.fori_loop(0, fine_rows // 2, row, 0)


def shifted_fine(fine_input, padded):
    planes, fine_rows, fine_depth, width = fine_input.shape
    return pl.pallas_call(
        shifted_kernel,
        grid=(planes,),
        in_specs=[pl.BlockSpec((1, fine_rows, fine_depth, width), lambda i: (i, 0, 0, 0))],
        out_specs=pl.BlockSpec((1, padded, 9 * width), lambda i: (i, 0, 0)),
        out_shape=jax.ShapeDtypeStruct((planes, padded, 9 * width), jnp.bfloat16),
        scratch_shapes=[pltpu.VMEM((fine_depth + 8, width), jnp.float32)],
        compiler_params=pltpu.CompilerParams(vmem_limit_bytes=32 << 20),
        cost_estimate=pl.CostEstimate(
            flops=0,
            bytes_accessed=2 * (fine_input.size + planes * padded * 9 * width),
            transcendentals=0,
        ),
        name="shifted_fine",
    )(fine_input)


def input_kernel(here_ref, next_ref, taps_ref, out_ref, turned, product, wide):
    width = taps_ref.shape[1]
    fine_rows, fine_depth = out_ref.shape[1:3]
    depth = fine_depth // 2
    padded = here_ref.shape[1]
    px = pl.program_id(0)
    sides = ((0, here_ref), (1, next_ref))

    @pl.when(px == 0)
    def _():
        for slot, ref in sides:
            for start in range(0, padded, LANES):
                turned[slot, start : start + LANES, :] = ref[:, start : start + LANES].T

    def times(slot, kx, ky):
        taps = jnp.concatenate([taps_ref[9 * kx + 3 * ky + kz] for kz in range(3)], axis=0)
        return lax.dot_general(
            turned[slot],
            taps,
            (((1,), (1,)), ((), ())),
            preferred_element_type=jnp.float32,
        )

    for ky in range(3):
        columns = slice(3 * ky * width, (3 * ky + 3) * width)

        @pl.when(px == 0)
        def _(ky=ky, columns=columns):
            product[:, columns] = times(0, 1, ky)

        @pl.when(px == 1)
        def _(ky=ky, columns=columns):
            product[:, columns] = times(0, 2, ky) + times(1, 0, ky)

    inside = lax.broadcasted_iota(jnp.int32, (depth, width), 0) < depth - 1

    def row(y, carry):
        start = pl.multiple_of(y * depth, depth)

        def part(ky, kz):
            return slice((3 * ky + kz) * width, (3 * ky + kz + 1) * width)

        for py in range(2):
            if py:
                even = product[pl.ds(start, depth), part(2, 1)] + product[
                    pl.ds(start + depth, depth), part(0, 1)
                ]
                odd = product[pl.ds(start, depth), part(2, 2)] + product[
                    pl.ds(start + depth, depth), part(0, 2)
                ]
                after = product[pl.ds(start, depth), part(2, 0)] + product[
                    pl.ds(start + depth, depth), part(0, 0)
                ]
            else:
                even = product[pl.ds(start, depth), part(1, 1)]
                odd = product[pl.ds(start, depth), part(1, 2)]
                after = product[pl.ds(start, depth), part(1, 0)]
            wide[pl.ds(0, depth, stride=2), :] = even
            after = pltpu.roll(after, depth - 1, 0)
            wide[pl.ds(1, depth, stride=2), :] = odd + jnp.where(inside, after, 0.0)
            out_ref[0, 2 * y + py] = wide[...].astype(jnp.bfloat16)
        return carry

    lax.fori_loop(0, fine_rows // 2, row, 0)


def input_gradient(here, after, w_down, fine_shape):
    planes, fine_rows, fine_depth, width = fine_shape
    width_deep, padded = here.shape
    whole = pl.BlockSpec((width_deep, padded), lambda i: (0, 0))
    return pl.pallas_call(
        input_kernel,
        grid=(planes,),
        in_specs=[whole, whole, pl.BlockSpec(w_down.shape, lambda i: (0, 0, 0))],
        out_specs=pl.BlockSpec((1, fine_rows, fine_depth, width), lambda i: (i, 0, 0, 0)),
        out_shape=jax.ShapeDtypeStruct(fine_shape, jnp.bfloat16),
        scratch_shapes=[
            pltpu.VMEM((2, padded, width_deep), jnp.bfloat16),
            pltpu.VMEM((padded, 9 * width), jnp.float32),
            pltpu.VMEM((fine_depth, width), jnp.float32),
        ],
        compiler_params=pltpu.CompilerParams(vmem_limit_bytes=40 << 20),
        cost_estimate=pl.CostEstimate(
            flops=2 * 27 * padded * width_deep * width,
            bytes_accessed=2 * (2 * here.size + w_down.size + math.prod(fine_shape)),
            transcendentals=0,
        ),
        name="input_gradient",
    )(here, after, w_down)


def local(fine_input, out_grad, pre_norm, act_out, norm_gain, w_down, w_up):
    slabs = lax.axis_size("slab")
    groups = lax.axis_size("grp")
    fine_rows, fine_depth, width_in = fine_input.shape[1:]
    depth = fine_depth // 2
    width_deep = w_up.shape[1]
    channels, slab_planes, cells = pre_norm.shape
    cell_total = slab_planes * cells * groups
    padded = -(-(cells + depth) // LANES) * LANES

    deep_bf = deep_gradient(out_grad, w_up).reshape(slabs, channels, cells)
    grad_vals = lax.all_to_all(deep_bf, "slab", split_axis=0, concat_axis=0, tiled=True)

    values = pre_norm.transpose(1, 0, 2)
    saved = act_out.transpose(1, 0, 2)
    edge_values, edge_saved = from_next(jnp.stack((values[:, :, :depth], saved[:, :, :depth])), "grp")
    wide_values = values.astype(jnp.float32)
    moments = sum_over_grp(
        jnp.stack((jnp.sum(wide_values, axis=(0, 2)), jnp.sum(wide_values * wide_values, axis=(0, 2))))
    )
    channel_mean = moments[0] / cell_total
    variance = moments[1] / cell_total - channel_mean * channel_mean
    inv_std = lax.rsqrt(variance + 1e-05)

    def per_channel(array):
        return array[None, :, None]

    def normed_of(array):
        return (array.astype(jnp.float32) - per_channel(channel_mean)) * per_channel(inv_std)

    def masked_of(grads, acts):
        return jnp.where(acts > 0, grads, jnp.zeros_like(grads)).astype(jnp.float32)

    edge_grads = from_next(grad_vals[:, :, :depth], "grp")
    masked = masked_of(grad_vals, saved)
    normed = normed_of(values)
    totals = sum_over_grp(
        jnp.stack((jnp.sum(masked, axis=(0, 2)), jnp.sum(masked * normed, axis=(0, 2))))
    )
    grad_shift = totals[0] / cell_total
    grad_gain = totals[1] / cell_total

    def grad_of(masked, normed):
        return (
            per_channel(norm_gain * inv_std)
            * (masked - per_channel(grad_shift) - normed * per_channel(grad_gain))
        ).astype(jnp.bfloat16)

    edge = grad_of(masked_of(edge_grads, edge_saved), normed_of(edge_values))
    edge = jnp.where(lax.axis_index("grp") < groups - 1, edge, jnp.zeros_like(edge))
    spare = jnp.zeros((slab_planes, channels, padded - cells - depth), jnp.bfloat16)
    act_grads = jnp.concatenate((grad_of(masked, normed), edge, spare), axis=2)
    here = lax.all_to_all(act_grads, "slab", split_axis=0, concat_axis=0, tiled=True)
    here = here.reshape(width_deep, padded)
    after = from_next(here, "slab")

    shifted = shifted_fine(fine_input, padded)
    grad_scale = 1.0 / math.sqrt(cell_total)

    def tap_sums(grads, planes):
        sums = [
            jnp.dot(grads, shifted[plane], preferred_element_type=jnp.float32) for plane in planes
        ]
        return (jnp.concatenate(sums, axis=1) * grad_scale).astype(jnp.bfloat16)

    later_taps = sum_to_owner(tap_sums(here, (0, 1)))
    first_taps = sum_to_owner(tap_sums(after, (1,)))
    grad_down = jnp.concatenate((first_taps, later_taps), axis=1).reshape(-1, 27, width_in)
    grad_input = input_gradient(here, after, w_down, fine_input.shape)
    return (grad_input, grad_down, grad_gain, grad_shift)


def solution(mesh):
    return jax.shard_map(
        local,
        mesh=mesh,
        in_specs=(
            P("slab", "grp", None, None),
            P("slab", "grp", None, None),
            P("slab", None, "grp"),
            P("slab", None, "grp"),
            P("slab"),
            P(),
            P(),
        ),
        out_specs=(
            P("slab", "grp", None, None),
            P(("slab", "grp"), None, None),
            P("slab"),
            P("slab"),
        ),
        check_vma=False,
    )
```

time: 139 us -> 113 us (0.81)
  matrix products: 37.2 us -> 6.72 us
  local copies, waits for them, and re-layouts: 27.4 us -> 8.09 us
  Pallas kernels: 0 us -> 9.91 us
  starting transfers between devices: 28 us -> 35.8 us
  waiting for transfers between devices: 38.5 us -> 44.5 us
    dot_general x55 -> x3, matrix products: 37.2 us -> 6.72 us  [tap_sums(): jnp.dot(grads, shifted[plane], preferred_element_type=jnp.float32)]
    all_to_all x2, waiting for transfers between devices: 15.5 us -> 25.8 us  [the longest x1 12.9 us: local(): lax.all_to_all(deep_bf, 'slab', split_axis=0, concat_axis=0, tiled=True)]
    convert_element_type x3 -> x0, local copies, waits for them, and re-layouts: 10 us -> none  [the longest x2 6.54 us: sum_to_owner(): held = partial.astype(jnp.bfloat16).reshape((2,) * bits + (rows, columns))]
    pallas_call x0 -> x3, Pallas kernels: none -> 9.91 us  [the longest x1 5.92 us: input_gradient(): pl.pallas_call(input_kernel, grid=(planes,), in_specs=[whole, whole, pl.B...]
    ppermute x7 -> x14, waiting for transfers between devices: 10.2 us -> 2.58 us  [sum_to_owner(): lax.ppermute(pick(held, dims, flips), ('slab', 'grp'), bit_pairs(slabs, g...]
    ppermute x2 -> x3, waiting for transfers between devices: 7.39 us -> 14.7 us  [from_next(): return lax.ppermute(shard, axis, [(i, i - 1) for i in range(1, devices)])]
    ppermute x7 -> x14, starting transfers between devices: 10.5 us -> 16.9 us  [sum_to_owner(): lax.ppermute(pick(held, dims, flips), ('slab', 'grp'), bit_pairs(slabs, g...]
    slice x2 -> x1, local copies, waits for them, and re-layouts: 5.57 us -> 0.02 us  [local(): edge_grads = from_next(grad_vals[:, :, :depth], 'grp')]
  transfers between devices with their start and end apart: 17 -> 25, of which waited for: 9 -> 9; matrix products, arithmetic and copies ran while one was open for 22% -> 7% of each run, Pallas kernels for 0% -> 9%
where the time goes in v2:
time: 113 us; the launch traced here: 112 us
  waiting for transfers between devices  44.5 us (39%)
  starting transfers between devices  35.8 us (32%)
  Pallas kernels  9.91 us (9%)
  local copies, waits for them, and re-layouts  8.09 us (7%)
  matrix products  6.72 us (6%)
  other arithmetic  6.42 us (6%)
    ppermute x14, starting transfers between devices, sum_to_owner(): lax.ppermute(pick(held, dims, flips), ('slab', 'grp'), bit_pairs(slabs, g...  16.9 us
    ppermute x3, waiting for transfers between devices, from_next(): return lax.ppermute(shard, axis, [(i, i - 1) for i in range(1, devices)])  14.7 us
    all_to_all x1, waiting for transfers between devices, local(): lax.all_to_all(deep_bf, 'slab', split_axis=0, concat_axis=0, tiled=True)  12.9 us
    all_to_all x1, waiting for transfers between devices, local(): lax.all_to_all(act_grads, 'slab', split_axis=0, concat_axis=0, tiled=True)  12.9 us
    dot_general x3, matrix products, tap_sums(): jnp.dot(grads, shifted[plane], preferred_element_type=jnp.float32)  6.72 us
    all_to_all x1, starting transfers between devices, local(): lax.all_to_all(deep_bf, 'slab', split_axis=0, concat_axis=0, tiled=True)  6.15 us
    unnamed x24, local copies, waits for them, and re-layouts  5.96 us
    pallas_call x1, Pallas kernels, input_gradient(): pl.pallas_call(input_kernel, grid=(planes,), in_specs=[whole, whole, pl.B...  5.92 us
  transfers between devices with their start and end apart: 25, of which 9 were waited for; matrix products, arithmetic and copies ran while one was open for 7% of the time, Pallas kernels for 9%

profile of v2, /device:TPU:0, one launch (start us, length us, event | category | flops | bytes accessed | tf_op | source)
XLA Modules:
  0.0 112.5 jit_solution(4372701113070071907)
XLA Ops:
  0.6 1.4 %convert_reduce_fusion.1 = (f32[32]{0:T(128)S(1)}, f32[32]{0:T(128)S(1)}) fusion(bf16[32,8,1024]{2,1,0:T(8,128)(2,1)} %param.9), kind=kLoop, calls=%fused_computation.16 | loop fusion | flops 1048512 | bytes 524544 | tf_op jit(solution)/shard_map/reduce_sum | solution.py:277
  2.6 2.6 %collective-permute-start.1 = (f32[2,32]{1,0:T(2,128)S(1)}, f32[2,32]{1,0:T(2,128)S(1)}, u32[]{:S(2)}, u32[]{:S(2)}) collective-permute-start(f32[2,32]{1,0:T(2,128)S(1)} %pad_maximum_fusion.1), channel_id=1, source_target_pairs={{0,2},{1,3},{2,0},{3,1},{4,6},{5,7},{6,4},{7,5},{8,10},{9,11},{10,... | collective-permute-start | bytes 776 | tf_op jit(solution)/shard_map/ppermute | solution.py:31
  5.3 1.6 %copy-done.3 = bf16[2,32,128,128]{3,2,1,0:T(8,128)(2,1)S(1)} copy-done((bf16[2,32,128,128]{3,2,1,0:T(8,128)(2,1)S(1)}, bf16[2,32,128,128]{3,2,1,0:T(8,128)(2,1)}, u32[]{:S(2)}) %copy-start.3) | copy-done | bytes 2097176
  7.9 2.6 %deep_gradient.1 = bf16[256,1024]{1,0:T(8,128)(2,1)} custom-call(bf16[2,32,128,128]{3,2,1,0:T(8,128)(2,1)S(1)} %copy-done.3, bf16[8,256,128]{2,1,0:T(8,128)(2,1)S(1)} %copy-done.4), custom_call_target="tpu_custom_call" | custom-call | flops 536870912 | bytes 3145728 | tf_op jit(solution)/shard_map/deep_gradient/pallas_call | solution.py:103
  10.5 6.1 %all-to-all-start = ((bf16[8,32,1024]{2,1,0:T(8,128)(2,1)}), bf16[8,32,1024]{2,1,0:T(8,128)(2,1)S(1)}, u32[]{:S(2)}, u32[]{:S(2)}) async-start(bf16[8,32,1024]{2,1,0:T(8,128)(2,1)} %bitcast.6), calls=%async_computation | async-start | bytes 1048576 | tf_op jit(solution)/shard_map/all_to_all | solution.py:270
  18.8 12.9 %all-to-all-done = bf16[8,32,1024]{2,1,0:T(8,128)(2,1)S(1)} async-done(((bf16[8,32,1024]{2,1,0:T(8,128)(2,1)}), bf16[8,32,1024]{2,1,0:T(8,128)(2,1)S(1)}, u32[]{:S(2)}, u32[]{:S(2)}) %all-to-all-start) | async-done | bytes 524320 | tf_op jit(solution)/shard_map/all_to_all | solution.py:270
  32.6 1.6 %collective-permute-start.4 = (f32[2,32]{1,0:T(2,128)S(1)}, f32[2,32]{1,0:T(2,128)S(1)}, u32[]{:S(2)}, u32[]{:S(2)}) collective-permute-start(f32[2,32]{1,0:T(2,128)S(1)} %pad_maximum_fusion.2), channel_id=1, source_target_pairs={{0,2},{1,3},{2,0},{3,1},{4,6},{5,7},{6,4},{7,5},{8,10},{9,11},{10,... | collective-permute-start | bytes 776 | tf_op jit(solution)/shard_map/ppermute | solution.py:31
  37.2 2.7 %fusion.15 = bf16[8,32,1024]{2,1,0:T(8,128)(2,1)} fusion(f32[32]{0:T(128)S(1)} %get-tuple-element.23, f32[32]{0:T(128)S(1)} %get-tuple-element.22, f32[32]{0:T(128)S(1)} %get-tuple-element.9, f32[32]{0:T(128)S(1)} %multiply_bitcast_fusion.2, f32[32]{0:T(128)S(1)} %get-tuple-element.8, bf16[32,8,1024]{2,1,0:T(8,128)(2,1)S(1)} %copy-done.6, ...), kind=kLoop, calls=%fused_computation.23 | loop fusion | flops 2883584 | bytes 2097792 | tf_op jit(solution)/shard_map/convert_element_type | solution.py:305
  40.1 1.9 %concatenate.10 = bf16[8,32,1152]{2,1,0:T(8,128)(2,1)} concatenate(bf16[8,32,1024]{2,1,0:T(8,128)(2,1)} %fusion.15, bf16[8,32,64]{2,1,0:T(8,128)(2,1)S(1)} %fusion.22, bf16[8,32,64]{2,1,0:T(8,128)(2,1)S(1)} %broadcast.50), dimensions={2} | concatenate | bytes 1179648 | tf_op jit(solution)/shard_map/concatenate | solution.py:310
  42.0 3.6 %all-to-all-start.1 = ((bf16[8,32,1152]{2,1,0:T(8,128)(2,1)}), bf16[8,32,1152]{2,1,0:T(8,128)(2,1)S(1)}, u32[]{:S(2)}, u32[]{:S(2)}) async-start(bf16[8,32,1152]{2,1,0:T(8,128)(2,1)} %concatenate.10), calls=%async_computation.1 | async-start | bytes 1179648 | tf_op jit(solution)/shard_map/all_to_all | solution.py:311
  47.0 2.3 %copy-done = bf16[2,1152,1152]{2,1,0:T(8,128)(2,1)} copy-done((bf16[2,1152,1152]{2,1,0:T(8,128)(2,1)}, bf16[2,1152,1152]{2,1,0:T(8,128)(2,1)S(1)}, u32[]{:S(2)}) %copy-start) | copy-done | bytes 5308440
  49.3 12.9 %all-to-all-done.1 = bf16[8,32,1152]{2,1,0:T(8,128)(2,1)S(1)} async-done(((bf16[8,32,1152]{2,1,0:T(8,128)(2,1)}), bf16[8,32,1152]{2,1,0:T(8,128)(2,1)S(1)}, u32[]{:S(2)}, u32[]{:S(2)}) %all-to-all-start.1) | async-done | bytes 589856 | tf_op jit(solution)/shard_map/all_to_all | solution.py:311
  62.2 2.9 %fusion = f32[2,2,2,2,2,8,1152]{6,5,4,3,2,1,0:T(8,128)S(1)} fusion(bf16[2,2,2,2,2,8,1152]{6,5,4,3,2,1,0:T(8,128)(2,1)S(1)} %bitcast.88, bf16[2,1152,1152]{2,1,0:T(8,128)(2,1)} %copy-done), kind=kOutput, calls=%fused_computation.2 | convolution fusion | flops 679477248 | bytes 4423680 | tf_op jit(solution)/shard_map/dot_general | solution.py:320
  66.6 1.5 %collective-permute-start.8 = (bf16[256,1152]{1,0:T(8,128)(2,1)S(1)}, bf16[256,1152]{1,0:T(8,128)(2,1)S(1)}, u32[]{:S(2)}, u32[]{:S(2)}) collective-permute-start(bf16[256,1152]{1,0:T(8,128)(2,1)S(1)} %bitcast.90), channel_id=1, source_target_pairs={{4,0},{8,4},{12,8},{16,12},{20,16},{24,20},{28,24},{5,1},{9,5},{13... | collective-permute-start | bytes 1769480 | tf_op jit(solution)/shard_map/ppermute | solution.py:24
  68.4 14.7 %collective-permute-done.8.next_ref = bf16[256,1152]{1,0:T(8,128)(2,1)S(1)} collective-permute-done((bf16[256,1152]{1,0:T(8,128)(2,1)S(1)}, bf16[256,1152]{1,0:T(8,128)(2,1)S(1)}, u32[]{:S(2)}, u32[]{:S(2)}) %collective-permute-start.8) | collective-permute-done | bytes 589856 | tf_op jit(solution)/shard_map/ppermute | solution.py:24
  83.2 2.7 %fusion.4 = bf16[256,1152]{1,0:T(8,128)(2,1)S(1)} fusion(bf16[256,1152]{1,0:T(8,128)(2,1)S(1)} %collective-permute-done.8.next_ref, bf16[2,1152,1152]{2,1,0:T(8,128)(2,1)} %copy-done), kind=kOutput, calls=%fused_computation.6 | convolution fusion | flops 680067072 | bytes 3833856 | tf_op jit(solution)/shard_map/dot_general | solution.py:320
  86.3 2.4 %collective-permute-start.17 = (bf16[2,2,1,1,1,8,2304]{6,5,4,3,2,1,0:T(8,128)(2,1)S(1)}, bf16[2,2,1,1,1,8,2304]{6,5,4,3,2,1,0:T(8,128)(2,1)S(1)}, u32[]{:S(2)}, u32[]{:S(2)}) collective-permute-start(bf16[2,2,1,1,1,8,2304]{6,5,4,3,2,1,0:T(8,128)(2,1)S(1)} %get-tuple-element.10), channel_id=1, source_target_pairs={{0,6},{1,7},{2,4},{3,5},{4,2},{5,3},{6,0},{7,1},{8,14},{9,15},{10,... | collective-permute-start | bytes 442376 | tf_op jit(solution)/shard_map/ppermute | solution.py:70
  88.8 1.4 %collective-permute-start.19 = (bf16[2,2,1,1,1,8,2304]{6,5,4,3,2,1,0:T(8,128)(2,1)S(1)}, bf16[2,2,1,1,1,8,2304]{6,5,4,3,2,1,0:T(8,128)(2,1)S(1)}, u32[]{:S(2)}, u32[]{:S(2)}) collective-permute-start(bf16[2,2,1,1,1,8,2304]{6,5,4,3,2,1,0:T(8,128)(2,1)S(1)} %get-tuple-element.11), channel_id=1, source_target_pairs={{0,2},{1,3},{2,0},{3,1},{4,6},{5,7},{6,4},{7,5},{8,10},{9,11},{10,... | collective-permute-start | bytes 442376 | tf_op jit(solution)/shard_map/ppermute | solution.py:70
  90.2 5.9 %input_gradient.1 = bf16[2,32,128,128]{3,2,1,0:T(8,128)(2,1)} custom-call(bf16[256,1152]{1,0:T(8,128)(2,1)S(1)} %bitcast.91, bf16[256,1152]{1,0:T(8,128)(2,1)S(1)} %collective-permute-done.8.next_ref, bf16[27,128,256]{2,1,0:T(8,128)(2,1)S(1)} %copy-done.5), custom_call_target="tpu_custom_call" | custom-call | flops 2038431744 | bytes 5046272 | tf_op jit(solution)/shard_map/input_gradient/pallas_call | solution.py:238
  96.9 2.5 %collective-permute-start.10 = (bf16[2,2,1,1,1,8,1152]{6,5,4,3,2,1,0:T(8,128)(2,1)S(1)}, bf16[2,2,1,1,1,8,1152]{6,5,4,3,2,1,0:T(8,128)(2,1)S(1)}, u32[]{:S(2)}, u32[]{:S(2)}) collective-permute-start(bf16[2,2,1,1,1,8,1152]{6,5,4,3,2,1,0:T(8,128)(2,1)S(1)} %get-tuple-element.13), channel_id=1, source_target_pairs={{0,6},{1,7},{2,4},{3,5},{4,2},{5,3},{6,0},{7,1},{8,14},{9,15},{10,... | collective-permute-start | bytes 221192 | tf_op jit(solution)/shard_map/ppermute | solution.py:70
  100.8 1.8 %collective-permute-start.20 = (bf16[1,1,1,1,1,8,2304]{6,5,4,3,2,1,0:T(8,128)(2,1)S(1)}, bf16[1,1,1,1,1,8,2304]{6,5,4,3,2,1,0:T(8,128)(2,1)S(1)}, u32[]{:S(2)}, u32[]{:S(2)}) collective-permute-start(bf16[1,1,1,1,1,8,2304]{6,5,4,3,2,1,0:T(8,128)(2,1)S(1)} %get-tuple-element.16), channel_id=1, source_target_pairs={{0,24},{1,25},{2,26},{3,27},{4,28},{5,29},{6,30},{7,31},{8,16},{9,... | collective-permute-start | bytes 110600 | tf_op jit(solution)/shard_map/ppermute | solution.py:70
  102.6 2.6 %collective-permute-start.22 = (bf16[1,1,1,1,1,8,2304]{6,5,4,3,2,1,0:T(8,128)(2,1)S(1)}, bf16[1,1,1,1,1,8,2304]{6,5,4,3,2,1,0:T(8,128)(2,1)S(1)}, u32[]{:S(2)}, u32[]{:S(2)}) collective-permute-start(bf16[1,1,1,1,1,8,2304]{6,5,4,3,2,1,0:T(8,128)(2,1)S(1)} %get-tuple-element.17), channel_id=1, source_target_pairs={{0,8},{1,9},{2,10},{3,11},{4,12},{5,13},{6,14},{7,15},{8,0},{9,1},... | collective-permute-start | bytes 110600 | tf_op jit(solution)/shard_map/ppermute | solution.py:70
  105.3 1.8 %collective-permute-start.13 = (bf16[1,1,1,1,1,8,1152]{6,5,4,3,2,1,0:T(8,128)(2,1)S(1)}, bf16[1,1,1,1,1,8,1152]{6,5,4,3,2,1,0:T(8,128)(2,1)S(1)}, u32[]{:S(2)}, u32[]{:S(2)}) collective-permute-start(bf16[1,1,1,1,1,8,1152]{6,5,4,3,2,1,0:T(8,128)(2,1)S(1)} %get-tuple-element.19), channel_id=1, source_target_pairs={{0,24},{1,25},{2,26},{3,27},{4,28},{5,29},{6,30},{7,31},{8,16},{9,... | collective-permute-start | bytes 55304 | tf_op jit(solution)/shard_map/ppermute | solution.py:70
  107.2 2.6 %collective-permute-start.15 = (bf16[1,1,1,1,1,8,1152]{6,5,4,3,2,1,0:T(8,128)(2,1)S(1)}, bf16[1,1,1,1,1,8,1152]{6,5,4,3,2,1,0:T(8,128)(2,1)S(1)}, u32[]{:S(2)}, u32[]{:S(2)}) collective-permute-start(bf16[1,1,1,1,1,8,1152]{6,5,4,3,2,1,0:T(8,128)(2,1)S(1)} %get-tuple-element.20), channel_id=1, source_target_pairs={{0,8},{1,9},{2,10},{3,11},{4,12},{5,13},{6,14},{7,15},{8,0},{9,1},... | collective-permute-start | bytes 55304 | tf_op jit(solution)/shard_map/ppermute | solution.py:70
  (86 shorter events, 16.2 us)
Async XLA Ops:
  2.1 16.6 %collective-permute-start = (f32[2,32]{1,0:T(2,128)S(1)}, f32[2,32]{1,0:T(2,128)S(1)}, u32[]{:S(2)}, u32[]{:S(2)}) collective-permute-start(f32[2,32]{1,0:T(2,128)S(1)} %pad_maximum_fusion.1), channel_id=1, source_target_pairs={{0,1},{1,0},{2,3},{3,2},{4,5},{5,4},{6,7},{7,6},{8,9},{9,8},{10,11... | collective-permute-start | bytes 776 | tf_op jit(solution)/shard_map/ppermute | solution.py:31
  2.6 16.1 %collective-permute-start.1 = (f32[2,32]{1,0:T(2,128)S(1)}, f32[2,32]{1,0:T(2,128)S(1)}, u32[]{:S(2)}, u32[]{:S(2)}) collective-permute-start(f32[2,32]{1,0:T(2,128)S(1)} %pad_maximum_fusion.1), channel_id=1, source_target_pairs={{0,2},{1,3},{2,0},{3,1},{4,6},{5,7},{6,4},{7,5},{8,10},{9,11},{10,... | collective-permute-start | bytes 776 | tf_op jit(solution)/shard_map/ppermute | solution.py:31
  5.2 13.5 %collective-permute-start.2 = (f32[2,32]{1,0:T(2,128)S(1)}, f32[2,32]{1,0:T(2,128)S(1)}, u32[]{:S(2)}, u32[]{:S(2)}) collective-permute-start(f32[2,32]{1,0:T(2,128)S(1)} %pad_maximum_fusion.1), channel_id=1, source_target_pairs={{0,3},{1,2},{2,1},{3,0},{4,7},{5,6},{6,5},{7,4},{8,11},{9,10},{10,... | collective-permute-start | bytes 776 | tf_op jit(solution)/shard_map/ppermute | solution.py:31
  10.5 21.1 %all-to-all-start = ((bf16[8,32,1024]{2,1,0:T(8,128)(2,1)}), bf16[8,32,1024]{2,1,0:T(8,128)(2,1)S(1)}, u32[]{:S(2)}, u32[]{:S(2)}) async-start(bf16[8,32,1024]{2,1,0:T(8,128)(2,1)} %bitcast.6), calls=%async_computation | async-start | bytes 1048576 | tf_op jit(solution)/shard_map/all_to_all | solution.py:270
  17.4 22.6 %collective-permute-start.6 = (bf16[2,8,32,64]{3,2,1,0:T(8,128)(2,1)S(1)}, bf16[2,8,32,64]{3,2,1,0:T(8,128)(2,1)S(1)}, u32[]{:S(2)}, u32[]{:S(2)}) collective-permute-start(bf16[2,8,32,64]{3,2,1,0:T(8,128)(2,1)S(1)} %pad_maximum_fusion), channel_id=1, source_target_pairs={{1,0},{2,1},{3,2},{5,4},{6,5},{7,6},{9,8},{10,9},{11,10},{13,12},{... | collective-permute-start | bytes 196616 | tf_op jit(solution)/shard_map/ppermute | solution.py:24
  32.5 3.3 %collective-permute-start.3 = (f32[2,32]{1,0:T(2,128)S(1)}, f32[2,32]{1,0:T(2,128)S(1)}, u32[]{:S(2)}, u32[]{:S(2)}) collective-permute-start(f32[2,32]{1,0:T(2,128)S(1)} %pad_maximum_fusion.2), channel_id=1, source_target_pairs={{0,1},{1,0},{2,3},{3,2},{4,5},{5,4},{6,7},{7,6},{8,9},{9,8},{10,11... | collective-permute-start | bytes 776 | tf_op jit(solution)/shard_map/ppermute | solution.py:31
  32.6 3.6 %collective-permute-start.4 = (f32[2,32]{1,0:T(2,128)S(1)}, f32[2,32]{1,0:T(2,128)S(1)}, u32[]{:S(2)}, u32[]{:S(2)}) collective-permute-start(f32[2,32]{1,0:T(2,128)S(1)} %pad_maximum_fusion.2), channel_id=1, source_target_pairs={{0,2},{1,3},{2,0},{3,1},{4,6},{5,7},{6,4},{7,5},{8,10},{9,11},{10,... | collective-permute-start | bytes 776 | tf_op jit(solution)/shard_map/ppermute | solution.py:31
  34.5 5.5 %collective-permute-start.7 = (bf16[8,32,64]{2,1,0:T(8,128)(2,1)S(1)}, bf16[8,32,64]{2,1,0:T(8,128)(2,1)S(1)}, u32[]{:S(2)}, u32[]{:S(2)}) collective-permute-start(bf16[8,32,64]{2,1,0:T(8,128)(2,1)S(1)} %slice.39), channel_id=1, source_target_pairs={{1,0},{2,1},{3,2},{5,4},{6,5},{7,6},{9,8},{10,9},{11,10},{13,12},{... | collective-permute-start | bytes 98312 | tf_op jit(solution)/shard_map/ppermute | solution.py:24
  42.0 20.2 %all-to-all-start.1 = ((bf16[8,32,1152]{2,1,0:T(8,128)(2,1)}), bf16[8,32,1152]{2,1,0:T(8,128)(2,1)S(1)}, u32[]{:S(2)}, u32[]{:S(2)}) async-start(bf16[8,32,1152]{2,1,0:T(8,128)(2,1)} %concatenate.10), calls=%async_computation.1 | async-start | bytes 1179648 | tf_op jit(solution)/shard_map/all_to_all | solution.py:311
  66.6 16.6 %collective-permute-start.8 = (bf16[256,1152]{1,0:T(8,128)(2,1)S(1)}, bf16[256,1152]{1,0:T(8,128)(2,1)S(1)}, u32[]{:S(2)}, u32[]{:S(2)}) collective-permute-start(bf16[256,1152]{1,0:T(8,128)(2,1)S(1)} %bitcast.90), channel_id=1, source_target_pairs={{4,0},{8,4},{12,8},{16,12},{20,16},{24,20},{28,24},{5,1},{9,5},{13... | collective-permute-start | bytes 1769480 | tf_op jit(solution)/shard_map/ppermute | solution.py:24
  68.3 17.7 %collective-permute-start.16 = (bf16[2,2,2,2,1,8,2304]{6,5,4,3,2,1,0:T(8,128)(2,1)S(1)}, bf16[2,2,2,2,1,8,2304]{6,5,4,3,2,1,0:T(8,128)(2,1)S(1)}, u32[]{:S(2)}, u32[]{:S(2)}) collective-permute-start(bf16[2,2,2,2,1,8,2304]{6,5,4,3,2,1,0:T(8,128)(2,1)S(1)} %constant_dynamic-slice_fusion.6), channel_id=1, source_target_pairs={{0,1},{1,0},{2,3},{3,2},{4,5},{5,4},{6,7},{7,6},{8,9},{9,8},{10,11... | collective-permute-start | bytes 1769480 | tf_op jit(solution)/shard_map/ppermute | solution.py:70
  86.0 10.8 %collective-permute-start.9 = (bf16[2,2,2,2,1,8,1152]{6,5,4,3,2,1,0:T(8,128)(2,1)S(1)}, bf16[2,2,2,2,1,8,1152]{6,5,4,3,2,1,0:T(8,128)(2,1)S(1)}, u32[]{:S(2)}, u32[]{:S(2)}) collective-permute-start(bf16[2,2,2,2,1,8,1152]{6,5,4,3,2,1,0:T(8,128)(2,1)S(1)} %constant_dynamic-slice_fusion.13), channel_id=1, source_target_pairs={{0,1},{1,0},{2,3},{3,2},{4,5},{5,4},{6,7},{7,6},{8,9},{9,8},{10,11... | collective-permute-start | bytes 884744 | tf_op jit(solution)/shard_map/ppermute | solution.py:70
  86.3 9.8 %collective-permute-start.17 = (bf16[2,2,1,1,1,8,2304]{6,5,4,3,2,1,0:T(8,128)(2,1)S(1)}, bf16[2,2,1,1,1,8,2304]{6,5,4,3,2,1,0:T(8,128)(2,1)S(1)}, u32[]{:S(2)}, u32[]{:S(2)}) collective-permute-start(bf16[2,2,1,1,1,8,2304]{6,5,4,3,2,1,0:T(8,128)(2,1)S(1)} %get-tuple-element.10), channel_id=1, source_target_pairs={{0,6},{1,7},{2,4},{3,5},{4,2},{5,3},{6,0},{7,1},{8,14},{9,15},{10,... | collective-permute-start | bytes 442376 | tf_op jit(solution)/shard_map/ppermute | solution.py:70
  88.6 7.7 %collective-permute-start.18 = (bf16[2,2,1,1,1,8,2304]{6,5,4,3,2,1,0:T(8,128)(2,1)S(1)}, bf16[2,2,1,1,1,8,2304]{6,5,4,3,2,1,0:T(8,128)(2,1)S(1)}, u32[]{:S(2)}, u32[]{:S(2)}) collective-permute-start(bf16[2,2,1,1,1,8,2304]{6,5,4,3,2,1,0:T(8,128)(2,1)S(1)} %get-tuple-element.12), channel_id=1, source_target_pairs={{0,4},{1,5},{2,6},{3,7},{4,0},{5,1},{6,2},{7,3},{8,12},{9,13},{10,... | collective-permute-start | bytes 442376 | tf_op jit(solution)/shard_map/ppermute | solution.py:70
  88.8 7.9 %collective-permute-start.19 = (bf16[2,2,1,1,1,8,2304]{6,5,4,3,2,1,0:T(8,128)(2,1)S(1)}, bf16[2,2,1,1,1,8,2304]{6,5,4,3,2,1,0:T(8,128)(2,1)S(1)}, u32[]{:S(2)}, u32[]{:S(2)}) collective-permute-start(bf16[2,2,1,1,1,8,2304]{6,5,4,3,2,1,0:T(8,128)(2,1)S(1)} %get-tuple-element.11), channel_id=1, source_target_pairs={{0,2},{1,3},{2,0},{3,1},{4,6},{5,7},{6,4},{7,5},{8,10},{9,11},{10,... | collective-permute-start | bytes 442376 | tf_op jit(solution)/shard_map/ppermute | solution.py:70
  96.9 5.8 %collective-permute-start.10 = (bf16[2,2,1,1,1,8,1152]{6,5,4,3,2,1,0:T(8,128)(2,1)S(1)}, bf16[2,2,1,1,1,8,1152]{6,5,4,3,2,1,0:T(8,128)(2,1)S(1)}, u32[]{:S(2)}, u32[]{:S(2)}) collective-permute-start(bf16[2,2,1,1,1,8,1152]{6,5,4,3,2,1,0:T(8,128)(2,1)S(1)} %get-tuple-element.13), channel_id=1, source_target_pairs={{0,6},{1,7},{2,4},{3,5},{4,2},{5,3},{6,0},{7,1},{8,14},{9,15},{10,... | collective-permute-start | bytes 221192 | tf_op jit(solution)/shard_map/ppermute | solution.py:70
  99.3 5.9 %collective-permute-start.11 = (bf16[2,2,1,1,1,8,1152]{6,5,4,3,2,1,0:T(8,128)(2,1)S(1)}, bf16[2,2,1,1,1,8,1152]{6,5,4,3,2,1,0:T(8,128)(2,1)S(1)}, u32[]{:S(2)}, u32[]{:S(2)}) collective-permute-start(bf16[2,2,1,1,1,8,1152]{6,5,4,3,2,1,0:T(8,128)(2,1)S(1)} %get-tuple-element.15), channel_id=1, source_target_pairs={{0,4},{1,5},{2,6},{3,7},{4,0},{5,1},{6,2},{7,3},{8,12},{9,13},{10,... | collective-permute-start | bytes 221192 | tf_op jit(solution)/shard_map/ppermute | solution.py:70
  99.6 5.7 %collective-permute-start.12 = (bf16[2,2,1,1,1,8,1152]{6,5,4,3,2,1,0:T(8,128)(2,1)S(1)}, bf16[2,2,1,1,1,8,1152]{6,5,4,3,2,1,0:T(8,128)(2,1)S(1)}, u32[]{:S(2)}, u32[]{:S(2)}) collective-permute-start(bf16[2,2,1,1,1,8,1152]{6,5,4,3,2,1,0:T(8,128)(2,1)S(1)} %get-tuple-element.14), channel_id=1, source_target_pairs={{0,2},{1,3},{2,0},{3,1},{4,6},{5,7},{6,4},{7,5},{8,10},{9,11},{10,... | collective-permute-start | bytes 221192 | tf_op jit(solution)/shard_map/ppermute | solution.py:70
  100.8 6.4 %collective-permute-start.20 = (bf16[1,1,1,1,1,8,2304]{6,5,4,3,2,1,0:T(8,128)(2,1)S(1)}, bf16[1,1,1,1,1,8,2304]{6,5,4,3,2,1,0:T(8,128)(2,1)S(1)}, u32[]{:S(2)}, u32[]{:S(2)}) collective-permute-start(bf16[1,1,1,1,1,8,2304]{6,5,4,3,2,1,0:T(8,128)(2,1)S(1)} %get-tuple-element.16), channel_id=1, source_target_pairs={{0,24},{1,25},{2,26},{3,27},{4,28},{5,29},{6,30},{7,31},{8,16},{9,... | collective-permute-start | bytes 110600 | tf_op jit(solution)/shard_map/ppermute | solution.py:70
  102.6 7.2 %collective-permute-start.21 = (bf16[1,1,1,1,1,8,2304]{6,5,4,3,2,1,0:T(8,128)(2,1)S(1)}, bf16[1,1,1,1,1,8,2304]{6,5,4,3,2,1,0:T(8,128)(2,1)S(1)}, u32[]{:S(2)}, u32[]{:S(2)}) collective-permute-start(bf16[1,1,1,1,1,8,2304]{6,5,4,3,2,1,0:T(8,128)(2,1)S(1)} %get-tuple-element.18), channel_id=1, source_target_pairs={{0,16},{1,17},{2,18},{3,19},{4,20},{5,21},{6,22},{7,23},{8,24},{9,... | collective-permute-start | bytes 110600 | tf_op jit(solution)/shard_map/ppermute | solution.py:70
  102.6 7.2 %collective-permute-start.22 = (bf16[1,1,1,1,1,8,2304]{6,5,4,3,2,1,0:T(8,128)(2,1)S(1)}, bf16[1,1,1,1,1,8,2304]{6,5,4,3,2,1,0:T(8,128)(2,1)S(1)}, u32[]{:S(2)}, u32[]{:S(2)}) collective-permute-start(bf16[1,1,1,1,1,8,2304]{6,5,4,3,2,1,0:T(8,128)(2,1)S(1)} %get-tuple-element.17), channel_id=1, source_target_pairs={{0,8},{1,9},{2,10},{3,11},{4,12},{5,13},{6,14},{7,15},{8,0},{9,1},... | collective-permute-start | bytes 110600 | tf_op jit(solution)/shard_map/ppermute | solution.py:70
  105.3 5.6 %collective-permute-start.13 = (bf16[1,1,1,1,1,8,1152]{6,5,4,3,2,1,0:T(8,128)(2,1)S(1)}, bf16[1,1,1,1,1,8,1152]{6,5,4,3,2,1,0:T(8,128)(2,1)S(1)}, u32[]{:S(2)}, u32[]{:S(2)}) collective-permute-start(bf16[1,1,1,1,1,8,1152]{6,5,4,3,2,1,0:T(8,128)(2,1)S(1)} %get-tuple-element.19), channel_id=1, source_target_pairs={{0,24},{1,25},{2,26},{3,27},{4,28},{5,29},{6,30},{7,31},{8,16},{9,... | collective-permute-start | bytes 55304 | tf_op jit(solution)/shard_map/ppermute | solution.py:70
  107.2 4.7 %collective-permute-start.14 = (bf16[1,1,1,1,1,8,1152]{6,5,4,3,2,1,0:T(8,128)(2,1)S(1)}, bf16[1,1,1,1,1,8,1152]{6,5,4,3,2,1,0:T(8,128)(2,1)S(1)}, u32[]{:S(2)}, u32[]{:S(2)}) collective-permute-start(bf16[1,1,1,1,1,8,1152]{6,5,4,3,2,1,0:T(8,128)(2,1)S(1)} %get-tuple-element.21), channel_id=1, source_target_pairs={{0,16},{1,17},{2,18},{3,19},{4,20},{5,21},{6,22},{7,23},{8,24},{9,... | collective-permute-start | bytes 55304 | tf_op jit(solution)/shard_map/ppermute | solution.py:70
  107.2 4.7 %collective-permute-start.15 = (bf16[1,1,1,1,1,8,1152]{6,5,4,3,2,1,0:T(8,128)(2,1)S(1)}, bf16[1,1,1,1,1,8,1152]{6,5,4,3,2,1,0:T(8,128)(2,1)S(1)}, u32[]{:S(2)}, u32[]{:S(2)}) collective-permute-start(bf16[1,1,1,1,1,8,1152]{6,5,4,3,2,1,0:T(8,128)(2,1)S(1)} %get-tuple-element.20), channel_id=1, source_target_pairs={{0,8},{1,9},{2,10},{3,11},{4,12},{5,13},{6,14},{7,15},{8,0},{9,1},... | collective-permute-start | bytes 55304 | tf_op jit(solution)/shard_map/ppermute | solution.py:70
  (12 other events, 59.6 us)

commit v3 on v0

v3 whole, which is shorter than its diff:
```python
import functools
import math

import jax
import jax.numpy as jnp
from jax import lax
from jax.experimental import pallas as pl
from jax.experimental.pallas import tpu as pltpu
from jax.sharding import PartitionSpec as P

LANES = 128


def bit_pairs(slabs, groups, slab_bits, grp_bits):
    return [
        (s * groups + g, (s ^ slab_bits) * groups + (g ^ grp_bits))
        for s in range(slabs)
        for g in range(groups)
    ]


def from_next(shard, axis):
    devices = lax.axis_size(axis)
    return lax.ppermute(shard, axis, [(i, i - 1) for i in range(1, devices)])


def grp_parts(values):
    groups = lax.axis_size("grp")
    return [values] + [
        lax.ppermute(values, "grp", [(i, i ^ step) for i in range(groups)])
        for step in range(1, groups)
    ]


def pair_sum(parts):
    while len(parts) > 1:
        parts = [first + second for first, second in zip(parts[::2], parts[1::2])]
    return parts[0]


def place_bits():
    return (lax.axis_size("slab") * lax.axis_size("grp")).bit_length() - 1


def split_places(partial):
    bits = place_bits()
    return partial.reshape((2,) * bits + (partial.shape[0] >> bits, partial.shape[1]))


def exchange(held, stage):
    slabs = lax.axis_size("slab")
    groups = lax.axis_size("grp")
    place = lax.axis_index("slab") * groups + lax.axis_index("grp")
    dims = [place_bits() - 1 - b for b in stage]

    def pick(flips):
        array = held
        for dim, bit, flip in zip(dims, stage, flips):
            array = lax.dynamic_slice_in_dim(array, (place >> bit & 1) ^ flip, 1, dim)
        return array

    total = pick([0] * len(dims)).astype(jnp.float32)
    for code in range((1 << len(stage)) - 1, 0, -1):
        flips = [code >> n & 1 for n in range(len(stage))]
        mask = sum(f << b for f, b in zip(flips, stage))
        pairs = bit_pairs(slabs, groups, mask // groups, mask % groups)
        arrived = lax.ppermute(pick(flips), ("slab", "grp"), pairs)
        total = total + arrived.astype(jnp.float32)
    return total.astype(jnp.bfloat16)


def halves(partial, bit):
    place = lax.axis_index("slab") * lax.axis_size("grp") + lax.axis_index("grp")
    held = split_places(partial)
    dim = place_bits() - 1 - bit
    own = place >> bit & 1
    return tuple(lax.dynamic_slice_in_dim(held, own ^ flip, 1, dim) for flip in range(2))


def exchange_halves(kept, sent, bit):
    slabs = lax.axis_size("slab")
    groups = lax.axis_size("grp")
    pairs = bit_pairs(slabs, groups, (1 << bit) // groups, (1 << bit) % groups)
    arrived = lax.ppermute(sent, ("slab", "grp"), pairs)
    return (kept.astype(jnp.float32) + arrived.astype(jnp.float32)).astype(jnp.bfloat16)


def deep_kernel(rows_ref, taps_ref, out_ref, rows, taps, wide, cells, row_sems, tap_sem):
    steps = row_sems.shape[0]
    depth = rows_ref.shape[2] // 2
    width = rows_ref.shape[3]
    step = rows_ref.shape[1] // steps
    count = step // 2 * depth
    taps_copy = pltpu.make_async_copy(taps_ref, taps, tap_sem)
    copies = [
        pltpu.make_async_copy(
            rows_ref.at[:, pl.ds(n * step, step)], rows.at[:, pl.ds(n * step, step)], row_sems.at[n]
        )
        for n in range(steps)
    ]
    copies[0].start()
    taps_copy.start()
    for copy in copies[1:]:
        copy.start()

    def split(n):
        for pair in range(step // 2):
            for px in range(2):
                for py in range(2):
                    tap = 4 * px + 2 * py
                    slot = wide.at[pair * 4 + px * 2 + py]
                    slot[...] = rows[px, n * step + 2 * pair + py].astype(jnp.float32)
                    for pz in range(2):
                        cells[
                            n % 2,
                            pair * depth : (pair + 1) * depth,
                            (tap + pz) * width : (tap + pz + 1) * width,
                        ] = slot[pl.ds(pz, depth, stride=2), :].astype(jnp.bfloat16)

    def multiply(n):
        sums = lax.dot_general(
            jnp.concatenate([taps[p] for p in range(8)], axis=1),
            cells[n % 2],
            (((1,), (1,)), ((), ())),
            preferred_element_type=jnp.float32,
        )
        out_ref[:, n * count : (n + 1) * count] = sums.astype(jnp.bfloat16)

    for n, copy in enumerate(copies):
        copy.wait()
        if n == 1:
            taps_copy.wait()
        if n:
            multiply(n - 1)
        split(n)
    multiply(steps - 1)


def deep_gradient(out_grad, w_up):
    _, rows, fine_depth, width_in = out_grad.shape
    width_deep = w_up.shape[1]
    cells = rows * fine_depth // 4
    steps = rows // 8
    return pl.pallas_call(
        deep_kernel,
        in_specs=[pl.BlockSpec(memory_space=pltpu.HBM)] * 2,
        out_specs=pl.BlockSpec(memory_space=pltpu.VMEM),
        out_shape=jax.ShapeDtypeStruct((width_deep, cells), jnp.bfloat16),
        scratch_shapes=[
            pltpu.VMEM(out_grad.shape, jnp.bfloat16),
            pltpu.VMEM(w_up.shape, jnp.bfloat16),
            pltpu.VMEM((rows // steps * 2, fine_depth, width_in), jnp.float32),
            pltpu.VMEM((2, cells // steps, 8 * width_in), jnp.bfloat16),
            pltpu.SemaphoreType.DMA((steps,)),
            pltpu.SemaphoreType.DMA,
        ],
        compiler_params=pltpu.CompilerParams(vmem_limit_bytes=60 << 20),
        cost_estimate=pl.CostEstimate(
            flops=2 * 8 * cells * width_deep * width_in,
            bytes_accessed=2 * (out_grad.size + w_up.size + width_deep * cells),
            transcendentals=0,
        ),
        name="deep_gradient",
    )(out_grad, w_up)


def shifted_kernel(fine_ref, out_ref, wide):
    planes, fine_rows, fine_depth, width = fine_ref.shape
    depth = fine_depth // 2
    cells = fine_rows // 2 * depth
    zeros = jnp.zeros((depth, out_ref.shape[1]), jnp.bfloat16)
    wide[:, 0:8, :] = jnp.zeros((wide.shape[0], 8, width), jnp.float32)
    out_ref[cells : cells + depth, :] = zeros
    out_ref[2 * cells + depth :, :] = zeros

    def row(y, carry):
        for px in range(planes):
            for py in range(2):
                slot = wide.at[2 * px + py]
                slot[8:, :] = fine_ref[px, 2 * y + py].astype(jnp.float32)
                start = pl.multiple_of(y * depth + py * (cells + depth), depth)
                for kz in range(3):
                    column = (3 * px + kz) * width
                    out_ref[pl.ds(start, depth), column : column + width] = slot[
                        pl.ds(7 + kz, depth, stride=2), :
                    ].astype(jnp.bfloat16)
        return carry

    lax.fori_loop(0, fine_rows // 2, row, 0)


def shifted_fine(fine_input, first):
    planes, fine_rows, fine_depth, width = fine_input.shape
    planes -= first
    depth = fine_depth // 2
    shape = (fine_rows * depth + 2 * depth, planes * 3 * width)
    return pl.pallas_call(
        shifted_kernel,
        grid=(1,),
        in_specs=[
            pl.BlockSpec((planes, fine_rows, fine_depth, width), lambda i: (first // planes, 0, 0, 0))
        ],
        out_specs=pl.BlockSpec(shape, lambda i: (0, 0)),
        out_shape=jax.ShapeDtypeStruct(shape, jnp.bfloat16),
        scratch_shapes=[pltpu.VMEM((2 * planes, fine_depth + 8, width), jnp.float32)],
        compiler_params=pltpu.CompilerParams(vmem_limit_bytes=16 << 20),
        cost_estimate=pl.CostEstimate(flops=0, bytes_accessed=0, transcendentals=0),
        name="shifted_fine",
    )(fine_input)


def tap_kernel(scale, depth, block, own_ref, grads_ref, shifted_ref, kept_ref, sent_ref=None):
    cells = (shifted_ref.shape[0] - 2 * depth) // 2
    width = 3 * LANES
    planes = shifted_ref.shape[1] // width
    own = own_ref[0] > 0
    for ky, start in ((1, 0), (0, cells), (2, cells + depth)):
        count = grads_ref.shape[1] if ky == 0 else cells
        grads = grads_ref[:, :count]
        for px in range(planes):
            sums = scale * jnp.dot(
                grads,
                shifted_ref[start : start + count, px * width : (px + 1) * width],
                preferred_element_type=jnp.float32,
            )
            first = (ky * planes + px) * width
            columns = slice(first, first + width)
            if not block:
                kept_ref[:, columns] = sums.astype(jnp.bfloat16)
                continue
            pairs = sums.reshape(sums.shape[0] // (2 * block), 2, block, width)
            low, high = (pairs[:, n].reshape(sums.shape[0] // 2, width) for n in range(2))
            kept_ref[:, columns] = jnp.where(own, high, low).astype(jnp.bfloat16)
            sent_ref[:, columns] = jnp.where(own, low, high).astype(jnp.bfloat16)


def tap_call(grads, shifted, depth, scale, bit, block):
    width_deep, padded = grads.shape
    columns = 3 * shifted.shape[1]
    place = lax.axis_index("slab") * lax.axis_size("grp") + lax.axis_index("grp")
    outs = 2 if block else 1
    return pl.pallas_call(
        functools.partial(tap_kernel, scale, depth, block),
        in_specs=[pl.BlockSpec(memory_space=pltpu.SMEM)]
        + [pl.BlockSpec(memory_space=pltpu.VMEM)] * 2,
        out_specs=[pl.BlockSpec(memory_space=pltpu.VMEM)] * outs,
        out_shape=[jax.ShapeDtypeStruct((width_deep // outs, columns), jnp.bfloat16)] * outs,
        compiler_params=pltpu.CompilerParams(vmem_limit_bytes=12 << 20),
        cost_estimate=pl.CostEstimate(
            flops=2 * width_deep * padded * columns,
            bytes_accessed=2 * (grads.size + padded * columns + width_deep * columns),
            transcendentals=0,
        ),
        name="tap_sums",
    )((place >> bit & 1).astype(jnp.int32).reshape(1), grads, shifted)


def tap_sums(grads, shifted, depth, scale):
    return tap_call(grads, shifted, depth, scale, 0, 0)[0]


def tap_halves(grads, shifted, depth, scale, bit):
    bits = place_bits()
    rows = grads.shape[0] >> bits
    if (rows << bit) % 8:
        return halves(tap_sums(grads, shifted, depth, scale), bit)
    dims = [2] * bits
    dims[bits - 1 - bit] = 1
    arrays = tap_call(grads, shifted, depth, scale, bit, rows << bit)
    return tuple(array.reshape(*dims, rows, array.shape[1]) for array in arrays)


def input_kernel(taps_of, *refs):
    grads_refs = refs[: len(taps_of)]
    taps_ref = refs[len(taps_of)]
    out_ref, turned, product, wide = refs[-4:]
    width = taps_ref.shape[1]
    fine_rows, fine_depth = out_ref.shape[1:3]
    depth = fine_depth // 2
    padded = turned.shape[1]
    for slot, ref in enumerate(grads_refs):
        for start in range(0, padded, LANES):
            turned[slot, start : start + LANES, :] = ref[:, start : start + LANES].T
    for ky in range(3):
        total = None
        for slot, kx in enumerate(taps_of):
            taps = jnp.concatenate([taps_ref[9 * kx + 3 * ky + kz] for kz in range(3)], axis=0)
            term = lax.dot_general(
                turned[slot],
                taps,
                (((1,), (1,)), ((), ())),
                preferred_element_type=jnp.float32,
            )
            total = term if total is None else total + term
        product[:, 3 * ky * width : (3 * ky + 3) * width] = total
    inside = lax.broadcasted_iota(jnp.int32, (depth, width), 0) < depth - 1

    def row(y, carry):
        start = pl.multiple_of(y * depth, depth)

        def at(ky, kz):
            offset = depth if ky == 0 else 0
            return product[
                pl.ds(start + offset, depth), (3 * ky + kz) * width : (3 * ky + kz + 1) * width
            ]

        for py in range(2):
            terms = (2, 0) if py else (1,)
            even, odd, following = (sum(at(ky, kz) for ky in terms) for kz in (1, 2, 0))
            following = pltpu.roll(following, depth - 1, 0)
            wide[pl.ds(0, depth, stride=2), :] = even
            wide[pl.ds(1, depth, stride=2), :] = odd + jnp.where(inside, following, 0.0)
            out_ref[0, 2 * y + py] = wide[...].astype(jnp.bfloat16)
        return carry

    lax.fori_loop(0, fine_rows // 2, row, 0)


def input_plane(px, grads, taps_of, w_down, fine_shape, earlier=None):
    _, fine_rows, fine_depth, width = fine_shape
    width_deep, padded = grads[0].shape
    operands = list(grads) + [w_down]
    in_specs = [pl.BlockSpec((width_deep, padded), lambda i: (0, 0)) for _ in grads]
    in_specs.append(pl.BlockSpec(w_down.shape, lambda i: (0, 0, 0)))
    aliases = {}
    if earlier is not None:
        aliases = {len(operands): 0}
        operands.append(earlier)
        in_specs.append(pl.BlockSpec(memory_space=pl.ANY))
    return pl.pallas_call(
        functools.partial(input_kernel, taps_of),
        grid=(1,),
        in_specs=in_specs,
        out_specs=pl.BlockSpec((1, fine_rows, fine_depth, width), lambda i: (px, 0, 0, 0)),
        out_shape=jax.ShapeDtypeStruct(fine_shape, jnp.bfloat16),
        input_output_aliases=aliases,
        scratch_shapes=[
            pltpu.VMEM((len(grads), padded, width_deep), jnp.bfloat16),
            pltpu.VMEM((padded, 9 * width), jnp.float32),
            pltpu.VMEM((fine_depth, width), jnp.float32),
        ],
        compiler_params=pltpu.CompilerParams(vmem_limit_bytes=20 << 20),
        cost_estimate=pl.CostEstimate(flops=0, bytes_accessed=0, transcendentals=0),
        name="input_gradient",
    )(*operands)


def mean_and_variance(first_sum, second_sum, count):
    mean = first_sum / count
    return mean, second_sum / count - mean * mean


def own_moments(first_sum, second_sum, count):
    mean, variance = mean_and_variance(first_sum, second_sum, count)
    return mean, lax.rsqrt(jnp.maximum(variance, 0.0) + 1e-05)


def norm_kernel(own_total, cell_total, parts, *refs):
    part_refs, refs = refs[:parts], refs[parts:]
    (gain_ref, edge_ref, values_ref, acts_ref, grads_ref, edge_values_ref, edge_acts_ref, edge_grads_ref) = refs[:8]
    out_ref, totals_ref = refs[8:]
    planes, channels, cells = values_ref.shape
    depth = edge_values_ref.shape[2]

    def columns(array):
        return [array[:, n : n + 1] for n in range(array.shape[1])]

    each = [ref[...] for ref in part_refs]
    sums = columns(pair_sum(each))
    mean, variance = mean_and_variance(sums[0], sums[1], cell_total)
    inv_std = lax.rsqrt(variance + 1e-05)

    def normed_total(part):
        own_mean, own_inv = own_moments(part[0], part[1], own_total)
        return inv_std * (part[3] / own_inv + (own_mean - mean) * part[2])

    shift = sums[2] / cell_total
    slope = pair_sum([normed_total(columns(part)) for part in each]) / cell_total
    totals_ref[:, 0:1] = slope
    totals_ref[:, 1:2] = shift
    gain = gain_ref[...] * inv_std
    edge_gain = gain * edge_ref[0]

    def grad_of(values, acts, grads, gain):
        normed = (values.astype(jnp.float32) - mean) * inv_std
        masked = jnp.where(acts.astype(jnp.float32) > 0, grads.astype(jnp.float32), 0.0)
        return (gain * (masked - shift - normed * slope)).astype(jnp.bfloat16)

    for plane in range(planes):
        out_ref[plane, :, 0:cells] = grad_of(
            values_ref[plane], acts_ref[plane], grads_ref[plane], gain
        )
        edge = grad_of(
            edge_values_ref[plane], edge_acts_ref[plane], edge_grads_ref[plane], edge_gain
        )
        spare = jnp.zeros((channels, out_ref.shape[2] - cells - depth), jnp.bfloat16)
        out_ref[plane, :, cells:] = jnp.concatenate((edge, spare), axis=1)


def local(fine_input, out_grad, pre_norm, act_out, norm_gain, w_down, w_up):
    slabs = lax.axis_size("slab")
    groups = lax.axis_size("grp")
    fine_rows, fine_depth, width_in = fine_input.shape[1:]
    depth = fine_depth // 2
    width_deep = w_up.shape[1]
    channels, slab_planes, cells = pre_norm.shape
    cell_total = slab_planes * cells * groups
    padded = -(-(cells + depth) // LANES) * LANES

    deep_bf = deep_gradient(out_grad, w_up)
    deep_bf, pre_norm, act_out, fine_input = lax.optimization_barrier(
        (deep_bf, pre_norm, act_out, fine_input)
    )
    deep_bf = deep_bf.reshape(slabs, channels, cells)
    grad_vals = lax.all_to_all(deep_bf, "slab", split_axis=0, concat_axis=0, tiled=True)

    values = pre_norm.transpose(1, 0, 2)
    acts = act_out.transpose(1, 0, 2)
    edge_values, edge_acts = from_next(jnp.stack((values[:, :, :depth], acts[:, :, :depth])), "grp")
    edge_grads = from_next(grad_vals[:, :, :depth], "grp")

    wide_values = values.astype(jnp.float32)
    first_sum = jnp.sum(wide_values, axis=(0, 2))
    second_sum = jnp.sum(wide_values * wide_values, axis=(0, 2))

    own_total = slab_planes * cells
    own_mean, own_inv = own_moments(first_sum, second_sum, own_total)
    masked = jnp.where(acts > 0, grad_vals, jnp.zeros_like(grad_vals)).astype(jnp.float32)
    own_normed = (wide_values - own_mean[None, :, None]) * own_inv[None, :, None]
    parts = grp_parts(
        jnp.stack(
            (
                first_sum,
                second_sum,
                jnp.sum(masked, axis=(0, 2)),
                jnp.sum(masked * own_normed, axis=(0, 2)),
            ),
            axis=1,
        )
    )
    inner = (lax.axis_index("grp") < groups - 1).astype(jnp.float32).reshape(1)
    vmem = pl.BlockSpec(memory_space=pltpu.VMEM)
    act_grads, totals = pl.pallas_call(
        functools.partial(norm_kernel, own_total, cell_total, len(parts)),
        in_specs=[vmem] * (len(parts) + 1) + [pl.BlockSpec(memory_space=pltpu.SMEM)] + [vmem] * 6,
        out_specs=[vmem] * 2,
        out_shape=[
            jax.ShapeDtypeStruct((slab_planes, channels, padded), jnp.bfloat16),
            jax.ShapeDtypeStruct((channels, 2), jnp.float32),
        ],
        compiler_params=pltpu.CompilerParams(vmem_limit_bytes=12 << 20),
        cost_estimate=pl.CostEstimate(
            flops=8 * values.size, bytes_accessed=8 * values.size, transcendentals=0
        ),
        name="act_gradient",
    )(*parts, norm_gain[:, None], inner, values, acts, grad_vals, edge_values, edge_acts, edge_grads)
    grad_gain = totals[:, 0]
    grad_shift = totals[:, 1]
    here = lax.all_to_all(act_grads, "slab", split_axis=0, concat_axis=0, tiled=True)
    here = here.reshape(width_deep, padded)
    ready, fine_now = lax.optimization_barrier((here, fine_input))
    shifted = shifted_fine(fine_now, 0)
    grad_scale = 1.0 / math.sqrt(cell_total)
    bits = place_bits()
    stages = [tuple(range(b, min(b + 2, bits))) for b in range(3, bits, 2)]
    later_taps = tap_sums(ready, shifted, depth, grad_scale)
    later_taps, fine_again = lax.optimization_barrier((later_taps, fine_input))
    later_taps = exchange(split_places(later_taps), (0, 1))
    after = from_next(here, "slab")
    shifted = shifted_fine(fine_again, fine_input.shape[0] - 1)
    first_taps = exchange_halves(*tap_halves(after, shifted, depth, grad_scale, 0), 0)
    grad_input = input_plane(0, (here,), (1,), w_down, fine_input.shape)
    first_taps, later_taps, after, grad_input = lax.optimization_barrier(
        (first_taps, later_taps, after, grad_input)
    )
    first_taps = exchange(first_taps, (1, 2))
    later_taps = exchange(later_taps, (2,))
    grad_input = input_plane(1, (here, after), (2, 0), w_down, fine_input.shape, grad_input)
    taps, grad_input = lax.optimization_barrier(
        (jnp.concatenate((first_taps, later_taps), axis=-1), grad_input)
    )
    for stage in stages:
        taps = exchange(taps, stage)
    rows = width_deep >> bits
    taps = taps.reshape(rows, 27, width_in)
    grad_down = jnp.concatenate(
        (taps[:, :9].reshape(rows, 3, 1, 3, width_in), taps[:, 9:].reshape(rows, 3, 2, 3, width_in)),
        axis=2,
    )
    grad_down = (
        grad_down.transpose(0, 2, 1, 3, 4).reshape(rows, 27, width_in).astype(jnp.float32)
    )

    return (grad_input, grad_down, grad_gain, grad_shift)


def solution(mesh):
    return jax.shard_map(
        local,
        mesh=mesh,
        in_specs=(
            P("slab", "grp", None, None),
            P("slab", "grp", None, None),
            P("slab", None, "grp"),
            P("slab", None, "grp"),
            P("slab"),
            P(),
            P(),
        ),
        out_specs=(
            P("slab", "grp", None, None),
            P(("slab", "grp"), None, None),
            P("slab"),
            P("slab"),
        ),
        check_vma=False,
    )
```

time: 214 us -> 100 us (0.47)
  waiting for transfers between devices: 106 us -> 41.8 us
  blocking collectives: 30.2 us -> 0 us
  matrix products: 24.3 us -> 0 us
  starting transfers between devices: 10.3 us -> 31.6 us
  Pallas kernels: 0 us -> 15.3 us
  between operations: 15.3 us -> 0.94 us
  local copies, waits for them, and re-layouts: 17.9 us -> 7.13 us
  other arithmetic: 9.67 us -> 2.87 us
    reduce_scatter x1 -> x0, waiting for transfers between devices: 65.3 us -> none  [local(): lax.psum_scatter(jnp.stack(rows_out, 1) * grad_scale, 'slab', scatter_dim...]
    unnamed x3 -> x0, waiting for transfers between devices: 24.9 us -> none
    dot_general x55 -> x0, matrix products: 24.3 us -> none  [the longest x27 15.2 us: local(): jnp.einsum('on,jo->nj', window((extended, shifted), offsets), w_down[tap_...]
    all_to_all x1 -> x2, waiting for transfers between devices: 7.41 us -> 27.6 us  [the longest x1 15.6 us: local(): lax.all_to_all(act_grads, 'slab', split_axis=0, concat_axis=0, tiled=True)]
    ppermute x2 -> x17, starting transfers between devices: 2.75 us -> 20.7 us  [the longest x10 14.2 us: exchange(): arrived = lax.ppermute(pick(flips), ('slab', 'grp'), pairs)]
    all_to_all x1 -> x0, blocking collectives: 17.9 us -> none  [local(): lax.all_to_all(grad_channels, 'slab', split_axis=1, concat_axis=0, tiled=...]
    pallas_call x0 -> x8, Pallas kernels: none -> 15.3 us  [the longest x2 6.14 us: input_plane(): pl.pallas_call(functools.partial(input_kernel, taps_of), grid=(1,), in_sp...]
    psum x2 -> x0, blocking collectives: 12.3 us -> none  [local(): lax.psum((first_sum, second_sum), 'grp')]
  transfers between devices with their start and end apart: 5 -> 19, of which waited for: 5 -> 10; matrix products, arithmetic and copies ran while one was open for 13% -> 5% of each run, Pallas kernels for 0% -> 10%
where the time goes in v3:
time: 100 us; the launch traced here: 99.7 us
  waiting for transfers between devices  41.8 us (42%)
  starting transfers between devices  31.6 us (32%)
  Pallas kernels  15.3 us (15%)
  local copies, waits for them, and re-layouts  7.13 us (7%)
  other arithmetic  2.87 us (3%)
    all_to_all x1, waiting for transfers between devices, local(): lax.all_to_all(act_grads, 'slab', split_axis=0, concat_axis=0, tiled=True)  15.6 us
    ppermute x10, starting transfers between devices, exchange(): arrived = lax.ppermute(pick(flips), ('slab', 'grp'), pairs)  14.2 us
    all_to_all x1, waiting for transfers between devices, local(): lax.all_to_all(deep_bf, 'slab', split_axis=0, concat_axis=0, tiled=True)  12 us
    ppermute x10, waiting for transfers between devices, exchange(): arrived = lax.ppermute(pick(flips), ('slab', 'grp'), pairs)  7.81 us
    all_to_all x1, starting transfers between devices, local(): lax.all_to_all(deep_bf, 'slab', split_axis=0, concat_axis=0, tiled=True)  7.27 us
    pallas_call x2, Pallas kernels, input_plane(): pl.pallas_call(functools.partial(input_kernel, taps_of), grid=(1,), in_sp...  6.14 us
    ppermute x3, waiting for transfers between devices, from_next(): return lax.ppermute(shard, axis, [(i, i - 1) for i in range(1, devices)])  4.87 us
    pallas_call x1, Pallas kernels, deep_gradient(): pl.pallas_call(deep_kernel, in_specs=[pl.BlockSpec(memory_space=pltpu.HBM...  4.24 us
  transfers between devices with their start and end apart: 19, of which 10 were waited for; matrix products, arithmetic and copies ran while one was open for 5% of the time, Pallas kernels for 10%

profile of v3, /device:TPU:0, one launch (start us, length us, event | category | flops | bytes accessed | tf_op | source)
XLA Modules:
  0.0 99.7 jit_solution(9103783541736754747)
XLA Ops:
  0.7 4.2 %deep_gradient.1 = bf16[256,1024]{1,0:T(8,128)(2,1)} custom-call(bf16[2,32,128,128]{3,2,1,0:T(8,128)(2,1)} %rows_ref.1, bf16[8,256,128]{2,1,0:T(8,128)(2,1)} %taps_ref.1), custom_call_target="tpu_custom_call" | custom-call | flops 536870912 | bytes 3145728 | tf_op jit(solution)/shard_map/deep_gradient/pallas_call | solution.py:144
  4.9 7.3 %all-to-all-start = ((bf16[8,32,1024]{2,1,0:T(8,128)(2,1)}), bf16[8,32,1024]{2,1,0:T(8,128)(2,1)S(1)}, u32[]{:S(2)}, u32[]{:S(2)}) async-start(bf16[8,32,1024]{2,1,0:T(8,128)(2,1)} %bitcast.52), calls=%async_computation | async-start | bytes 1048576 | tf_op jit(solution)/shard_map/all_to_all | solution.py:415
  12.9 1.3 %collective-permute-start.3 = (bf16[2,8,32,64]{3,2,1,0:T(8,128)(2,1)S(1)}, bf16[2,8,32,64]{3,2,1,0:T(8,128)(2,1)S(1)}, u32[]{:S(2)}, u32[]{:S(2)}) collective-permute-start(bf16[2,8,32,64]{3,2,1,0:T(8,128)(2,1)S(1)} %pad_maximum_fusion.1), channel_id=1, source_target_pairs={{1,0},{2,1},{3,2},{5,4},{6,5},{7,6},{9,8},{10,9},{11,10},{13,12},{... | collective-permute-start | bytes 196616 | tf_op jit(solution)/shard_map/ppermute | solution.py:24
  14.7 12.0 %all-to-all-done.refs_8_ = bf16[8,32,1024]{2,1,0:T(8,128)(2,1)S(1)} async-done(((bf16[8,32,1024]{2,1,0:T(8,128)(2,1)}), bf16[8,32,1024]{2,1,0:T(8,128)(2,1)S(1)}, u32[]{:S(2)}, u32[]{:S(2)}) %all-to-all-start) | async-done | bytes 524320 | tf_op jit(solution)/shard_map/all_to_all | solution.py:415
  27.6 1.6 %collective-permute-start.1 = (f32[32,4]{1,0:T(8,128)S(1)}, f32[32,4]{1,0:T(8,128)S(1)}, u32[]{:S(2)}, u32[]{:S(2)}) collective-permute-start(f32[32,4]{1,0:T(8,128)S(1)} %copy.42.refs_0_), channel_id=1, source_target_pairs={{0,2},{1,3},{2,0},{3,1},{4,6},{5,7},{6,4},{7,5},{8,10},{9,11},{10,... | collective-permute-start | bytes 1544 | tf_op jit(solution)/shard_map/ppermute | solution.py:30
  29.5 1.3 %collective-permute-start.4 = (bf16[8,32,64]{2,1,0:T(8,128)(2,1)S(1)}, bf16[8,32,64]{2,1,0:T(8,128)(2,1)S(1)}, u32[]{:S(2)}, u32[]{:S(2)}) collective-permute-start(bf16[8,32,64]{2,1,0:T(8,128)(2,1)S(1)} %slice.30), channel_id=1, source_target_pairs={{1,0},{2,1},{3,2},{5,4},{6,5},{7,6},{9,8},{10,9},{11,10},{13,12},{... | collective-permute-start | bytes 98312 | tf_op jit(solution)/shard_map/ppermute | solution.py:24
  32.6 1.0 %copy-done.4 = bf16[8,32,1024]{2,1,0:T(8,128)(2,1)S(1)} copy-done((bf16[8,32,1024]{2,1,0:T(8,128)(2,1)S(1)}, bf16[8,32,1024]{2,1,0:T(8,128)(2,1)}, u32[]{:S(2)}) %copy-start.4) | copy-done | bytes 524312
  35.2 3.6 %all-to-all-start.1 = ((bf16[8,32,1152]{2,1,0:T(8,128)(2,1)}), bf16[8,32,1152]{2,1,0:T(8,128)(2,1)S(1)}, u32[]{:S(2)}, u32[]{:S(2)}) async-start(bf16[8,32,1152]{2,1,0:T(8,128)(2,1)} %copy-done.5), calls=%async_computation.1 | async-start | bytes 1179648 | tf_op jit(solution)/shard_map/all_to_all | solution.py:459
  38.9 15.6 %all-to-all-done.1 = bf16[8,32,1152]{2,1,0:T(8,128)(2,1)S(1)} async-done(((bf16[8,32,1152]{2,1,0:T(8,128)(2,1)}), bf16[8,32,1152]{2,1,0:T(8,128)(2,1)S(1)}, u32[]{:S(2)}, u32[]{:S(2)}) %all-to-all-start.1) | async-done | bytes 589856 | tf_op jit(solution)/shard_map/all_to_all | solution.py:459
  54.4 1.5 %collective-permute-start.5 = (bf16[256,1152]{1,0:T(8,128)(2,1)S(1)}, bf16[256,1152]{1,0:T(8,128)(2,1)S(1)}, u32[]{:S(2)}, u32[]{:S(2)}) collective-permute-start(bf16[256,1152]{1,0:T(8,128)(2,1)S(1)} %bitcast.44), channel_id=1, source_target_pairs={{4,0},{8,4},{12,8},{16,12},{20,16},{24,20},{28,24},{5,1},{9,5},{13... | collective-permute-start | bytes 1769480 | tf_op jit(solution)/shard_map/ppermute | solution.py:24
  56.8 1.9 %tap_sums.2 = bf16[256,2304]{1,0:T(8,128)(2,1)S(1)} custom-call(s32[1]{0:T(128)} %bitcast.own_ref, bf16[256,1152]{1,0:T(8,128)(2,1)S(1)} %bitcast.45, bf16[2176,768]{1,0:T(8,128)(2,1)S(1)} %shifted_fine.2.shifted_ref), custom_call_target="tpu_custom_call" | custom-call | flops 1358954496 | bytes 7077888 | tf_op jit(solution)/shard_map/tap_sums/pallas_call | solution.py:242
  60.6 1.5 %collective-permute-start.9 = (bf16[2,2,2,1,1,8,2304]{6,5,4,3,2,1,0:T(8,128)(2,1)}, bf16[2,2,2,1,1,8,2304]{6,5,4,3,2,1,0:T(8,128)(2,1)}, u32[]{:S(2)}, u32[]{:S(2)}) collective-permute-start(bf16[2,2,2,1,1,8,2304]{6,5,4,3,2,1,0:T(8,128)(2,1)} %get-tuple-element.47), channel_id=1, source_target_pairs={{0,1},{1,0},{2,3},{3,2},{4,5},{5,4},{6,7},{7,6},{8,9},{9,8},{10,11... | collective-permute-start | bytes 884744 | tf_op jit(solution)/shard_map/ppermute | solution.py:67
  65.0 2.6 %input_gradient.2.refs_3_ = bf16[2,32,128,128]{3,2,1,0:T(8,128)(2,1)} custom-call(bf16[256,1152]{1,0:T(8,128)(2,1)S(1)} %bitcast.46, bf16[27,128,256]{2,1,0:T(8,128)(2,1)S(1)} %copy-done.1), custom_call_target="tpu_custom_call" | custom-call | tf_op jit(solution)/shard_map/input_gradient/pallas_call | solution.py:330
  67.6 4.6 %collective-permute-done.5.grads_ref.refs_1_ = bf16[256,1152]{1,0:T(8,128)(2,1)S(1)} collective-permute-done((bf16[256,1152]{1,0:T(8,128)(2,1)S(1)}, bf16[256,1152]{1,0:T(8,128)(2,1)S(1)}, u32[]{:S(2)}, u32[]{:S(2)}) %collective-permute-start.5) | collective-permute-done | bytes 589856 | tf_op jit(solution)/shard_map/ppermute | solution.py:24
  72.2 1.0 %tap_sums.3 = (bf16[128,1152]{1,0:T(8,128)(2,1)S(1)}, bf16[128,1152]{1,0:T(8,128)(2,1)S(1)}) custom-call(s32[1]{0:T(128)} %bitcast.own_ref, bf16[256,1152]{1,0:T(8,128)(2,1)S(1)} %collective-permute-done.5.grads_ref.refs_1_, bf16[2176,384]{1,0:T(8,128)(2,1)S(1)} %shifted_fine.3.shifted_ref), custom_call_target="tpu_custom_call" | custom-call | flops 679477248 | bytes 3833856 | tf_op jit(solution)/shard_map/tap_sums/pallas_call | solution.py:242
  74.0 2.8 %collective-permute-done.7 = bf16[2,2,2,1,1,8,2304]{6,5,4,3,2,1,0:T(8,128)(2,1)} collective-permute-done((bf16[2,2,2,1,1,8,2304]{6,5,4,3,2,1,0:T(8,128)(2,1)}, bf16[2,2,2,1,1,8,2304]{6,5,4,3,2,1,0:T(8,128)(2,1)}, u32[]{:S(2)}, u32[]{:S(2)}) %collective-permute-start.7) | collective-permute-done | bytes 294944 | tf_op jit(solution)/shard_map/ppermute | solution.py:67
  76.8 1.4 %add_convert_fusion = bf16[2,2,2,1,1,8,2304]{6,5,4,3,2,1,0:T(8,128)(2,1)S(1)} fusion(bf16[2,2,2,1,1,8,2304]{6,5,4,3,2,1,0:T(8,128)(2,1)} %collective-permute-done.9, bf16[2,2,2,1,1,8,2304]{6,5,4,3,2,1,0:T(8,128)(2,1)} %collective-permute-done.8, bf16[2,2,2,1,1,8,2304]{6,5,4,3,2,1,0:T(8,128)(2,1)} %collective-permute-done.7, ...), kind=kLoop, calls=%fused_computation.11 | loop fusion | flops 1179648 | bytes 1474568 | tf_op jit(solution)/shard_map/convert_element_type | solution.py:69
  78.3 1.9 %collective-permute-start.12 = (bf16[2,2,1,1,1,8,1152]{6,5,3,2,1,0,4:T(8,128)(2,1)S(1)}, bf16[2,2,1,1,1,8,1152]{6,5,3,2,1,0,4:T(8,128)(2,1)S(1)}, u32[]{:S(2)}, u32[]{:S(2)}) collective-permute-start(bf16[2,2,1,1,1,8,1152]{6,5,3,2,1,0,4:T(8,128)(2,1)S(1)} %get-tuple-element.50), channel_id=1, source_target_pairs={{0,2},{1,3},{2,0},{3,1},{4,6},{5,7},{6,4},{7,5},{8,10},{9,11},{10,... | collective-permute-start | bytes 221192 | tf_op jit(solution)/shard_map/ppermute | solution.py:67
  80.2 2.6 %collective-permute-start.11 = (bf16[2,2,1,1,1,8,1152]{6,5,3,2,1,0,4:T(8,128)(2,1)S(1)}, bf16[2,2,1,1,1,8,1152]{6,5,3,2,1,0,4:T(8,128)(2,1)S(1)}, u32[]{:S(2)}, u32[]{:S(2)}) collective-permute-start(bf16[2,2,1,1,1,8,1152]{6,5,3,2,1,0,4:T(8,128)(2,1)S(1)} %get-tuple-element.51), channel_id=1, source_target_pairs={{0,4},{1,5},{2,6},{3,7},{4,0},{5,1},{6,2},{7,3},{8,12},{9,13},{10,... | collective-permute-start | bytes 221192 | tf_op jit(solution)/shard_map/ppermute | solution.py:67
  82.8 1.6 %collective-permute-start.13 = (bf16[2,2,1,1,1,8,2304]{6,5,4,3,2,1,0:T(8,128)(2,1)S(1)}, bf16[2,2,1,1,1,8,2304]{6,5,4,3,2,1,0:T(8,128)(2,1)S(1)}, u32[]{:S(2)}, u32[]{:S(2)}) collective-permute-start(bf16[2,2,1,1,1,8,2304]{6,5,4,3,2,1,0:T(8,128)(2,1)S(1)} %constant_dynamic-slice_fusion.3), channel_id=1, source_target_pairs={{0,4},{1,5},{2,6},{3,7},{4,0},{5,1},{6,2},{7,3},{8,12},{9,13},{10,... | collective-permute-start | bytes 442376 | tf_op jit(solution)/shard_map/ppermute | solution.py:67
  84.5 3.5 %input_gradient.3 = bf16[2,32,128,128]{3,2,1,0:T(8,128)(2,1)} custom-call(bf16[256,1152]{1,0:T(8,128)(2,1)S(1)} %bitcast.47, bf16[256,1152]{1,0:T(8,128)(2,1)S(1)} %collective-permute-done.5.grads_ref.refs_1_, bf16[27,128,256]{2,1,0:T(8,128)(2,1)S(1)} %copy-done.1, bf16[2,32,128,128]{3,2,1,0:T(8,128)(2,1)} %input_gradient.2.refs_3_), custom_call_target="tpu_custom_call", output_to_operand_aliasing={{}: (3, {})} | custom-call | tf_op jit(solution)/shard_map/input_gradient/pallas_call | solution.py:330
  90.0 2.7 %collective-permute-start.16 = (bf16[1,1,1,1,1,8,3456]{6,5,4,3,2,1,0:T(8,128)(2,1)S(1)}, bf16[1,1,1,1,1,8,3456]{6,5,4,3,2,1,0:T(8,128)(2,1)S(1)}, u32[]{:S(2)}, u32[]{:S(2)}) collective-permute-start(bf16[1,1,1,1,1,8,3456]{6,5,4,3,2,1,0:T(8,128)(2,1)S(1)} %get-tuple-element.53), channel_id=1, source_target_pairs={{0,8},{1,9},{2,10},{3,11},{4,12},{5,13},{6,14},{7,15},{8,0},{9,1},... | collective-permute-start | bytes 165896 | tf_op jit(solution)/shard_map/ppermute | solution.py:67
  92.7 2.4 %collective-permute-start.14 = (bf16[1,1,1,1,1,8,3456]{6,5,4,3,2,1,0:T(8,128)(2,1)S(1)}, bf16[1,1,1,1,1,8,3456]{6,5,4,3,2,1,0:T(8,128)(2,1)S(1)}, u32[]{:S(2)}, u32[]{:S(2)}) collective-permute-start(bf16[1,1,1,1,1,8,3456]{6,5,4,3,2,1,0:T(8,128)(2,1)S(1)} %get-tuple-element.52), channel_id=1, source_target_pairs={{0,24},{1,25},{2,26},{3,27},{4,28},{5,29},{6,30},{7,31},{8,16},{9,... | collective-permute-start | bytes 165896 | tf_op jit(solution)/shard_map/ppermute | solution.py:67
  95.8 3.1 %collective-permute-done.15 = bf16[1,1,1,1,1,8,3456]{6,5,4,3,2,1,0:T(8,128)(2,1)S(1)} collective-permute-done((bf16[1,1,1,1,1,8,3456]{6,5,4,3,2,1,0:T(8,128)(2,1)S(1)}, bf16[1,1,1,1,1,8,3456]{6,5,4,3,2,1,0:T(8,128)(2,1)S(1)}, u32[]{:S(2)}, u32[]{:S(2)}) %collective-permute-start.15) | collective-permute-done | bytes 55328 | tf_op jit(solution)/shard_map/ppermute | solution.py:67
  (67 shorter events, 15.6 us)
Async XLA Ops:
  0.6 11.5 %copy-start.6 = (bf16[32,8,1024]{2,1,0:T(8,128)(2,1)S(1)}, bf16[32,8,1024]{2,1,0:T(8,128)(2,1)}, u32[]{:S(2)}) copy-start(bf16[32,8,1024]{2,1,0:T(8,128)(2,1)} %param.9) | copy-start | bytes 1572868
  0.6 11.5 %copy-start.7 = (bf16[32,8,1024]{2,1,0:T(8,128)(2,1)S(1)}, bf16[32,8,1024]{2,1,0:T(8,128)(2,1)}, u32[]{:S(2)}) copy-start(bf16[32,8,1024]{2,1,0:T(8,128)(2,1)} %param.10) | copy-start | bytes 1572868
  4.9 9.3 %copy-start.8 = (f32[32]{0:T(128)S(1)}, f32[32]{0:T(128)}, u32[]{:S(2)}) copy-start(f32[32]{0:T(128)} %param.11) | copy-start | bytes 388
  4.9 21.8 %all-to-all-start = ((bf16[8,32,1024]{2,1,0:T(8,128)(2,1)}), bf16[8,32,1024]{2,1,0:T(8,128)(2,1)S(1)}, u32[]{:S(2)}, u32[]{:S(2)}) async-start(bf16[8,32,1024]{2,1,0:T(8,128)(2,1)} %bitcast.52), calls=%async_computation | async-start | bytes 1048576 | tf_op jit(solution)/shard_map/all_to_all | solution.py:415
  12.8 13.9 %copy-start.3 = (bf16[8,32,1024]{2,1,0:T(8,128)(2,1)}, bf16[8,32,1024]{2,1,0:T(8,128)(2,1)S(1)}, u32[]{:S(2)}) copy-start(bf16[8,32,1024]{2,1,0:T(8,128)(2,1)S(1)} %get-tuple-element.60.refs_6_) | copy-start | bytes 1572868
  12.9 17.9 %collective-permute-start.3 = (bf16[2,8,32,64]{3,2,1,0:T(8,128)(2,1)S(1)}, bf16[2,8,32,64]{3,2,1,0:T(8,128)(2,1)S(1)}, u32[]{:S(2)}, u32[]{:S(2)}) collective-permute-start(bf16[2,8,32,64]{3,2,1,0:T(8,128)(2,1)S(1)} %pad_maximum_fusion.1), channel_id=1, source_target_pairs={{1,0},{2,1},{3,2},{5,4},{6,5},{7,6},{9,8},{10,9},{11,10},{13,12},{... | collective-permute-start | bytes 196616 | tf_op jit(solution)/shard_map/ppermute | solution.py:24
  27.5 28.4 %copy-start = (bf16[2,32,128,128]{3,2,1,0:T(8,128)(2,1)S(1)}, bf16[2,32,128,128]{3,2,1,0:T(8,128)(2,1)}, u32[]{:S(2)}) copy-start(bf16[2,32,128,128]{3,2,1,0:T(8,128)(2,1)} %fine_ref.1) | copy-start | bytes 6291460
  27.6 3.2 %collective-permute-start = (f32[32,4]{1,0:T(8,128)S(1)}, f32[32,4]{1,0:T(8,128)S(1)}, u32[]{:S(2)}, u32[]{:S(2)}) collective-permute-start(f32[32,4]{1,0:T(8,128)S(1)} %copy.42.refs_0_), channel_id=1, source_target_pairs={{0,1},{1,0},{2,3},{3,2},{4,5},{5,4},{6,7},{7,6},{8,9},{9,8},{10,11... | collective-permute-start | bytes 1544 | tf_op jit(solution)/shard_map/ppermute | solution.py:30
  27.6 3.8 %collective-permute-start.1 = (f32[32,4]{1,0:T(8,128)S(1)}, f32[32,4]{1,0:T(8,128)S(1)}, u32[]{:S(2)}, u32[]{:S(2)}) collective-permute-start(f32[32,4]{1,0:T(8,128)S(1)} %copy.42.refs_0_), channel_id=1, source_target_pairs={{0,2},{1,3},{2,0},{3,1},{4,6},{5,7},{6,4},{7,5},{8,10},{9,11},{10,... | collective-permute-start | bytes 1544 | tf_op jit(solution)/shard_map/ppermute | solution.py:30
  29.2 3.2 %collective-permute-start.2 = (f32[32,4]{1,0:T(8,128)S(1)}, f32[32,4]{1,0:T(8,128)S(1)}, u32[]{:S(2)}, u32[]{:S(2)}) collective-permute-start(f32[32,4]{1,0:T(8,128)S(1)} %copy.42.refs_0_), channel_id=1, source_target_pairs={{0,3},{1,2},{2,1},{3,0},{4,7},{5,6},{6,5},{7,4},{8,11},{9,10},{10,... | collective-permute-start | bytes 1544 | tf_op jit(solution)/shard_map/ppermute | solution.py:30
  29.5 3.1 %collective-permute-start.4 = (bf16[8,32,64]{2,1,0:T(8,128)(2,1)S(1)}, bf16[8,32,64]{2,1,0:T(8,128)(2,1)S(1)}, u32[]{:S(2)}, u32[]{:S(2)}) collective-permute-start(bf16[8,32,64]{2,1,0:T(8,128)(2,1)S(1)} %slice.30), channel_id=1, source_target_pairs={{1,0},{2,1},{3,2},{5,4},{6,5},{7,6},{9,8},{10,9},{11,10},{13,12},{... | collective-permute-start | bytes 98312 | tf_op jit(solution)/shard_map/ppermute | solution.py:24
  35.2 19.2 %all-to-all-start.1 = ((bf16[8,32,1152]{2,1,0:T(8,128)(2,1)}), bf16[8,32,1152]{2,1,0:T(8,128)(2,1)S(1)}, u32[]{:S(2)}, u32[]{:S(2)}) async-start(bf16[8,32,1152]{2,1,0:T(8,128)(2,1)} %copy-done.5), calls=%async_computation.1 | async-start | bytes 1179648 | tf_op jit(solution)/shard_map/all_to_all | solution.py:459
  54.4 17.8 %collective-permute-start.5 = (bf16[256,1152]{1,0:T(8,128)(2,1)S(1)}, bf16[256,1152]{1,0:T(8,128)(2,1)S(1)}, u32[]{:S(2)}, u32[]{:S(2)}) collective-permute-start(bf16[256,1152]{1,0:T(8,128)(2,1)S(1)} %bitcast.44), channel_id=1, source_target_pairs={{4,0},{8,4},{12,8},{16,12},{20,16},{24,20},{28,24},{5,1},{9,5},{13... | collective-permute-start | bytes 1769480 | tf_op jit(solution)/shard_map/ppermute | solution.py:24
  60.6 13.3 %collective-permute-start.9 = (bf16[2,2,2,1,1,8,2304]{6,5,4,3,2,1,0:T(8,128)(2,1)}, bf16[2,2,2,1,1,8,2304]{6,5,4,3,2,1,0:T(8,128)(2,1)}, u32[]{:S(2)}, u32[]{:S(2)}) collective-permute-start(bf16[2,2,2,1,1,8,2304]{6,5,4,3,2,1,0:T(8,128)(2,1)} %get-tuple-element.47), channel_id=1, source_target_pairs={{0,1},{1,0},{2,3},{3,2},{4,5},{5,4},{6,7},{7,6},{8,9},{9,8},{10,11... | collective-permute-start | bytes 884744 | tf_op jit(solution)/shard_map/ppermute | solution.py:67
  62.2 11.8 %collective-permute-start.8 = (bf16[2,2,2,1,1,8,2304]{6,5,4,3,2,1,0:T(8,128)(2,1)}, bf16[2,2,2,1,1,8,2304]{6,5,4,3,2,1,0:T(8,128)(2,1)}, u32[]{:S(2)}, u32[]{:S(2)}) collective-permute-start(bf16[2,2,2,1,1,8,2304]{6,5,4,3,2,1,0:T(8,128)(2,1)} %get-tuple-element.48), channel_id=1, source_target_pairs={{0,2},{1,3},{2,0},{3,1},{4,6},{5,7},{6,4},{7,5},{8,10},{9,11},{10,... | collective-permute-start | bytes 884744 | tf_op jit(solution)/shard_map/ppermute | solution.py:67
  62.9 13.8 %collective-permute-start.7 = (bf16[2,2,2,1,1,8,2304]{6,5,4,3,2,1,0:T(8,128)(2,1)}, bf16[2,2,2,1,1,8,2304]{6,5,4,3,2,1,0:T(8,128)(2,1)}, u32[]{:S(2)}, u32[]{:S(2)}) collective-permute-start(bf16[2,2,2,1,1,8,2304]{6,5,4,3,2,1,0:T(8,128)(2,1)} %get-tuple-element.46), channel_id=1, source_target_pairs={{0,3},{1,2},{2,1},{3,0},{4,7},{5,6},{6,5},{7,4},{8,11},{9,10},{10,... | collective-permute-start | bytes 884744 | tf_op jit(solution)/shard_map/ppermute | solution.py:67
  73.3 4.9 %collective-permute-start.6 = (bf16[2,2,2,2,1,8,1152]{6,5,3,2,1,0,4:T(8,128)(2,1)S(1)}, bf16[2,2,2,2,1,8,1152]{6,5,3,2,1,0,4:T(8,128)(2,1)S(1)}, u32[]{:S(2)}, u32[]{:S(2)}) collective-permute-start(bf16[2,2,2,2,1,8,1152]{6,5,3,2,1,0,4:T(8,128)(2,1)S(1)} %bitcast.51), channel_id=1, source_target_pairs={{0,1},{1,0},{2,3},{3,2},{4,5},{5,4},{6,7},{7,6},{8,9},{9,8},{10,11... | collective-permute-start | bytes 884744 | tf_op jit(solution)/shard_map/ppermute | solution.py:84
  78.3 9.7 %collective-permute-start.12 = (bf16[2,2,1,1,1,8,1152]{6,5,3,2,1,0,4:T(8,128)(2,1)S(1)}, bf16[2,2,1,1,1,8,1152]{6,5,3,2,1,0,4:T(8,128)(2,1)S(1)}, u32[]{:S(2)}, u32[]{:S(2)}) collective-permute-start(bf16[2,2,1,1,1,8,1152]{6,5,3,2,1,0,4:T(8,128)(2,1)S(1)} %get-tuple-element.50), channel_id=1, source_target_pairs={{0,2},{1,3},{2,0},{3,1},{4,6},{5,7},{6,4},{7,5},{8,10},{9,11},{10,... | collective-permute-start | bytes 221192 | tf_op jit(solution)/shard_map/ppermute | solution.py:67
  80.2 7.8 %collective-permute-start.11 = (bf16[2,2,1,1,1,8,1152]{6,5,3,2,1,0,4:T(8,128)(2,1)S(1)}, bf16[2,2,1,1,1,8,1152]{6,5,3,2,1,0,4:T(8,128)(2,1)S(1)}, u32[]{:S(2)}, u32[]{:S(2)}) collective-permute-start(bf16[2,2,1,1,1,8,1152]{6,5,3,2,1,0,4:T(8,128)(2,1)S(1)} %get-tuple-element.51), channel_id=1, source_target_pairs={{0,4},{1,5},{2,6},{3,7},{4,0},{5,1},{6,2},{7,3},{8,12},{9,13},{10,... | collective-permute-start | bytes 221192 | tf_op jit(solution)/shard_map/ppermute | solution.py:67
  82.8 6.1 %collective-permute-start.10 = (bf16[2,2,1,1,1,8,1152]{6,5,3,2,1,0,4:T(8,128)(2,1)S(1)}, bf16[2,2,1,1,1,8,1152]{6,5,3,2,1,0,4:T(8,128)(2,1)S(1)}, u32[]{:S(2)}, u32[]{:S(2)}) collective-permute-start(bf16[2,2,1,1,1,8,1152]{6,5,3,2,1,0,4:T(8,128)(2,1)S(1)} %get-tuple-element.49), channel_id=1, source_target_pairs={{0,6},{1,7},{2,4},{3,5},{4,2},{5,3},{6,0},{7,1},{8,14},{9,15},{10,... | collective-permute-start | bytes 221192 | tf_op jit(solution)/shard_map/ppermute | solution.py:67
  82.8 7.1 %collective-permute-start.13 = (bf16[2,2,1,1,1,8,2304]{6,5,4,3,2,1,0:T(8,128)(2,1)S(1)}, bf16[2,2,1,1,1,8,2304]{6,5,4,3,2,1,0:T(8,128)(2,1)S(1)}, u32[]{:S(2)}, u32[]{:S(2)}) collective-permute-start(bf16[2,2,1,1,1,8,2304]{6,5,4,3,2,1,0:T(8,128)(2,1)S(1)} %constant_dynamic-slice_fusion.3), channel_id=1, source_target_pairs={{0,4},{1,5},{2,6},{3,7},{4,0},{5,1},{6,2},{7,3},{8,12},{9,13},{10,... | collective-permute-start | bytes 442376 | tf_op jit(solution)/shard_map/ppermute | solution.py:67
  90.0 5.8 %collective-permute-start.16 = (bf16[1,1,1,1,1,8,3456]{6,5,4,3,2,1,0:T(8,128)(2,1)S(1)}, bf16[1,1,1,1,1,8,3456]{6,5,4,3,2,1,0:T(8,128)(2,1)S(1)}, u32[]{:S(2)}, u32[]{:S(2)}) collective-permute-start(bf16[1,1,1,1,1,8,3456]{6,5,4,3,2,1,0:T(8,128)(2,1)S(1)} %get-tuple-element.53), channel_id=1, source_target_pairs={{0,8},{1,9},{2,10},{3,11},{4,12},{5,13},{6,14},{7,15},{8,0},{9,1},... | collective-permute-start | bytes 165896 | tf_op jit(solution)/shard_map/ppermute | solution.py:67
  92.7 6.2 %collective-permute-start.15 = (bf16[1,1,1,1,1,8,3456]{6,5,4,3,2,1,0:T(8,128)(2,1)S(1)}, bf16[1,1,1,1,1,8,3456]{6,5,4,3,2,1,0:T(8,128)(2,1)S(1)}, u32[]{:S(2)}, u32[]{:S(2)}) collective-permute-start(bf16[1,1,1,1,1,8,3456]{6,5,4,3,2,1,0:T(8,128)(2,1)S(1)} %get-tuple-element.54), channel_id=1, source_target_pairs={{0,16},{1,17},{2,18},{3,19},{4,20},{5,21},{6,22},{7,23},{8,24},{9,... | collective-permute-start | bytes 165896 | tf_op jit(solution)/shard_map/ppermute | solution.py:67
  92.7 6.2 %collective-permute-start.14 = (bf16[1,1,1,1,1,8,3456]{6,5,4,3,2,1,0:T(8,128)(2,1)S(1)}, bf16[1,1,1,1,1,8,3456]{6,5,4,3,2,1,0:T(8,128)(2,1)S(1)}, u32[]{:S(2)}, u32[]{:S(2)}) collective-permute-start(bf16[1,1,1,1,1,8,3456]{6,5,4,3,2,1,0:T(8,128)(2,1)S(1)} %get-tuple-element.52), channel_id=1, source_target_pairs={{0,24},{1,25},{2,26},{3,27},{4,28},{5,29},{6,30},{7,31},{8,16},{9,... | collective-permute-start | bytes 165896 | tf_op jit(solution)/shard_map/ppermute | solution.py:67
  (4 other events, 4.4 us)

commit v4 on v3

--- a/solution.py
+++ b/solution.py
@@ -40,11 +40,6 @@
 
 def place_bits():
     return (lax.axis_size("slab") * lax.axis_size("grp")).bit_length() - 1
-
-
-def split_places(partial):
-    bits = place_bits()
-    return partial.reshape((2,) * bits + (partial.shape[0] >> bits, partial.shape[1]))
 
 
 def exchange(held, stage):
@@ -69,20 +64,16 @@
     return total.astype(jnp.bfloat16)
 
 
-def halves(partial, bit):
-    place = lax.axis_index("slab") * lax.axis_size("grp") + lax.axis_index("grp")
-    held = split_places(partial)
-    dim = place_bits() - 1 - bit
-    own = place >> bit & 1
-    return tuple(lax.dynamic_slice_in_dim(held, own ^ flip, 1, dim) for flip in range(2))
-
-
-def exchange_halves(kept, sent, bit):
+def exchange_parts(parts, bits):
     slabs = lax.axis_size("slab")
     groups = lax.axis_size("grp")
-    pairs = bit_pairs(slabs, groups, (1 << bit) // groups, (1 << bit) % groups)
-    arrived = lax.ppermute(sent, ("slab", "grp"), pairs)
-    return (kept.astype(jnp.float32) + arrived.astype(jnp.float32)).astype(jnp.bfloat16)
+    rows = parts[0].shape[0] >> (place_bits() - bits)
+    total = parts[0].astype(jnp.float32)
+    for mask, part in reversed(list(enumerate(parts[1:], 1))):
+        pairs = bit_pairs(slabs, groups, mask // groups, mask % groups)
+        total = total + lax.ppermute(part, ("slab", "grp"), pairs).astype(jnp.float32)
+    dims = (2,) * (place_bits() - bits) + (1,) * bits
+    return total.astype(jnp.bfloat16).reshape(*dims, rows, total.shape[1])
 
 
 def deep_kernel(rows_ref, taps_ref, out_ref, rows, taps, wide, cells, row_sems, tap_sem):
@@ -193,7 +184,7 @@
     planes, fine_rows, fine_depth, width = fine_input.shape
     planes -= first
     depth = fine_depth // 2
-    shape = (fine_rows * depth + 2 * depth, planes * 3 * width)
+    shape = shifted_shape(fine_input, planes)
     return pl.pallas_call(
         shifted_kernel,
         grid=(1,),
@@ -209,65 +200,91 @@
     )(fine_input)
 
 
-def tap_kernel(scale, depth, block, own_ref, grads_ref, shifted_ref, kept_ref, sent_ref=None):
+def tap_kernel(scale, depth, rows, jobs, own_ref, grads_ref, shifted_ref, *out_refs):
     cells = (shifted_ref.shape[0] - 2 * depth) // 2
     width = 3 * LANES
-    planes = shifted_ref.shape[1] // width
-    own = own_ref[0] > 0
-    for ky, start in ((1, 0), (0, cells), (2, cells + depth)):
-        count = grads_ref.shape[1] if ky == 0 else cells
-        grads = grads_ref[:, :count]
-        for px in range(planes):
+    for px, bits in jobs:
+        count = 1 << bits if rows else 1
+        outs, out_refs = out_refs[:count], out_refs[count:]
+        for ky, start in ((1, 0), (0, cells), (2, cells + depth)):
+            span = grads_ref.shape[1] if ky == 0 else cells
             sums = scale * jnp.dot(
-                grads,
-                shifted_ref[start : start + count, px * width : (px + 1) * width],
+                grads_ref[:, :span],
+                shifted_ref[start : start + span, px * width : (px + 1) * width],
                 preferred_element_type=jnp.float32,
             )
-            first = (ky * planes + px) * width
-            columns = slice(first, first + width)
-            if not block:
-                kept_ref[:, columns] = sums.astype(jnp.bfloat16)
-                continue
-            pairs = sums.reshape(sums.shape[0] // (2 * block), 2, block, width)
-            low, high = (pairs[:, n].reshape(sums.shape[0] // 2, width) for n in range(2))
-            kept_ref[:, columns] = jnp.where(own, high, low).astype(jnp.bfloat16)
-            sent_ref[:, columns] = jnp.where(own, low, high).astype(jnp.bfloat16)
-
-
-def tap_call(grads, shifted, depth, scale, bit, block):
+            parts = [sums]
+            if rows:
+                sums = sums.reshape(-1, count, rows, width)
+                parts = [sums[:, n].reshape(-1, width) for n in range(count)]
+                for bit in range(bits):
+                    own = (own_ref[0] >> bit & 1) > 0
+                    parts = [
+                        jnp.where(own, parts[n ^ (1 << bit)], part) for n, part in enumerate(parts)
+                    ]
+            for out_ref, part in zip(outs, parts):
+                out_ref[:, ky * width : (ky + 1) * width] = part.astype(jnp.bfloat16)
+
+
+def shift_and_tap_kernel(scale, depth, rows, jobs, own_ref, grads_ref, fine_ref, *refs):
+    *out_refs, shifted, wide = refs
+    shifted_kernel(fine_ref, shifted, wide)
+    tap_kernel(scale, depth, rows, jobs, own_ref, grads_ref, shifted, *out_refs)
+
+
+def shifted_shape(fine_input, planes):
+    _, fine_rows, fine_depth, width = fine_input.shape
+    return ((fine_rows + 2) * (fine_depth // 2), planes * 3 * width)
+
+
+def tap_sums(grads, source, depth, scale, jobs):
     width_deep, padded = grads.shape
-    columns = 3 * shifted.shape[1]
+    scratch = []
+    kernel = tap_kernel
+    if source.ndim == 4:
+        kernel = shift_and_tap_kernel
+        planes, _, fine_depth, width = source.shape
+        scratch = [
+            pltpu.VMEM(shifted_shape(source, planes), jnp.bfloat16),
+            pltpu.VMEM((2 * planes, fine_depth + 8, width), jnp.float32),
+        ]
+    columns = 9 * LANES
+    rows = width_deep >> place_bits()
     place = lax.axis_index("slab") * lax.axis_size("grp") + lax.axis_index("grp")
-    outs = 2 if block else 1
-    return pl.pallas_call(
-        functools.partial(tap_kernel, scale, depth, block),
+    inside = rows % 8 == 0
+    counts = [1 << bits if inside else 1 for _, bits in jobs]
+    outs = [
+        jax.ShapeDtypeStruct((width_deep // count, columns), jnp.bfloat16)
+        for count in counts
+        for _ in range(count)
+    ]
+    arrays = pl.pallas_call(
+        functools.partial(kernel, scale, depth, rows if inside else 0, jobs),
         in_specs=[pl.BlockSpec(memory_space=pltpu.SMEM)]
         + [pl.BlockSpec(memory_space=pltpu.VMEM)] * 2,
-        out_specs=[pl.BlockSpec(memory_space=pltpu.VMEM)] * outs,
-        out_shape=[jax.ShapeDtypeStruct((width_deep // outs, columns), jnp.bfloat16)] * outs,
-        compiler_params=pltpu.CompilerParams(vmem_limit_bytes=12 << 20),
+        out_specs=[pl.BlockSpec(memory_space=pltpu.VMEM)] * len(outs),
+        out_shape=outs,
+        scratch_shapes=scratch,
+        compiler_params=pltpu.CompilerParams(vmem_limit_bytes=20 << 20),
         cost_estimate=pl.CostEstimate(
-            flops=2 * width_deep * padded * columns,
-            bytes_accessed=2 * (grads.size + padded * columns + width_deep * columns),
+            flops=2 * width_deep * padded * columns * len(jobs),
+            bytes_accessed=2 * (grads.size + (padded + width_deep) * columns * len(jobs)),
             transcendentals=0,
         ),
         name="tap_sums",
-    )((place >> bit & 1).astype(jnp.int32).reshape(1), grads, shifted)
-
-
-def tap_sums(grads, shifted, depth, scale):
-    return tap_call(grads, shifted, depth, scale, 0, 0)[0]
-
-
-def tap_halves(grads, shifted, depth, scale, bit):
-    bits = place_bits()
-    rows = grads.shape[0] >> bits
-    if (rows << bit) % 8:
-        return halves(tap_sums(grads, shifted, depth, scale), bit)
-    dims = [2] * bits
-    dims[bits - 1 - bit] = 1
-    arrays = tap_call(grads, shifted, depth, scale, bit, rows << bit)
-    return tuple(array.reshape(*dims, rows, array.shape[1]) for array in arrays)
+    )(place.astype(jnp.int32).reshape(1), grads, source)
+    results = []
+    for (_, bits), count in zip(jobs, counts):
+        parts, arrays = tuple(arrays[:count]), arrays[count:]
+        if not inside:
+            held = parts[0].reshape(-1, 1 << bits, rows, columns)
+            own = place & ((1 << bits) - 1)
+            parts = tuple(
+                lax.dynamic_index_in_dim(held, own ^ n, 1, False).reshape(-1, columns)
+                for n in range(1 << bits)
+            )
+        results.append(parts)
+    return results
 
 
 def input_kernel(taps_of, *refs):
@@ -357,8 +374,8 @@
 
 def norm_kernel(own_total, cell_total, parts, *refs):
     part_refs, refs = refs[:parts], refs[parts:]
-    (gain_ref, edge_ref, values_ref, acts_ref, grads_ref, edge_values_ref, edge_acts_ref, edge_grads_ref) = refs[:8]
-    out_ref, totals_ref = refs[8:]
+    gain_ref, edge_ref, values_ref, masked_ref, edge_values_ref, edge_masked_ref = refs[:6]
+    out_ref, totals_ref = refs[6:]
     planes, channels, cells = values_ref.shape
     depth = edge_values_ref.shape[2]
 
@@ -381,18 +398,13 @@
     gain = gain_ref[...] * inv_std
     edge_gain = gain * edge_ref[0]
 
-    def grad_of(values, acts, grads, gain):
+    def grad_of(values, masked, gain):
         normed = (values.astype(jnp.float32) - mean) * inv_std
-        masked = jnp.where(acts.astype(jnp.float32) > 0, grads.astype(jnp.float32), 0.0)
-        return (gain * (masked - shift - normed * slope)).astype(jnp.bfloat16)
+        return (gain * (masked.astype(jnp.float32) - shift - normed * slope)).astype(jnp.bfloat16)
 
     for plane in range(planes):
-        out_ref[plane, :, 0:cells] = grad_of(
-            values_ref[plane], acts_ref[plane], grads_ref[plane], gain
-        )
-        edge = grad_of(
-            edge_values_ref[plane], edge_acts_ref[plane], edge_grads_ref[plane], edge_gain
-        )
+        out_ref[plane, :, 0:cells] = grad_of(values_ref[plane], masked_ref[plane], gain)
+        edge = grad_of(edge_values_ref[plane], edge_masked_ref[plane], edge_gain)
         spare = jnp.zeros((channels, out_ref.shape[2] - cells - depth), jnp.bfloat16)
         out_ref[plane, :, cells:] = jnp.concatenate((edge, spare), axis=1)
 
@@ -416,6 +428,7 @@
 
     values = pre_norm.transpose(1, 0, 2)
     acts = act_out.transpose(1, 0, 2)
+    values, acts = lax.optimization_barrier((values, acts))
     edge_values, edge_acts = from_next(jnp.stack((values[:, :, :depth], acts[:, :, :depth])), "grp")
     edge_grads = from_next(grad_vals[:, :, :depth], "grp")
 
@@ -425,7 +438,11 @@
 
     own_total = slab_planes * cells
     own_mean, own_inv = own_moments(first_sum, second_sum, own_total)
-    masked = jnp.where(acts > 0, grad_vals, jnp.zeros_like(grad_vals)).astype(jnp.float32)
+    def masked_of(grads, acts):
+        return jnp.where(acts > 0, grads, jnp.zeros_like(grads))
+
+    masked_bf = masked_of(grad_vals, acts)
+    masked = masked_bf.astype(jnp.float32)
     own_normed = (wide_values - own_mean[None, :, None]) * own_inv[None, :, None]
     parts = grp_parts(
         jnp.stack(
@@ -442,7 +459,7 @@
     vmem = pl.BlockSpec(memory_space=pltpu.VMEM)
     act_grads, totals = pl.pallas_call(
         functools.partial(norm_kernel, own_total, cell_total, len(parts)),
-        in_specs=[vmem] * (len(parts) + 1) + [pl.BlockSpec(memory_space=pltpu.SMEM)] + [vmem] * 6,
+        in_specs=[vmem] * (len(parts) + 1) + [pl.BlockSpec(memory_space=pltpu.SMEM)] + [vmem] * 4,
         out_specs=[vmem] * 2,
         out_shape=[
             jax.ShapeDtypeStruct((slab_planes, channels, padded), jnp.bfloat16),
@@ -453,44 +470,40 @@
             flops=8 * values.size, bytes_accessed=8 * values.size, transcendentals=0
         ),
         name="act_gradient",
-    )(*parts, norm_gain[:, None], inner, values, acts, grad_vals, edge_values, edge_acts, edge_grads)
+    )(*parts, norm_gain[:, None], inner, values, masked_bf, edge_values, masked_of(edge_grads, edge_acts))
     grad_gain = totals[:, 0]
     grad_shift = totals[:, 1]
     here = lax.all_to_all(act_grads, "slab", split_axis=0, concat_axis=0, tiled=True)
     here = here.reshape(width_deep, padded)
-    ready, fine_now = lax.optimization_barrier((here, fine_input))
-    shifted = shifted_fine(fine_now, 0)
     grad_scale = 1.0 / math.sqrt(cell_total)
     bits = place_bits()
     stages = [tuple(range(b, min(b + 2, bits))) for b in range(3, bits, 2)]
-    later_taps = tap_sums(ready, shifted, depth, grad_scale)
-    later_taps, fine_again = lax.optimization_barrier((later_taps, fine_input))
-    later_taps = exchange(split_places(later_taps), (0, 1))
+    parts = tap_sums(here, fine_input, depth, grad_scale, ((0, 2), (1, 1)))
+    parts, here_again = lax.optimization_barrier((parts, here))
+    middle_parts, last_parts = parts
     after = from_next(here, "slab")
+    grad_input = input_plane(0, (here_again,), (1,), w_down, fine_input.shape)
+    grad_input, fine_again = lax.optimization_barrier((grad_input, fine_input))
     shifted = shifted_fine(fine_again, fine_input.shape[0] - 1)
-    first_taps = exchange_halves(*tap_halves(after, shifted, depth, grad_scale, 0), 0)
-    grad_input = input_plane(0, (here,), (1,), w_down, fine_input.shape)
-    first_taps, later_taps, after, grad_input = lax.optimization_barrier(
-        (first_taps, later_taps, after, grad_input)
+    (parts,) = tap_sums(after, shifted, depth, grad_scale, ((0, 1),))
+    kept, last_kept, parts = lax.optimization_barrier((middle_parts[0], last_parts[0], parts))
+    middle_taps = exchange_parts((kept, *middle_parts[1:]), 2)
+    last_taps = exchange_parts((last_kept, *last_parts[1:]), 1)
+    first_taps = exchange_parts(parts, 1)
+    first_taps, middle_taps, last_taps, after, grad_input = lax.optimization_barrier(
+        (first_taps, middle_taps, last_taps, after, grad_input)
     )
-    first_taps = exchange(first_taps, (1, 2))
-    later_taps = exchange(later_taps, (2,))
+    outer_taps = exchange(jnp.concatenate((first_taps, last_taps), axis=-1), (1, 2))
+    middle_taps = exchange(middle_taps, (2,))
     grad_input = input_plane(1, (here, after), (2, 0), w_down, fine_input.shape, grad_input)
     taps, grad_input = lax.optimization_barrier(
-        (jnp.concatenate((first_taps, later_taps), axis=-1), grad_input)
+        (jnp.concatenate((outer_taps, middle_taps), axis=-1), grad_input)
     )
     for stage in stages:
         taps = exchange(taps, stage)
     rows = width_deep >> bits
     taps = taps.reshape(rows, 27, width_in)
-    grad_down = jnp.concatenate(
-        (taps[:, :9].reshape(rows, 3, 1, 3, width_in), taps[:, 9:].reshape(rows, 3, 2, 3, width_in)),
-        axis=2,
-    )
-    grad_down = (
-        grad_down.transpose(0, 2, 1, 3, 4).reshape(rows, 27, width_in).astype(jnp.float32)
-    )
-
+    grad_down = jnp.concatenate((taps[:, :9], taps[:, 18:], taps[:, 9:18]), axis=1).astype(jnp.float32)
     return (grad_input, grad_down, grad_gain, grad_shift)
 
 

time: 100 us -> 93.3 us (0.933)
  blocking collectives: 0 us -> 19.2 us
  waiting for transfers between devices: 41.8 us -> 23.2 us
  starting transfers between devices: 31.6 us -> 26.3 us
  local copies, waits for them, and re-layouts: 7.13 us -> 4.6 us
    all_to_all x0 -> x1, blocking collectives: none -> 19.2 us  [local(): lax.all_to_all(act_grads, 'slab', split_axis=0, concat_axis=0, tiled=True)]
    all_to_all x1 -> x0, waiting for transfers between devices: 15.6 us -> none  [local(): lax.all_to_all(act_grads, 'slab', split_axis=0, concat_axis=0, tiled=True)]
    ppermute x10 -> x7, starting transfers between devices: 14.2 us -> 10.2 us  [exchange(): arrived = lax.ppermute(pick(flips), ('slab', 'grp'), pairs)]
    all_to_all x1 -> x0, starting transfers between devices: 3.64 us -> none  [local(): lax.all_to_all(act_grads, 'slab', split_axis=0, concat_axis=0, tiled=True)]
    ppermute x10 -> x7, waiting for transfers between devices: 7.81 us -> 5.24 us  [exchange(): arrived = lax.ppermute(pick(flips), ('slab', 'grp'), pairs)]
    convert_element_type x2 -> x4, other arithmetic: 0.08 us -> 1.86 us  [the longest x3 1.2 us: exchange_parts(): return total.astype(jnp.bfloat16).reshape(*dims, rows, total.shape[1])]
    ppermute x3, waiting for transfers between devices: 1.54 us -> 3.21 us  [grp_parts(): lax.ppermute(values, 'grp', [(i, i ^ step) for i in range(groups)])]
    pallas_call x2, Pallas kernels: 2.93 us -> 4.47 us  [tap_sums(): pl.pallas_call(functools.partial(kernel, scale, depth, rows if inside els...]
  transfers between devices with their start and end apart: 19 -> 19, of which waited for: 10 -> 10; matrix products, arithmetic and copies ran while one was open for 5% -> 4% of each run, Pallas kernels for 10% -> 12%
where the time goes in v4:
time: 93.3 us; the launch traced here: 93 us
  starting transfers between devices  26.3 us (28%)
  waiting for transfers between devices  23.2 us (25%)
  blocking collectives  19.2 us (21%)
  Pallas kernels  15.9 us (17%)
  local copies, waits for them, and re-layouts  4.6 us (5%)
  other arithmetic  2.84 us (3%)
    all_to_all x1, blocking collectives, local(): lax.all_to_all(act_grads, 'slab', split_axis=0, concat_axis=0, tiled=True)  19.2 us
    all_to_all x1, waiting for transfers between devices, local(): lax.all_to_all(deep_bf, 'slab', split_axis=0, concat_axis=0, tiled=True)  10.5 us
    ppermute x7, starting transfers between devices, exchange(): arrived = lax.ppermute(pick(flips), ('slab', 'grp'), pairs)  10.2 us
    all_to_all x1, starting transfers between devices, local(): lax.all_to_all(deep_bf, 'slab', split_axis=0, concat_axis=0, tiled=True)  7.26 us
    pallas_call x2, Pallas kernels, input_plane(): pl.pallas_call(functools.partial(input_kernel, taps_of), grid=(1,), in_sp...  6.14 us
    ppermute x7, waiting for transfers between devices, exchange(): arrived = lax.ppermute(pick(flips), ('slab', 'grp'), pairs)  5.24 us
    pallas_call x2, Pallas kernels, tap_sums(): pl.pallas_call(functools.partial(kernel, scale, depth, rows if inside els...  4.47 us
    pallas_call x1, Pallas kernels, deep_gradient(): pl.pallas_call(deep_kernel, in_specs=[pl.BlockSpec(memory_space=pltpu.HBM...  4.24 us
  transfers between devices with their start and end apart: 19, of which 10 were waited for; matrix products, arithmetic and copies ran while one was open for 4% of the time, Pallas kernels for 12%

profile of v4, /device:TPU:0, one launch (start us, length us, event | category | flops | bytes accessed | tf_op | source)
XLA Modules:
  0.0 93.0 jit_solution(10175067474193475449)
XLA Ops:
  0.7 4.2 %deep_gradient.1 = bf16[256,1024]{1,0:T(8,128)(2,1)} custom-call(bf16[2,32,128,128]{3,2,1,0:T(8,128)(2,1)} %rows_ref.1, bf16[8,256,128]{2,1,0:T(8,128)(2,1)} %taps_ref.1), custom_call_target="tpu_custom_call" | custom-call | flops 536870912 | bytes 3145728 | tf_op jit(solution)/shard_map/deep_gradient/pallas_call | solution.py:135
  4.9 7.3 %all-to-all-start = ((bf16[8,32,1024]{2,1,0:T(8,128)(2,1)}), bf16[8,32,1024]{2,1,0:T(8,128)(2,1)S(1)}, u32[]{:S(2)}, u32[]{:S(2)}) async-start(bf16[8,32,1024]{2,1,0:T(8,128)(2,1)} %bitcast.31), calls=%async_computation | async-start | bytes 1048576 | tf_op jit(solution)/shard_map/all_to_all | solution.py:427
  12.9 1.3 %collective-permute-start.3 = (bf16[2,8,32,64]{3,2,1,0:T(8,128)(2,1)S(1)}, bf16[2,8,32,64]{3,2,1,0:T(8,128)(2,1)S(1)}, u32[]{:S(2)}, u32[]{:S(2)}) collective-permute-start(bf16[2,8,32,64]{3,2,1,0:T(8,128)(2,1)S(1)} %pad_maximum_fusion.1), channel_id=1, source_target_pairs={{1,0},{2,1},{3,2},{5,4},{6,5},{7,6},{9,8},{10,9},{11,10},{13,12},{... | collective-permute-start | bytes 196616 | tf_op jit(solution)/shard_map/ppermute | solution.py:24
  14.6 1.5 %collective-permute-done.3 = bf16[2,8,32,64]{3,2,1,0:T(8,128)(2,1)S(1)} collective-permute-done((bf16[2,8,32,64]{3,2,1,0:T(8,128)(2,1)S(1)}, bf16[2,8,32,64]{3,2,1,0:T(8,128)(2,1)S(1)}, u32[]{:S(2)}, u32[]{:S(2)}) %collective-permute-start.3) | collective-permute-done | bytes 65568 | tf_op jit(solution)/shard_map/ppermute | solution.py:24
  16.1 10.5 %all-to-all-done = bf16[8,32,1024]{2,1,0:T(8,128)(2,1)S(1)} async-done(((bf16[8,32,1024]{2,1,0:T(8,128)(2,1)}), bf16[8,32,1024]{2,1,0:T(8,128)(2,1)S(1)}, u32[]{:S(2)}, u32[]{:S(2)}) %all-to-all-start) | async-done | bytes 524320 | tf_op jit(solution)/shard_map/all_to_all | solution.py:427
  26.7 1.3 %collective-permute-start.4 = (bf16[8,32,64]{2,1,0:T(8,128)(2,1)S(1)}, bf16[8,32,64]{2,1,0:T(8,128)(2,1)S(1)}, u32[]{:S(2)}, u32[]{:S(2)}) collective-permute-start(bf16[8,32,64]{2,1,0:T(8,128)(2,1)S(1)} %slice.32), channel_id=1, source_target_pairs={{1,0},{2,1},{3,2},{5,4},{6,5},{7,6},{9,8},{10,9},{11,10},{13,12},{... | collective-permute-start | bytes 98312 | tf_op jit(solution)/shard_map/ppermute | solution.py:24
  28.6 2.3 %collective-permute-start.2 = (f32[32,4]{1,0:T(8,128)S(1)}, f32[32,4]{1,0:T(8,128)S(1)}, u32[]{:S(2)}, u32[]{:S(2)}) collective-permute-start(f32[32,4]{1,0:T(8,128)S(1)} %copy.35.refs_0_), channel_id=1, source_target_pairs={{0,3},{1,2},{2,1},{3,0},{4,7},{5,6},{6,5},{7,4},{8,11},{9,10},{10,... | collective-permute-start | bytes 1544 | tf_op jit(solution)/shard_map/ppermute | solution.py:30
  32.3 2.2 %collective-permute-done.1.refs_2_ = f32[32,4]{1,0:T(8,128)S(1)} collective-permute-done((f32[32,4]{1,0:T(8,128)S(1)}, f32[32,4]{1,0:T(8,128)S(1)}, u32[]{:S(2)}, u32[]{:S(2)}) %collective-permute-start.1) | collective-permute-done | bytes 544 | tf_op jit(solution)/shard_map/ppermute | solution.py:30
  35.2 19.2 %all_to_all.10 = bf16[8,32,1152]{2,1,0:T(8,128)(2,1)S(1)} all-to-all(bf16[8,32,1152]{2,1,0:T(8,128)(2,1)S(1)} %get-tuple-element.45), channel_id=1, replica_groups=mesh['slab'=8,'grp'=4] {'slab'}, dimensions={0} | all-to-all | bytes 1179648 | tf_op jit(solution)/shard_map/all_to_all | solution.py:476
  54.4 1.3 %collective-permute-start.5 = (bf16[256,1152]{1,0:T(8,128)(2,1)S(1)}, bf16[256,1152]{1,0:T(8,128)(2,1)S(1)}, u32[]{:S(2)}, u32[]{:S(2)}) collective-permute-start(bf16[256,1152]{1,0:T(8,128)(2,1)S(1)} %bitcast.27), channel_id=1, source_target_pairs={{4,0},{8,4},{12,8},{16,12},{20,16},{24,20},{28,24},{5,1},{9,5},{13... | collective-permute-start | bytes 1769480 | tf_op jit(solution)/shard_map/ppermute | solution.py:24
  55.7 1.6 %copy-done.1 = bf16[2,32,128,128]{3,2,1,0:T(8,128)(2,1)S(1)} copy-done((bf16[2,32,128,128]{3,2,1,0:T(8,128)(2,1)S(1)}, bf16[2,32,128,128]{3,2,1,0:T(8,128)(2,1)}, u32[]{:S(2)}) %copy-start.1) | copy-done | bytes 2097176
  57.3 3.4 %tap_sums.2 = (bf16[64,1152]{1,0:T(8,128)(2,1)S(1)}, bf16[64,1152]{1,0:T(8,128)(2,1)S(1)}, bf16[64,1152]{1,0:T(8,128)(2,1)S(1)}, bf16[64,1152]{1,0:T(8,128)(2,1)...) custom-call(s32[1]{0:T(128)} %bitcast.own_ref, bf16[256,1152]{1,0:T(8,128)(2,1)S(1)} %bitcast.28, ...), custom_call_target="tpu_custom_call" | custom-call | flops 1358954496 | bytes 7077888 | tf_op jit(solution)/shard_map/tap_sums/pallas_call | solution.py:261
  63.0 1.2 %collective-permute-start.8 = (bf16[64,1152]{1,0:T(8,128)(2,1)}, bf16[64,1152]{1,0:T(8,128)(2,1)S(1)}, u32[]{:S(2)}, u32[]{:S(2)}) collective-permute-start(bf16[64,1152]{1,0:T(8,128)(2,1)} %copy-done.3), channel_id=1, source_target_pairs={{0,2},{1,3},{2,0},{3,1},{4,6},{5,7},{6,4},{7,5},{8,10},{9,11},{10,... | collective-permute-start | bytes 442376 | tf_op jit(solution)/shard_map/ppermute | solution.py:74
  64.2 2.6 %input_gradient.2.refs_3_ = bf16[2,32,128,128]{3,2,1,0:T(8,128)(2,1)} custom-call(bf16[256,1152]{1,0:T(8,128)(2,1)S(1)} %bitcast.29, bf16[27,128,256]{2,1,0:T(8,128)(2,1)S(1)} %copy-done), custom_call_target="tpu_custom_call" | custom-call | tf_op jit(solution)/shard_map/input_gradient/pallas_call | solution.py:347
  67.2 2.2 %collective-permute-done.5.grads_ref.refs_1_ = bf16[256,1152]{1,0:T(8,128)(2,1)S(1)} collective-permute-done((bf16[256,1152]{1,0:T(8,128)(2,1)S(1)}, bf16[256,1152]{1,0:T(8,128)(2,1)S(1)}, u32[]{:S(2)}, u32[]{:S(2)}) %collective-permute-start.5) | collective-permute-done | bytes 589856 | tf_op jit(solution)/shard_map/ppermute | solution.py:24
  70.6 1.0 %add_convert_fusion = bf16[128,1152]{1,0:T(8,128)(2,1)S(1)} fusion(bf16[128,1152]{1,0:T(8,128)(2,1)} %collective-permute-done.10, bf16[128,1152]{1,0:T(8,128)(2,1)S(1)} %get-tuple-element.65), kind=kLoop, calls=%fused_computation.9 | loop fusion | flops 589824 | bytes 884736 | tf_op jit(solution)/shard_map/convert_element_type | solution.py:76
  72.3 2.2 %collective-permute-start.14 = (bf16[2,2,1,1,1,8,1152]{6,5,3,2,1,0,4:T(8,128)(2,1)S(1)}, bf16[2,2,1,1,1,8,1152]{6,5,3,2,1,0,4:T(8,128)(2,1)S(1)}, u32[]{:S(2)}, u32[]{:S(2)}) collective-permute-start(bf16[2,2,1,1,1,8,1152]{6,5,3,2,1,0,4:T(8,128)(2,1)S(1)} %constant_dynamic-slice_fusion.3), channel_id=1, source_target_pairs={{0,4},{1,5},{2,6},{3,7},{4,0},{5,1},{6,2},{7,3},{8,12},{9,13},{10,... | collective-permute-start | bytes 221192 | tf_op jit(solution)/shard_map/ppermute | solution.py:62
  76.1 2.0 %collective-permute-start.12 = (bf16[2,2,1,1,1,8,2304]{6,5,3,2,1,0,4:T(8,128)(2,1)S(1)}, bf16[2,2,1,1,1,8,2304]{6,5,3,2,1,0,4:T(8,128)(2,1)S(1)}, u32[]{:S(2)}, u32[]{:S(2)}) collective-permute-start(bf16[2,2,1,1,1,8,2304]{6,5,3,2,1,0,4:T(8,128)(2,1)S(1)} %get-tuple-element.85), channel_id=1, source_target_pairs={{0,4},{1,5},{2,6},{3,7},{4,0},{5,1},{6,2},{7,3},{8,12},{9,13},{10,... | collective-permute-start | bytes 442376 | tf_op jit(solution)/shard_map/ppermute | solution.py:62
  78.1 3.5 %input_gradient.3 = bf16[2,32,128,128]{3,2,1,0:T(8,128)(2,1)} custom-call(bf16[256,1152]{1,0:T(8,128)(2,1)S(1)} %bitcast.30, bf16[256,1152]{1,0:T(8,128)(2,1)S(1)} %collective-permute-done.5.grads_ref.refs_1_, bf16[27,128,256]{2,1,0:T(8,128)(2,1)S(1)} %copy-done, bf16[2,32,128,128]{3,2,1,0:T(8,128)(2,1)} %input_gradient.2.refs_3_), custom_call_target="tpu_custom_call", output_to_operand_aliasing={{}: (3, {})} | custom-call | tf_op jit(solution)/shard_map/input_gradient/pallas_call | solution.py:347
  82.3 1.5 %collective-permute-done.13 = bf16[2,2,1,1,1,8,2304]{6,5,3,2,1,0,4:T(8,128)(2,1)S(1)} collective-permute-done((bf16[2,2,1,1,1,8,2304]{6,5,3,2,1,0,4:T(8,128)(2,1)S(1)}, bf16[2,2,1,1,1,8,2304]{6,5,3,2,1,0,4:T(8,128)(2,1)S(1)}, u32[]{:S(2)}, u32[]{:S(2)}) %collective-permute-start.13) | collective-permute-done | bytes 147488 | tf_op jit(solution)/shard_map/ppermute | solution.py:62
  84.0 1.5 %collective-permute-start.15 = (bf16[1,1,1,1,1,8,3456]{6,5,3,2,1,0,4:T(8,128)(2,1)S(1)}, bf16[1,1,1,1,1,8,3456]{6,5,3,2,1,0,4:T(8,128)(2,1)S(1)}, u32[]{:S(2)}, u32[]{:S(2)}) collective-permute-start(bf16[1,1,1,1,1,8,3456]{6,5,3,2,1,0,4:T(8,128)(2,1)S(1)} %get-tuple-element.86), channel_id=1, source_target_pairs={{0,24},{1,25},{2,26},{3,27},{4,28},{5,29},{6,30},{7,31},{8,16},{9,... | collective-permute-start | bytes 165896 | tf_op jit(solution)/shard_map/ppermute | solution.py:62
  86.0 2.4 %collective-permute-start.16 = (bf16[1,1,1,1,1,8,3456]{6,5,3,2,1,0,4:T(8,128)(2,1)S(1)}, bf16[1,1,1,1,1,8,3456]{6,5,3,2,1,0,4:T(8,128)(2,1)S(1)}, u32[]{:S(2)}, u32[]{:S(2)}) collective-permute-start(bf16[1,1,1,1,1,8,3456]{6,5,3,2,1,0,4:T(8,128)(2,1)S(1)} %get-tuple-element.88), channel_id=1, source_target_pairs={{0,16},{1,17},{2,18},{3,19},{4,20},{5,21},{6,22},{7,23},{8,24},{9,... | collective-permute-start | bytes 165896 | tf_op jit(solution)/shard_map/ppermute | solution.py:62
  89.1 1.3 %collective-permute-done.15 = bf16[1,1,1,1,1,8,3456]{6,5,3,2,1,0,4:T(8,128)(2,1)S(1)} collective-permute-done((bf16[1,1,1,1,1,8,3456]{6,5,3,2,1,0,4:T(8,128)(2,1)S(1)}, bf16[1,1,1,1,1,8,3456]{6,5,3,2,1,0,4:T(8,128)(2,1)S(1)}, u32[]{:S(2)}, u32[]{:S(2)}) %collective-permute-start.15) | collective-permute-done | bytes 55328 | tf_op jit(solution)/shard_map/ppermute | solution.py:62
  90.5 1.8 %collective-permute-done.16 = bf16[1,1,1,1,1,8,3456]{6,5,3,2,1,0,4:T(8,128)(2,1)S(1)} collective-permute-done((bf16[1,1,1,1,1,8,3456]{6,5,3,2,1,0,4:T(8,128)(2,1)S(1)}, bf16[1,1,1,1,1,8,3456]{6,5,3,2,1,0,4:T(8,128)(2,1)S(1)}, u32[]{:S(2)}, u32[]{:S(2)}) %collective-permute-start.16) | collective-permute-done | bytes 55328 | tf_op jit(solution)/shard_map/ppermute | solution.py:62
  (66 shorter events, 12.6 us)
Async XLA Ops:
  0.6 11.5 %copy-start.5 = (bf16[32,8,1024]{2,1,0:T(8,128)(2,1)S(1)}, bf16[32,8,1024]{2,1,0:T(8,128)(2,1)}, u32[]{:S(2)}) copy-start(bf16[32,8,1024]{2,1,0:T(8,128)(2,1)} %param.10) | copy-start | bytes 1572868
  0.6 11.5 %copy-start.6 = (bf16[32,8,1024]{2,1,0:T(8,128)(2,1)S(1)}, bf16[32,8,1024]{2,1,0:T(8,128)(2,1)}, u32[]{:S(2)}) copy-start(bf16[32,8,1024]{2,1,0:T(8,128)(2,1)} %param.9) | copy-start | bytes 1572868
  4.9 9.6 %copy-start.7 = (f32[32]{0:T(128)S(1)}, f32[32]{0:T(128)}, u32[]{:S(2)}) copy-start(f32[32]{0:T(128)} %param.11) | copy-start | bytes 388
  4.9 21.8 %all-to-all-start = ((bf16[8,32,1024]{2,1,0:T(8,128)(2,1)}), bf16[8,32,1024]{2,1,0:T(8,128)(2,1)S(1)}, u32[]{:S(2)}, u32[]{:S(2)}) async-start(bf16[8,32,1024]{2,1,0:T(8,128)(2,1)} %bitcast.31), calls=%async_computation | async-start | bytes 1048576 | tf_op jit(solution)/shard_map/all_to_all | solution.py:427
  12.9 3.2 %collective-permute-start.3 = (bf16[2,8,32,64]{3,2,1,0:T(8,128)(2,1)S(1)}, bf16[2,8,32,64]{3,2,1,0:T(8,128)(2,1)S(1)}, u32[]{:S(2)}, u32[]{:S(2)}) collective-permute-start(bf16[2,8,32,64]{3,2,1,0:T(8,128)(2,1)S(1)} %pad_maximum_fusion.1), channel_id=1, source_target_pairs={{1,0},{2,1},{3,2},{5,4},{6,5},{7,6},{9,8},{10,9},{11,10},{13,12},{... | collective-permute-start | bytes 196616 | tf_op jit(solution)/shard_map/ppermute | solution.py:24
  26.7 4.7 %collective-permute-start.4 = (bf16[8,32,64]{2,1,0:T(8,128)(2,1)S(1)}, bf16[8,32,64]{2,1,0:T(8,128)(2,1)S(1)}, u32[]{:S(2)}, u32[]{:S(2)}) collective-permute-start(bf16[8,32,64]{2,1,0:T(8,128)(2,1)S(1)} %slice.32), channel_id=1, source_target_pairs={{1,0},{2,1},{3,2},{5,4},{6,5},{7,6},{9,8},{10,9},{11,10},{13,12},{... | collective-permute-start | bytes 98312 | tf_op jit(solution)/shard_map/ppermute | solution.py:24
  28.6 3.8 %collective-permute-start.2 = (f32[32,4]{1,0:T(8,128)S(1)}, f32[32,4]{1,0:T(8,128)S(1)}, u32[]{:S(2)}, u32[]{:S(2)}) collective-permute-start(f32[32,4]{1,0:T(8,128)S(1)} %copy.35.refs_0_), channel_id=1, source_target_pairs={{0,3},{1,2},{2,1},{3,0},{4,7},{5,6},{6,5},{7,4},{8,11},{9,10},{10,... | collective-permute-start | bytes 1544 | tf_op jit(solution)/shard_map/ppermute | solution.py:30
  30.8 3.7 %collective-permute-start.1 = (f32[32,4]{1,0:T(8,128)S(1)}, f32[32,4]{1,0:T(8,128)S(1)}, u32[]{:S(2)}, u32[]{:S(2)}) collective-permute-start(f32[32,4]{1,0:T(8,128)S(1)} %copy.35.refs_0_), channel_id=1, source_target_pairs={{0,2},{1,3},{2,0},{3,1},{4,6},{5,7},{6,4},{7,5},{8,10},{9,11},{10,... | collective-permute-start | bytes 1544 | tf_op jit(solution)/shard_map/ppermute | solution.py:30
  31.3 3.2 %collective-permute-start = (f32[32,4]{1,0:T(8,128)S(1)}, f32[32,4]{1,0:T(8,128)S(1)}, u32[]{:S(2)}, u32[]{:S(2)}) collective-permute-start(f32[32,4]{1,0:T(8,128)S(1)} %copy.35.refs_0_), channel_id=1, source_target_pairs={{0,1},{1,0},{2,3},{3,2},{4,5},{5,4},{6,7},{7,6},{8,9},{9,8},{10,11... | collective-permute-start | bytes 1544 | tf_op jit(solution)/shard_map/ppermute | solution.py:30
  54.4 15.1 %collective-permute-start.5 = (bf16[256,1152]{1,0:T(8,128)(2,1)S(1)}, bf16[256,1152]{1,0:T(8,128)(2,1)S(1)}, u32[]{:S(2)}, u32[]{:S(2)}) collective-permute-start(bf16[256,1152]{1,0:T(8,128)(2,1)S(1)} %bitcast.27), channel_id=1, source_target_pairs={{4,0},{8,4},{12,8},{16,12},{20,16},{24,20},{28,24},{5,1},{9,5},{13... | collective-permute-start | bytes 1769480 | tf_op jit(solution)/shard_map/ppermute | solution.py:24
  57.3 6.9 %copy-start = (bf16[27,128,256]{2,1,0:T(8,128)(2,1)S(1)}, bf16[27,128,256]{2,1,0:T(8,128)(2,1)}, u32[]{:S(2)}) copy-start(bf16[27,128,256]{2,1,0:T(8,128)(2,1)} %refs_2_.1) | copy-start | bytes 5308420
  62.0 8.6 %collective-permute-start.10 = (bf16[128,1152]{1,0:T(8,128)(2,1)}, bf16[128,1152]{1,0:T(8,128)(2,1)}, u32[]{:S(2)}, u32[]{:S(2)}) collective-permute-start(bf16[128,1152]{1,0:T(8,128)(2,1)} %get-tuple-element.66), channel_id=1, source_target_pairs={{0,1},{1,0},{2,3},{3,2},{4,5},{5,4},{6,7},{7,6},{8,9},{9,8},{10,11... | collective-permute-start | bytes 884744 | tf_op jit(solution)/shard_map/ppermute | solution.py:74
  62.0 4.8 %copy-start.2 = (bf16[2,32,128,128]{3,2,1,0:T(8,128)(2,1)S(1)}, bf16[2,32,128,128]{3,2,1,0:T(8,128)(2,1)}, u32[]{:S(2)}) copy-start(bf16[2,32,128,128]{3,2,1,0:T(8,128)(2,1)} %fine_ref.1) | copy-start | bytes 6291460
  62.0 9.6 %collective-permute-start.7 = (bf16[64,1152]{1,0:T(8,128)(2,1)}, bf16[64,1152]{1,0:T(8,128)(2,1)S(1)}, u32[]{:S(2)}, u32[]{:S(2)}) collective-permute-start(bf16[64,1152]{1,0:T(8,128)(2,1)} %copy-done.4), channel_id=1, source_target_pairs={{0,3},{1,2},{2,1},{3,0},{4,7},{5,6},{6,5},{7,4},{8,11},{9,10},{10,... | collective-permute-start | bytes 442376 | tf_op jit(solution)/shard_map/ppermute | solution.py:74
  63.0 8.7 %collective-permute-start.8 = (bf16[64,1152]{1,0:T(8,128)(2,1)}, bf16[64,1152]{1,0:T(8,128)(2,1)S(1)}, u32[]{:S(2)}, u32[]{:S(2)}) collective-permute-start(bf16[64,1152]{1,0:T(8,128)(2,1)} %copy-done.3), channel_id=1, source_target_pairs={{0,2},{1,3},{2,0},{3,1},{4,6},{5,7},{6,4},{7,5},{8,10},{9,11},{10,... | collective-permute-start | bytes 442376 | tf_op jit(solution)/shard_map/ppermute | solution.py:74
  64.2 7.5 %collective-permute-start.9 = (bf16[64,1152]{1,0:T(8,128)(2,1)S(1)}, bf16[64,1152]{1,0:T(8,128)(2,1)S(1)}, u32[]{:S(2)}, u32[]{:S(2)}) collective-permute-start(bf16[64,1152]{1,0:T(8,128)(2,1)S(1)} %get-tuple-element.64), channel_id=1, source_target_pairs={{0,1},{1,0},{2,3},{3,2},{4,5},{5,4},{6,7},{7,6},{8,9},{9,8},{10,11... | collective-permute-start | bytes 442376 | tf_op jit(solution)/shard_map/ppermute | solution.py:74
  70.5 1.6 %collective-permute-start.6 = (bf16[128,1152]{1,0:T(8,128)(2,1)S(1)}, bf16[128,1152]{1,0:T(8,128)(2,1)S(1)}, u32[]{:S(2)}, u32[]{:S(2)}) collective-permute-start(bf16[128,1152]{1,0:T(8,128)(2,1)S(1)} %get-tuple-element.60), channel_id=1, source_target_pairs={{0,1},{1,0},{2,3},{3,2},{4,5},{5,4},{6,7},{7,6},{8,9},{9,8},{10,11... | collective-permute-start | bytes 884744 | tf_op jit(solution)/shard_map/ppermute | solution.py:74
  72.3 9.4 %collective-permute-start.14 = (bf16[2,2,1,1,1,8,1152]{6,5,3,2,1,0,4:T(8,128)(2,1)S(1)}, bf16[2,2,1,1,1,8,1152]{6,5,3,2,1,0,4:T(8,128)(2,1)S(1)}, u32[]{:S(2)}, u32[]{:S(2)}) collective-permute-start(bf16[2,2,1,1,1,8,1152]{6,5,3,2,1,0,4:T(8,128)(2,1)S(1)} %constant_dynamic-slice_fusion.3), channel_id=1, source_target_pairs={{0,4},{1,5},{2,6},{3,7},{4,0},{5,1},{6,2},{7,3},{8,12},{9,13},{10,... | collective-permute-start | bytes 221192 | tf_op jit(solution)/shard_map/ppermute | solution.py:62
  74.6 7.7 %collective-permute-start.11 = (bf16[2,2,1,1,1,8,2304]{6,5,3,2,1,0,4:T(8,128)(2,1)S(1)}, bf16[2,2,1,1,1,8,2304]{6,5,3,2,1,0,4:T(8,128)(2,1)S(1)}, u32[]{:S(2)}, u32[]{:S(2)}) collective-permute-start(bf16[2,2,1,1,1,8,2304]{6,5,3,2,1,0,4:T(8,128)(2,1)S(1)} %get-tuple-element.83), channel_id=1, source_target_pairs={{0,6},{1,7},{2,4},{3,5},{4,2},{5,3},{6,0},{7,1},{8,14},{9,15},{10,... | collective-permute-start | bytes 442376 | tf_op jit(solution)/shard_map/ppermute | solution.py:62
  75.4 8.5 %collective-permute-start.13 = (bf16[2,2,1,1,1,8,2304]{6,5,3,2,1,0,4:T(8,128)(2,1)S(1)}, bf16[2,2,1,1,1,8,2304]{6,5,3,2,1,0,4:T(8,128)(2,1)S(1)}, u32[]{:S(2)}, u32[]{:S(2)}) collective-permute-start(bf16[2,2,1,1,1,8,2304]{6,5,3,2,1,0,4:T(8,128)(2,1)S(1)} %get-tuple-element.84), channel_id=1, source_target_pairs={{0,2},{1,3},{2,0},{3,1},{4,6},{5,7},{6,4},{7,5},{8,10},{9,11},{10,... | collective-permute-start | bytes 442376 | tf_op jit(solution)/shard_map/ppermute | solution.py:62
  76.1 7.7 %collective-permute-start.12 = (bf16[2,2,1,1,1,8,2304]{6,5,3,2,1,0,4:T(8,128)(2,1)S(1)}, bf16[2,2,1,1,1,8,2304]{6,5,3,2,1,0,4:T(8,128)(2,1)S(1)}, u32[]{:S(2)}, u32[]{:S(2)}) collective-permute-start(bf16[2,2,1,1,1,8,2304]{6,5,3,2,1,0,4:T(8,128)(2,1)S(1)} %get-tuple-element.85), channel_id=1, source_target_pairs={{0,4},{1,5},{2,6},{3,7},{4,0},{5,1},{6,2},{7,3},{8,12},{9,13},{10,... | collective-permute-start | bytes 442376 | tf_op jit(solution)/shard_map/ppermute | solution.py:62
  84.0 6.5 %collective-permute-start.15 = (bf16[1,1,1,1,1,8,3456]{6,5,3,2,1,0,4:T(8,128)(2,1)S(1)}, bf16[1,1,1,1,1,8,3456]{6,5,3,2,1,0,4:T(8,128)(2,1)S(1)}, u32[]{:S(2)}, u32[]{:S(2)}) collective-permute-start(bf16[1,1,1,1,1,8,3456]{6,5,3,2,1,0,4:T(8,128)(2,1)S(1)} %get-tuple-element.86), channel_id=1, source_target_pairs={{0,24},{1,25},{2,26},{3,27},{4,28},{5,29},{6,30},{7,31},{8,16},{9,... | collective-permute-start | bytes 165896 | tf_op jit(solution)/shard_map/ppermute | solution.py:62
  85.5 5.0 %collective-permute-start.17 = (bf16[1,1,1,1,1,8,3456]{6,5,3,2,1,0,4:T(8,128)(2,1)S(1)}, bf16[1,1,1,1,1,8,3456]{6,5,3,2,1,0,4:T(8,128)(2,1)S(1)}, u32[]{:S(2)}, u32[]{:S(2)}) collective-permute-start(bf16[1,1,1,1,1,8,3456]{6,5,3,2,1,0,4:T(8,128)(2,1)S(1)} %get-tuple-element.87), channel_id=1, source_target_pairs={{0,8},{1,9},{2,10},{3,11},{4,12},{5,13},{6,14},{7,15},{8,0},{9,1},... | collective-permute-start | bytes 165896 | tf_op jit(solution)/shard_map/ppermute | solution.py:62
  86.0 6.2 %collective-permute-start.16 = (bf16[1,1,1,1,1,8,3456]{6,5,3,2,1,0,4:T(8,128)(2,1)S(1)}, bf16[1,1,1,1,1,8,3456]{6,5,3,2,1,0,4:T(8,128)(2,1)S(1)}, u32[]{:S(2)}, u32[]{:S(2)}) collective-permute-start(bf16[1,1,1,1,1,8,3456]{6,5,3,2,1,0,4:T(8,128)(2,1)S(1)} %get-tuple-element.88), channel_id=1, source_target_pairs={{0,16},{1,17},{2,18},{3,19},{4,20},{5,21},{6,22},{7,23},{8,24},{9,... | collective-permute-start | bytes 165896 | tf_op jit(solution)/shard_map/ppermute | solution.py:62
  (3 other events, 2.9 us)

commit v5 on v4

--- a/solution.py
+++ b/solution.py
@@ -200,7 +200,28 @@
     )(fine_input)
 
 
-def tap_kernel(scale, depth, rows, jobs, own_ref, grads_ref, shifted_ref, *out_refs):
+def block_of(ref, block, width_deep):
+    if len(ref.shape) == 2:
+        return ref[:, block * LANES : (block + 1) * LANES]
+    slabs = ref.shape[0]
+    channels = width_deep // slabs
+    start = block * channels
+    if start + channels <= ref.shape[1]:
+        return jnp.concatenate([ref[t, start : start + channels, :] for t in range(slabs)], axis=0)
+    left = lax.broadcasted_iota(jnp.int32, (channels // 2, LANES), 1) < LANES // 2
+    pieces = []
+    for t in range(slabs):
+        both = ref[t, start:, :].astype(jnp.float32)
+        for half in (both, pltpu.roll(both, LANES // 2, 1)):
+            pieces.append(jnp.where(left, half, 0.0))
+    return jnp.concatenate(pieces, axis=0).astype(jnp.bfloat16)
+
+
+def tap_kernel(scale, depth, rows, jobs, own_ref, packed_ref, shifted_ref, *refs):
+    *out_refs, grads_ref = refs
+    for block in range(grads_ref.shape[1] // LANES):
+        columns = slice(block * LANES, (block + 1) * LANES)
+        grads_ref[:, columns] = block_of(packed_ref, block, grads_ref.shape[0])
     cells = (shifted_ref.shape[0] - 2 * depth) // 2
     width = 3 * LANES
     for px, bits in jobs:
@@ -227,9 +248,9 @@
 
 
 def shift_and_tap_kernel(scale, depth, rows, jobs, own_ref, grads_ref, fine_ref, *refs):
-    *out_refs, shifted, wide = refs
+    *out_refs, shifted, wide, grads = refs
     shifted_kernel(fine_ref, shifted, wide)
-    tap_kernel(scale, depth, rows, jobs, own_ref, grads_ref, shifted, *out_refs)
+    tap_kernel(scale, depth, rows, jobs, own_ref, grads_ref, shifted, *out_refs, grads)
 
 
 def shifted_shape(fine_input, planes):
@@ -237,8 +258,8 @@
     return ((fine_rows + 2) * (fine_depth // 2), planes * 3 * width)
 
 
-def tap_sums(grads, source, depth, scale, jobs):
-    width_deep, padded = grads.shape
+def tap_sums(grads, source, depth, scale, jobs, shape):
+    width_deep, padded = shape
     scratch = []
     kernel = tap_kernel
     if source.ndim == 4:
@@ -264,11 +285,11 @@
         + [pl.BlockSpec(memory_space=pltpu.VMEM)] * 2,
         out_specs=[pl.BlockSpec(memory_space=pltpu.VMEM)] * len(outs),
         out_shape=outs,
-        scratch_shapes=scratch,
+        scratch_shapes=[*scratch, pltpu.VMEM(shape, jnp.bfloat16)],
         compiler_params=pltpu.CompilerParams(vmem_limit_bytes=20 << 20),
         cost_estimate=pl.CostEstimate(
             flops=2 * width_deep * padded * columns * len(jobs),
-            bytes_accessed=2 * (grads.size + (padded + width_deep) * columns * len(jobs)),
+            bytes_accessed=2 * (width_deep * padded + (padded + width_deep) * columns * len(jobs)),
             transcendentals=0,
         ),
         name="tap_sums",
@@ -296,8 +317,9 @@
     depth = fine_depth // 2
     padded = turned.shape[1]
     for slot, ref in enumerate(grads_refs):
-        for start in range(0, padded, LANES):
-            turned[slot, start : start + LANES, :] = ref[:, start : start + LANES].T
+        for block in range(padded // LANES):
+            rows = slice(block * LANES, (block + 1) * LANES)
+            turned[slot, rows, :] = block_of(ref, block, turned.shape[2]).T
     for ky in range(3):
         total = None
         for slot, kx in enumerate(taps_of):
@@ -333,11 +355,11 @@
     lax.fori_loop(0, fine_rows // 2, row, 0)
 
 
-def input_plane(px, grads, taps_of, w_down, fine_shape, earlier=None):
+def input_plane(px, grads, taps_of, w_down, fine_shape, padded, earlier=None):
     _, fine_rows, fine_depth, width = fine_shape
-    width_deep, padded = grads[0].shape
+    width_deep = w_down.shape[2]
     operands = list(grads) + [w_down]
-    in_specs = [pl.BlockSpec((width_deep, padded), lambda i: (0, 0)) for _ in grads]
+    in_specs = [pl.BlockSpec(array.shape, lambda i, n=array.ndim: (0,) * n) for array in grads]
     in_specs.append(pl.BlockSpec(w_down.shape, lambda i: (0, 0, 0)))
     aliases = {}
     if earlier is not None:
@@ -374,8 +396,8 @@
 
 def norm_kernel(own_total, cell_total, parts, *refs):
     part_refs, refs = refs[:parts], refs[parts:]
-    gain_ref, edge_ref, values_ref, masked_ref, edge_values_ref, edge_masked_ref = refs[:6]
-    out_ref, totals_ref = refs[6:]
+    gain_ref, take_ref, values_ref, masked_ref, edge_values_ref, edge_acts_ref, *edge_refs = refs[:-2]
+    out_ref, totals_ref = refs[-2:]
     planes, channels, cells = values_ref.shape
     depth = edge_values_ref.shape[2]
 
@@ -396,17 +418,32 @@
     totals_ref[:, 0:1] = slope
     totals_ref[:, 1:2] = shift
     gain = gain_ref[...] * inv_std
-    edge_gain = gain * edge_ref[0]
 
     def grad_of(values, masked, gain):
         normed = (values.astype(jnp.float32) - mean) * inv_std
-        return (gain * (masked.astype(jnp.float32) - shift - normed * slope)).astype(jnp.bfloat16)
+        return gain * (masked.astype(jnp.float32) - shift - normed * slope)
 
     for plane in range(planes):
-        out_ref[plane, :, 0:cells] = grad_of(values_ref[plane], masked_ref[plane], gain)
-        edge = grad_of(edge_values_ref[plane], edge_masked_ref[plane], edge_gain)
-        spare = jnp.zeros((channels, out_ref.shape[2] - cells - depth), jnp.bfloat16)
-        out_ref[plane, :, cells:] = jnp.concatenate((edge, spare), axis=1)
+        main = grad_of(values_ref[plane], masked_ref[plane], gain).astype(jnp.bfloat16)
+        edge_grads = jnp.zeros(edge_values_ref.shape[1:], jnp.float32)
+        for n, ref in enumerate(edge_refs):
+            edge_grads = jnp.where(take_ref[n] > 0, ref[plane].astype(jnp.float32), edge_grads)
+        edge_masked = jnp.where(edge_acts_ref[plane].astype(jnp.float32) > 0, edge_grads, 0.0)
+        edge = grad_of(edge_values_ref[plane], edge_masked, gain)
+        edge = jnp.where(take_ref[len(edge_refs)] > 0, jnp.zeros_like(edge), edge)
+        if out_ref.shape[2] > LANES:
+            spare = jnp.zeros((channels, out_ref.shape[2] - cells - depth), jnp.float32)
+            out_ref[plane, :, 0:cells] = main
+            out_ref[plane, :, cells:] = jnp.concatenate((edge, spare), axis=1).astype(jnp.bfloat16)
+            continue
+        for block in range(cells // LANES):
+            out_ref[plane, block * channels : (block + 1) * channels, :] = main[
+                :, block * LANES : (block + 1) * LANES
+            ]
+        half = channels // 2
+        out_ref[plane, cells // LANES * channels :, :] = jnp.concatenate(
+            (edge[:half], edge[half:]), axis=1
+        ).astype(jnp.bfloat16)
 
 
 def local(fine_input, out_grad, pre_norm, act_out, norm_gain, w_down, w_up):
@@ -430,7 +467,8 @@
     acts = act_out.transpose(1, 0, 2)
     values, acts = lax.optimization_barrier((values, acts))
     edge_values, edge_acts = from_next(jnp.stack((values[:, :, :depth], acts[:, :, :depth])), "grp")
-    edge_grads = from_next(grad_vals[:, :, :depth], "grp")
+    first_row = grad_vals[:, :, :depth]
+    masks = [(2 << n) - 1 for n in range(groups.bit_length() - 1)]
 
     wide_values = values.astype(jnp.float32)
     first_sum = jnp.sum(wide_values, axis=(0, 2))
@@ -438,10 +476,7 @@
 
     own_total = slab_planes * cells
     own_mean, own_inv = own_moments(first_sum, second_sum, own_total)
-    def masked_of(grads, acts):
-        return jnp.where(acts > 0, grads, jnp.zeros_like(grads))
-
-    masked_bf = masked_of(grad_vals, acts)
+    masked_bf = jnp.where(acts > 0, grad_vals, jnp.zeros_like(grad_vals))
     masked = masked_bf.astype(jnp.float32)
     own_normed = (wide_values - own_mean[None, :, None]) * own_inv[None, :, None]
     parts = grp_parts(
@@ -455,14 +490,22 @@
             axis=1,
         )
     )
-    inner = (lax.axis_index("grp") < groups - 1).astype(jnp.float32).reshape(1)
+    edge_grads = [
+        lax.ppermute(first_row, "grp", [(i, i ^ mask) for i in range(groups)]) for mask in masks
+    ]
+    grp = lax.axis_index("grp")
+    takes = jnp.stack([grp ^ (grp + 1) == mask for mask in masks] + [grp == groups - 1])
     vmem = pl.BlockSpec(memory_space=pltpu.VMEM)
+    packed = channels % 32 == 0 and 2 * depth == LANES
+    act_shape = (slab_planes, channels, padded)
+    if packed:
+        act_shape = (slab_planes, channels * cells // LANES + channels // 2, LANES)
     act_grads, totals = pl.pallas_call(
         functools.partial(norm_kernel, own_total, cell_total, len(parts)),
-        in_specs=[vmem] * (len(parts) + 1) + [pl.BlockSpec(memory_space=pltpu.SMEM)] + [vmem] * 4,
+        in_specs=[vmem] * (len(parts) + 1) + [pl.BlockSpec(memory_space=pltpu.SMEM)] + [vmem] * (4 + len(masks)),
         out_specs=[vmem] * 2,
         out_shape=[
-            jax.ShapeDtypeStruct((slab_planes, channels, padded), jnp.bfloat16),
+            jax.ShapeDtypeStruct(act_shape, jnp.bfloat16),
             jax.ShapeDtypeStruct((channels, 2), jnp.float32),
         ],
         compiler_params=pltpu.CompilerParams(vmem_limit_bytes=12 << 20),
@@ -470,22 +513,23 @@
             flops=8 * values.size, bytes_accessed=8 * values.size, transcendentals=0
         ),
         name="act_gradient",
-    )(*parts, norm_gain[:, None], inner, values, masked_bf, edge_values, masked_of(edge_grads, edge_acts))
+    )(*parts, norm_gain[:, None], takes.astype(jnp.int32), values, masked_bf, edge_values, edge_acts, *edge_grads)
     grad_gain = totals[:, 0]
     grad_shift = totals[:, 1]
     here = lax.all_to_all(act_grads, "slab", split_axis=0, concat_axis=0, tiled=True)
-    here = here.reshape(width_deep, padded)
+    if not packed:
+        here = here.reshape(width_deep, padded)
     grad_scale = 1.0 / math.sqrt(cell_total)
     bits = place_bits()
     stages = [tuple(range(b, min(b + 2, bits))) for b in range(3, bits, 2)]
-    parts = tap_sums(here, fine_input, depth, grad_scale, ((0, 2), (1, 1)))
+    parts = tap_sums(here, fine_input, depth, grad_scale, ((0, 2), (1, 1)), (width_deep, padded))
     parts, here_again = lax.optimization_barrier((parts, here))
     middle_parts, last_parts = parts
     after = from_next(here, "slab")
-    grad_input = input_plane(0, (here_again,), (1,), w_down, fine_input.shape)
+    grad_input = input_plane(0, (here_again,), (1,), w_down, fine_input.shape, padded)
     grad_input, fine_again = lax.optimization_barrier((grad_input, fine_input))
     shifted = shifted_fine(fine_again, fine_input.shape[0] - 1)
-    (parts,) = tap_sums(after, shifted, depth, grad_scale, ((0, 1),))
+    (parts,) = tap_sums(after, shifted, depth, grad_scale, ((0, 1),), (width_deep, padded))
     kept, last_kept, parts = lax.optimization_barrier((middle_parts[0], last_parts[0], parts))
     middle_taps = exchange_parts((kept, *middle_parts[1:]), 2)
     last_taps = exchange_parts((last_kept, *last_parts[1:]), 1)
@@ -495,7 +539,7 @@
     )
     outer_taps = exchange(jnp.concatenate((first_taps, last_taps), axis=-1), (1, 2))
     middle_taps = exchange(middle_taps, (2,))
-    grad_input = input_plane(1, (here, after), (2, 0), w_down, fine_input.shape, grad_input)
+    grad_input = input_plane(1, (here, after), (2, 0), w_down, fine_input.shape, padded, grad_input)
     taps, grad_input = lax.optimization_barrier(
         (jnp.concatenate((outer_taps, middle_taps), axis=-1), grad_input)
     )

time: 93.3 us -> 92.1 us (0.987)
  waiting for transfers between devices: 23.2 us -> 21.8 us
    ppermute x0 -> x2, starting transfers between devices: none -> 1.69 us  [local(): lax.ppermute(first_row, 'grp', [(i, i ^ mask) for i in range(groups)])]
    ppermute x3 -> x2, waiting for transfers between devices: 3.78 us -> 2.19 us  [from_next(): return lax.ppermute(shard, axis, [(i, i - 1) for i in range(1, devices)])]
    all_to_all x1, waiting for transfers between devices: 10.5 us -> 12 us  [local(): lax.all_to_all(deep_bf, 'slab', split_axis=0, concat_axis=0, tiled=True)]
    ppermute x3 -> x2, starting transfers between devices: 3.86 us -> 2.57 us  [from_next(): return lax.ppermute(shard, axis, [(i, i - 1) for i in range(1, devices)])]
    ppermute x3, waiting for transfers between devices: 3.21 us -> 1.98 us  [grp_parts(): lax.ppermute(values, 'grp', [(i, i ^ step) for i in range(groups)])]
  transfers between devices with their start and end apart: 19 -> 20, of which waited for: 10 -> 9; matrix products, arithmetic and copies ran while one was open for 4% -> 4% of each run, Pallas kernels for 12% -> 12%
where the time goes in v5:
time: 92.1 us; the launch traced here: 91.8 us
  starting transfers between devices  25.8 us (28%)
  waiting for transfers between devices  21.8 us (24%)
  blocking collectives  19.1 us (21%)
  Pallas kernels  16.6 us (18%)
  local copies, waits for them, and re-layouts  4.6 us (5%)
  other arithmetic  2.91 us (3%)
  between operations  0.93 us (1%)
    all_to_all x1, blocking collectives, local(): lax.all_to_all(act_grads, 'slab', split_axis=0, concat_axis=0, tiled=True)  19.1 us
    all_to_all x1, waiting for transfers between devices, local(): lax.all_to_all(deep_bf, 'slab', split_axis=0, concat_axis=0, tiled=True)  12 us
    ppermute x7, starting transfers between devices, exchange(): arrived = lax.ppermute(pick(flips), ('slab', 'grp'), pairs)  10.2 us
    all_to_all x1, starting transfers between devices, local(): lax.all_to_all(deep_bf, 'slab', split_axis=0, concat_axis=0, tiled=True)  7.26 us
    pallas_call x2, Pallas kernels, input_plane(): pl.pallas_call(functools.partial(input_kernel, taps_of), grid=(1,), in_sp...  6.14 us
    ppermute x7, waiting for transfers between devices, exchange(): arrived = lax.ppermute(pick(flips), ('slab', 'grp'), pairs)  5.25 us
    pallas_call x2, Pallas kernels, tap_sums(): pl.pallas_call(functools.partial(kernel, scale, depth, rows if inside els...  4.5 us
    pallas_call x1, Pallas kernels, deep_gradient(): pl.pallas_call(deep_kernel, in_specs=[pl.BlockSpec(memory_space=pltpu.HBM...  4.24 us
  transfers between devices with their start and end apart: 20, of which 9 were waited for; matrix products, arithmetic and copies ran while one was open for 4% of the time, Pallas kernels for 12%

profile of v5, /device:TPU:0, one launch (start us, length us, event | category | flops | bytes accessed | tf_op | source)
XLA Modules:
  0.0 91.8 jit_solution(3221858964280881082)
XLA Ops:
  0.7 4.2 %deep_gradient.1 = bf16[256,1024]{1,0:T(8,128)(2,1)} custom-call(bf16[2,32,128,128]{3,2,1,0:T(8,128)(2,1)} %rows_ref.1, bf16[8,256,128]{2,1,0:T(8,128)(2,1)} %taps_ref.1), custom_call_target="tpu_custom_call" | custom-call | flops 536870912 | bytes 3145728 | tf_op jit(solution)/shard_map/deep_gradient/pallas_call | solution.py:135
  4.9 7.3 %all-to-all-start = ((bf16[8,32,1024]{2,1,0:T(8,128)(2,1)}), bf16[8,32,1024]{2,1,0:T(8,128)(2,1)S(1)}, u32[]{:S(2)}, u32[]{:S(2)}) async-start(bf16[8,32,1024]{2,1,0:T(8,128)(2,1)} %bitcast.28), calls=%async_computation | async-start | bytes 1048576 | tf_op jit(solution)/shard_map/all_to_all | solution.py:464
  12.9 1.3 %collective-permute-start.3 = (bf16[2,8,32,64]{3,2,1,0:T(8,128)(2,1)S(1)}, bf16[2,8,32,64]{3,2,1,0:T(8,128)(2,1)S(1)}, u32[]{:S(2)}, u32[]{:S(2)}) collective-permute-start(bf16[2,8,32,64]{3,2,1,0:T(8,128)(2,1)S(1)} %pad_maximum_fusion.1), channel_id=1, source_target_pairs={{1,0},{2,1},{3,2},{5,4},{6,5},{7,6},{9,8},{10,9},{11,10},{13,12},{... | collective-permute-start | bytes 196616 | tf_op jit(solution)/shard_map/ppermute | solution.py:24
  14.6 12.0 %all-to-all-done = bf16[8,32,1024]{2,1,0:T(8,128)(2,1)S(1)} async-done(((bf16[8,32,1024]{2,1,0:T(8,128)(2,1)}), bf16[8,32,1024]{2,1,0:T(8,128)(2,1)S(1)}, u32[]{:S(2)}, u32[]{:S(2)}) %all-to-all-start) | async-done | bytes 524320 | tf_op jit(solution)/shard_map/all_to_all | solution.py:464
  26.8 1.6 %collective-permute-start.4 = (bf16[8,32,64]{2,1,0:T(8,128)(2,1)S(1)}, bf16[8,32,64]{2,1,0:T(8,128)(2,1)S(1)}, u32[]{:S(2)}, u32[]{:S(2)}) collective-permute-start(bf16[8,32,64]{2,1,0:T(8,128)(2,1)S(1)} %slice.32), channel_id=1, source_target_pairs={{0,1},{1,0},{2,3},{3,2},{4,5},{5,4},{6,7},{7,6},{8,9},{9,8},{10,11... | collective-permute-start | bytes 98312 | tf_op jit(solution)/shard_map/ppermute | solution.py:494
  29.1 1.5 %collective-permute-start.1 = (f32[32,4]{1,0:T(8,128)S(1)}, f32[32,4]{1,0:T(8,128)S(1)}, u32[]{:S(2)}, u32[]{:S(2)}) collective-permute-start(f32[32,4]{1,0:T(8,128)S(1)} %copy.35.refs_0_), channel_id=1, source_target_pairs={{0,2},{1,3},{2,0},{3,1},{4,6},{5,7},{6,4},{7,5},{8,10},{9,11},{10,... | collective-permute-start | bytes 1544 | tf_op jit(solution)/shard_map/ppermute | solution.py:30
  30.9 1.3 %collective-permute-done.2.refs_3_ = f32[32,4]{1,0:T(8,128)S(1)} collective-permute-done((f32[32,4]{1,0:T(8,128)S(1)}, f32[32,4]{1,0:T(8,128)S(1)}, u32[]{:S(2)}, u32[]{:S(2)}) %collective-permute-start.2) | collective-permute-done | bytes 544 | tf_op jit(solution)/shard_map/ppermute | solution.py:30
  32.9 1.2 %act_gradient.1 = (bf16[8,272,128]{2,1,0:T(8,128)(2,1)S(1)}, f32[32,2]{1,0:T(8,128)S(1)}) custom-call(f32[32,4]{1,0:T(8,128)S(1)} %copy.35.refs_0_, f32[32,4]{1,0:T(8,128)S(1)} %collective-permute-done.refs_1_, f32[32,4]{1,0:T(8,128)S(1)} %collective-permute-done.1.refs_2_, f32[32,4]{1,0:T(8,128)S(1)} %collective-permute-done.2.refs_3_, ...), custom_call_target="tpu_custom_call" | custom-call | flops 2097152 | bytes 2097152 | tf_op jit(solution)/shard_map/act_gradient/pallas_call | solution.py:503
  34.1 19.1 %all_to_all.10.grads_ref.refs_0_ = bf16[8,272,128]{2,1,0:T(8,128)(2,1)S(1)} all-to-all(bf16[8,272,128]{2,1,0:T(8,128)(2,1)S(1)} %get-tuple-element.45), channel_id=1, replica_groups=mesh['slab'=8,'grp'=4] {'slab'}, dimensions={0} | all-to-all | bytes 1114112 | tf_op jit(solution)/shard_map/all_to_all | solution.py:519
  53.2 1.3 %collective-permute-start.6 = (bf16[8,272,128]{2,1,0:T(8,128)(2,1)S(1)}, bf16[8,272,128]{2,1,0:T(8,128)(2,1)S(1)}, u32[]{:S(2)}, u32[]{:S(2)}) collective-permute-start(bf16[8,272,128]{2,1,0:T(8,128)(2,1)S(1)} %all_to_all.10.grads_ref.refs_0_), channel_id=1, source_target_pairs={{4,0},{8,4},{12,8},{16,12},{20,16},{24,20},{28,24},{5,1},{9,5},{13... | collective-permute-start | bytes 1671176 | tf_op jit(solution)/shard_map/ppermute | solution.py:24
  54.5 1.6 %copy-done.1 = bf16[2,32,128,128]{3,2,1,0:T(8,128)(2,1)S(1)} copy-done((bf16[2,32,128,128]{3,2,1,0:T(8,128)(2,1)S(1)}, bf16[2,32,128,128]{3,2,1,0:T(8,128)(2,1)}, u32[]{:S(2)}) %copy-start.1) | copy-done | bytes 2097176
  56.1 3.5 %tap_sums.2 = (bf16[64,1152]{1,0:T(8,128)(2,1)S(1)}, bf16[64,1152]{1,0:T(8,128)(2,1)S(1)}, bf16[64,1152]{1,0:T(8,128)(2,1)S(1)}, bf16[64,1152]{1,0:T(8,128)(2,1)...) custom-call(s32[1]{0:T(128)} %bitcast.own_ref, bf16[8,272,128]{2,1,0:T(8,128)(2,1)S(1)} %all_to_all.10.grads_ref.refs_0_, ...), custom_call_target="tpu_custom_call" | custom-call | flops 1358954496 | bytes 7077888 | tf_op jit(solution)/shard_map/tap_sums/pallas_call | solution.py:282
  60.9 1.5 %collective-permute-start.8 = (bf16[64,1152]{1,0:T(8,128)(2,1)}, bf16[64,1152]{1,0:T(8,128)(2,1)S(1)}, u32[]{:S(2)}, u32[]{:S(2)}) collective-permute-start(bf16[64,1152]{1,0:T(8,128)(2,1)} %copy-done.4), channel_id=1, source_target_pairs={{0,3},{1,2},{2,1},{3,0},{4,7},{5,6},{6,5},{7,4},{8,11},{9,10},{10,... | collective-permute-start | bytes 442376 | tf_op jit(solution)/shard_map/ppermute | solution.py:74
  63.0 2.6 %input_gradient.2.refs_3_ = bf16[2,32,128,128]{3,2,1,0:T(8,128)(2,1)} custom-call(bf16[8,272,128]{2,1,0:T(8,128)(2,1)S(1)} %all_to_all.10.grads_ref.refs_0_, bf16[27,128,256]{2,1,0:T(8,128)(2,1)S(1)} %copy-done), custom_call_target="tpu_custom_call" | custom-call | tf_op jit(solution)/shard_map/input_gradient/pallas_call | solution.py:369
  66.1 2.2 %collective-permute-done.6.packed_ref.refs_1_ = bf16[8,272,128]{2,1,0:T(8,128)(2,1)S(1)} collective-permute-done((bf16[8,272,128]{2,1,0:T(8,128)(2,1)S(1)}, bf16[8,272,128]{2,1,0:T(8,128)(2,1)S(1)}, u32[]{:S(2)}, u32[]{:S(2)}) %collective-permute-start.6) | collective-permute-done | bytes 557088 | tf_op jit(solution)/shard_map/ppermute | solution.py:24
  68.3 1.0 %tap_sums.3 = (bf16[128,1152]{1,0:T(8,128)(2,1)S(1)}, bf16[128,1152]{1,0:T(8,128)(2,1)S(1)}) custom-call(s32[1]{0:T(128)} %bitcast.own_ref, bf16[8,272,128]{2,1,0:T(8,128)(2,1)S(1)} %collective-permute-done.6.packed_ref.refs_1_, bf16[2176,384]{1,0:T(8,128)(2,1)S(1)} %shifted_fine.1.shifted_ref), custom_call_target="tpu_custom_call" | custom-call | flops 679477248 | bytes 3833856 | tf_op jit(solution)/shard_map/tap_sums/pallas_call | solution.py:282
  71.1 2.2 %collective-permute-start.15 = (bf16[2,2,1,1,1,8,1152]{6,5,3,2,1,0,4:T(8,128)(2,1)S(1)}, bf16[2,2,1,1,1,8,1152]{6,5,3,2,1,0,4:T(8,128)(2,1)S(1)}, u32[]{:S(2)}, u32[]{:S(2)}) collective-permute-start(bf16[2,2,1,1,1,8,1152]{6,5,3,2,1,0,4:T(8,128)(2,1)S(1)} %constant_dynamic-slice_fusion.3), channel_id=1, source_target_pairs={{0,4},{1,5},{2,6},{3,7},{4,0},{5,1},{6,2},{7,3},{8,12},{9,13},{10,... | collective-permute-start | bytes 221192 | tf_op jit(solution)/shard_map/ppermute | solution.py:62
  75.0 2.0 %collective-permute-start.13 = (bf16[2,2,1,1,1,8,2304]{6,5,3,2,1,0,4:T(8,128)(2,1)S(1)}, bf16[2,2,1,1,1,8,2304]{6,5,3,2,1,0,4:T(8,128)(2,1)S(1)}, u32[]{:S(2)}, u32[]{:S(2)}) collective-permute-start(bf16[2,2,1,1,1,8,2304]{6,5,3,2,1,0,4:T(8,128)(2,1)S(1)} %get-tuple-element.85), channel_id=1, source_target_pairs={{0,4},{1,5},{2,6},{3,7},{4,0},{5,1},{6,2},{7,3},{8,12},{9,13},{10,... | collective-permute-start | bytes 442376 | tf_op jit(solution)/shard_map/ppermute | solution.py:62
  77.0 3.5 %input_gradient.3 = bf16[2,32,128,128]{3,2,1,0:T(8,128)(2,1)} custom-call(bf16[8,272,128]{2,1,0:T(8,128)(2,1)S(1)} %all_to_all.10.grads_ref.refs_0_, bf16[8,272,128]{2,1,0:T(8,128)(2,1)S(1)} %collective-permute-done.6.packed_ref.refs_1_, bf16[27,128,256]{2,1,0:T(8,128)(2,1)S(1)} %copy-done, ...), custom_call_target="tpu_custom_call", output_to_operand_aliasing={{}: (3, {})} | custom-call | tf_op jit(solution)/shard_map/input_gradient/pallas_call | solution.py:369
  81.2 1.4 %collective-permute-done.14 = bf16[2,2,1,1,1,8,2304]{6,5,3,2,1,0,4:T(8,128)(2,1)S(1)} collective-permute-done((bf16[2,2,1,1,1,8,2304]{6,5,3,2,1,0,4:T(8,128)(2,1)S(1)}, bf16[2,2,1,1,1,8,2304]{6,5,3,2,1,0,4:T(8,128)(2,1)S(1)}, u32[]{:S(2)}, u32[]{:S(2)}) %collective-permute-start.14) | collective-permute-done | bytes 147488 | tf_op jit(solution)/shard_map/ppermute | solution.py:62
  82.7 1.6 %collective-permute-start.16 = (bf16[1,1,1,1,1,8,3456]{6,5,3,2,1,0,4:T(8,128)(2,1)S(1)}, bf16[1,1,1,1,1,8,3456]{6,5,3,2,1,0,4:T(8,128)(2,1)S(1)}, u32[]{:S(2)}, u32[]{:S(2)}) collective-permute-start(bf16[1,1,1,1,1,8,3456]{6,5,3,2,1,0,4:T(8,128)(2,1)S(1)} %get-tuple-element.86), channel_id=1, source_target_pairs={{0,24},{1,25},{2,26},{3,27},{4,28},{5,29},{6,30},{7,31},{8,16},{9,... | collective-permute-start | bytes 165896 | tf_op jit(solution)/shard_map/ppermute | solution.py:62
  84.8 2.3 %collective-permute-start.17 = (bf16[1,1,1,1,1,8,3456]{6,5,3,2,1,0,4:T(8,128)(2,1)S(1)}, bf16[1,1,1,1,1,8,3456]{6,5,3,2,1,0,4:T(8,128)(2,1)S(1)}, u32[]{:S(2)}, u32[]{:S(2)}) collective-permute-start(bf16[1,1,1,1,1,8,3456]{6,5,3,2,1,0,4:T(8,128)(2,1)S(1)} %get-tuple-element.88), channel_id=1, source_target_pairs={{0,16},{1,17},{2,18},{3,19},{4,20},{5,21},{6,22},{7,23},{8,24},{9,... | collective-permute-start | bytes 165896 | tf_op jit(solution)/shard_map/ppermute | solution.py:62
  87.8 1.6 %collective-permute-done.16 = bf16[1,1,1,1,1,8,3456]{6,5,3,2,1,0,4:T(8,128)(2,1)S(1)} collective-permute-done((bf16[1,1,1,1,1,8,3456]{6,5,3,2,1,0,4:T(8,128)(2,1)S(1)}, bf16[1,1,1,1,1,8,3456]{6,5,3,2,1,0,4:T(8,128)(2,1)S(1)}, u32[]{:S(2)}, u32[]{:S(2)}) %collective-permute-start.16) | collective-permute-done | bytes 55328 | tf_op jit(solution)/shard_map/ppermute | solution.py:62
  89.4 1.7 %collective-permute-done.17 = bf16[1,1,1,1,1,8,3456]{6,5,3,2,1,0,4:T(8,128)(2,1)S(1)} collective-permute-done((bf16[1,1,1,1,1,8,3456]{6,5,3,2,1,0,4:T(8,128)(2,1)S(1)}, bf16[1,1,1,1,1,8,3456]{6,5,3,2,1,0,4:T(8,128)(2,1)S(1)}, u32[]{:S(2)}, u32[]{:S(2)}) %collective-permute-start.17) | collective-permute-done | bytes 55328 | tf_op jit(solution)/shard_map/ppermute | solution.py:62
  (68 shorter events, 11.4 us)
Async XLA Ops:
  0.6 11.5 %copy-start.5 = (bf16[32,8,1024]{2,1,0:T(8,128)(2,1)S(1)}, bf16[32,8,1024]{2,1,0:T(8,128)(2,1)}, u32[]{:S(2)}) copy-start(bf16[32,8,1024]{2,1,0:T(8,128)(2,1)} %param.10) | copy-start | bytes 1572868
  0.6 11.5 %copy-start.6 = (bf16[32,8,1024]{2,1,0:T(8,128)(2,1)S(1)}, bf16[32,8,1024]{2,1,0:T(8,128)(2,1)}, u32[]{:S(2)}) copy-start(bf16[32,8,1024]{2,1,0:T(8,128)(2,1)} %param.9) | copy-start | bytes 1572868
  4.9 9.3 %copy-start.7 = (f32[32]{0:T(128)S(1)}, f32[32]{0:T(128)}, u32[]{:S(2)}) copy-start(f32[32]{0:T(128)} %param.11) | copy-start | bytes 388
  4.9 21.8 %all-to-all-start = ((bf16[8,32,1024]{2,1,0:T(8,128)(2,1)}), bf16[8,32,1024]{2,1,0:T(8,128)(2,1)S(1)}, u32[]{:S(2)}, u32[]{:S(2)}) async-start(bf16[8,32,1024]{2,1,0:T(8,128)(2,1)} %bitcast.28), calls=%async_computation | async-start | bytes 1048576 | tf_op jit(solution)/shard_map/all_to_all | solution.py:464
  12.9 17.8 %collective-permute-start.3 = (bf16[2,8,32,64]{3,2,1,0:T(8,128)(2,1)S(1)}, bf16[2,8,32,64]{3,2,1,0:T(8,128)(2,1)S(1)}, u32[]{:S(2)}, u32[]{:S(2)}) collective-permute-start(bf16[2,8,32,64]{3,2,1,0:T(8,128)(2,1)S(1)} %pad_maximum_fusion.1), channel_id=1, source_target_pairs={{1,0},{2,1},{3,2},{5,4},{6,5},{7,6},{9,8},{10,9},{11,10},{13,12},{... | collective-permute-start | bytes 196616 | tf_op jit(solution)/shard_map/ppermute | solution.py:24
  26.7 6.2 %collective-permute-start.5 = (bf16[8,32,64]{2,1,0:T(8,128)(2,1)S(1)}, bf16[8,32,64]{2,1,0:T(8,128)(2,1)S(1)}, u32[]{:S(2)}, u32[]{:S(2)}) collective-permute-start(bf16[8,32,64]{2,1,0:T(8,128)(2,1)S(1)} %slice.32), channel_id=1, source_target_pairs={{0,3},{1,2},{2,1},{3,0},{4,7},{5,6},{6,5},{7,4},{8,11},{9,10},{10,... | collective-permute-start | bytes 98312 | tf_op jit(solution)/shard_map/ppermute | solution.py:494
  26.8 6.1 %collective-permute-start.4 = (bf16[8,32,64]{2,1,0:T(8,128)(2,1)S(1)}, bf16[8,32,64]{2,1,0:T(8,128)(2,1)S(1)}, u32[]{:S(2)}, u32[]{:S(2)}) collective-permute-start(bf16[8,32,64]{2,1,0:T(8,128)(2,1)S(1)} %slice.32), channel_id=1, source_target_pairs={{0,1},{1,0},{2,3},{3,2},{4,5},{5,4},{6,7},{7,6},{8,9},{9,8},{10,11... | collective-permute-start | bytes 98312 | tf_op jit(solution)/shard_map/ppermute | solution.py:494
  29.0 3.2 %collective-permute-start.2 = (f32[32,4]{1,0:T(8,128)S(1)}, f32[32,4]{1,0:T(8,128)S(1)}, u32[]{:S(2)}, u32[]{:S(2)}) collective-permute-start(f32[32,4]{1,0:T(8,128)S(1)} %copy.35.refs_0_), channel_id=1, source_target_pairs={{0,3},{1,2},{2,1},{3,0},{4,7},{5,6},{6,5},{7,4},{8,11},{9,10},{10,... | collective-permute-start | bytes 1544 | tf_op jit(solution)/shard_map/ppermute | solution.py:30
  29.1 3.7 %collective-permute-start.1 = (f32[32,4]{1,0:T(8,128)S(1)}, f32[32,4]{1,0:T(8,128)S(1)}, u32[]{:S(2)}, u32[]{:S(2)}) collective-permute-start(f32[32,4]{1,0:T(8,128)S(1)} %copy.35.refs_0_), channel_id=1, source_target_pairs={{0,2},{1,3},{2,0},{3,1},{4,6},{5,7},{6,4},{7,5},{8,10},{9,11},{10,... | collective-permute-start | bytes 1544 | tf_op jit(solution)/shard_map/ppermute | solution.py:30
  30.6 2.2 %collective-permute-start = (f32[32,4]{1,0:T(8,128)S(1)}, f32[32,4]{1,0:T(8,128)S(1)}, u32[]{:S(2)}, u32[]{:S(2)}) collective-permute-start(f32[32,4]{1,0:T(8,128)S(1)} %copy.35.refs_0_), channel_id=1, source_target_pairs={{0,1},{1,0},{2,3},{3,2},{4,5},{5,4},{6,7},{7,6},{8,9},{9,8},{10,11... | collective-permute-start | bytes 1544 | tf_op jit(solution)/shard_map/ppermute | solution.py:30
  53.2 15.1 %collective-permute-start.6 = (bf16[8,272,128]{2,1,0:T(8,128)(2,1)S(1)}, bf16[8,272,128]{2,1,0:T(8,128)(2,1)S(1)}, u32[]{:S(2)}, u32[]{:S(2)}) collective-permute-start(bf16[8,272,128]{2,1,0:T(8,128)(2,1)S(1)} %all_to_all.10.grads_ref.refs_0_), channel_id=1, source_target_pairs={{4,0},{8,4},{12,8},{16,12},{20,16},{24,20},{28,24},{5,1},{9,5},{13... | collective-permute-start | bytes 1671176 | tf_op jit(solution)/shard_map/ppermute | solution.py:24
  56.1 6.9 %copy-start = (bf16[27,128,256]{2,1,0:T(8,128)(2,1)S(1)}, bf16[27,128,256]{2,1,0:T(8,128)(2,1)}, u32[]{:S(2)}) copy-start(bf16[27,128,256]{2,1,0:T(8,128)(2,1)} %refs_2_.1) | copy-start | bytes 5308420
  60.9 8.5 %collective-permute-start.11 = (bf16[128,1152]{1,0:T(8,128)(2,1)}, bf16[128,1152]{1,0:T(8,128)(2,1)}, u32[]{:S(2)}, u32[]{:S(2)}) collective-permute-start(bf16[128,1152]{1,0:T(8,128)(2,1)} %get-tuple-element.66), channel_id=1, source_target_pairs={{0,1},{1,0},{2,3},{3,2},{4,5},{5,4},{6,7},{7,6},{8,9},{9,8},{10,11... | collective-permute-start | bytes 884744 | tf_op jit(solution)/shard_map/ppermute | solution.py:74
  60.9 9.6 %collective-permute-start.8 = (bf16[64,1152]{1,0:T(8,128)(2,1)}, bf16[64,1152]{1,0:T(8,128)(2,1)S(1)}, u32[]{:S(2)}, u32[]{:S(2)}) collective-permute-start(bf16[64,1152]{1,0:T(8,128)(2,1)} %copy-done.4), channel_id=1, source_target_pairs={{0,3},{1,2},{2,1},{3,0},{4,7},{5,6},{6,5},{7,4},{8,11},{9,10},{10,... | collective-permute-start | bytes 442376 | tf_op jit(solution)/shard_map/ppermute | solution.py:74
  62.4 8.1 %collective-permute-start.9 = (bf16[64,1152]{1,0:T(8,128)(2,1)}, bf16[64,1152]{1,0:T(8,128)(2,1)S(1)}, u32[]{:S(2)}, u32[]{:S(2)}) collective-permute-start(bf16[64,1152]{1,0:T(8,128)(2,1)} %copy-done.3), channel_id=1, source_target_pairs={{0,2},{1,3},{2,0},{3,1},{4,6},{5,7},{6,4},{7,5},{8,10},{9,11},{10,... | collective-permute-start | bytes 442376 | tf_op jit(solution)/shard_map/ppermute | solution.py:74
  63.0 7.5 %collective-permute-start.10 = (bf16[64,1152]{1,0:T(8,128)(2,1)S(1)}, bf16[64,1152]{1,0:T(8,128)(2,1)S(1)}, u32[]{:S(2)}, u32[]{:S(2)}) collective-permute-start(bf16[64,1152]{1,0:T(8,128)(2,1)S(1)} %get-tuple-element.64), channel_id=1, source_target_pairs={{0,1},{1,0},{2,3},{3,2},{4,5},{5,4},{6,7},{7,6},{8,9},{9,8},{10,11... | collective-permute-start | bytes 442376 | tf_op jit(solution)/shard_map/ppermute | solution.py:74
  69.3 1.6 %collective-permute-start.7 = (bf16[128,1152]{1,0:T(8,128)(2,1)S(1)}, bf16[128,1152]{1,0:T(8,128)(2,1)S(1)}, u32[]{:S(2)}, u32[]{:S(2)}) collective-permute-start(bf16[128,1152]{1,0:T(8,128)(2,1)S(1)} %get-tuple-element.60), channel_id=1, source_target_pairs={{0,1},{1,0},{2,3},{3,2},{4,5},{5,4},{6,7},{7,6},{8,9},{9,8},{10,11... | collective-permute-start | bytes 884744 | tf_op jit(solution)/shard_map/ppermute | solution.py:74
  71.1 9.4 %collective-permute-start.15 = (bf16[2,2,1,1,1,8,1152]{6,5,3,2,1,0,4:T(8,128)(2,1)S(1)}, bf16[2,2,1,1,1,8,1152]{6,5,3,2,1,0,4:T(8,128)(2,1)S(1)}, u32[]{:S(2)}, u32[]{:S(2)}) collective-permute-start(bf16[2,2,1,1,1,8,1152]{6,5,3,2,1,0,4:T(8,128)(2,1)S(1)} %constant_dynamic-slice_fusion.3), channel_id=1, source_target_pairs={{0,4},{1,5},{2,6},{3,7},{4,0},{5,1},{6,2},{7,3},{8,12},{9,13},{10,... | collective-permute-start | bytes 221192 | tf_op jit(solution)/shard_map/ppermute | solution.py:62
  73.4 7.8 %collective-permute-start.12 = (bf16[2,2,1,1,1,8,2304]{6,5,3,2,1,0,4:T(8,128)(2,1)S(1)}, bf16[2,2,1,1,1,8,2304]{6,5,3,2,1,0,4:T(8,128)(2,1)S(1)}, u32[]{:S(2)}, u32[]{:S(2)}) collective-permute-start(bf16[2,2,1,1,1,8,2304]{6,5,3,2,1,0,4:T(8,128)(2,1)S(1)} %get-tuple-element.83), channel_id=1, source_target_pairs={{0,6},{1,7},{2,4},{3,5},{4,2},{5,3},{6,0},{7,1},{8,14},{9,15},{10,... | collective-permute-start | bytes 442376 | tf_op jit(solution)/shard_map/ppermute | solution.py:62
  74.3 8.2 %collective-permute-start.14 = (bf16[2,2,1,1,1,8,2304]{6,5,3,2,1,0,4:T(8,128)(2,1)S(1)}, bf16[2,2,1,1,1,8,2304]{6,5,3,2,1,0,4:T(8,128)(2,1)S(1)}, u32[]{:S(2)}, u32[]{:S(2)}) collective-permute-start(bf16[2,2,1,1,1,8,2304]{6,5,3,2,1,0,4:T(8,128)(2,1)S(1)} %get-tuple-element.84), channel_id=1, source_target_pairs={{0,2},{1,3},{2,0},{3,1},{4,6},{5,7},{6,4},{7,5},{8,10},{9,11},{10,... | collective-permute-start | bytes 442376 | tf_op jit(solution)/shard_map/ppermute | solution.py:62
  75.0 7.6 %collective-permute-start.13 = (bf16[2,2,1,1,1,8,2304]{6,5,3,2,1,0,4:T(8,128)(2,1)S(1)}, bf16[2,2,1,1,1,8,2304]{6,5,3,2,1,0,4:T(8,128)(2,1)S(1)}, u32[]{:S(2)}, u32[]{:S(2)}) collective-permute-start(bf16[2,2,1,1,1,8,2304]{6,5,3,2,1,0,4:T(8,128)(2,1)S(1)} %get-tuple-element.85), channel_id=1, source_target_pairs={{0,4},{1,5},{2,6},{3,7},{4,0},{5,1},{6,2},{7,3},{8,12},{9,13},{10,... | collective-permute-start | bytes 442376 | tf_op jit(solution)/shard_map/ppermute | solution.py:62
  82.7 6.7 %collective-permute-start.16 = (bf16[1,1,1,1,1,8,3456]{6,5,3,2,1,0,4:T(8,128)(2,1)S(1)}, bf16[1,1,1,1,1,8,3456]{6,5,3,2,1,0,4:T(8,128)(2,1)S(1)}, u32[]{:S(2)}, u32[]{:S(2)}) collective-permute-start(bf16[1,1,1,1,1,8,3456]{6,5,3,2,1,0,4:T(8,128)(2,1)S(1)} %get-tuple-element.86), channel_id=1, source_target_pairs={{0,24},{1,25},{2,26},{3,27},{4,28},{5,29},{6,30},{7,31},{8,16},{9,... | collective-permute-start | bytes 165896 | tf_op jit(solution)/shard_map/ppermute | solution.py:62
  84.3 5.1 %collective-permute-start.18 = (bf16[1,1,1,1,1,8,3456]{6,5,3,2,1,0,4:T(8,128)(2,1)S(1)}, bf16[1,1,1,1,1,8,3456]{6,5,3,2,1,0,4:T(8,128)(2,1)S(1)}, u32[]{:S(2)}, u32[]{:S(2)}) collective-permute-start(bf16[1,1,1,1,1,8,3456]{6,5,3,2,1,0,4:T(8,128)(2,1)S(1)} %get-tuple-element.87), channel_id=1, source_target_pairs={{0,8},{1,9},{2,10},{3,11},{4,12},{5,13},{6,14},{7,15},{8,0},{9,1},... | collective-permute-start | bytes 165896 | tf_op jit(solution)/shard_map/ppermute | solution.py:62
  84.8 6.2 %collective-permute-start.17 = (bf16[1,1,1,1,1,8,3456]{6,5,3,2,1,0,4:T(8,128)(2,1)S(1)}, bf16[1,1,1,1,1,8,3456]{6,5,3,2,1,0,4:T(8,128)(2,1)S(1)}, u32[]{:S(2)}, u32[]{:S(2)}) collective-permute-start(bf16[1,1,1,1,1,8,3456]{6,5,3,2,1,0,4:T(8,128)(2,1)S(1)} %get-tuple-element.88), channel_id=1, source_target_pairs={{0,16},{1,17},{2,18},{3,19},{4,20},{5,21},{6,22},{7,23},{8,24},{9,... | collective-permute-start | bytes 165896 | tf_op jit(solution)/shard_map/ppermute | solution.py:62
  (4 other events, 7.7 us)

commit v6 on v5

--- a/solution.py
+++ b/solution.py
@@ -55,7 +55,7 @@
         return array
 
     total = pick([0] * len(dims)).astype(jnp.float32)
-    for code in range((1 << len(stage)) - 1, 0, -1):
+    for code in (3, 1, 2) if len(stage) == 2 else (1,):
         flips = [code >> n & 1 for n in range(len(stage))]
         mask = sum(f << b for f, b in zip(flips, stage))
         pairs = bit_pairs(slabs, groups, mask // groups, mask % groups)
@@ -394,10 +394,10 @@
     return mean, lax.rsqrt(jnp.maximum(variance, 0.0) + 1e-05)
 
 
-def norm_kernel(own_total, cell_total, parts, *refs):
+def norm_kernel(own_total, cell_total, parts, direct, *refs):
     part_refs, refs = refs[:parts], refs[parts:]
-    gain_ref, take_ref, values_ref, masked_ref, edge_values_ref, edge_acts_ref, *edge_refs = refs[:-2]
-    out_ref, totals_ref = refs[-2:]
+    gain_ref, inner_ref, slab_ref, values_ref, masked_ref, edge_values_ref, edge_masked_ref = refs[:7]
+    *out_refs, totals_ref = refs[7:]
     planes, channels, cells = values_ref.shape
     depth = edge_values_ref.shape[2]
 
@@ -418,32 +418,36 @@
     totals_ref[:, 0:1] = slope
     totals_ref[:, 1:2] = shift
     gain = gain_ref[...] * inv_std
+    edge_gain = gain * inner_ref[0]
 
     def grad_of(values, masked, gain):
         normed = (values.astype(jnp.float32) - mean) * inv_std
         return gain * (masked.astype(jnp.float32) - shift - normed * slope)
 
-    for plane in range(planes):
+    for n in range(planes):
+        plane = n ^ slab_ref[0] if direct else n
+        out_ref = out_refs[n] if direct else out_refs[0].at[n]
         main = grad_of(values_ref[plane], masked_ref[plane], gain).astype(jnp.bfloat16)
-        edge_grads = jnp.zeros(edge_values_ref.shape[1:], jnp.float32)
-        for n, ref in enumerate(edge_refs):
-            edge_grads = jnp.where(take_ref[n] > 0, ref[plane].astype(jnp.float32), edge_grads)
-        edge_masked = jnp.where(edge_acts_ref[plane].astype(jnp.float32) > 0, edge_grads, 0.0)
-        edge = grad_of(edge_values_ref[plane], edge_masked, gain)
-        edge = jnp.where(take_ref[len(edge_refs)] > 0, jnp.zeros_like(edge), edge)
-        if out_ref.shape[2] > LANES:
-            spare = jnp.zeros((channels, out_ref.shape[2] - cells - depth), jnp.float32)
-            out_ref[plane, :, 0:cells] = main
-            out_ref[plane, :, cells:] = jnp.concatenate((edge, spare), axis=1).astype(jnp.bfloat16)
+        edge = grad_of(edge_values_ref[plane], edge_masked_ref[plane], edge_gain)
+        if out_ref.shape[1] > LANES:
+            spare = jnp.zeros((channels, out_ref.shape[1] - cells - depth), jnp.float32)
+            out_ref[:, 0:cells] = main
+            out_ref[:, cells:] = jnp.concatenate((edge, spare), axis=1).astype(jnp.bfloat16)
             continue
         for block in range(cells // LANES):
-            out_ref[plane, block * channels : (block + 1) * channels, :] = main[
+            out_ref[block * channels : (block + 1) * channels, :] = main[
                 :, block * LANES : (block + 1) * LANES
             ]
         half = channels // 2
-        out_ref[plane, cells // LANES * channels :, :] = jnp.concatenate(
+        out_ref[cells // LANES * channels :, :] = jnp.concatenate(
             (edge[:half], edge[half:]), axis=1
         ).astype(jnp.bfloat16)
+
+
+def place_kernel(slab_ref, *refs):
+    *block_refs, out_ref = refs
+    for n, block_ref in enumerate(block_refs):
+        out_ref[n ^ slab_ref[0]] = block_ref[...]
 
 
 def local(fine_input, out_grad, pre_norm, act_out, norm_gain, w_down, w_up):
@@ -494,29 +498,48 @@
         lax.ppermute(first_row, "grp", [(i, i ^ mask) for i in range(groups)]) for mask in masks
     ]
     grp = lax.axis_index("grp")
-    takes = jnp.stack([grp ^ (grp + 1) == mask for mask in masks] + [grp == groups - 1])
+    edge_masked = jnp.zeros_like(first_row)
+    for mask, grads in zip(masks, edge_grads):
+        edge_masked = jnp.where((grp ^ (grp + 1) == mask) & (edge_acts > 0), grads, edge_masked)
+    inner = (grp < groups - 1).astype(jnp.float32).reshape(1)
     vmem = pl.BlockSpec(memory_space=pltpu.VMEM)
     packed = channels % 32 == 0 and 2 * depth == LANES
     act_shape = (slab_planes, channels, padded)
     if packed:
         act_shape = (slab_planes, channels * cells // LANES + channels // 2, LANES)
-    act_grads, totals = pl.pallas_call(
-        functools.partial(norm_kernel, own_total, cell_total, len(parts)),
-        in_specs=[vmem] * (len(parts) + 1) + [pl.BlockSpec(memory_space=pltpu.SMEM)] + [vmem] * (4 + len(masks)),
-        out_specs=[vmem] * 2,
-        out_shape=[
-            jax.ShapeDtypeStruct(act_shape, jnp.bfloat16),
-            jax.ShapeDtypeStruct((channels, 2), jnp.float32),
-        ],
+    direct = packed and slabs <= 8
+    blocks = slab_planes if direct else 1
+    smem = pl.BlockSpec(memory_space=pltpu.SMEM)
+    slab = lax.axis_index("slab").astype(jnp.int32).reshape(1)
+    *act_grads, totals = pl.pallas_call(
+        functools.partial(norm_kernel, own_total, cell_total, len(parts), direct),
+        in_specs=[vmem] * (len(parts) + 1) + [smem] * 2 + [vmem] * 4,
+        out_specs=[vmem] * (blocks + 1),
+        out_shape=[jax.ShapeDtypeStruct(act_shape[1:] if direct else act_shape, jnp.bfloat16)] * blocks
+        + [jax.ShapeDtypeStruct((channels, 2), jnp.float32)],
         compiler_params=pltpu.CompilerParams(vmem_limit_bytes=12 << 20),
         cost_estimate=pl.CostEstimate(
             flops=8 * values.size, bytes_accessed=8 * values.size, transcendentals=0
         ),
         name="act_gradient",
-    )(*parts, norm_gain[:, None], takes.astype(jnp.int32), values, masked_bf, edge_values, edge_acts, *edge_grads)
+    )(*parts, norm_gain[:, None], inner, slab, values, masked_bf, edge_values, edge_masked)
     grad_gain = totals[:, 0]
     grad_shift = totals[:, 1]
-    here = lax.all_to_all(act_grads, "slab", split_axis=0, concat_axis=0, tiled=True)
+    if direct:
+        for mask in sorted(range(1, slabs), key=lambda mask: -(mask >> 1)):
+            act_grads[mask] = lax.ppermute(
+                act_grads[mask], "slab", [(i, i ^ mask) for i in range(slabs)]
+            )
+        here = pl.pallas_call(
+            place_kernel,
+            in_specs=[smem] + [vmem] * slabs,
+            out_specs=vmem,
+            out_shape=jax.ShapeDtypeStruct(act_shape, jnp.bfloat16),
+            compiler_params=pltpu.CompilerParams(vmem_limit_bytes=12 << 20),
+            name="place_blocks",
+        )(slab, *act_grads)
+    else:
+        here = lax.all_to_all(act_grads[0], "slab", split_axis=0, concat_axis=0, tiled=True)
     if not packed:
         here = here.reshape(width_deep, padded)
     grad_scale = 1.0 / math.sqrt(cell_total)

time: 92.1 us -> 89.9 us (0.976)
  blocking collectives: 19.1 us -> 0 us
  starting transfers between devices: 25.8 us -> 38.2 us
  waiting for transfers between devices: 21.8 us -> 27 us
    all_to_all x1 -> x0, blocking collectives: 19.1 us -> none  [local(): lax.all_to_all(act_grads, 'slab', split_axis=0, concat_axis=0, tiled=True)]
    ppermute x0 -> x7, starting transfers between devices: none -> 11.2 us  [local(): lax.ppermute(act_grads[mask], 'slab', [(i, i ^ mask) for i in range(slabs)])]
    ppermute x0 -> x7, waiting for transfers between devices: none -> 5.34 us  [local(): lax.ppermute(act_grads[mask], 'slab', [(i, i ^ mask) for i in range(slabs)])]
    all_to_all x1, waiting for transfers between devices: 12 us -> 10.5 us  [local(): lax.all_to_all(deep_bf, 'slab', split_axis=0, concat_axis=0, tiled=True)]
    ppermute x5, waiting for transfers between devices: 0.41 us -> 1.62 us  [exchange_parts(): lax.ppermute(part, ('slab', 'grp'), pairs).astype(jnp.float32)]
  transfers between devices with their start and end apart: 20 -> 27, of which waited for: 9 -> 12; matrix products, arithmetic and copies ran while one was open for 4% -> 4% of each run, Pallas kernels for 12% -> 12%
where the time goes in v6:
time: 89.9 us; the launch traced here: 89.6 us
  starting transfers between devices  38.2 us (42%)
  waiting for transfers between devices  27 us (30%)
  Pallas kernels  16 us (18%)
  local copies, waits for them, and re-layouts  4.58 us (5%)
  other arithmetic  2.89 us (3%)
  between operations  0.93 us (1%)
    ppermute x7, starting transfers between devices, local(): lax.ppermute(act_grads[mask], 'slab', [(i, i ^ mask) for i in range(slabs)])  11.2 us
    ppermute x7, starting transfers between devices, exchange(): arrived = lax.ppermute(pick(flips), ('slab', 'grp'), pairs)  10.7 us
    all_to_all x1, waiting for transfers between devices, local(): lax.all_to_all(deep_bf, 'slab', split_axis=0, concat_axis=0, tiled=True)  10.5 us
    all_to_all x1, starting transfers between devices, local(): lax.all_to_all(deep_bf, 'slab', split_axis=0, concat_axis=0, tiled=True)  7.27 us
    pallas_call x2, Pallas kernels, input_plane(): pl.pallas_call(functools.partial(input_kernel, taps_of), grid=(1,), in_sp...  6.14 us
    ppermute x7, waiting for transfers between devices, exchange(): arrived = lax.ppermute(pick(flips), ('slab', 'grp'), pairs)  5.93 us
    ppermute x7, waiting for transfers between devices, local(): lax.ppermute(act_grads[mask], 'slab', [(i, i ^ mask) for i in range(slabs)])  5.34 us
    pallas_call x2, Pallas kernels, tap_sums(): pl.pallas_call(functools.partial(kernel, scale, depth, rows if inside els...  4.5 us
  transfers between devices with their start and end apart: 27, of which 12 were waited for; matrix products, arithmetic and copies ran while one was open for 4% of the time, Pallas kernels for 12%

profile of v6, /device:TPU:0, one launch (start us, length us, event | category | flops | bytes accessed | tf_op | source)
XLA Modules:
  0.0 89.6 jit_solution(17417484832771783440)
XLA Ops:
  0.7 4.2 %deep_gradient.1 = bf16[256,1024]{1,0:T(8,128)(2,1)} custom-call(bf16[2,32,128,128]{3,2,1,0:T(8,128)(2,1)} %rows_ref.1, bf16[8,256,128]{2,1,0:T(8,128)(2,1)} %taps_ref.1), custom_call_target="tpu_custom_call" | custom-call | flops 536870912 | bytes 3145728 | tf_op jit(solution)/shard_map/deep_gradient/pallas_call | solution.py:135
  4.9 7.3 %all-to-all-start = ((bf16[8,32,1024]{2,1,0:T(8,128)(2,1)}), bf16[8,32,1024]{2,1,0:T(8,128)(2,1)S(1)}, u32[]{:S(2)}, u32[]{:S(2)}) async-start(bf16[8,32,1024]{2,1,0:T(8,128)(2,1)} %bitcast.31), calls=%async_computation | async-start | bytes 1048576 | tf_op jit(solution)/shard_map/all_to_all | solution.py:468
  14.6 1.5 %collective-permute-done.3 = bf16[2,8,32,64]{3,2,1,0:T(8,128)(2,1)S(1)} collective-permute-done((bf16[2,8,32,64]{3,2,1,0:T(8,128)(2,1)S(1)}, bf16[2,8,32,64]{3,2,1,0:T(8,128)(2,1)S(1)}, u32[]{:S(2)}, u32[]{:S(2)}) %collective-permute-start.3) | collective-permute-done | bytes 65568 | tf_op jit(solution)/shard_map/ppermute | solution.py:24
  16.1 10.5 %all-to-all-done = bf16[8,32,1024]{2,1,0:T(8,128)(2,1)S(1)} async-done(((bf16[8,32,1024]{2,1,0:T(8,128)(2,1)}), bf16[8,32,1024]{2,1,0:T(8,128)(2,1)S(1)}, u32[]{:S(2)}, u32[]{:S(2)}) %all-to-all-start) | async-done | bytes 524320 | tf_op jit(solution)/shard_map/all_to_all | solution.py:468
  26.8 1.6 %collective-permute-start.4 = (bf16[8,32,64]{2,1,0:T(8,128)(2,1)S(1)}, bf16[8,32,64]{2,1,0:T(8,128)(2,1)S(1)}, u32[]{:S(2)}, u32[]{:S(2)}) collective-permute-start(bf16[8,32,64]{2,1,0:T(8,128)(2,1)S(1)} %slice.32), channel_id=1, source_target_pairs={{0,3},{1,2},{2,1},{3,0},{4,7},{5,6},{6,5},{7,4},{8,11},{9,10},{10,... | collective-permute-start | bytes 98312 | tf_op jit(solution)/shard_map/ppermute | solution.py:498
  29.2 1.5 %collective-permute-start.1 = (f32[32,4]{1,0:T(8,128)S(1)}, f32[32,4]{1,0:T(8,128)S(1)}, u32[]{:S(2)}, u32[]{:S(2)}) collective-permute-start(f32[32,4]{1,0:T(8,128)S(1)} %copy.35.refs_0_), channel_id=1, source_target_pairs={{0,2},{1,3},{2,0},{3,1},{4,6},{5,7},{6,4},{7,5},{8,10},{9,11},{10,... | collective-permute-start | bytes 1544 | tf_op jit(solution)/shard_map/ppermute | solution.py:30
  33.6 1.5 %collective-permute-start.6 = (bf16[272,128]{1,0:T(8,128)(2,1)S(1)}, bf16[272,128]{1,0:T(8,128)(2,1)S(1)}, u32[]{:S(2)}, u32[]{:S(2)}) collective-permute-start(bf16[272,128]{1,0:T(8,128)(2,1)S(1)} %get-tuple-element.53), channel_id=1, source_target_pairs={{0,4},{4,0},{8,12},{12,8},{16,20},{20,16},{24,28},{28,24},{1,5},{5... | collective-permute-start | bytes 208904 | tf_op jit(solution)/shard_map/ppermute | solution.py:530
  35.1 2.0 %collective-permute-start.8 = (bf16[272,128]{1,0:T(8,128)(2,1)S(1)}, bf16[272,128]{1,0:T(8,128)(2,1)S(1)}, u32[]{:S(2)}, u32[]{:S(2)}) collective-permute-start(bf16[272,128]{1,0:T(8,128)(2,1)S(1)} %get-tuple-element.55), channel_id=1, source_target_pairs={{0,12},{4,8},{8,4},{12,0},{16,28},{20,24},{24,20},{28,16},{1,13},{... | collective-permute-start | bytes 208904 | tf_op jit(solution)/shard_map/ppermute | solution.py:530
  37.3 3.7 %collective-permute-start.10 = (bf16[272,128]{1,0:T(8,128)(2,1)S(1)}, bf16[272,128]{1,0:T(8,128)(2,1)S(1)}, u32[]{:S(2)}, u32[]{:S(2)}) collective-permute-start(bf16[272,128]{1,0:T(8,128)(2,1)S(1)} %get-tuple-element.57), channel_id=1, source_target_pairs={{0,20},{4,16},{8,28},{12,24},{16,4},{20,0},{24,12},{28,8},{1,21},{... | collective-permute-start | bytes 208904 | tf_op jit(solution)/shard_map/ppermute | solution.py:530
  40.9 1.5 %collective-permute-start.11 = (bf16[272,128]{1,0:T(8,128)(2,1)S(1)}, bf16[272,128]{1,0:T(8,128)(2,1)S(1)}, u32[]{:S(2)}, u32[]{:S(2)}) collective-permute-start(bf16[272,128]{1,0:T(8,128)(2,1)S(1)} %get-tuple-element.58), channel_id=1, source_target_pairs={{0,24},{4,28},{8,16},{12,20},{16,8},{20,12},{24,0},{28,4},{1,25},{... | collective-permute-start | bytes 208904 | tf_op jit(solution)/shard_map/ppermute | solution.py:530
  42.4 2.4 %collective-permute-start.12 = (bf16[272,128]{1,0:T(8,128)(2,1)S(1)}, bf16[272,128]{1,0:T(8,128)(2,1)S(1)}, u32[]{:S(2)}, u32[]{:S(2)}) collective-permute-start(bf16[272,128]{1,0:T(8,128)(2,1)S(1)} %get-tuple-element.59), channel_id=1, source_target_pairs={{0,28},{4,24},{8,20},{12,16},{16,12},{20,8},{24,4},{28,0},{1,29},{... | collective-permute-start | bytes 208904 | tf_op jit(solution)/shard_map/ppermute | solution.py:530
  44.8 2.7 %collective-permute-done.9.refs_4_ = bf16[272,128]{1,0:T(8,128)(2,1)S(1)} collective-permute-done((bf16[272,128]{1,0:T(8,128)(2,1)S(1)}, bf16[272,128]{1,0:T(8,128)(2,1)S(1)}, u32[]{:S(2)}, u32[]{:S(2)}) %collective-permute-start.9) | collective-permute-done | bytes 69664 | tf_op jit(solution)/shard_map/ppermute | solution.py:530
  47.5 2.6 %collective-permute-done.10.refs_5_ = bf16[272,128]{1,0:T(8,128)(2,1)S(1)} collective-permute-done((bf16[272,128]{1,0:T(8,128)(2,1)S(1)}, bf16[272,128]{1,0:T(8,128)(2,1)S(1)}, u32[]{:S(2)}, u32[]{:S(2)}) %collective-permute-start.10) | collective-permute-done | bytes 69664 | tf_op jit(solution)/shard_map/ppermute | solution.py:530
  50.1 1.5 %collective-permute-start.13 = (bf16[8,272,128]{2,1,0:T(8,128)(2,1)S(1)}, bf16[8,272,128]{2,1,0:T(8,128)(2,1)S(1)}, u32[]{:S(2)}, u32[]{:S(2)}) collective-permute-start(bf16[8,272,128]{2,1,0:T(8,128)(2,1)S(1)} %place_blocks.1.grads_ref.refs_0_), channel_id=1, source_target_pairs={{4,0},{8,4},{12,8},{16,12},{20,16},{24,20},{28,24},{5,1},{9,5},{13... | collective-permute-start | bytes 1671176 | tf_op jit(solution)/shard_map/ppermute | solution.py:24
  51.6 1.6 %copy-done.1 = bf16[2,32,128,128]{3,2,1,0:T(8,128)(2,1)S(1)} copy-done((bf16[2,32,128,128]{3,2,1,0:T(8,128)(2,1)S(1)}, bf16[2,32,128,128]{3,2,1,0:T(8,128)(2,1)}, u32[]{:S(2)}) %copy-start.1) | copy-done | bytes 2097176
  53.2 3.5 %tap_sums.2 = (bf16[64,1152]{1,0:T(8,128)(2,1)S(1)}, bf16[64,1152]{1,0:T(8,128)(2,1)S(1)}, bf16[64,1152]{1,0:T(8,128)(2,1)S(1)}, bf16[64,1152]{1,0:T(8,128)(2,1)...) custom-call(s32[1]{0:T(128)} %bitcast.own_ref, bf16[8,272,128]{2,1,0:T(8,128)(2,1)S(1)} %place_blocks.1.grads_ref.refs_0_, ...), custom_call_target="tpu_custom_call" | custom-call | flops 1358954496 | bytes 7077888 | tf_op jit(solution)/shard_map/tap_sums/pallas_call | solution.py:282
  58.0 1.5 %collective-permute-start.15 = (bf16[64,1152]{1,0:T(8,128)(2,1)}, bf16[64,1152]{1,0:T(8,128)(2,1)S(1)}, u32[]{:S(2)}, u32[]{:S(2)}) collective-permute-start(bf16[64,1152]{1,0:T(8,128)(2,1)} %copy-done.4), channel_id=1, source_target_pairs={{0,3},{1,2},{2,1},{3,0},{4,7},{5,6},{6,5},{7,4},{8,11},{9,10},{10,... | collective-permute-start | bytes 442376 | tf_op jit(solution)/shard_map/ppermute | solution.py:74
  60.1 2.6 %input_gradient.2.refs_3_ = bf16[2,32,128,128]{3,2,1,0:T(8,128)(2,1)} custom-call(bf16[8,272,128]{2,1,0:T(8,128)(2,1)S(1)} %place_blocks.1.grads_ref.refs_0_, bf16[27,128,256]{2,1,0:T(8,128)(2,1)S(1)} %copy-done), custom_call_target="tpu_custom_call" | custom-call | tf_op jit(solution)/shard_map/input_gradient/pallas_call | solution.py:369
  65.9 1.6 %collective-permute-done.16 = bf16[64,1152]{1,0:T(8,128)(2,1)S(1)} collective-permute-done((bf16[64,1152]{1,0:T(8,128)(2,1)}, bf16[64,1152]{1,0:T(8,128)(2,1)S(1)}, u32[]{:S(2)}, u32[]{:S(2)}) %collective-permute-start.16) | collective-permute-done | bytes 147488 | tf_op jit(solution)/shard_map/ppermute | solution.py:74
  67.7 2.7 %collective-permute-start.22 = (bf16[2,2,1,1,1,8,1152]{6,5,3,2,1,0,4:T(8,128)(2,1)S(1)}, bf16[2,2,1,1,1,8,1152]{6,5,3,2,1,0,4:T(8,128)(2,1)S(1)}, u32[]{:S(2)}, u32[]{:S(2)}) collective-permute-start(bf16[2,2,1,1,1,8,1152]{6,5,3,2,1,0,4:T(8,128)(2,1)S(1)} %constant_dynamic-slice_fusion.3), channel_id=1, source_target_pairs={{0,4},{1,5},{2,6},{3,7},{4,0},{5,1},{6,2},{7,3},{8,12},{9,13},{10,... | collective-permute-start | bytes 221192 | tf_op jit(solution)/shard_map/ppermute | solution.py:62
  71.5 2.0 %collective-permute-start.21 = (bf16[2,2,1,1,1,8,2304]{6,5,3,2,1,0,4:T(8,128)(2,1)S(1)}, bf16[2,2,1,1,1,8,2304]{6,5,3,2,1,0,4:T(8,128)(2,1)S(1)}, u32[]{:S(2)}, u32[]{:S(2)}) collective-permute-start(bf16[2,2,1,1,1,8,2304]{6,5,3,2,1,0,4:T(8,128)(2,1)S(1)} %get-tuple-element.98), channel_id=1, source_target_pairs={{0,4},{1,5},{2,6},{3,7},{4,0},{5,1},{6,2},{7,3},{8,12},{9,13},{10,... | collective-permute-start | bytes 442376 | tf_op jit(solution)/shard_map/ppermute | solution.py:62
  74.1 3.5 %input_gradient.3 = bf16[2,32,128,128]{3,2,1,0:T(8,128)(2,1)} custom-call(bf16[8,272,128]{2,1,0:T(8,128)(2,1)S(1)} %place_blocks.1.grads_ref.refs_0_, bf16[8,272,128]{2,1,0:T(8,128)(2,1)S(1)} %collective-permute-done.13.packed_ref.refs_1_, bf16[27,128,256]{2,1,0:T(8,128)(2,1)S(1)} %copy-done, ...), custom_call_target="tpu_custom_call", output_to_operand_aliasing={{}: (3, {})} | custom-call | tf_op jit(solution)/shard_map/input_gradient/pallas_call | solution.py:369
  80.0 3.2 %collective-permute-start.23 = (bf16[1,1,1,1,1,8,3456]{6,5,3,2,1,0,4:T(8,128)(2,1)S(1)}, bf16[1,1,1,1,1,8,3456]{6,5,3,2,1,0,4:T(8,128)(2,1)S(1)}, u32[]{:S(2)}, u32[]{:S(2)}) collective-permute-start(bf16[1,1,1,1,1,8,3456]{6,5,3,2,1,0,4:T(8,128)(2,1)S(1)} %get-tuple-element.100), channel_id=1, source_target_pairs={{0,24},{1,25},{2,26},{3,27},{4,28},{5,29},{6,30},{7,31},{8,16},{9,... | collective-permute-start | bytes 165896 | tf_op jit(solution)/shard_map/ppermute | solution.py:62
  86.3 2.6 %collective-permute-done.25 = bf16[1,1,1,1,1,8,3456]{6,5,3,2,1,0,4:T(8,128)(2,1)S(1)} collective-permute-done((bf16[1,1,1,1,1,8,3456]{6,5,3,2,1,0,4:T(8,128)(2,1)S(1)}, bf16[1,1,1,1,1,8,3456]{6,5,3,2,1,0,4:T(8,128)(2,1)S(1)}, u32[]{:S(2)}, u32[]{:S(2)}) %collective-permute-start.25) | collective-permute-done | bytes 55328 | tf_op jit(solution)/shard_map/ppermute | solution.py:62
  (82 shorter events, 19.3 us)
Async XLA Ops:
  4.9 21.8 %all-to-all-start = ((bf16[8,32,1024]{2,1,0:T(8,128)(2,1)}), bf16[8,32,1024]{2,1,0:T(8,128)(2,1)S(1)}, u32[]{:S(2)}, u32[]{:S(2)}) async-start(bf16[8,32,1024]{2,1,0:T(8,128)(2,1)} %bitcast.31), calls=%async_computation | async-start | bytes 1048576 | tf_op jit(solution)/shard_map/all_to_all | solution.py:468
  26.7 4.2 %collective-permute-start.5 = (bf16[8,32,64]{2,1,0:T(8,128)(2,1)S(1)}, bf16[8,32,64]{2,1,0:T(8,128)(2,1)S(1)}, u32[]{:S(2)}, u32[]{:S(2)}) collective-permute-start(bf16[8,32,64]{2,1,0:T(8,128)(2,1)S(1)} %slice.32), channel_id=1, source_target_pairs={{0,1},{1,0},{2,3},{3,2},{4,5},{5,4},{6,7},{7,6},{8,9},{9,8},{10,11... | collective-permute-start | bytes 98312 | tf_op jit(solution)/shard_map/ppermute | solution.py:498
  26.8 4.1 %collective-permute-start.4 = (bf16[8,32,64]{2,1,0:T(8,128)(2,1)S(1)}, bf16[8,32,64]{2,1,0:T(8,128)(2,1)S(1)}, u32[]{:S(2)}, u32[]{:S(2)}) collective-permute-start(bf16[8,32,64]{2,1,0:T(8,128)(2,1)S(1)} %slice.32), channel_id=1, source_target_pairs={{0,3},{1,2},{2,1},{3,0},{4,7},{5,6},{6,5},{7,4},{8,11},{9,10},{10,... | collective-permute-start | bytes 98312 | tf_op jit(solution)/shard_map/ppermute | solution.py:498
  29.2 3.7 %collective-permute-start.1 = (f32[32,4]{1,0:T(8,128)S(1)}, f32[32,4]{1,0:T(8,128)S(1)}, u32[]{:S(2)}, u32[]{:S(2)}) collective-permute-start(f32[32,4]{1,0:T(8,128)S(1)} %copy.35.refs_0_), channel_id=1, source_target_pairs={{0,2},{1,3},{2,0},{3,1},{4,6},{5,7},{6,4},{7,5},{8,10},{9,11},{10,... | collective-permute-start | bytes 1544 | tf_op jit(solution)/shard_map/ppermute | solution.py:30
  33.6 7.4 %collective-permute-start.6 = (bf16[272,128]{1,0:T(8,128)(2,1)S(1)}, bf16[272,128]{1,0:T(8,128)(2,1)S(1)}, u32[]{:S(2)}, u32[]{:S(2)}) collective-permute-start(bf16[272,128]{1,0:T(8,128)(2,1)S(1)} %get-tuple-element.53), channel_id=1, source_target_pairs={{0,4},{4,0},{8,12},{12,8},{16,20},{20,16},{24,28},{28,24},{1,5},{5... | collective-permute-start | bytes 208904 | tf_op jit(solution)/shard_map/ppermute | solution.py:530
  35.1 7.3 %collective-permute-start.7 = (bf16[272,128]{1,0:T(8,128)(2,1)S(1)}, bf16[272,128]{1,0:T(8,128)(2,1)S(1)}, u32[]{:S(2)}, u32[]{:S(2)}) collective-permute-start(bf16[272,128]{1,0:T(8,128)(2,1)S(1)} %get-tuple-element.54), channel_id=1, source_target_pairs={{0,8},{4,12},{8,0},{12,4},{16,24},{20,28},{24,16},{28,20},{1,9},{5... | collective-permute-start | bytes 208904 | tf_op jit(solution)/shard_map/ppermute | solution.py:530
  35.1 9.7 %collective-permute-start.8 = (bf16[272,128]{1,0:T(8,128)(2,1)S(1)}, bf16[272,128]{1,0:T(8,128)(2,1)S(1)}, u32[]{:S(2)}, u32[]{:S(2)}) collective-permute-start(bf16[272,128]{1,0:T(8,128)(2,1)S(1)} %get-tuple-element.55), channel_id=1, source_target_pairs={{0,12},{4,8},{8,4},{12,0},{16,28},{20,24},{24,20},{28,16},{1,13},{... | collective-permute-start | bytes 208904 | tf_op jit(solution)/shard_map/ppermute | solution.py:530
  37.1 10.3 %collective-permute-start.9 = (bf16[272,128]{1,0:T(8,128)(2,1)S(1)}, bf16[272,128]{1,0:T(8,128)(2,1)S(1)}, u32[]{:S(2)}, u32[]{:S(2)}) collective-permute-start(bf16[272,128]{1,0:T(8,128)(2,1)S(1)} %get-tuple-element.56), channel_id=1, source_target_pairs={{0,16},{4,20},{8,24},{12,28},{16,0},{20,4},{24,8},{28,12},{1,17},{... | collective-permute-start | bytes 208904 | tf_op jit(solution)/shard_map/ppermute | solution.py:530
  37.3 12.8 %collective-permute-start.10 = (bf16[272,128]{1,0:T(8,128)(2,1)S(1)}, bf16[272,128]{1,0:T(8,128)(2,1)S(1)}, u32[]{:S(2)}, u32[]{:S(2)}) collective-permute-start(bf16[272,128]{1,0:T(8,128)(2,1)S(1)} %get-tuple-element.57), channel_id=1, source_target_pairs={{0,20},{4,16},{8,28},{12,24},{16,4},{20,0},{24,12},{28,8},{1,21},{... | collective-permute-start | bytes 208904 | tf_op jit(solution)/shard_map/ppermute | solution.py:530
  40.9 9.2 %collective-permute-start.11 = (bf16[272,128]{1,0:T(8,128)(2,1)S(1)}, bf16[272,128]{1,0:T(8,128)(2,1)S(1)}, u32[]{:S(2)}, u32[]{:S(2)}) collective-permute-start(bf16[272,128]{1,0:T(8,128)(2,1)S(1)} %get-tuple-element.58), channel_id=1, source_target_pairs={{0,24},{4,28},{8,16},{12,20},{16,8},{20,12},{24,0},{28,4},{1,25},{... | collective-permute-start | bytes 208904 | tf_op jit(solution)/shard_map/ppermute | solution.py:530
  42.4 7.7 %collective-permute-start.12 = (bf16[272,128]{1,0:T(8,128)(2,1)S(1)}, bf16[272,128]{1,0:T(8,128)(2,1)S(1)}, u32[]{:S(2)}, u32[]{:S(2)}) collective-permute-start(bf16[272,128]{1,0:T(8,128)(2,1)S(1)} %get-tuple-element.59), channel_id=1, source_target_pairs={{0,28},{4,24},{8,20},{12,16},{16,12},{20,8},{24,4},{28,0},{1,29},{... | collective-permute-start | bytes 208904 | tf_op jit(solution)/shard_map/ppermute | solution.py:530
  50.1 13.1 %collective-permute-start.13 = (bf16[8,272,128]{2,1,0:T(8,128)(2,1)S(1)}, bf16[8,272,128]{2,1,0:T(8,128)(2,1)S(1)}, u32[]{:S(2)}, u32[]{:S(2)}) collective-permute-start(bf16[8,272,128]{2,1,0:T(8,128)(2,1)S(1)} %place_blocks.1.grads_ref.refs_0_), channel_id=1, source_target_pairs={{4,0},{8,4},{12,8},{16,12},{20,16},{24,20},{28,24},{5,1},{9,5},{13... | collective-permute-start | bytes 1671176 | tf_op jit(solution)/shard_map/ppermute | solution.py:24
  58.0 6.9 %collective-permute-start.18 = (bf16[128,1152]{1,0:T(8,128)(2,1)}, bf16[128,1152]{1,0:T(8,128)(2,1)}, u32[]{:S(2)}, u32[]{:S(2)}) collective-permute-start(bf16[128,1152]{1,0:T(8,128)(2,1)} %get-tuple-element.80), channel_id=1, source_target_pairs={{0,1},{1,0},{2,3},{3,2},{4,5},{5,4},{6,7},{7,6},{8,9},{9,8},{10,11... | collective-permute-start | bytes 884744 | tf_op jit(solution)/shard_map/ppermute | solution.py:74
  58.0 7.9 %collective-permute-start.15 = (bf16[64,1152]{1,0:T(8,128)(2,1)}, bf16[64,1152]{1,0:T(8,128)(2,1)S(1)}, u32[]{:S(2)}, u32[]{:S(2)}) collective-permute-start(bf16[64,1152]{1,0:T(8,128)(2,1)} %copy-done.4), channel_id=1, source_target_pairs={{0,3},{1,2},{2,1},{3,0},{4,7},{5,6},{6,5},{7,4},{8,11},{9,10},{10,... | collective-permute-start | bytes 442376 | tf_op jit(solution)/shard_map/ppermute | solution.py:74
  59.5 8.0 %collective-permute-start.16 = (bf16[64,1152]{1,0:T(8,128)(2,1)}, bf16[64,1152]{1,0:T(8,128)(2,1)S(1)}, u32[]{:S(2)}, u32[]{:S(2)}) collective-permute-start(bf16[64,1152]{1,0:T(8,128)(2,1)} %copy-done.3), channel_id=1, source_target_pairs={{0,2},{1,3},{2,0},{3,1},{4,6},{5,7},{6,4},{7,5},{8,10},{9,11},{10,... | collective-permute-start | bytes 442376 | tf_op jit(solution)/shard_map/ppermute | solution.py:74
  60.1 7.4 %collective-permute-start.17 = (bf16[64,1152]{1,0:T(8,128)(2,1)S(1)}, bf16[64,1152]{1,0:T(8,128)(2,1)S(1)}, u32[]{:S(2)}, u32[]{:S(2)}) collective-permute-start(bf16[64,1152]{1,0:T(8,128)(2,1)S(1)} %get-tuple-element.78), channel_id=1, source_target_pairs={{0,1},{1,0},{2,3},{3,2},{4,5},{5,4},{6,7},{7,6},{8,9},{9,8},{10,11... | collective-permute-start | bytes 442376 | tf_op jit(solution)/shard_map/ppermute | solution.py:74
  64.3 3.3 %collective-permute-start.14 = (bf16[128,1152]{1,0:T(8,128)(2,1)S(1)}, bf16[128,1152]{1,0:T(8,128)(2,1)S(1)}, u32[]{:S(2)}, u32[]{:S(2)}) collective-permute-start(bf16[128,1152]{1,0:T(8,128)(2,1)S(1)} %get-tuple-element.74), channel_id=1, source_target_pairs={{0,1},{1,0},{2,3},{3,2},{4,5},{5,4},{6,7},{7,6},{8,9},{9,8},{10,11... | collective-permute-start | bytes 884744 | tf_op jit(solution)/shard_map/ppermute | solution.py:74
  67.7 9.9 %collective-permute-start.22 = (bf16[2,2,1,1,1,8,1152]{6,5,3,2,1,0,4:T(8,128)(2,1)S(1)}, bf16[2,2,1,1,1,8,1152]{6,5,3,2,1,0,4:T(8,128)(2,1)S(1)}, u32[]{:S(2)}, u32[]{:S(2)}) collective-permute-start(bf16[2,2,1,1,1,8,1152]{6,5,3,2,1,0,4:T(8,128)(2,1)S(1)} %constant_dynamic-slice_fusion.3), channel_id=1, source_target_pairs={{0,4},{1,5},{2,6},{3,7},{4,0},{5,1},{6,2},{7,3},{8,12},{9,13},{10,... | collective-permute-start | bytes 221192 | tf_op jit(solution)/shard_map/ppermute | solution.py:62
  70.6 7.8 %collective-permute-start.19 = (bf16[2,2,1,1,1,8,2304]{6,5,3,2,1,0,4:T(8,128)(2,1)S(1)}, bf16[2,2,1,1,1,8,2304]{6,5,3,2,1,0,4:T(8,128)(2,1)S(1)}, u32[]{:S(2)}, u32[]{:S(2)}) collective-permute-start(bf16[2,2,1,1,1,8,2304]{6,5,3,2,1,0,4:T(8,128)(2,1)S(1)} %get-tuple-element.97), channel_id=1, source_target_pairs={{0,6},{1,7},{2,4},{3,5},{4,2},{5,3},{6,0},{7,1},{8,14},{9,15},{10,... | collective-permute-start | bytes 442376 | tf_op jit(solution)/shard_map/ppermute | solution.py:62
  71.5 8.3 %collective-permute-start.21 = (bf16[2,2,1,1,1,8,2304]{6,5,3,2,1,0,4:T(8,128)(2,1)S(1)}, bf16[2,2,1,1,1,8,2304]{6,5,3,2,1,0,4:T(8,128)(2,1)S(1)}, u32[]{:S(2)}, u32[]{:S(2)}) collective-permute-start(bf16[2,2,1,1,1,8,2304]{6,5,3,2,1,0,4:T(8,128)(2,1)S(1)} %get-tuple-element.98), channel_id=1, source_target_pairs={{0,4},{1,5},{2,6},{3,7},{4,0},{5,1},{6,2},{7,3},{8,12},{9,13},{10,... | collective-permute-start | bytes 442376 | tf_op jit(solution)/shard_map/ppermute | solution.py:62
  73.5 6.4 %collective-permute-start.20 = (bf16[2,2,1,1,1,8,2304]{6,5,3,2,1,0,4:T(8,128)(2,1)S(1)}, bf16[2,2,1,1,1,8,2304]{6,5,3,2,1,0,4:T(8,128)(2,1)S(1)}, u32[]{:S(2)}, u32[]{:S(2)}) collective-permute-start(bf16[2,2,1,1,1,8,2304]{6,5,3,2,1,0,4:T(8,128)(2,1)S(1)} %get-tuple-element.99), channel_id=1, source_target_pairs={{0,2},{1,3},{2,0},{3,1},{4,6},{5,7},{6,4},{7,5},{8,10},{9,11},{10,... | collective-permute-start | bytes 442376 | tf_op jit(solution)/shard_map/ppermute | solution.py:62
  80.0 6.2 %collective-permute-start.23 = (bf16[1,1,1,1,1,8,3456]{6,5,3,2,1,0,4:T(8,128)(2,1)S(1)}, bf16[1,1,1,1,1,8,3456]{6,5,3,2,1,0,4:T(8,128)(2,1)S(1)}, u32[]{:S(2)}, u32[]{:S(2)}) collective-permute-start(bf16[1,1,1,1,1,8,3456]{6,5,3,2,1,0,4:T(8,128)(2,1)S(1)} %get-tuple-element.100), channel_id=1, source_target_pairs={{0,24},{1,25},{2,26},{3,27},{4,28},{5,29},{6,30},{7,31},{8,16},{9,... | collective-permute-start | bytes 165896 | tf_op jit(solution)/shard_map/ppermute | solution.py:62
  83.2 5.6 %collective-permute-start.25 = (bf16[1,1,1,1,1,8,3456]{6,5,3,2,1,0,4:T(8,128)(2,1)S(1)}, bf16[1,1,1,1,1,8,3456]{6,5,3,2,1,0,4:T(8,128)(2,1)S(1)}, u32[]{:S(2)}, u32[]{:S(2)}) collective-permute-start(bf16[1,1,1,1,1,8,3456]{6,5,3,2,1,0,4:T(8,128)(2,1)S(1)} %get-tuple-element.101), channel_id=1, source_target_pairs={{0,16},{1,17},{2,18},{3,19},{4,20},{5,21},{6,22},{7,23},{8,24},{9,... | collective-permute-start | bytes 165896 | tf_op jit(solution)/shard_map/ppermute | solution.py:62
  84.0 4.8 %collective-permute-start.24 = (bf16[1,1,1,1,1,8,3456]{6,5,3,2,1,0,4:T(8,128)(2,1)S(1)}, bf16[1,1,1,1,1,8,3456]{6,5,3,2,1,0,4:T(8,128)(2,1)S(1)}, u32[]{:S(2)}, u32[]{:S(2)}) collective-permute-start(bf16[1,1,1,1,1,8,3456]{6,5,3,2,1,0,4:T(8,128)(2,1)S(1)} %get-tuple-element.102), channel_id=1, source_target_pairs={{0,8},{1,9},{2,10},{3,11},{4,12},{5,13},{6,14},{7,15},{8,0},{9,1},... | collective-permute-start | bytes 165896 | tf_op jit(solution)/shard_map/ppermute | solution.py:62
  (11 other events, 55.9 us)

commit v7 on v6

--- a/solution.py
+++ b/solution.py
@@ -131,7 +131,7 @@
     _, rows, fine_depth, width_in = out_grad.shape
     width_deep = w_up.shape[1]
     cells = rows * fine_depth // 4
-    steps = rows // 8
+    steps = rows // 16
     return pl.pallas_call(
         deep_kernel,
         in_specs=[pl.BlockSpec(memory_space=pltpu.HBM)] * 2,
@@ -224,14 +224,15 @@
         grads_ref[:, columns] = block_of(packed_ref, block, grads_ref.shape[0])
     cells = (shifted_ref.shape[0] - 2 * depth) // 2
     width = 3 * LANES
-    for px, bits in jobs:
+    starts = (cells, 0, cells + depth)
+    for pieces, bits in jobs:
         count = 1 << bits if rows else 1
         outs, out_refs = out_refs[:count], out_refs[count:]
-        for ky, start in ((1, 0), (0, cells), (2, cells + depth)):
+        for place, (px, ky) in enumerate(pieces):
             span = grads_ref.shape[1] if ky == 0 else cells
             sums = scale * jnp.dot(
                 grads_ref[:, :span],
-                shifted_ref[start : start + span, px * width : (px + 1) * width],
+                shifted_ref[starts[ky] : starts[ky] + span, px * width : (px + 1) * width],
                 preferred_element_type=jnp.float32,
             )
             parts = [sums]
@@ -244,7 +245,7 @@
                         jnp.where(own, parts[n ^ (1 << bit)], part) for n, part in enumerate(parts)
                     ]
             for out_ref, part in zip(outs, parts):
-                out_ref[:, ky * width : (ky + 1) * width] = part.astype(jnp.bfloat16)
+                out_ref[:, place * width : (place + 1) * width] = part.astype(jnp.bfloat16)
 
 
 def shift_and_tap_kernel(scale, depth, rows, jobs, own_ref, grads_ref, fine_ref, *refs):
@@ -269,14 +270,14 @@
             pltpu.VMEM(shifted_shape(source, planes), jnp.bfloat16),
             pltpu.VMEM((2 * planes, fine_depth + 8, width), jnp.float32),
         ]
-    columns = 9 * LANES
+    widths = [3 * LANES * len(pieces) for pieces, _ in jobs]
     rows = width_deep >> place_bits()
     place = lax.axis_index("slab") * lax.axis_size("grp") + lax.axis_index("grp")
     inside = rows % 8 == 0
     counts = [1 << bits if inside else 1 for _, bits in jobs]
     outs = [
         jax.ShapeDtypeStruct((width_deep // count, columns), jnp.bfloat16)
-        for count in counts
+        for count, columns in zip(counts, widths)
         for _ in range(count)
     ]
     arrays = pl.pallas_call(
@@ -288,14 +289,14 @@
         scratch_shapes=[*scratch, pltpu.VMEM(shape, jnp.bfloat16)],
         compiler_params=pltpu.CompilerParams(vmem_limit_bytes=20 << 20),
         cost_estimate=pl.CostEstimate(
-            flops=2 * width_deep * padded * columns * len(jobs),
-            bytes_accessed=2 * (width_deep * padded + (padded + width_deep) * columns * len(jobs)),
+            flops=2 * width_deep * padded * sum(widths),
+            bytes_accessed=2 * (width_deep * padded + (padded + width_deep) * sum(widths)),
             transcendentals=0,
         ),
         name="tap_sums",
     )(place.astype(jnp.int32).reshape(1), grads, source)
     results = []
-    for (_, bits), count in zip(jobs, counts):
+    for (_, bits), count, columns in zip(jobs, counts, widths):
         parts, arrays = tuple(arrays[:count]), arrays[count:]
         if not inside:
             held = parts[0].reshape(-1, 1 << bits, rows, columns)
@@ -545,14 +546,16 @@
     grad_scale = 1.0 / math.sqrt(cell_total)
     bits = place_bits()
     stages = [tuple(range(b, min(b + 2, bits))) for b in range(3, bits, 2)]
-    parts = tap_sums(here, fine_input, depth, grad_scale, ((0, 2), (1, 1)), (width_deep, padded))
+    row = tuple((0, ky) for ky in range(3))
+    jobs = ((tuple((1, ky) for ky in range(3)), 1), (row, 2))
+    parts = tap_sums(here, fine_input, depth, grad_scale, jobs, (width_deep, padded))
     parts, here_again = lax.optimization_barrier((parts, here))
-    middle_parts, last_parts = parts
+    last_parts, middle_parts = parts
     after = from_next(here, "slab")
     grad_input = input_plane(0, (here_again,), (1,), w_down, fine_input.shape, padded)
     grad_input, fine_again = lax.optimization_barrier((grad_input, fine_input))
     shifted = shifted_fine(fine_again, fine_input.shape[0] - 1)
-    (parts,) = tap_sums(after, shifted, depth, grad_scale, ((0, 1),), (width_deep, padded))
+    (parts,) = tap_sums(after, shifted, depth, grad_scale, ((row, 1),), (width_deep, padded))
     kept, last_kept, parts = lax.optimization_barrier((middle_parts[0], last_parts[0], parts))
     middle_taps = exchange_parts((kept, *middle_parts[1:]), 2)
     last_taps = exchange_parts((last_kept, *last_parts[1:]), 1)

time: 89.9 us -> 89 us (0.990)
  Pallas kernels: 16 us -> 14.6 us
  transfers between devices with their start and end apart: 27 -> 27, of which waited for: 12 -> 13; matrix products, arithmetic and copies ran while one was open for 4% -> 4% of each run, Pallas kernels for 12% -> 12%
where the time goes in v7:
time: 89 us; the launch traced here: 88.7 us
  starting transfers between devices  38.4 us (43%)
  waiting for transfers between devices  27.3 us (31%)
  Pallas kernels  14.6 us (16%)
  local copies, waits for them, and re-layouts  4.58 us (5%)
  other arithmetic  2.89 us (3%)
  between operations  0.94 us (1%)
    ppermute x7, starting transfers between devices, local(): lax.ppermute(act_grads[mask], 'slab', [(i, i ^ mask) for i in range(slabs)])  11.2 us
    ppermute x7, starting transfers between devices, exchange(): arrived = lax.ppermute(pick(flips), ('slab', 'grp'), pairs)  11 us
    all_to_all x1, waiting for transfers between devices, local(): lax.all_to_all(deep_bf, 'slab', split_axis=0, concat_axis=0, tiled=True)  10.5 us
    all_to_all x1, starting transfers between devices, local(): lax.all_to_all(deep_bf, 'slab', split_axis=0, concat_axis=0, tiled=True)  7.27 us
    ppermute x7, waiting for transfers between devices, exchange(): arrived = lax.ppermute(pick(flips), ('slab', 'grp'), pairs)  6.19 us
    pallas_call x2, Pallas kernels, input_plane(): pl.pallas_call(functools.partial(input_kernel, taps_of), grid=(1,), in_sp...  6.14 us
    ppermute x7, waiting for transfers between devices, local(): lax.ppermute(act_grads[mask], 'slab', [(i, i ^ mask) for i in range(slabs)])  5.34 us
    pallas_call x2, Pallas kernels, tap_sums(): pl.pallas_call(functools.partial(kernel, scale, depth, rows if inside els...  3.81 us
  transfers between devices with their start and end apart: 27, of which 13 were waited for; matrix products, arithmetic and copies ran while one was open for 4% of the time, Pallas kernels for 12%

profile of v7, /device:TPU:0, one launch (start us, length us, event | category | flops | bytes accessed | tf_op | source)
XLA Modules:
  0.0 88.7 jit_solution(7197415417029758521)
XLA Ops:
  0.7 3.5 %deep_gradient.1 = bf16[256,1024]{1,0:T(8,128)(2,1)} custom-call(bf16[2,32,128,128]{3,2,1,0:T(8,128)(2,1)} %rows_ref.1, bf16[8,256,128]{2,1,0:T(8,128)(2,1)} %taps_ref.1), custom_call_target="tpu_custom_call" | custom-call | flops 536870912 | bytes 3145728 | tf_op jit(solution)/shard_map/deep_gradient/pallas_call | solution.py:135
  4.2 7.3 %all-to-all-start = ((bf16[8,32,1024]{2,1,0:T(8,128)(2,1)}), bf16[8,32,1024]{2,1,0:T(8,128)(2,1)S(1)}, u32[]{:S(2)}, u32[]{:S(2)}) async-start(bf16[8,32,1024]{2,1,0:T(8,128)(2,1)} %bitcast.31), calls=%async_computation | async-start | bytes 1048576 | tf_op jit(solution)/shard_map/all_to_all | solution.py:469
  13.8 1.5 %collective-permute-done.3 = bf16[2,8,32,64]{3,2,1,0:T(8,128)(2,1)S(1)} collective-permute-done((bf16[2,8,32,64]{3,2,1,0:T(8,128)(2,1)S(1)}, bf16[2,8,32,64]{3,2,1,0:T(8,128)(2,1)S(1)}, u32[]{:S(2)}, u32[]{:S(2)}) %collective-permute-start.3) | collective-permute-done | bytes 65568 | tf_op jit(solution)/shard_map/ppermute | solution.py:24
  15.4 10.5 %all-to-all-done = bf16[8,32,1024]{2,1,0:T(8,128)(2,1)S(1)} async-done(((bf16[8,32,1024]{2,1,0:T(8,128)(2,1)}), bf16[8,32,1024]{2,1,0:T(8,128)(2,1)S(1)}, u32[]{:S(2)}, u32[]{:S(2)}) %all-to-all-start) | async-done | bytes 524320 | tf_op jit(solution)/shard_map/all_to_all | solution.py:469
  26.0 1.6 %collective-permute-start.4 = (bf16[8,32,64]{2,1,0:T(8,128)(2,1)S(1)}, bf16[8,32,64]{2,1,0:T(8,128)(2,1)S(1)}, u32[]{:S(2)}, u32[]{:S(2)}) collective-permute-start(bf16[8,32,64]{2,1,0:T(8,128)(2,1)S(1)} %slice.32), channel_id=1, source_target_pairs={{0,3},{1,2},{2,1},{3,0},{4,7},{5,6},{6,5},{7,4},{8,11},{9,10},{10,... | collective-permute-start | bytes 98312 | tf_op jit(solution)/shard_map/ppermute | solution.py:499
  28.4 1.5 %collective-permute-start.1 = (f32[32,4]{1,0:T(8,128)S(1)}, f32[32,4]{1,0:T(8,128)S(1)}, u32[]{:S(2)}, u32[]{:S(2)}) collective-permute-start(f32[32,4]{1,0:T(8,128)S(1)} %copy.35.refs_0_), channel_id=1, source_target_pairs={{0,2},{1,3},{2,0},{3,1},{4,6},{5,7},{6,4},{7,5},{8,10},{9,11},{10,... | collective-permute-start | bytes 1544 | tf_op jit(solution)/shard_map/ppermute | solution.py:30
  32.8 1.5 %collective-permute-start.6 = (bf16[272,128]{1,0:T(8,128)(2,1)S(1)}, bf16[272,128]{1,0:T(8,128)(2,1)S(1)}, u32[]{:S(2)}, u32[]{:S(2)}) collective-permute-start(bf16[272,128]{1,0:T(8,128)(2,1)S(1)} %get-tuple-element.53), channel_id=1, source_target_pairs={{0,4},{4,0},{8,12},{12,8},{16,20},{20,16},{24,28},{28,24},{1,5},{5... | collective-permute-start | bytes 208904 | tf_op jit(solution)/shard_map/ppermute | solution.py:531
  34.4 2.0 %collective-permute-start.8 = (bf16[272,128]{1,0:T(8,128)(2,1)S(1)}, bf16[272,128]{1,0:T(8,128)(2,1)S(1)}, u32[]{:S(2)}, u32[]{:S(2)}) collective-permute-start(bf16[272,128]{1,0:T(8,128)(2,1)S(1)} %get-tuple-element.55), channel_id=1, source_target_pairs={{0,12},{4,8},{8,4},{12,0},{16,28},{20,24},{24,20},{28,16},{1,13},{... | collective-permute-start | bytes 208904 | tf_op jit(solution)/shard_map/ppermute | solution.py:531
  36.5 3.7 %collective-permute-start.10 = (bf16[272,128]{1,0:T(8,128)(2,1)S(1)}, bf16[272,128]{1,0:T(8,128)(2,1)S(1)}, u32[]{:S(2)}, u32[]{:S(2)}) collective-permute-start(bf16[272,128]{1,0:T(8,128)(2,1)S(1)} %get-tuple-element.57), channel_id=1, source_target_pairs={{0,20},{4,16},{8,28},{12,24},{16,4},{20,0},{24,12},{28,8},{1,21},{... | collective-permute-start | bytes 208904 | tf_op jit(solution)/shard_map/ppermute | solution.py:531
  41.7 2.4 %collective-permute-start.12 = (bf16[272,128]{1,0:T(8,128)(2,1)S(1)}, bf16[272,128]{1,0:T(8,128)(2,1)S(1)}, u32[]{:S(2)}, u32[]{:S(2)}) collective-permute-start(bf16[272,128]{1,0:T(8,128)(2,1)S(1)} %get-tuple-element.59), channel_id=1, source_target_pairs={{0,28},{4,24},{8,20},{12,16},{16,12},{20,8},{24,4},{28,0},{1,29},{... | collective-permute-start | bytes 208904 | tf_op jit(solution)/shard_map/ppermute | solution.py:531
  44.0 2.7 %collective-permute-done.9.refs_4_ = bf16[272,128]{1,0:T(8,128)(2,1)S(1)} collective-permute-done((bf16[272,128]{1,0:T(8,128)(2,1)S(1)}, bf16[272,128]{1,0:T(8,128)(2,1)S(1)}, u32[]{:S(2)}, u32[]{:S(2)}) %collective-permute-start.9) | collective-permute-done | bytes 69664 | tf_op jit(solution)/shard_map/ppermute | solution.py:531
  46.7 2.6 %collective-permute-done.10.refs_5_ = bf16[272,128]{1,0:T(8,128)(2,1)S(1)} collective-permute-done((bf16[272,128]{1,0:T(8,128)(2,1)S(1)}, bf16[272,128]{1,0:T(8,128)(2,1)S(1)}, u32[]{:S(2)}, u32[]{:S(2)}) %collective-permute-start.10) | collective-permute-done | bytes 69664 | tf_op jit(solution)/shard_map/ppermute | solution.py:531
  49.4 1.5 %collective-permute-start.13 = (bf16[8,272,128]{2,1,0:T(8,128)(2,1)S(1)}, bf16[8,272,128]{2,1,0:T(8,128)(2,1)S(1)}, u32[]{:S(2)}, u32[]{:S(2)}) collective-permute-start(bf16[8,272,128]{2,1,0:T(8,128)(2,1)S(1)} %place_blocks.1.grads_ref.refs_0_), channel_id=1, source_target_pairs={{4,0},{8,4},{12,8},{16,12},{20,16},{24,20},{28,24},{5,1},{9,5},{13... | collective-permute-start | bytes 1671176 | tf_op jit(solution)/shard_map/ppermute | solution.py:24
  50.9 1.6 %copy-done.1 = bf16[2,32,128,128]{3,2,1,0:T(8,128)(2,1)S(1)} copy-done((bf16[2,32,128,128]{3,2,1,0:T(8,128)(2,1)S(1)}, bf16[2,32,128,128]{3,2,1,0:T(8,128)(2,1)}, u32[]{:S(2)}) %copy-start.1) | copy-done | bytes 2097176
  52.5 2.7 %tap_sums.2 = (bf16[128,1152]{1,0:T(8,128)(2,1)S(1)}, bf16[128,1152]{1,0:T(8,128)(2,1)}, bf16[64,1152]{1,0:T(8,128)(2,1)S(1)}, bf16[64,1152]{1,0:T(8,128)(2,1)S(...) custom-call(s32[1]{0:T(128)} %bitcast.own_ref, bf16[8,272,128]{2,1,0:T(8,128)(2,1)S(1)} %place_blocks.1.grads_ref.refs_0_, ...), custom_call_target="tpu_custom_call" | custom-call | flops 1358954496 | bytes 7077888 | tf_op jit(solution)/shard_map/tap_sums/pallas_call | solution.py:283
  56.6 1.5 %collective-permute-start.15 = (bf16[64,1152]{1,0:T(8,128)(2,1)}, bf16[64,1152]{1,0:T(8,128)(2,1)S(1)}, u32[]{:S(2)}, u32[]{:S(2)}) collective-permute-start(bf16[64,1152]{1,0:T(8,128)(2,1)} %copy-done.4), channel_id=1, source_target_pairs={{0,3},{1,2},{2,1},{3,0},{4,7},{5,6},{6,5},{7,4},{8,11},{9,10},{10,... | collective-permute-start | bytes 442376 | tf_op jit(solution)/shard_map/ppermute | solution.py:74
  58.7 2.6 %input_gradient.2.refs_3_ = bf16[2,32,128,128]{3,2,1,0:T(8,128)(2,1)} custom-call(bf16[8,272,128]{2,1,0:T(8,128)(2,1)S(1)} %place_blocks.1.grads_ref.refs_0_, bf16[27,128,256]{2,1,0:T(8,128)(2,1)S(1)} %copy-done), custom_call_target="tpu_custom_call" | custom-call | tf_op jit(solution)/shard_map/input_gradient/pallas_call | solution.py:370
  64.5 1.6 %collective-permute-done.16 = bf16[64,1152]{1,0:T(8,128)(2,1)S(1)} collective-permute-done((bf16[64,1152]{1,0:T(8,128)(2,1)}, bf16[64,1152]{1,0:T(8,128)(2,1)S(1)}, u32[]{:S(2)}, u32[]{:S(2)}) %collective-permute-start.16) | collective-permute-done | bytes 147488 | tf_op jit(solution)/shard_map/ppermute | solution.py:74
  66.3 3.0 %collective-permute-start.22 = (bf16[2,2,1,1,1,8,1152]{6,5,3,2,1,0,4:T(8,128)(2,1)S(1)}, bf16[2,2,1,1,1,8,1152]{6,5,3,2,1,0,4:T(8,128)(2,1)S(1)}, u32[]{:S(2)}, u32[]{:S(2)}) collective-permute-start(bf16[2,2,1,1,1,8,1152]{6,5,3,2,1,0,4:T(8,128)(2,1)S(1)} %constant_dynamic-slice_fusion.3), channel_id=1, source_target_pairs={{0,4},{1,5},{2,6},{3,7},{4,0},{5,1},{6,2},{7,3},{8,12},{9,13},{10,... | collective-permute-start | bytes 221192 | tf_op jit(solution)/shard_map/ppermute | solution.py:62
  70.3 2.0 %collective-permute-start.21 = (bf16[2,2,1,1,1,8,2304]{6,5,3,2,1,0,4:T(8,128)(2,1)S(1)}, bf16[2,2,1,1,1,8,2304]{6,5,3,2,1,0,4:T(8,128)(2,1)S(1)}, u32[]{:S(2)}, u32[]{:S(2)}) collective-permute-start(bf16[2,2,1,1,1,8,2304]{6,5,3,2,1,0,4:T(8,128)(2,1)S(1)} %get-tuple-element.98), channel_id=1, source_target_pairs={{0,4},{1,5},{2,6},{3,7},{4,0},{5,1},{6,2},{7,3},{8,12},{9,13},{10,... | collective-permute-start | bytes 442376 | tf_op jit(solution)/shard_map/ppermute | solution.py:62
  72.9 3.5 %input_gradient.3 = bf16[2,32,128,128]{3,2,1,0:T(8,128)(2,1)} custom-call(bf16[8,272,128]{2,1,0:T(8,128)(2,1)S(1)} %place_blocks.1.grads_ref.refs_0_, bf16[8,272,128]{2,1,0:T(8,128)(2,1)S(1)} %collective-permute-done.13.packed_ref.refs_1_, bf16[27,128,256]{2,1,0:T(8,128)(2,1)S(1)} %copy-done, ...), custom_call_target="tpu_custom_call", output_to_operand_aliasing={{}: (3, {})} | custom-call | tf_op jit(solution)/shard_map/input_gradient/pallas_call | solution.py:370
  77.1 2.0 %collective-permute-done.21 = bf16[2,2,1,1,1,8,2304]{6,5,3,2,1,0,4:T(8,128)(2,1)S(1)} collective-permute-done((bf16[2,2,1,1,1,8,2304]{6,5,3,2,1,0,4:T(8,128)(2,1)S(1)}, bf16[2,2,1,1,1,8,2304]{6,5,3,2,1,0,4:T(8,128)(2,1)S(1)}, u32[]{:S(2)}, u32[]{:S(2)}) %collective-permute-start.21) | collective-permute-done | bytes 147488 | tf_op jit(solution)/shard_map/ppermute | solution.py:62
  79.3 2.5 %collective-permute-start.23 = (bf16[1,1,1,1,1,8,3456]{6,5,3,2,1,0,4:T(8,128)(2,1)S(1)}, bf16[1,1,1,1,1,8,3456]{6,5,3,2,1,0,4:T(8,128)(2,1)S(1)}, u32[]{:S(2)}, u32[]{:S(2)}) collective-permute-start(bf16[1,1,1,1,1,8,3456]{6,5,3,2,1,0,4:T(8,128)(2,1)S(1)} %get-tuple-element.100), channel_id=1, source_target_pairs={{0,24},{1,25},{2,26},{3,27},{4,28},{5,29},{6,30},{7,31},{8,16},{9,... | collective-permute-start | bytes 165896 | tf_op jit(solution)/shard_map/ppermute | solution.py:62
  85.4 2.6 %collective-permute-done.25 = bf16[1,1,1,1,1,8,3456]{6,5,3,2,1,0,4:T(8,128)(2,1)S(1)} collective-permute-done((bf16[1,1,1,1,1,8,3456]{6,5,3,2,1,0,4:T(8,128)(2,1)S(1)}, bf16[1,1,1,1,1,8,3456]{6,5,3,2,1,0,4:T(8,128)(2,1)S(1)}, u32[]{:S(2)}, u32[]{:S(2)}) %collective-permute-start.25) | collective-permute-done | bytes 55328 | tf_op jit(solution)/shard_map/ppermute | solution.py:62
  (82 shorter events, 19.8 us)
Async XLA Ops:
  4.2 21.8 %all-to-all-start = ((bf16[8,32,1024]{2,1,0:T(8,128)(2,1)}), bf16[8,32,1024]{2,1,0:T(8,128)(2,1)S(1)}, u32[]{:S(2)}, u32[]{:S(2)}) async-start(bf16[8,32,1024]{2,1,0:T(8,128)(2,1)} %bitcast.31), calls=%async_computation | async-start | bytes 1048576 | tf_op jit(solution)/shard_map/all_to_all | solution.py:469
  12.1 3.2 %collective-permute-start.3 = (bf16[2,8,32,64]{3,2,1,0:T(8,128)(2,1)S(1)}, bf16[2,8,32,64]{3,2,1,0:T(8,128)(2,1)S(1)}, u32[]{:S(2)}, u32[]{:S(2)}) collective-permute-start(bf16[2,8,32,64]{3,2,1,0:T(8,128)(2,1)S(1)} %pad_maximum_fusion.1), channel_id=1, source_target_pairs={{1,0},{2,1},{3,2},{5,4},{6,5},{7,6},{9,8},{10,9},{11,10},{13,12},{... | collective-permute-start | bytes 196616 | tf_op jit(solution)/shard_map/ppermute | solution.py:24
  25.9 4.2 %collective-permute-start.5 = (bf16[8,32,64]{2,1,0:T(8,128)(2,1)S(1)}, bf16[8,32,64]{2,1,0:T(8,128)(2,1)S(1)}, u32[]{:S(2)}, u32[]{:S(2)}) collective-permute-start(bf16[8,32,64]{2,1,0:T(8,128)(2,1)S(1)} %slice.32), channel_id=1, source_target_pairs={{0,1},{1,0},{2,3},{3,2},{4,5},{5,4},{6,7},{7,6},{8,9},{9,8},{10,11... | collective-permute-start | bytes 98312 | tf_op jit(solution)/shard_map/ppermute | solution.py:499
  26.0 4.1 %collective-permute-start.4 = (bf16[8,32,64]{2,1,0:T(8,128)(2,1)S(1)}, bf16[8,32,64]{2,1,0:T(8,128)(2,1)S(1)}, u32[]{:S(2)}, u32[]{:S(2)}) collective-permute-start(bf16[8,32,64]{2,1,0:T(8,128)(2,1)S(1)} %slice.32), channel_id=1, source_target_pairs={{0,3},{1,2},{2,1},{3,0},{4,7},{5,6},{6,5},{7,4},{8,11},{9,10},{10,... | collective-permute-start | bytes 98312 | tf_op jit(solution)/shard_map/ppermute | solution.py:499
  28.4 3.7 %collective-permute-start.1 = (f32[32,4]{1,0:T(8,128)S(1)}, f32[32,4]{1,0:T(8,128)S(1)}, u32[]{:S(2)}, u32[]{:S(2)}) collective-permute-start(f32[32,4]{1,0:T(8,128)S(1)} %copy.35.refs_0_), channel_id=1, source_target_pairs={{0,2},{1,3},{2,0},{3,1},{4,6},{5,7},{6,4},{7,5},{8,10},{9,11},{10,... | collective-permute-start | bytes 1544 | tf_op jit(solution)/shard_map/ppermute | solution.py:30
  32.8 7.4 %collective-permute-start.6 = (bf16[272,128]{1,0:T(8,128)(2,1)S(1)}, bf16[272,128]{1,0:T(8,128)(2,1)S(1)}, u32[]{:S(2)}, u32[]{:S(2)}) collective-permute-start(bf16[272,128]{1,0:T(8,128)(2,1)S(1)} %get-tuple-element.53), channel_id=1, source_target_pairs={{0,4},{4,0},{8,12},{12,8},{16,20},{20,16},{24,28},{28,24},{1,5},{5... | collective-permute-start | bytes 208904 | tf_op jit(solution)/shard_map/ppermute | solution.py:531
  34.3 7.3 %collective-permute-start.7 = (bf16[272,128]{1,0:T(8,128)(2,1)S(1)}, bf16[272,128]{1,0:T(8,128)(2,1)S(1)}, u32[]{:S(2)}, u32[]{:S(2)}) collective-permute-start(bf16[272,128]{1,0:T(8,128)(2,1)S(1)} %get-tuple-element.54), channel_id=1, source_target_pairs={{0,8},{4,12},{8,0},{12,4},{16,24},{20,28},{24,16},{28,20},{1,9},{5... | collective-permute-start | bytes 208904 | tf_op jit(solution)/shard_map/ppermute | solution.py:531
  34.4 9.7 %collective-permute-start.8 = (bf16[272,128]{1,0:T(8,128)(2,1)S(1)}, bf16[272,128]{1,0:T(8,128)(2,1)S(1)}, u32[]{:S(2)}, u32[]{:S(2)}) collective-permute-start(bf16[272,128]{1,0:T(8,128)(2,1)S(1)} %get-tuple-element.55), channel_id=1, source_target_pairs={{0,12},{4,8},{8,4},{12,0},{16,28},{20,24},{24,20},{28,16},{1,13},{... | collective-permute-start | bytes 208904 | tf_op jit(solution)/shard_map/ppermute | solution.py:531
  36.4 10.3 %collective-permute-start.9 = (bf16[272,128]{1,0:T(8,128)(2,1)S(1)}, bf16[272,128]{1,0:T(8,128)(2,1)S(1)}, u32[]{:S(2)}, u32[]{:S(2)}) collective-permute-start(bf16[272,128]{1,0:T(8,128)(2,1)S(1)} %get-tuple-element.56), channel_id=1, source_target_pairs={{0,16},{4,20},{8,24},{12,28},{16,0},{20,4},{24,8},{28,12},{1,17},{... | collective-permute-start | bytes 208904 | tf_op jit(solution)/shard_map/ppermute | solution.py:531
  36.5 12.8 %collective-permute-start.10 = (bf16[272,128]{1,0:T(8,128)(2,1)S(1)}, bf16[272,128]{1,0:T(8,128)(2,1)S(1)}, u32[]{:S(2)}, u32[]{:S(2)}) collective-permute-start(bf16[272,128]{1,0:T(8,128)(2,1)S(1)} %get-tuple-element.57), channel_id=1, source_target_pairs={{0,20},{4,16},{8,28},{12,24},{16,4},{20,0},{24,12},{28,8},{1,21},{... | collective-permute-start | bytes 208904 | tf_op jit(solution)/shard_map/ppermute | solution.py:531
  40.2 9.2 %collective-permute-start.11 = (bf16[272,128]{1,0:T(8,128)(2,1)S(1)}, bf16[272,128]{1,0:T(8,128)(2,1)S(1)}, u32[]{:S(2)}, u32[]{:S(2)}) collective-permute-start(bf16[272,128]{1,0:T(8,128)(2,1)S(1)} %get-tuple-element.58), channel_id=1, source_target_pairs={{0,24},{4,28},{8,16},{12,20},{16,8},{20,12},{24,0},{28,4},{1,25},{... | collective-permute-start | bytes 208904 | tf_op jit(solution)/shard_map/ppermute | solution.py:531
  41.7 7.7 %collective-permute-start.12 = (bf16[272,128]{1,0:T(8,128)(2,1)S(1)}, bf16[272,128]{1,0:T(8,128)(2,1)S(1)}, u32[]{:S(2)}, u32[]{:S(2)}) collective-permute-start(bf16[272,128]{1,0:T(8,128)(2,1)S(1)} %get-tuple-element.59), channel_id=1, source_target_pairs={{0,28},{4,24},{8,20},{12,16},{16,12},{20,8},{24,4},{28,0},{1,29},{... | collective-permute-start | bytes 208904 | tf_op jit(solution)/shard_map/ppermute | solution.py:531
  49.4 12.5 %collective-permute-start.13 = (bf16[8,272,128]{2,1,0:T(8,128)(2,1)S(1)}, bf16[8,272,128]{2,1,0:T(8,128)(2,1)S(1)}, u32[]{:S(2)}, u32[]{:S(2)}) collective-permute-start(bf16[8,272,128]{2,1,0:T(8,128)(2,1)S(1)} %place_blocks.1.grads_ref.refs_0_), channel_id=1, source_target_pairs={{4,0},{8,4},{12,8},{16,12},{20,16},{24,20},{28,24},{5,1},{9,5},{13... | collective-permute-start | bytes 1671176 | tf_op jit(solution)/shard_map/ppermute | solution.py:24
  56.5 6.9 %collective-permute-start.18 = (bf16[128,1152]{1,0:T(8,128)(2,1)}, bf16[128,1152]{1,0:T(8,128)(2,1)}, u32[]{:S(2)}, u32[]{:S(2)}) collective-permute-start(bf16[128,1152]{1,0:T(8,128)(2,1)} %get-tuple-element.80), channel_id=1, source_target_pairs={{0,1},{1,0},{2,3},{3,2},{4,5},{5,4},{6,7},{7,6},{8,9},{9,8},{10,11... | collective-permute-start | bytes 884744 | tf_op jit(solution)/shard_map/ppermute | solution.py:74
  56.6 7.9 %collective-permute-start.15 = (bf16[64,1152]{1,0:T(8,128)(2,1)}, bf16[64,1152]{1,0:T(8,128)(2,1)S(1)}, u32[]{:S(2)}, u32[]{:S(2)}) collective-permute-start(bf16[64,1152]{1,0:T(8,128)(2,1)} %copy-done.4), channel_id=1, source_target_pairs={{0,3},{1,2},{2,1},{3,0},{4,7},{5,6},{6,5},{7,4},{8,11},{9,10},{10,... | collective-permute-start | bytes 442376 | tf_op jit(solution)/shard_map/ppermute | solution.py:74
  58.0 8.0 %collective-permute-start.16 = (bf16[64,1152]{1,0:T(8,128)(2,1)}, bf16[64,1152]{1,0:T(8,128)(2,1)S(1)}, u32[]{:S(2)}, u32[]{:S(2)}) collective-permute-start(bf16[64,1152]{1,0:T(8,128)(2,1)} %copy-done.3), channel_id=1, source_target_pairs={{0,2},{1,3},{2,0},{3,1},{4,6},{5,7},{6,4},{7,5},{8,10},{9,11},{10,... | collective-permute-start | bytes 442376 | tf_op jit(solution)/shard_map/ppermute | solution.py:74
  58.7 7.4 %collective-permute-start.17 = (bf16[64,1152]{1,0:T(8,128)(2,1)S(1)}, bf16[64,1152]{1,0:T(8,128)(2,1)S(1)}, u32[]{:S(2)}, u32[]{:S(2)}) collective-permute-start(bf16[64,1152]{1,0:T(8,128)(2,1)S(1)} %get-tuple-element.78), channel_id=1, source_target_pairs={{0,1},{1,0},{2,3},{3,2},{4,5},{5,4},{6,7},{7,6},{8,9},{9,8},{10,11... | collective-permute-start | bytes 442376 | tf_op jit(solution)/shard_map/ppermute | solution.py:74
  66.3 10.2 %collective-permute-start.22 = (bf16[2,2,1,1,1,8,1152]{6,5,3,2,1,0,4:T(8,128)(2,1)S(1)}, bf16[2,2,1,1,1,8,1152]{6,5,3,2,1,0,4:T(8,128)(2,1)S(1)}, u32[]{:S(2)}, u32[]{:S(2)}) collective-permute-start(bf16[2,2,1,1,1,8,1152]{6,5,3,2,1,0,4:T(8,128)(2,1)S(1)} %constant_dynamic-slice_fusion.3), channel_id=1, source_target_pairs={{0,4},{1,5},{2,6},{3,7},{4,0},{5,1},{6,2},{7,3},{8,12},{9,13},{10,... | collective-permute-start | bytes 221192 | tf_op jit(solution)/shard_map/ppermute | solution.py:62
  69.4 7.7 %collective-permute-start.19 = (bf16[2,2,1,1,1,8,2304]{6,5,3,2,1,0,4:T(8,128)(2,1)S(1)}, bf16[2,2,1,1,1,8,2304]{6,5,3,2,1,0,4:T(8,128)(2,1)S(1)}, u32[]{:S(2)}, u32[]{:S(2)}) collective-permute-start(bf16[2,2,1,1,1,8,2304]{6,5,3,2,1,0,4:T(8,128)(2,1)S(1)} %get-tuple-element.97), channel_id=1, source_target_pairs={{0,6},{1,7},{2,4},{3,5},{4,2},{5,3},{6,0},{7,1},{8,14},{9,15},{10,... | collective-permute-start | bytes 442376 | tf_op jit(solution)/shard_map/ppermute | solution.py:62
  70.3 8.8 %collective-permute-start.21 = (bf16[2,2,1,1,1,8,2304]{6,5,3,2,1,0,4:T(8,128)(2,1)S(1)}, bf16[2,2,1,1,1,8,2304]{6,5,3,2,1,0,4:T(8,128)(2,1)S(1)}, u32[]{:S(2)}, u32[]{:S(2)}) collective-permute-start(bf16[2,2,1,1,1,8,2304]{6,5,3,2,1,0,4:T(8,128)(2,1)S(1)} %get-tuple-element.98), channel_id=1, source_target_pairs={{0,4},{1,5},{2,6},{3,7},{4,0},{5,1},{6,2},{7,3},{8,12},{9,13},{10,... | collective-permute-start | bytes 442376 | tf_op jit(solution)/shard_map/ppermute | solution.py:62
  72.3 6.8 %collective-permute-start.20 = (bf16[2,2,1,1,1,8,2304]{6,5,3,2,1,0,4:T(8,128)(2,1)S(1)}, bf16[2,2,1,1,1,8,2304]{6,5,3,2,1,0,4:T(8,128)(2,1)S(1)}, u32[]{:S(2)}, u32[]{:S(2)}) collective-permute-start(bf16[2,2,1,1,1,8,2304]{6,5,3,2,1,0,4:T(8,128)(2,1)S(1)} %get-tuple-element.99), channel_id=1, source_target_pairs={{0,2},{1,3},{2,0},{3,1},{4,6},{5,7},{6,4},{7,5},{8,10},{9,11},{10,... | collective-permute-start | bytes 442376 | tf_op jit(solution)/shard_map/ppermute | solution.py:62
  79.3 6.2 %collective-permute-start.23 = (bf16[1,1,1,1,1,8,3456]{6,5,3,2,1,0,4:T(8,128)(2,1)S(1)}, bf16[1,1,1,1,1,8,3456]{6,5,3,2,1,0,4:T(8,128)(2,1)S(1)}, u32[]{:S(2)}, u32[]{:S(2)}) collective-permute-start(bf16[1,1,1,1,1,8,3456]{6,5,3,2,1,0,4:T(8,128)(2,1)S(1)} %get-tuple-element.100), channel_id=1, source_target_pairs={{0,24},{1,25},{2,26},{3,27},{4,28},{5,29},{6,30},{7,31},{8,16},{9,... | collective-permute-start | bytes 165896 | tf_op jit(solution)/shard_map/ppermute | solution.py:62
  81.8 6.2 %collective-permute-start.25 = (bf16[1,1,1,1,1,8,3456]{6,5,3,2,1,0,4:T(8,128)(2,1)S(1)}, bf16[1,1,1,1,1,8,3456]{6,5,3,2,1,0,4:T(8,128)(2,1)S(1)}, u32[]{:S(2)}, u32[]{:S(2)}) collective-permute-start(bf16[1,1,1,1,1,8,3456]{6,5,3,2,1,0,4:T(8,128)(2,1)S(1)} %get-tuple-element.101), channel_id=1, source_target_pairs={{0,16},{1,17},{2,18},{3,19},{4,20},{5,21},{6,22},{7,23},{8,24},{9,... | collective-permute-start | bytes 165896 | tf_op jit(solution)/shard_map/ppermute | solution.py:62
  82.7 5.3 %collective-permute-start.24 = (bf16[1,1,1,1,1,8,3456]{6,5,3,2,1,0,4:T(8,128)(2,1)S(1)}, bf16[1,1,1,1,1,8,3456]{6,5,3,2,1,0,4:T(8,128)(2,1)S(1)}, u32[]{:S(2)}, u32[]{:S(2)}) collective-permute-start(bf16[1,1,1,1,1,8,3456]{6,5,3,2,1,0,4:T(8,128)(2,1)S(1)} %get-tuple-element.102), channel_id=1, source_target_pairs={{0,8},{1,9},{2,10},{3,11},{4,12},{5,13},{6,14},{7,15},{8,0},{9,1},... | collective-permute-start | bytes 165896 | tf_op jit(solution)/shard_map/ppermute | solution.py:62
  (11 other events, 53.6 us)

commit v8 on v7

--- a/solution.py
+++ b/solution.py
@@ -42,7 +42,7 @@
     return (lax.axis_size("slab") * lax.axis_size("grp")).bit_length() - 1
 
 
-def exchange(held, stage):
+def exchange(held, stage, kind=jnp.bfloat16):
     slabs = lax.axis_size("slab")
     groups = lax.axis_size("grp")
     place = lax.axis_index("slab") * groups + lax.axis_index("grp")
@@ -61,7 +61,7 @@
         pairs = bit_pairs(slabs, groups, mask // groups, mask % groups)
         arrived = lax.ppermute(pick(flips), ("slab", "grp"), pairs)
         total = total + arrived.astype(jnp.float32)
-    return total.astype(jnp.bfloat16)
+    return total.astype(kind)
 
 
 def exchange_parts(parts, bits):
@@ -287,7 +287,7 @@
         out_specs=[pl.BlockSpec(memory_space=pltpu.VMEM)] * len(outs),
         out_shape=outs,
         scratch_shapes=[*scratch, pltpu.VMEM(shape, jnp.bfloat16)],
-        compiler_params=pltpu.CompilerParams(vmem_limit_bytes=20 << 20),
+        compiler_params=pltpu.CompilerParams(vmem_limit_bytes=(61 if scratch else 20) << 20),
         cost_estimate=pl.CostEstimate(
             flops=2 * width_deep * padded * sum(widths),
             bytes_accessed=2 * (width_deep * padded + (padded + width_deep) * sum(widths)),
@@ -570,7 +570,7 @@
         (jnp.concatenate((outer_taps, middle_taps), axis=-1), grad_input)
     )
     for stage in stages:
-        taps = exchange(taps, stage)
+        taps = exchange(taps, stage, jnp.float32 if stage is stages[-1] else jnp.bfloat16)
     rows = width_deep >> bits
     taps = taps.reshape(rows, 27, width_in)
     grad_down = jnp.concatenate((taps[:, :9], taps[:, 18:], taps[:, 9:18]), axis=1).astype(jnp.float32)

time: 89 us -> 89 us (level)
  Pallas kernels: 14.6 us -> 17.3 us
  local copies, waits for them, and re-layouts: 4.58 us -> 2.77 us
  other arithmetic: 2.89 us -> 1.92 us
    pallas_call x2, Pallas kernels: 3.81 us -> 6.54 us  [tap_sums(): pl.pallas_call(functools.partial(kernel, scale, depth, rows if inside els...]
    unnamed x17 -> x21, local copies, waits for them, and re-layouts: 2.93 us -> 1.12 us
    convert_element_type x3, other arithmetic: 1.2 us -> 0.24 us  [exchange_parts(): return total.astype(jnp.bfloat16).reshape(*dims, rows, total.shape[1])]
  transfers between devices with their start and end apart: 27 -> 27, of which waited for: 13 -> 12; matrix products, arithmetic and copies ran while one was open for 4% -> 3% of each run, Pallas kernels for 12% -> 15%
where the time goes in v8:
time: 89 us; the launch traced here: 88.7 us
  starting transfers between devices  38.7 us (43%)
  waiting for transfers between devices  27.1 us (30%)
  Pallas kernels  17.3 us (19%)
  local copies, waits for them, and re-layouts  2.77 us (3%)
  other arithmetic  1.92 us (2%)
  between operations  0.97 us (1%)
    ppermute x7, starting transfers between devices, local(): lax.ppermute(act_grads[mask], 'slab', [(i, i ^ mask) for i in range(slabs)])  11.2 us
    ppermute x7, starting transfers between devices, exchange(): arrived = lax.ppermute(pick(flips), ('slab', 'grp'), pairs)  11.2 us
    all_to_all x1, waiting for transfers between devices, local(): lax.all_to_all(deep_bf, 'slab', split_axis=0, concat_axis=0, tiled=True)  10.5 us
    all_to_all x1, starting transfers between devices, local(): lax.all_to_all(deep_bf, 'slab', split_axis=0, concat_axis=0, tiled=True)  7.27 us
    pallas_call x2, Pallas kernels, tap_sums(): pl.pallas_call(functools.partial(kernel, scale, depth, rows if inside els...  6.54 us
    ppermute x7, waiting for transfers between devices, exchange(): arrived = lax.ppermute(pick(flips), ('slab', 'grp'), pairs)  6.18 us
    pallas_call x2, Pallas kernels, input_plane(): pl.pallas_call(functools.partial(input_kernel, taps_of), grid=(1,), in_sp...  6.14 us
    ppermute x7, waiting for transfers between devices, local(): lax.ppermute(act_grads[mask], 'slab', [(i, i ^ mask) for i in range(slabs)])  5.34 us
  transfers between devices with their start and end apart: 27, of which 12 were waited for; matrix products, arithmetic and copies ran while one was open for 3% of the time, Pallas kernels for 15%

profile of v8, /device:TPU:0, one launch (start us, length us, event | category | flops | bytes accessed | tf_op | source)
XLA Modules:
  0.0 88.7 jit_solution(514868468387484272)
XLA Ops:
  0.7 3.5 %deep_gradient.1 = bf16[256,1024]{1,0:T(8,128)(2,1)} custom-call(bf16[2,32,128,128]{3,2,1,0:T(8,128)(2,1)} %rows_ref.1, bf16[8,256,128]{2,1,0:T(8,128)(2,1)} %taps_ref.1), custom_call_target="tpu_custom_call" | custom-call | flops 536870912 | bytes 3145728 | tf_op jit(solution)/shard_map/deep_gradient/pallas_call | solution.py:135
  4.2 7.3 %all-to-all-start = ((bf16[8,32,1024]{2,1,0:T(8,128)(2,1)}), bf16[8,32,1024]{2,1,0:T(8,128)(2,1)S(1)}, u32[]{:S(2)}, u32[]{:S(2)}) async-start(bf16[8,32,1024]{2,1,0:T(8,128)(2,1)} %bitcast.31), calls=%async_computation | async-start | bytes 1048576 | tf_op jit(solution)/shard_map/all_to_all | solution.py:469
  13.8 1.5 %collective-permute-done.3 = bf16[2,8,32,64]{3,2,1,0:T(8,128)(2,1)S(1)} collective-permute-done((bf16[2,8,32,64]{3,2,1,0:T(8,128)(2,1)S(1)}, bf16[2,8,32,64]{3,2,1,0:T(8,128)(2,1)S(1)}, u32[]{:S(2)}, u32[]{:S(2)}) %collective-permute-start.3) | collective-permute-done | bytes 65568 | tf_op jit(solution)/shard_map/ppermute | solution.py:24
  15.4 10.5 %all-to-all-done = bf16[8,32,1024]{2,1,0:T(8,128)(2,1)S(1)} async-done(((bf16[8,32,1024]{2,1,0:T(8,128)(2,1)}), bf16[8,32,1024]{2,1,0:T(8,128)(2,1)S(1)}, u32[]{:S(2)}, u32[]{:S(2)}) %all-to-all-start) | async-done | bytes 524320 | tf_op jit(solution)/shard_map/all_to_all | solution.py:469
  26.0 1.6 %collective-permute-start.4 = (bf16[8,32,64]{2,1,0:T(8,128)(2,1)S(1)}, bf16[8,32,64]{2,1,0:T(8,128)(2,1)S(1)}, u32[]{:S(2)}, u32[]{:S(2)}) collective-permute-start(bf16[8,32,64]{2,1,0:T(8,128)(2,1)S(1)} %slice.32), channel_id=1, source_target_pairs={{0,3},{1,2},{2,1},{3,0},{4,7},{5,6},{6,5},{7,4},{8,11},{9,10},{10,... | collective-permute-start | bytes 98312 | tf_op jit(solution)/shard_map/ppermute | solution.py:499
  28.4 1.5 %collective-permute-start.1 = (f32[32,4]{1,0:T(8,128)S(1)}, f32[32,4]{1,0:T(8,128)S(1)}, u32[]{:S(2)}, u32[]{:S(2)}) collective-permute-start(f32[32,4]{1,0:T(8,128)S(1)} %copy.35.refs_0_), channel_id=1, source_target_pairs={{0,2},{1,3},{2,0},{3,1},{4,6},{5,7},{6,4},{7,5},{8,10},{9,11},{10,... | collective-permute-start | bytes 1544 | tf_op jit(solution)/shard_map/ppermute | solution.py:30
  32.8 1.5 %collective-permute-start.6 = (bf16[272,128]{1,0:T(8,128)(2,1)S(1)}, bf16[272,128]{1,0:T(8,128)(2,1)S(1)}, u32[]{:S(2)}, u32[]{:S(2)}) collective-permute-start(bf16[272,128]{1,0:T(8,128)(2,1)S(1)} %get-tuple-element.53), channel_id=1, source_target_pairs={{0,4},{4,0},{8,12},{12,8},{16,20},{20,16},{24,28},{28,24},{1,5},{5... | collective-permute-start | bytes 208904 | tf_op jit(solution)/shard_map/ppermute | solution.py:531
  34.4 2.0 %collective-permute-start.8 = (bf16[272,128]{1,0:T(8,128)(2,1)S(1)}, bf16[272,128]{1,0:T(8,128)(2,1)S(1)}, u32[]{:S(2)}, u32[]{:S(2)}) collective-permute-start(bf16[272,128]{1,0:T(8,128)(2,1)S(1)} %get-tuple-element.55), channel_id=1, source_target_pairs={{0,12},{4,8},{8,4},{12,0},{16,28},{20,24},{24,20},{28,16},{1,13},{... | collective-permute-start | bytes 208904 | tf_op jit(solution)/shard_map/ppermute | solution.py:531
  36.5 3.7 %collective-permute-start.10 = (bf16[272,128]{1,0:T(8,128)(2,1)S(1)}, bf16[272,128]{1,0:T(8,128)(2,1)S(1)}, u32[]{:S(2)}, u32[]{:S(2)}) collective-permute-start(bf16[272,128]{1,0:T(8,128)(2,1)S(1)} %get-tuple-element.57), channel_id=1, source_target_pairs={{0,20},{4,16},{8,28},{12,24},{16,4},{20,0},{24,12},{28,8},{1,21},{... | collective-permute-start | bytes 208904 | tf_op jit(solution)/shard_map/ppermute | solution.py:531
  40.2 1.5 %collective-permute-start.11 = (bf16[272,128]{1,0:T(8,128)(2,1)S(1)}, bf16[272,128]{1,0:T(8,128)(2,1)S(1)}, u32[]{:S(2)}, u32[]{:S(2)}) collective-permute-start(bf16[272,128]{1,0:T(8,128)(2,1)S(1)} %get-tuple-element.58), channel_id=1, source_target_pairs={{0,24},{4,28},{8,16},{12,20},{16,8},{20,12},{24,0},{28,4},{1,25},{... | collective-permute-start | bytes 208904 | tf_op jit(solution)/shard_map/ppermute | solution.py:531
  41.7 2.4 %collective-permute-start.12 = (bf16[272,128]{1,0:T(8,128)(2,1)S(1)}, bf16[272,128]{1,0:T(8,128)(2,1)S(1)}, u32[]{:S(2)}, u32[]{:S(2)}) collective-permute-start(bf16[272,128]{1,0:T(8,128)(2,1)S(1)} %get-tuple-element.59), channel_id=1, source_target_pairs={{0,28},{4,24},{8,20},{12,16},{16,12},{20,8},{24,4},{28,0},{1,29},{... | collective-permute-start | bytes 208904 | tf_op jit(solution)/shard_map/ppermute | solution.py:531
  44.0 2.7 %collective-permute-done.9.refs_4_ = bf16[272,128]{1,0:T(8,128)(2,1)S(1)} collective-permute-done((bf16[272,128]{1,0:T(8,128)(2,1)S(1)}, bf16[272,128]{1,0:T(8,128)(2,1)S(1)}, u32[]{:S(2)}, u32[]{:S(2)}) %collective-permute-start.9) | collective-permute-done | bytes 69664 | tf_op jit(solution)/shard_map/ppermute | solution.py:531
  46.7 2.6 %collective-permute-done.10.refs_5_ = bf16[272,128]{1,0:T(8,128)(2,1)S(1)} collective-permute-done((bf16[272,128]{1,0:T(8,128)(2,1)S(1)}, bf16[272,128]{1,0:T(8,128)(2,1)S(1)}, u32[]{:S(2)}, u32[]{:S(2)}) %collective-permute-start.10) | collective-permute-done | bytes 69664 | tf_op jit(solution)/shard_map/ppermute | solution.py:531
  49.4 1.5 %collective-permute-start.13 = (bf16[8,272,128]{2,1,0:T(8,128)(2,1)S(1)}, bf16[8,272,128]{2,1,0:T(8,128)(2,1)S(1)}, u32[]{:S(2)}, u32[]{:S(2)}) collective-permute-start(bf16[8,272,128]{2,1,0:T(8,128)(2,1)S(1)} %place_blocks.1.grads_ref.refs_0_), channel_id=1, source_target_pairs={{4,0},{8,4},{12,8},{16,12},{20,16},{24,20},{28,24},{5,1},{9,5},{13... | collective-permute-start | bytes 1671176 | tf_op jit(solution)/shard_map/ppermute | solution.py:24
  50.9 5.5 %tap_sums.2 = (bf16[128,1152]{1,0:T(8,128)(2,1)}, bf16[128,1152]{1,0:T(8,128)(2,1)}, bf16[64,1152]{1,0:T(8,128)(2,1)}, bf16[64,1152]{1,0:T(8,128)(2,1)}, bf16[64...) custom-call(s32[1]{0:T(128)} %bitcast.own_ref, bf16[8,272,128]{2,1,0:T(8,128)(2,1)} %copy-done.1, ...), custom_call_target="tpu_custom_call" | custom-call | flops 1358954496 | bytes 7077888 | tf_op jit(solution)/shard_map/tap_sums/pallas_call | solution.py:283
  56.4 1.5 %collective-permute-start.15 = (bf16[64,1152]{1,0:T(8,128)(2,1)}, bf16[64,1152]{1,0:T(8,128)(2,1)S(1)}, u32[]{:S(2)}, u32[]{:S(2)}) collective-permute-start(bf16[64,1152]{1,0:T(8,128)(2,1)} %get-tuple-element.76), channel_id=1, source_target_pairs={{0,3},{1,2},{2,1},{3,0},{4,7},{5,6},{6,5},{7,4},{8,11},{9,10},{10,... | collective-permute-start | bytes 442376 | tf_op jit(solution)/shard_map/ppermute | solution.py:74
  59.6 2.6 %input_gradient.2.refs_3_ = bf16[2,32,128,128]{3,2,1,0:T(8,128)(2,1)} custom-call(bf16[8,272,128]{2,1,0:T(8,128)(2,1)S(1)} %copy-done.2, bf16[27,128,256]{2,1,0:T(8,128)(2,1)S(1)} %copy-done), custom_call_target="tpu_custom_call" | custom-call | tf_op jit(solution)/shard_map/input_gradient/pallas_call | solution.py:370
  64.5 1.4 %collective-permute-done.16 = bf16[64,1152]{1,0:T(8,128)(2,1)S(1)} collective-permute-done((bf16[64,1152]{1,0:T(8,128)(2,1)}, bf16[64,1152]{1,0:T(8,128)(2,1)S(1)}, u32[]{:S(2)}, u32[]{:S(2)}) %collective-permute-start.16) | collective-permute-done | bytes 147488 | tf_op jit(solution)/shard_map/ppermute | solution.py:74
  66.1 3.1 %collective-permute-start.22 = (bf16[2,2,1,1,1,8,1152]{6,5,3,2,1,0,4:T(8,128)(2,1)S(1)}, bf16[2,2,1,1,1,8,1152]{6,5,3,2,1,0,4:T(8,128)(2,1)S(1)}, u32[]{:S(2)}, u32[]{:S(2)}) collective-permute-start(bf16[2,2,1,1,1,8,1152]{6,5,3,2,1,0,4:T(8,128)(2,1)S(1)} %constant_dynamic-slice_fusion.3), channel_id=1, source_target_pairs={{0,4},{1,5},{2,6},{3,7},{4,0},{5,1},{6,2},{7,3},{8,12},{9,13},{10,... | collective-permute-start | bytes 221192 | tf_op jit(solution)/shard_map/ppermute | solution.py:62
  70.3 2.0 %collective-permute-start.21 = (bf16[2,2,1,1,1,8,2304]{6,5,3,2,1,0,4:T(8,128)(2,1)S(1)}, bf16[2,2,1,1,1,8,2304]{6,5,3,2,1,0,4:T(8,128)(2,1)S(1)}, u32[]{:S(2)}, u32[]{:S(2)}) collective-permute-start(bf16[2,2,1,1,1,8,2304]{6,5,3,2,1,0,4:T(8,128)(2,1)S(1)} %get-tuple-element.98), channel_id=1, source_target_pairs={{0,4},{1,5},{2,6},{3,7},{4,0},{5,1},{6,2},{7,3},{8,12},{9,13},{10,... | collective-permute-start | bytes 442376 | tf_op jit(solution)/shard_map/ppermute | solution.py:62
  73.0 3.5 %input_gradient.3 = bf16[2,32,128,128]{3,2,1,0:T(8,128)(2,1)} custom-call(bf16[8,272,128]{2,1,0:T(8,128)(2,1)S(1)} %copy-done.3, bf16[8,272,128]{2,1,0:T(8,128)(2,1)S(1)} %collective-permute-done.13.packed_ref.refs_1_, bf16[27,128,256]{2,1,0:T(8,128)(2,1)S(1)} %copy-done, bf16[2,32,128,128]{3,2,1,0:T(8,128)(2,1)} %input_gradient.2.refs_3_), custom_call_target="tpu_custom_call", output_to_operand_aliasing={{}: (3, {})} | custom-call | tf_op jit(solution)/shard_map/input_gradient/pallas_call | solution.py:370
  77.1 2.0 %collective-permute-done.21 = bf16[2,2,1,1,1,8,2304]{6,5,3,2,1,0,4:T(8,128)(2,1)S(1)} collective-permute-done((bf16[2,2,1,1,1,8,2304]{6,5,3,2,1,0,4:T(8,128)(2,1)S(1)}, bf16[2,2,1,1,1,8,2304]{6,5,3,2,1,0,4:T(8,128)(2,1)S(1)}, u32[]{:S(2)}, u32[]{:S(2)}) %collective-permute-start.21) | collective-permute-done | bytes 147488 | tf_op jit(solution)/shard_map/ppermute | solution.py:62
  79.3 2.9 %collective-permute-start.23 = (bf16[1,1,1,1,1,8,3456]{6,5,3,2,1,0,4:T(8,128)(2,1)S(1)}, bf16[1,1,1,1,1,8,3456]{6,5,3,2,1,0,4:T(8,128)(2,1)S(1)}, u32[]{:S(2)}, u32[]{:S(2)}) collective-permute-start(bf16[1,1,1,1,1,8,3456]{6,5,3,2,1,0,4:T(8,128)(2,1)S(1)} %get-tuple-element.100), channel_id=1, source_target_pairs={{0,24},{1,25},{2,26},{3,27},{4,28},{5,29},{6,30},{7,31},{8,16},{9,... | collective-permute-start | bytes 165896 | tf_op jit(solution)/shard_map/ppermute | solution.py:62
  85.5 2.5 %collective-permute-done.25 = bf16[1,1,1,1,1,8,3456]{6,5,3,2,1,0,4:T(8,128)(2,1)S(1)} collective-permute-done((bf16[1,1,1,1,1,8,3456]{6,5,3,2,1,0,4:T(8,128)(2,1)S(1)}, bf16[1,1,1,1,1,8,3456]{6,5,3,2,1,0,4:T(8,128)(2,1)S(1)}, u32[]{:S(2)}, u32[]{:S(2)}) %collective-permute-start.25) | collective-permute-done | bytes 55328 | tf_op jit(solution)/shard_map/ppermute | solution.py:62
  (86 shorter events, 16.8 us)
Async XLA Ops:
  4.2 21.8 %all-to-all-start = ((bf16[8,32,1024]{2,1,0:T(8,128)(2,1)}), bf16[8,32,1024]{2,1,0:T(8,128)(2,1)S(1)}, u32[]{:S(2)}, u32[]{:S(2)}) async-start(bf16[8,32,1024]{2,1,0:T(8,128)(2,1)} %bitcast.31), calls=%async_computation | async-start | bytes 1048576 | tf_op jit(solution)/shard_map/all_to_all | solution.py:469
  12.1 3.2 %collective-permute-start.3 = (bf16[2,8,32,64]{3,2,1,0:T(8,128)(2,1)S(1)}, bf16[2,8,32,64]{3,2,1,0:T(8,128)(2,1)S(1)}, u32[]{:S(2)}, u32[]{:S(2)}) collective-permute-start(bf16[2,8,32,64]{3,2,1,0:T(8,128)(2,1)S(1)} %pad_maximum_fusion.1), channel_id=1, source_target_pairs={{1,0},{2,1},{3,2},{5,4},{6,5},{7,6},{9,8},{10,9},{11,10},{13,12},{... | collective-permute-start | bytes 196616 | tf_op jit(solution)/shard_map/ppermute | solution.py:24
  25.9 4.2 %collective-permute-start.5 = (bf16[8,32,64]{2,1,0:T(8,128)(2,1)S(1)}, bf16[8,32,64]{2,1,0:T(8,128)(2,1)S(1)}, u32[]{:S(2)}, u32[]{:S(2)}) collective-permute-start(bf16[8,32,64]{2,1,0:T(8,128)(2,1)S(1)} %slice.32), channel_id=1, source_target_pairs={{0,1},{1,0},{2,3},{3,2},{4,5},{5,4},{6,7},{7,6},{8,9},{9,8},{10,11... | collective-permute-start | bytes 98312 | tf_op jit(solution)/shard_map/ppermute | solution.py:499
  26.0 4.1 %collective-permute-start.4 = (bf16[8,32,64]{2,1,0:T(8,128)(2,1)S(1)}, bf16[8,32,64]{2,1,0:T(8,128)(2,1)S(1)}, u32[]{:S(2)}, u32[]{:S(2)}) collective-permute-start(bf16[8,32,64]{2,1,0:T(8,128)(2,1)S(1)} %slice.32), channel_id=1, source_target_pairs={{0,3},{1,2},{2,1},{3,0},{4,7},{5,6},{6,5},{7,4},{8,11},{9,10},{10,... | collective-permute-start | bytes 98312 | tf_op jit(solution)/shard_map/ppermute | solution.py:499
  28.4 3.7 %collective-permute-start.1 = (f32[32,4]{1,0:T(8,128)S(1)}, f32[32,4]{1,0:T(8,128)S(1)}, u32[]{:S(2)}, u32[]{:S(2)}) collective-permute-start(f32[32,4]{1,0:T(8,128)S(1)} %copy.35.refs_0_), channel_id=1, source_target_pairs={{0,2},{1,3},{2,0},{3,1},{4,6},{5,7},{6,4},{7,5},{8,10},{9,11},{10,... | collective-permute-start | bytes 1544 | tf_op jit(solution)/shard_map/ppermute | solution.py:30
  32.8 7.4 %collective-permute-start.6 = (bf16[272,128]{1,0:T(8,128)(2,1)S(1)}, bf16[272,128]{1,0:T(8,128)(2,1)S(1)}, u32[]{:S(2)}, u32[]{:S(2)}) collective-permute-start(bf16[272,128]{1,0:T(8,128)(2,1)S(1)} %get-tuple-element.53), channel_id=1, source_target_pairs={{0,4},{4,0},{8,12},{12,8},{16,20},{20,16},{24,28},{28,24},{1,5},{5... | collective-permute-start | bytes 208904 | tf_op jit(solution)/shard_map/ppermute | solution.py:531
  34.4 7.3 %collective-permute-start.7 = (bf16[272,128]{1,0:T(8,128)(2,1)S(1)}, bf16[272,128]{1,0:T(8,128)(2,1)S(1)}, u32[]{:S(2)}, u32[]{:S(2)}) collective-permute-start(bf16[272,128]{1,0:T(8,128)(2,1)S(1)} %get-tuple-element.54), channel_id=1, source_target_pairs={{0,8},{4,12},{8,0},{12,4},{16,24},{20,28},{24,16},{28,20},{1,9},{5... | collective-permute-start | bytes 208904 | tf_op jit(solution)/shard_map/ppermute | solution.py:531
  34.4 9.7 %collective-permute-start.8 = (bf16[272,128]{1,0:T(8,128)(2,1)S(1)}, bf16[272,128]{1,0:T(8,128)(2,1)S(1)}, u32[]{:S(2)}, u32[]{:S(2)}) collective-permute-start(bf16[272,128]{1,0:T(8,128)(2,1)S(1)} %get-tuple-element.55), channel_id=1, source_target_pairs={{0,12},{4,8},{8,4},{12,0},{16,28},{20,24},{24,20},{28,16},{1,13},{... | collective-permute-start | bytes 208904 | tf_op jit(solution)/shard_map/ppermute | solution.py:531
  36.4 10.3 %collective-permute-start.9 = (bf16[272,128]{1,0:T(8,128)(2,1)S(1)}, bf16[272,128]{1,0:T(8,128)(2,1)S(1)}, u32[]{:S(2)}, u32[]{:S(2)}) collective-permute-start(bf16[272,128]{1,0:T(8,128)(2,1)S(1)} %get-tuple-element.56), channel_id=1, source_target_pairs={{0,16},{4,20},{8,24},{12,28},{16,0},{20,4},{24,8},{28,12},{1,17},{... | collective-permute-start | bytes 208904 | tf_op jit(solution)/shard_map/ppermute | solution.py:531
  36.5 12.8 %collective-permute-start.10 = (bf16[272,128]{1,0:T(8,128)(2,1)S(1)}, bf16[272,128]{1,0:T(8,128)(2,1)S(1)}, u32[]{:S(2)}, u32[]{:S(2)}) collective-permute-start(bf16[272,128]{1,0:T(8,128)(2,1)S(1)} %get-tuple-element.57), channel_id=1, source_target_pairs={{0,20},{4,16},{8,28},{12,24},{16,4},{20,0},{24,12},{28,8},{1,21},{... | collective-permute-start | bytes 208904 | tf_op jit(solution)/shard_map/ppermute | solution.py:531
  40.2 9.2 %collective-permute-start.11 = (bf16[272,128]{1,0:T(8,128)(2,1)S(1)}, bf16[272,128]{1,0:T(8,128)(2,1)S(1)}, u32[]{:S(2)}, u32[]{:S(2)}) collective-permute-start(bf16[272,128]{1,0:T(8,128)(2,1)S(1)} %get-tuple-element.58), channel_id=1, source_target_pairs={{0,24},{4,28},{8,16},{12,20},{16,8},{20,12},{24,0},{28,4},{1,25},{... | collective-permute-start | bytes 208904 | tf_op jit(solution)/shard_map/ppermute | solution.py:531
  41.7 7.7 %collective-permute-start.12 = (bf16[272,128]{1,0:T(8,128)(2,1)S(1)}, bf16[272,128]{1,0:T(8,128)(2,1)S(1)}, u32[]{:S(2)}, u32[]{:S(2)}) collective-permute-start(bf16[272,128]{1,0:T(8,128)(2,1)S(1)} %get-tuple-element.59), channel_id=1, source_target_pairs={{0,28},{4,24},{8,20},{12,16},{16,12},{20,8},{24,4},{28,0},{1,29},{... | collective-permute-start | bytes 208904 | tf_op jit(solution)/shard_map/ppermute | solution.py:531
  49.4 13.3 %collective-permute-start.13 = (bf16[8,272,128]{2,1,0:T(8,128)(2,1)S(1)}, bf16[8,272,128]{2,1,0:T(8,128)(2,1)S(1)}, u32[]{:S(2)}, u32[]{:S(2)}) collective-permute-start(bf16[8,272,128]{2,1,0:T(8,128)(2,1)S(1)} %place_blocks.1.grads_ref.refs_0_), channel_id=1, source_target_pairs={{4,0},{8,4},{12,8},{16,12},{20,16},{24,20},{28,24},{5,1},{9,5},{13... | collective-permute-start | bytes 1671176 | tf_op jit(solution)/shard_map/ppermute | solution.py:24
  56.4 8.0 %collective-permute-start.18 = (bf16[128,1152]{1,0:T(8,128)(2,1)}, bf16[128,1152]{1,0:T(8,128)(2,1)S(1)}, u32[]{:S(2)}, u32[]{:S(2)}) collective-permute-start(bf16[128,1152]{1,0:T(8,128)(2,1)} %get-tuple-element.80), channel_id=1, source_target_pairs={{0,1},{1,0},{2,3},{3,2},{4,5},{5,4},{6,7},{7,6},{8,9},{9,8},{10,11... | collective-permute-start | bytes 884744 | tf_op jit(solution)/shard_map/ppermute | solution.py:74
  56.4 8.1 %collective-permute-start.15 = (bf16[64,1152]{1,0:T(8,128)(2,1)}, bf16[64,1152]{1,0:T(8,128)(2,1)S(1)}, u32[]{:S(2)}, u32[]{:S(2)}) collective-permute-start(bf16[64,1152]{1,0:T(8,128)(2,1)} %get-tuple-element.76), channel_id=1, source_target_pairs={{0,3},{1,2},{2,1},{3,0},{4,7},{5,6},{6,5},{7,4},{8,11},{9,10},{10,... | collective-permute-start | bytes 442376 | tf_op jit(solution)/shard_map/ppermute | solution.py:74
  57.9 8.0 %collective-permute-start.16 = (bf16[64,1152]{1,0:T(8,128)(2,1)}, bf16[64,1152]{1,0:T(8,128)(2,1)S(1)}, u32[]{:S(2)}, u32[]{:S(2)}) collective-permute-start(bf16[64,1152]{1,0:T(8,128)(2,1)} %get-tuple-element.77), channel_id=1, source_target_pairs={{0,2},{1,3},{2,0},{3,1},{4,6},{5,7},{6,4},{7,5},{8,10},{9,11},{10,... | collective-permute-start | bytes 442376 | tf_op jit(solution)/shard_map/ppermute | solution.py:74
  58.5 7.4 %collective-permute-start.17 = (bf16[64,1152]{1,0:T(8,128)(2,1)}, bf16[64,1152]{1,0:T(8,128)(2,1)S(1)}, u32[]{:S(2)}, u32[]{:S(2)}) collective-permute-start(bf16[64,1152]{1,0:T(8,128)(2,1)} %get-tuple-element.78), channel_id=1, source_target_pairs={{0,1},{1,0},{2,3},{3,2},{4,5},{5,4},{6,7},{7,6},{8,9},{9,8},{10,11... | collective-permute-start | bytes 442376 | tf_op jit(solution)/shard_map/ppermute | solution.py:74
  66.1 10.4 %collective-permute-start.22 = (bf16[2,2,1,1,1,8,1152]{6,5,3,2,1,0,4:T(8,128)(2,1)S(1)}, bf16[2,2,1,1,1,8,1152]{6,5,3,2,1,0,4:T(8,128)(2,1)S(1)}, u32[]{:S(2)}, u32[]{:S(2)}) collective-permute-start(bf16[2,2,1,1,1,8,1152]{6,5,3,2,1,0,4:T(8,128)(2,1)S(1)} %constant_dynamic-slice_fusion.3), channel_id=1, source_target_pairs={{0,4},{1,5},{2,6},{3,7},{4,0},{5,1},{6,2},{7,3},{8,12},{9,13},{10,... | collective-permute-start | bytes 221192 | tf_op jit(solution)/shard_map/ppermute | solution.py:62
  69.4 7.7 %collective-permute-start.19 = (bf16[2,2,1,1,1,8,2304]{6,5,3,2,1,0,4:T(8,128)(2,1)S(1)}, bf16[2,2,1,1,1,8,2304]{6,5,3,2,1,0,4:T(8,128)(2,1)S(1)}, u32[]{:S(2)}, u32[]{:S(2)}) collective-permute-start(bf16[2,2,1,1,1,8,2304]{6,5,3,2,1,0,4:T(8,128)(2,1)S(1)} %get-tuple-element.97), channel_id=1, source_target_pairs={{0,6},{1,7},{2,4},{3,5},{4,2},{5,3},{6,0},{7,1},{8,14},{9,15},{10,... | collective-permute-start | bytes 442376 | tf_op jit(solution)/shard_map/ppermute | solution.py:62
  70.3 8.8 %collective-permute-start.21 = (bf16[2,2,1,1,1,8,2304]{6,5,3,2,1,0,4:T(8,128)(2,1)S(1)}, bf16[2,2,1,1,1,8,2304]{6,5,3,2,1,0,4:T(8,128)(2,1)S(1)}, u32[]{:S(2)}, u32[]{:S(2)}) collective-permute-start(bf16[2,2,1,1,1,8,2304]{6,5,3,2,1,0,4:T(8,128)(2,1)S(1)} %get-tuple-element.98), channel_id=1, source_target_pairs={{0,4},{1,5},{2,6},{3,7},{4,0},{5,1},{6,2},{7,3},{8,12},{9,13},{10,... | collective-permute-start | bytes 442376 | tf_op jit(solution)/shard_map/ppermute | solution.py:62
  72.3 6.8 %collective-permute-start.20 = (bf16[2,2,1,1,1,8,2304]{6,5,3,2,1,0,4:T(8,128)(2,1)S(1)}, bf16[2,2,1,1,1,8,2304]{6,5,3,2,1,0,4:T(8,128)(2,1)S(1)}, u32[]{:S(2)}, u32[]{:S(2)}) collective-permute-start(bf16[2,2,1,1,1,8,2304]{6,5,3,2,1,0,4:T(8,128)(2,1)S(1)} %get-tuple-element.99), channel_id=1, source_target_pairs={{0,2},{1,3},{2,0},{3,1},{4,6},{5,7},{6,4},{7,5},{8,10},{9,11},{10,... | collective-permute-start | bytes 442376 | tf_op jit(solution)/shard_map/ppermute | solution.py:62
  79.3 6.2 %collective-permute-start.23 = (bf16[1,1,1,1,1,8,3456]{6,5,3,2,1,0,4:T(8,128)(2,1)S(1)}, bf16[1,1,1,1,1,8,3456]{6,5,3,2,1,0,4:T(8,128)(2,1)S(1)}, u32[]{:S(2)}, u32[]{:S(2)}) collective-permute-start(bf16[1,1,1,1,1,8,3456]{6,5,3,2,1,0,4:T(8,128)(2,1)S(1)} %get-tuple-element.100), channel_id=1, source_target_pairs={{0,24},{1,25},{2,26},{3,27},{4,28},{5,29},{6,30},{7,31},{8,16},{9,... | collective-permute-start | bytes 165896 | tf_op jit(solution)/shard_map/ppermute | solution.py:62
  82.2 5.8 %collective-permute-start.25 = (bf16[1,1,1,1,1,8,3456]{6,5,3,2,1,0,4:T(8,128)(2,1)S(1)}, bf16[1,1,1,1,1,8,3456]{6,5,3,2,1,0,4:T(8,128)(2,1)S(1)}, u32[]{:S(2)}, u32[]{:S(2)}) collective-permute-start(bf16[1,1,1,1,1,8,3456]{6,5,3,2,1,0,4:T(8,128)(2,1)S(1)} %get-tuple-element.101), channel_id=1, source_target_pairs={{0,16},{1,17},{2,18},{3,19},{4,20},{5,21},{6,22},{7,23},{8,24},{9,... | collective-permute-start | bytes 165896 | tf_op jit(solution)/shard_map/ppermute | solution.py:62
  82.7 5.3 %collective-permute-start.24 = (bf16[1,1,1,1,1,8,3456]{6,5,3,2,1,0,4:T(8,128)(2,1)S(1)}, bf16[1,1,1,1,1,8,3456]{6,5,3,2,1,0,4:T(8,128)(2,1)S(1)}, u32[]{:S(2)}, u32[]{:S(2)}) collective-permute-start(bf16[1,1,1,1,1,8,3456]{6,5,3,2,1,0,4:T(8,128)(2,1)S(1)} %get-tuple-element.102), channel_id=1, source_target_pairs={{0,8},{1,9},{2,10},{3,11},{4,12},{5,13},{6,14},{7,15},{8,0},{9,1},... | collective-permute-start | bytes 165896 | tf_op jit(solution)/shard_map/ppermute | solution.py:62
  (13 other events, 65.0 us)

commit v9 on v8

--- a/solution.py
+++ b/solution.py
@@ -287,7 +287,7 @@
         out_specs=[pl.BlockSpec(memory_space=pltpu.VMEM)] * len(outs),
         out_shape=outs,
         scratch_shapes=[*scratch, pltpu.VMEM(shape, jnp.bfloat16)],
-        compiler_params=pltpu.CompilerParams(vmem_limit_bytes=(61 if scratch else 20) << 20),
+        compiler_params=pltpu.CompilerParams(vmem_limit_bytes=(61 if scratch else 40) << 20),
         cost_estimate=pl.CostEstimate(
             flops=2 * width_deep * padded * sum(widths),
             bytes_accessed=2 * (width_deep * padded + (padded + width_deep) * sum(widths)),

time: 89 us -> 89 us (level)
  no operation moved by 1% of the time
where the time goes in v9:
time: 89 us; the launch traced here: 88.7 us
  starting transfers between devices  38.7 us (43%)
  waiting for transfers between devices  27.1 us (30%)
  Pallas kernels  17.3 us (19%)
  local copies, waits for them, and re-layouts  2.77 us (3%)
  other arithmetic  1.92 us (2%)
  between operations  0.97 us (1%)
    ppermute x7, starting transfers between devices, local(): lax.ppermute(act_grads[mask], 'slab', [(i, i ^ mask) for i in range(slabs)])  11.2 us
    ppermute x7, starting transfers between devices, exchange(): arrived = lax.ppermute(pick(flips), ('slab', 'grp'), pairs)  11.2 us
    all_to_all x1, waiting for transfers between devices, local(): lax.all_to_all(deep_bf, 'slab', split_axis=0, concat_axis=0, tiled=True)  10.5 us
    all_to_all x1, starting transfers between devices, local(): lax.all_to_all(deep_bf, 'slab', split_axis=0, concat_axis=0, tiled=True)  7.27 us
    pallas_call x2, Pallas kernels, tap_sums(): pl.pallas_call(functools.partial(kernel, scale, depth, rows if inside els...  6.54 us
    ppermute x7, waiting for transfers between devices, exchange(): arrived = lax.ppermute(pick(flips), ('slab', 'grp'), pairs)  6.18 us
    pallas_call x2, Pallas kernels, input_plane(): pl.pallas_call(functools.partial(input_kernel, taps_of), grid=(1,), in_sp...  6.14 us
    ppermute x7, waiting for transfers between devices, local(): lax.ppermute(act_grads[mask], 'slab', [(i, i ^ mask) for i in range(slabs)])  5.34 us
  transfers between devices with their start and end apart: 27, of which 12 were waited for; matrix products, arithmetic and copies ran while one was open for 3% of the time, Pallas kernels for 15%

profile of v9, /device:TPU:0, one launch (start us, length us, event | category | flops | bytes accessed | tf_op | source)
XLA Modules:
  0.0 88.7 jit_solution(4439198791072465590)
XLA Ops:
  0.7 3.5 %deep_gradient.1 = bf16[256,1024]{1,0:T(8,128)(2,1)} custom-call(bf16[2,32,128,128]{3,2,1,0:T(8,128)(2,1)} %rows_ref.1, bf16[8,256,128]{2,1,0:T(8,128)(2,1)} %taps_ref.1), custom_call_target="tpu_custom_call" | custom-call | flops 536870912 | bytes 3145728 | tf_op jit(solution)/shard_map/deep_gradient/pallas_call | solution.py:135
  4.2 7.3 %all-to-all-start = ((bf16[8,32,1024]{2,1,0:T(8,128)(2,1)}), bf16[8,32,1024]{2,1,0:T(8,128)(2,1)S(1)}, u32[]{:S(2)}, u32[]{:S(2)}) async-start(bf16[8,32,1024]{2,1,0:T(8,128)(2,1)} %bitcast.31), calls=%async_computation | async-start | bytes 1048576 | tf_op jit(solution)/shard_map/all_to_all | solution.py:469
  13.8 1.5 %collective-permute-done.3 = bf16[2,8,32,64]{3,2,1,0:T(8,128)(2,1)S(1)} collective-permute-done((bf16[2,8,32,64]{3,2,1,0:T(8,128)(2,1)S(1)}, bf16[2,8,32,64]{3,2,1,0:T(8,128)(2,1)S(1)}, u32[]{:S(2)}, u32[]{:S(2)}) %collective-permute-start.3) | collective-permute-done | bytes 65568 | tf_op jit(solution)/shard_map/ppermute | solution.py:24
  15.4 10.5 %all-to-all-done = bf16[8,32,1024]{2,1,0:T(8,128)(2,1)S(1)} async-done(((bf16[8,32,1024]{2,1,0:T(8,128)(2,1)}), bf16[8,32,1024]{2,1,0:T(8,128)(2,1)S(1)}, u32[]{:S(2)}, u32[]{:S(2)}) %all-to-all-start) | async-done | bytes 524320 | tf_op jit(solution)/shard_map/all_to_all | solution.py:469
  26.0 1.6 %collective-permute-start.4 = (bf16[8,32,64]{2,1,0:T(8,128)(2,1)S(1)}, bf16[8,32,64]{2,1,0:T(8,128)(2,1)S(1)}, u32[]{:S(2)}, u32[]{:S(2)}) collective-permute-start(bf16[8,32,64]{2,1,0:T(8,128)(2,1)S(1)} %slice.32), channel_id=1, source_target_pairs={{0,3},{1,2},{2,1},{3,0},{4,7},{5,6},{6,5},{7,4},{8,11},{9,10},{10,... | collective-permute-start | bytes 98312 | tf_op jit(solution)/shard_map/ppermute | solution.py:499
  28.4 1.5 %collective-permute-start.1 = (f32[32,4]{1,0:T(8,128)S(1)}, f32[32,4]{1,0:T(8,128)S(1)}, u32[]{:S(2)}, u32[]{:S(2)}) collective-permute-start(f32[32,4]{1,0:T(8,128)S(1)} %copy.35.refs_0_), channel_id=1, source_target_pairs={{0,2},{1,3},{2,0},{3,1},{4,6},{5,7},{6,4},{7,5},{8,10},{9,11},{10,... | collective-permute-start | bytes 1544 | tf_op jit(solution)/shard_map/ppermute | solution.py:30
  32.8 1.5 %collective-permute-start.6 = (bf16[272,128]{1,0:T(8,128)(2,1)S(1)}, bf16[272,128]{1,0:T(8,128)(2,1)S(1)}, u32[]{:S(2)}, u32[]{:S(2)}) collective-permute-start(bf16[272,128]{1,0:T(8,128)(2,1)S(1)} %get-tuple-element.53), channel_id=1, source_target_pairs={{0,4},{4,0},{8,12},{12,8},{16,20},{20,16},{24,28},{28,24},{1,5},{5... | collective-permute-start | bytes 208904 | tf_op jit(solution)/shard_map/ppermute | solution.py:531
  34.4 2.0 %collective-permute-start.8 = (bf16[272,128]{1,0:T(8,128)(2,1)S(1)}, bf16[272,128]{1,0:T(8,128)(2,1)S(1)}, u32[]{:S(2)}, u32[]{:S(2)}) collective-permute-start(bf16[272,128]{1,0:T(8,128)(2,1)S(1)} %get-tuple-element.55), channel_id=1, source_target_pairs={{0,12},{4,8},{8,4},{12,0},{16,28},{20,24},{24,20},{28,16},{1,13},{... | collective-permute-start | bytes 208904 | tf_op jit(solution)/shard_map/ppermute | solution.py:531
  36.5 3.7 %collective-permute-start.10 = (bf16[272,128]{1,0:T(8,128)(2,1)S(1)}, bf16[272,128]{1,0:T(8,128)(2,1)S(1)}, u32[]{:S(2)}, u32[]{:S(2)}) collective-permute-start(bf16[272,128]{1,0:T(8,128)(2,1)S(1)} %get-tuple-element.57), channel_id=1, source_target_pairs={{0,20},{4,16},{8,28},{12,24},{16,4},{20,0},{24,12},{28,8},{1,21},{... | collective-permute-start | bytes 208904 | tf_op jit(solution)/shard_map/ppermute | solution.py:531
  40.2 1.5 %collective-permute-start.11 = (bf16[272,128]{1,0:T(8,128)(2,1)S(1)}, bf16[272,128]{1,0:T(8,128)(2,1)S(1)}, u32[]{:S(2)}, u32[]{:S(2)}) collective-permute-start(bf16[272,128]{1,0:T(8,128)(2,1)S(1)} %get-tuple-element.58), channel_id=1, source_target_pairs={{0,24},{4,28},{8,16},{12,20},{16,8},{20,12},{24,0},{28,4},{1,25},{... | collective-permute-start | bytes 208904 | tf_op jit(solution)/shard_map/ppermute | solution.py:531
  41.7 2.4 %collective-permute-start.12 = (bf16[272,128]{1,0:T(8,128)(2,1)S(1)}, bf16[272,128]{1,0:T(8,128)(2,1)S(1)}, u32[]{:S(2)}, u32[]{:S(2)}) collective-permute-start(bf16[272,128]{1,0:T(8,128)(2,1)S(1)} %get-tuple-element.59), channel_id=1, source_target_pairs={{0,28},{4,24},{8,20},{12,16},{16,12},{20,8},{24,4},{28,0},{1,29},{... | collective-permute-start | bytes 208904 | tf_op jit(solution)/shard_map/ppermute | solution.py:531
  44.0 2.7 %collective-permute-done.9.refs_4_ = bf16[272,128]{1,0:T(8,128)(2,1)S(1)} collective-permute-done((bf16[272,128]{1,0:T(8,128)(2,1)S(1)}, bf16[272,128]{1,0:T(8,128)(2,1)S(1)}, u32[]{:S(2)}, u32[]{:S(2)}) %collective-permute-start.9) | collective-permute-done | bytes 69664 | tf_op jit(solution)/shard_map/ppermute | solution.py:531
  46.7 2.6 %collective-permute-done.10.refs_5_ = bf16[272,128]{1,0:T(8,128)(2,1)S(1)} collective-permute-done((bf16[272,128]{1,0:T(8,128)(2,1)S(1)}, bf16[272,128]{1,0:T(8,128)(2,1)S(1)}, u32[]{:S(2)}, u32[]{:S(2)}) %collective-permute-start.10) | collective-permute-done | bytes 69664 | tf_op jit(solution)/shard_map/ppermute | solution.py:531
  49.4 1.5 %collective-permute-start.13 = (bf16[8,272,128]{2,1,0:T(8,128)(2,1)S(1)}, bf16[8,272,128]{2,1,0:T(8,128)(2,1)S(1)}, u32[]{:S(2)}, u32[]{:S(2)}) collective-permute-start(bf16[8,272,128]{2,1,0:T(8,128)(2,1)S(1)} %place_blocks.1.grads_ref.refs_0_), channel_id=1, source_target_pairs={{4,0},{8,4},{12,8},{16,12},{20,16},{24,20},{28,24},{5,1},{9,5},{13... | collective-permute-start | bytes 1671176 | tf_op jit(solution)/shard_map/ppermute | solution.py:24
  50.9 5.5 %tap_sums.2 = (bf16[128,1152]{1,0:T(8,128)(2,1)}, bf16[128,1152]{1,0:T(8,128)(2,1)}, bf16[64,1152]{1,0:T(8,128)(2,1)}, bf16[64,1152]{1,0:T(8,128)(2,1)}, bf16[64...) custom-call(s32[1]{0:T(128)} %bitcast.own_ref, bf16[8,272,128]{2,1,0:T(8,128)(2,1)} %copy-done.1, ...), custom_call_target="tpu_custom_call" | custom-call | flops 1358954496 | bytes 7077888 | tf_op jit(solution)/shard_map/tap_sums/pallas_call | solution.py:283
  56.4 1.5 %collective-permute-start.15 = (bf16[64,1152]{1,0:T(8,128)(2,1)}, bf16[64,1152]{1,0:T(8,128)(2,1)S(1)}, u32[]{:S(2)}, u32[]{:S(2)}) collective-permute-start(bf16[64,1152]{1,0:T(8,128)(2,1)} %get-tuple-element.76), channel_id=1, source_target_pairs={{0,3},{1,2},{2,1},{3,0},{4,7},{5,6},{6,5},{7,4},{8,11},{9,10},{10,... | collective-permute-start | bytes 442376 | tf_op jit(solution)/shard_map/ppermute | solution.py:74
  59.6 2.6 %input_gradient.2.refs_3_ = bf16[2,32,128,128]{3,2,1,0:T(8,128)(2,1)} custom-call(bf16[8,272,128]{2,1,0:T(8,128)(2,1)S(1)} %copy-done.2, bf16[27,128,256]{2,1,0:T(8,128)(2,1)S(1)} %copy-done), custom_call_target="tpu_custom_call" | custom-call | tf_op jit(solution)/shard_map/input_gradient/pallas_call | solution.py:370
  64.5 1.4 %collective-permute-done.16 = bf16[64,1152]{1,0:T(8,128)(2,1)S(1)} collective-permute-done((bf16[64,1152]{1,0:T(8,128)(2,1)}, bf16[64,1152]{1,0:T(8,128)(2,1)S(1)}, u32[]{:S(2)}, u32[]{:S(2)}) %collective-permute-start.16) | collective-permute-done | bytes 147488 | tf_op jit(solution)/shard_map/ppermute | solution.py:74
  66.1 3.1 %collective-permute-start.22 = (bf16[2,2,1,1,1,8,1152]{6,5,3,2,1,0,4:T(8,128)(2,1)S(1)}, bf16[2,2,1,1,1,8,1152]{6,5,3,2,1,0,4:T(8,128)(2,1)S(1)}, u32[]{:S(2)}, u32[]{:S(2)}) collective-permute-start(bf16[2,2,1,1,1,8,1152]{6,5,3,2,1,0,4:T(8,128)(2,1)S(1)} %constant_dynamic-slice_fusion.3), channel_id=1, source_target_pairs={{0,4},{1,5},{2,6},{3,7},{4,0},{5,1},{6,2},{7,3},{8,12},{9,13},{10,... | collective-permute-start | bytes 221192 | tf_op jit(solution)/shard_map/ppermute | solution.py:62
  70.3 2.0 %collective-permute-start.21 = (bf16[2,2,1,1,1,8,2304]{6,5,3,2,1,0,4:T(8,128)(2,1)S(1)}, bf16[2,2,1,1,1,8,2304]{6,5,3,2,1,0,4:T(8,128)(2,1)S(1)}, u32[]{:S(2)}, u32[]{:S(2)}) collective-permute-start(bf16[2,2,1,1,1,8,2304]{6,5,3,2,1,0,4:T(8,128)(2,1)S(1)} %get-tuple-element.98), channel_id=1, source_target_pairs={{0,4},{1,5},{2,6},{3,7},{4,0},{5,1},{6,2},{7,3},{8,12},{9,13},{10,... | collective-permute-start | bytes 442376 | tf_op jit(solution)/shard_map/ppermute | solution.py:62
  73.0 3.5 %input_gradient.3 = bf16[2,32,128,128]{3,2,1,0:T(8,128)(2,1)} custom-call(bf16[8,272,128]{2,1,0:T(8,128)(2,1)S(1)} %copy-done.3, bf16[8,272,128]{2,1,0:T(8,128)(2,1)S(1)} %collective-permute-done.13.packed_ref.refs_1_, bf16[27,128,256]{2,1,0:T(8,128)(2,1)S(1)} %copy-done, bf16[2,32,128,128]{3,2,1,0:T(8,128)(2,1)} %input_gradient.2.refs_3_), custom_call_target="tpu_custom_call", output_to_operand_aliasing={{}: (3, {})} | custom-call | tf_op jit(solution)/shard_map/input_gradient/pallas_call | solution.py:370
  77.1 2.0 %collective-permute-done.21 = bf16[2,2,1,1,1,8,2304]{6,5,3,2,1,0,4:T(8,128)(2,1)S(1)} collective-permute-done((bf16[2,2,1,1,1,8,2304]{6,5,3,2,1,0,4:T(8,128)(2,1)S(1)}, bf16[2,2,1,1,1,8,2304]{6,5,3,2,1,0,4:T(8,128)(2,1)S(1)}, u32[]{:S(2)}, u32[]{:S(2)}) %collective-permute-start.21) | collective-permute-done | bytes 147488 | tf_op jit(solution)/shard_map/ppermute | solution.py:62
  79.3 2.9 %collective-permute-start.23 = (bf16[1,1,1,1,1,8,3456]{6,5,3,2,1,0,4:T(8,128)(2,1)S(1)}, bf16[1,1,1,1,1,8,3456]{6,5,3,2,1,0,4:T(8,128)(2,1)S(1)}, u32[]{:S(2)}, u32[]{:S(2)}) collective-permute-start(bf16[1,1,1,1,1,8,3456]{6,5,3,2,1,0,4:T(8,128)(2,1)S(1)} %get-tuple-element.100), channel_id=1, source_target_pairs={{0,24},{1,25},{2,26},{3,27},{4,28},{5,29},{6,30},{7,31},{8,16},{9,... | collective-permute-start | bytes 165896 | tf_op jit(solution)/shard_map/ppermute | solution.py:62
  85.5 2.5 %collective-permute-done.25 = bf16[1,1,1,1,1,8,3456]{6,5,3,2,1,0,4:T(8,128)(2,1)S(1)} collective-permute-done((bf16[1,1,1,1,1,8,3456]{6,5,3,2,1,0,4:T(8,128)(2,1)S(1)}, bf16[1,1,1,1,1,8,3456]{6,5,3,2,1,0,4:T(8,128)(2,1)S(1)}, u32[]{:S(2)}, u32[]{:S(2)}) %collective-permute-start.25) | collective-permute-done | bytes 55328 | tf_op jit(solution)/shard_map/ppermute | solution.py:62
  (86 shorter events, 16.8 us)
Async XLA Ops:
  4.2 21.8 %all-to-all-start = ((bf16[8,32,1024]{2,1,0:T(8,128)(2,1)}), bf16[8,32,1024]{2,1,0:T(8,128)(2,1)S(1)}, u32[]{:S(2)}, u32[]{:S(2)}) async-start(bf16[8,32,1024]{2,1,0:T(8,128)(2,1)} %bitcast.31), calls=%async_computation | async-start | bytes 1048576 | tf_op jit(solution)/shard_map/all_to_all | solution.py:469
  12.1 3.2 %collective-permute-start.3 = (bf16[2,8,32,64]{3,2,1,0:T(8,128)(2,1)S(1)}, bf16[2,8,32,64]{3,2,1,0:T(8,128)(2,1)S(1)}, u32[]{:S(2)}, u32[]{:S(2)}) collective-permute-start(bf16[2,8,32,64]{3,2,1,0:T(8,128)(2,1)S(1)} %pad_maximum_fusion.1), channel_id=1, source_target_pairs={{1,0},{2,1},{3,2},{5,4},{6,5},{7,6},{9,8},{10,9},{11,10},{13,12},{... | collective-permute-start | bytes 196616 | tf_op jit(solution)/shard_map/ppermute | solution.py:24
  25.9 4.2 %collective-permute-start.5 = (bf16[8,32,64]{2,1,0:T(8,128)(2,1)S(1)}, bf16[8,32,64]{2,1,0:T(8,128)(2,1)S(1)}, u32[]{:S(2)}, u32[]{:S(2)}) collective-permute-start(bf16[8,32,64]{2,1,0:T(8,128)(2,1)S(1)} %slice.32), channel_id=1, source_target_pairs={{0,1},{1,0},{2,3},{3,2},{4,5},{5,4},{6,7},{7,6},{8,9},{9,8},{10,11... | collective-permute-start | bytes 98312 | tf_op jit(solution)/shard_map/ppermute | solution.py:499
  26.0 4.1 %collective-permute-start.4 = (bf16[8,32,64]{2,1,0:T(8,128)(2,1)S(1)}, bf16[8,32,64]{2,1,0:T(8,128)(2,1)S(1)}, u32[]{:S(2)}, u32[]{:S(2)}) collective-permute-start(bf16[8,32,64]{2,1,0:T(8,128)(2,1)S(1)} %slice.32), channel_id=1, source_target_pairs={{0,3},{1,2},{2,1},{3,0},{4,7},{5,6},{6,5},{7,4},{8,11},{9,10},{10,... | collective-permute-start | bytes 98312 | tf_op jit(solution)/shard_map/ppermute | solution.py:499
  28.4 3.7 %collective-permute-start.1 = (f32[32,4]{1,0:T(8,128)S(1)}, f32[32,4]{1,0:T(8,128)S(1)}, u32[]{:S(2)}, u32[]{:S(2)}) collective-permute-start(f32[32,4]{1,0:T(8,128)S(1)} %copy.35.refs_0_), channel_id=1, source_target_pairs={{0,2},{1,3},{2,0},{3,1},{4,6},{5,7},{6,4},{7,5},{8,10},{9,11},{10,... | collective-permute-start | bytes 1544 | tf_op jit(solution)/shard_map/ppermute | solution.py:30
  32.8 7.4 %collective-permute-start.6 = (bf16[272,128]{1,0:T(8,128)(2,1)S(1)}, bf16[272,128]{1,0:T(8,128)(2,1)S(1)}, u32[]{:S(2)}, u32[]{:S(2)}) collective-permute-start(bf16[272,128]{1,0:T(8,128)(2,1)S(1)} %get-tuple-element.53), channel_id=1, source_target_pairs={{0,4},{4,0},{8,12},{12,8},{16,20},{20,16},{24,28},{28,24},{1,5},{5... | collective-permute-start | bytes 208904 | tf_op jit(solution)/shard_map/ppermute | solution.py:531
  34.4 7.3 %collective-permute-start.7 = (bf16[272,128]{1,0:T(8,128)(2,1)S(1)}, bf16[272,128]{1,0:T(8,128)(2,1)S(1)}, u32[]{:S(2)}, u32[]{:S(2)}) collective-permute-start(bf16[272,128]{1,0:T(8,128)(2,1)S(1)} %get-tuple-element.54), channel_id=1, source_target_pairs={{0,8},{4,12},{8,0},{12,4},{16,24},{20,28},{24,16},{28,20},{1,9},{5... | collective-permute-start | bytes 208904 | tf_op jit(solution)/shard_map/ppermute | solution.py:531
  34.4 9.7 %collective-permute-start.8 = (bf16[272,128]{1,0:T(8,128)(2,1)S(1)}, bf16[272,128]{1,0:T(8,128)(2,1)S(1)}, u32[]{:S(2)}, u32[]{:S(2)}) collective-permute-start(bf16[272,128]{1,0:T(8,128)(2,1)S(1)} %get-tuple-element.55), channel_id=1, source_target_pairs={{0,12},{4,8},{8,4},{12,0},{16,28},{20,24},{24,20},{28,16},{1,13},{... | collective-permute-start | bytes 208904 | tf_op jit(solution)/shard_map/ppermute | solution.py:531
  36.4 10.3 %collective-permute-start.9 = (bf16[272,128]{1,0:T(8,128)(2,1)S(1)}, bf16[272,128]{1,0:T(8,128)(2,1)S(1)}, u32[]{:S(2)}, u32[]{:S(2)}) collective-permute-start(bf16[272,128]{1,0:T(8,128)(2,1)S(1)} %get-tuple-element.56), channel_id=1, source_target_pairs={{0,16},{4,20},{8,24},{12,28},{16,0},{20,4},{24,8},{28,12},{1,17},{... | collective-permute-start | bytes 208904 | tf_op jit(solution)/shard_map/ppermute | solution.py:531
  36.5 12.8 %collective-permute-start.10 = (bf16[272,128]{1,0:T(8,128)(2,1)S(1)}, bf16[272,128]{1,0:T(8,128)(2,1)S(1)}, u32[]{:S(2)}, u32[]{:S(2)}) collective-permute-start(bf16[272,128]{1,0:T(8,128)(2,1)S(1)} %get-tuple-element.57), channel_id=1, source_target_pairs={{0,20},{4,16},{8,28},{12,24},{16,4},{20,0},{24,12},{28,8},{1,21},{... | collective-permute-start | bytes 208904 | tf_op jit(solution)/shard_map/ppermute | solution.py:531
  40.2 9.2 %collective-permute-start.11 = (bf16[272,128]{1,0:T(8,128)(2,1)S(1)}, bf16[272,128]{1,0:T(8,128)(2,1)S(1)}, u32[]{:S(2)}, u32[]{:S(2)}) collective-permute-start(bf16[272,128]{1,0:T(8,128)(2,1)S(1)} %get-tuple-element.58), channel_id=1, source_target_pairs={{0,24},{4,28},{8,16},{12,20},{16,8},{20,12},{24,0},{28,4},{1,25},{... | collective-permute-start | bytes 208904 | tf_op jit(solution)/shard_map/ppermute | solution.py:531
  41.7 7.7 %collective-permute-start.12 = (bf16[272,128]{1,0:T(8,128)(2,1)S(1)}, bf16[272,128]{1,0:T(8,128)(2,1)S(1)}, u32[]{:S(2)}, u32[]{:S(2)}) collective-permute-start(bf16[272,128]{1,0:T(8,128)(2,1)S(1)} %get-tuple-element.59), channel_id=1, source_target_pairs={{0,28},{4,24},{8,20},{12,16},{16,12},{20,8},{24,4},{28,0},{1,29},{... | collective-permute-start | bytes 208904 | tf_op jit(solution)/shard_map/ppermute | solution.py:531
  49.4 13.3 %collective-permute-start.13 = (bf16[8,272,128]{2,1,0:T(8,128)(2,1)S(1)}, bf16[8,272,128]{2,1,0:T(8,128)(2,1)S(1)}, u32[]{:S(2)}, u32[]{:S(2)}) collective-permute-start(bf16[8,272,128]{2,1,0:T(8,128)(2,1)S(1)} %place_blocks.1.grads_ref.refs_0_), channel_id=1, source_target_pairs={{4,0},{8,4},{12,8},{16,12},{20,16},{24,20},{28,24},{5,1},{9,5},{13... | collective-permute-start | bytes 1671176 | tf_op jit(solution)/shard_map/ppermute | solution.py:24
  56.4 8.0 %collective-permute-start.18 = (bf16[128,1152]{1,0:T(8,128)(2,1)}, bf16[128,1152]{1,0:T(8,128)(2,1)S(1)}, u32[]{:S(2)}, u32[]{:S(2)}) collective-permute-start(bf16[128,1152]{1,0:T(8,128)(2,1)} %get-tuple-element.80), channel_id=1, source_target_pairs={{0,1},{1,0},{2,3},{3,2},{4,5},{5,4},{6,7},{7,6},{8,9},{9,8},{10,11... | collective-permute-start | bytes 884744 | tf_op jit(solution)/shard_map/ppermute | solution.py:74
  56.4 8.1 %collective-permute-start.15 = (bf16[64,1152]{1,0:T(8,128)(2,1)}, bf16[64,1152]{1,0:T(8,128)(2,1)S(1)}, u32[]{:S(2)}, u32[]{:S(2)}) collective-permute-start(bf16[64,1152]{1,0:T(8,128)(2,1)} %get-tuple-element.76), channel_id=1, source_target_pairs={{0,3},{1,2},{2,1},{3,0},{4,7},{5,6},{6,5},{7,4},{8,11},{9,10},{10,... | collective-permute-start | bytes 442376 | tf_op jit(solution)/shard_map/ppermute | solution.py:74
  57.9 8.0 %collective-permute-start.16 = (bf16[64,1152]{1,0:T(8,128)(2,1)}, bf16[64,1152]{1,0:T(8,128)(2,1)S(1)}, u32[]{:S(2)}, u32[]{:S(2)}) collective-permute-start(bf16[64,1152]{1,0:T(8,128)(2,1)} %get-tuple-element.77), channel_id=1, source_target_pairs={{0,2},{1,3},{2,0},{3,1},{4,6},{5,7},{6,4},{7,5},{8,10},{9,11},{10,... | collective-permute-start | bytes 442376 | tf_op jit(solution)/shard_map/ppermute | solution.py:74
  58.5 7.4 %collective-permute-start.17 = (bf16[64,1152]{1,0:T(8,128)(2,1)}, bf16[64,1152]{1,0:T(8,128)(2,1)S(1)}, u32[]{:S(2)}, u32[]{:S(2)}) collective-permute-start(bf16[64,1152]{1,0:T(8,128)(2,1)} %get-tuple-element.78), channel_id=1, source_target_pairs={{0,1},{1,0},{2,3},{3,2},{4,5},{5,4},{6,7},{7,6},{8,9},{9,8},{10,11... | collective-permute-start | bytes 442376 | tf_op jit(solution)/shard_map/ppermute | solution.py:74
  66.1 10.4 %collective-permute-start.22 = (bf16[2,2,1,1,1,8,1152]{6,5,3,2,1,0,4:T(8,128)(2,1)S(1)}, bf16[2,2,1,1,1,8,1152]{6,5,3,2,1,0,4:T(8,128)(2,1)S(1)}, u32[]{:S(2)}, u32[]{:S(2)}) collective-permute-start(bf16[2,2,1,1,1,8,1152]{6,5,3,2,1,0,4:T(8,128)(2,1)S(1)} %constant_dynamic-slice_fusion.3), channel_id=1, source_target_pairs={{0,4},{1,5},{2,6},{3,7},{4,0},{5,1},{6,2},{7,3},{8,12},{9,13},{10,... | collective-permute-start | bytes 221192 | tf_op jit(solution)/shard_map/ppermute | solution.py:62
  69.4 7.7 %collective-permute-start.19 = (bf16[2,2,1,1,1,8,2304]{6,5,3,2,1,0,4:T(8,128)(2,1)S(1)}, bf16[2,2,1,1,1,8,2304]{6,5,3,2,1,0,4:T(8,128)(2,1)S(1)}, u32[]{:S(2)}, u32[]{:S(2)}) collective-permute-start(bf16[2,2,1,1,1,8,2304]{6,5,3,2,1,0,4:T(8,128)(2,1)S(1)} %get-tuple-element.97), channel_id=1, source_target_pairs={{0,6},{1,7},{2,4},{3,5},{4,2},{5,3},{6,0},{7,1},{8,14},{9,15},{10,... | collective-permute-start | bytes 442376 | tf_op jit(solution)/shard_map/ppermute | solution.py:62
  70.3 8.8 %collective-permute-start.21 = (bf16[2,2,1,1,1,8,2304]{6,5,3,2,1,0,4:T(8,128)(2,1)S(1)}, bf16[2,2,1,1,1,8,2304]{6,5,3,2,1,0,4:T(8,128)(2,1)S(1)}, u32[]{:S(2)}, u32[]{:S(2)}) collective-permute-start(bf16[2,2,1,1,1,8,2304]{6,5,3,2,1,0,4:T(8,128)(2,1)S(1)} %get-tuple-element.98), channel_id=1, source_target_pairs={{0,4},{1,5},{2,6},{3,7},{4,0},{5,1},{6,2},{7,3},{8,12},{9,13},{10,... | collective-permute-start | bytes 442376 | tf_op jit(solution)/shard_map/ppermute | solution.py:62
  72.3 6.8 %collective-permute-start.20 = (bf16[2,2,1,1,1,8,2304]{6,5,3,2,1,0,4:T(8,128)(2,1)S(1)}, bf16[2,2,1,1,1,8,2304]{6,5,3,2,1,0,4:T(8,128)(2,1)S(1)}, u32[]{:S(2)}, u32[]{:S(2)}) collective-permute-start(bf16[2,2,1,1,1,8,2304]{6,5,3,2,1,0,4:T(8,128)(2,1)S(1)} %get-tuple-element.99), channel_id=1, source_target_pairs={{0,2},{1,3},{2,0},{3,1},{4,6},{5,7},{6,4},{7,5},{8,10},{9,11},{10,... | collective-permute-start | bytes 442376 | tf_op jit(solution)/shard_map/ppermute | solution.py:62
  79.3 6.2 %collective-permute-start.23 = (bf16[1,1,1,1,1,8,3456]{6,5,3,2,1,0,4:T(8,128)(2,1)S(1)}, bf16[1,1,1,1,1,8,3456]{6,5,3,2,1,0,4:T(8,128)(2,1)S(1)}, u32[]{:S(2)}, u32[]{:S(2)}) collective-permute-start(bf16[1,1,1,1,1,8,3456]{6,5,3,2,1,0,4:T(8,128)(2,1)S(1)} %get-tuple-element.100), channel_id=1, source_target_pairs={{0,24},{1,25},{2,26},{3,27},{4,28},{5,29},{6,30},{7,31},{8,16},{9,... | collective-permute-start | bytes 165896 | tf_op jit(solution)/shard_map/ppermute | solution.py:62
  82.2 5.8 %collective-permute-start.25 = (bf16[1,1,1,1,1,8,3456]{6,5,3,2,1,0,4:T(8,128)(2,1)S(1)}, bf16[1,1,1,1,1,8,3456]{6,5,3,2,1,0,4:T(8,128)(2,1)S(1)}, u32[]{:S(2)}, u32[]{:S(2)}) collective-permute-start(bf16[1,1,1,1,1,8,3456]{6,5,3,2,1,0,4:T(8,128)(2,1)S(1)} %get-tuple-element.101), channel_id=1, source_target_pairs={{0,16},{1,17},{2,18},{3,19},{4,20},{5,21},{6,22},{7,23},{8,24},{9,... | collective-permute-start | bytes 165896 | tf_op jit(solution)/shard_map/ppermute | solution.py:62
  82.7 5.3 %collective-permute-start.24 = (bf16[1,1,1,1,1,8,3456]{6,5,3,2,1,0,4:T(8,128)(2,1)S(1)}, bf16[1,1,1,1,1,8,3456]{6,5,3,2,1,0,4:T(8,128)(2,1)S(1)}, u32[]{:S(2)}, u32[]{:S(2)}) collective-permute-start(bf16[1,1,1,1,1,8,3456]{6,5,3,2,1,0,4:T(8,128)(2,1)S(1)} %get-tuple-element.102), channel_id=1, source_target_pairs={{0,8},{1,9},{2,10},{3,11},{4,12},{5,13},{6,14},{7,15},{8,0},{9,1},... | collective-permute-start | bytes 165896 | tf_op jit(solution)/shard_map/ppermute | solution.py:62
  (13 other events, 65.0 us)
